TPU v7x, 128 devices: a whole 4x4x4 slice. The times are simulated.
128 devices in a mesh: blk: 8 (over x, z_hi), fsdp: 16 (over z_lo, y, core).
Axes of the slice: x: 4, y: 4, z: 4 (z_hi: 2, z_lo: 2; z = z_hi * 2 + z_lo), core: 2. Of those that a mesh axis runs over, the one named last changes fastest.
Arguments:
- tokens: bfloat16 [8, 8192, 2048], P('blk', 'fsdp'), may hold values from -21 to 21
- student_weight: float32 [8, 2560, 2048], P('blk', 'fsdp'), may hold values from -0.125 to 0.125
- snapshot: bfloat16 [8, 2560, 2048], P('blk', 'fsdp'), may hold values from -0.125 to 0.125
- moment_one: float32 [8, 2560, 2048], P('blk', 'fsdp'), may hold values from -0.6 to 0.6
- moment_two: float32 [8, 2560, 2048], P('blk', 'fsdp'), may hold values from 0.001 to 0.1
Outputs:
- new_weight: float32 [8, 2560, 2048], P('blk', 'fsdp')
- new_moment_one: float32 [8, 2560, 2048], P('blk', 'fsdp')
- new_moment_two: float32 [8, 2560, 2048], P('blk', 'fsdp')
All inputs are finite; a program needn't handle non-finite values.
Results may differ from a plain program's by a relative error of at most 0.0045.
The roundings to bfloat16 on the way count: a program that leaves them out, or rounds other values in their place, can miss the bound.
Values may be sent and summed in bfloat16 or wider, within the bound.
No kernel may reach another device: no remote copies, remote signals or barrier semaphores. Data moves between devices by JAX's collectives and lax.ppermute only.
A program may use at most 128 MiB of HBM per device.

v0:
```python
import math

import jax
import jax.numpy as jnp
from jax import lax
from jax.sharding import PartitionSpec as P

HEADS = 16
KVH = 4
HD = 128
SEQ = 256
STEP = 100


THETA = 500000.0
BETA_ONE = 0.9
BETA_TWO = 0.95
LEARN_RATE = 0.002
DECAY = 0.1
EPSILON = 1e-08
MASKED = -1e30


def shifted(value, axis, steps):
    count = lax.axis_size(axis)
    pairs = [(source, (source + steps) % count) for source in range(count)]
    return lax.ppermute(value, axis, pairs)


def rotary_tables(row_count, seq_len, head_size):
    positions = (jnp.arange(row_count) % seq_len).astype(jnp.float32)
    exponents = jnp.arange(head_size // 2).astype(jnp.float32) * (2.0 / head_size)
    frequency = THETA ** (-exponents)
    angles = positions[:, None] * frequency[None, :]
    return (jnp.cos(angles)[:, None, :], jnp.sin(angles)[:, None, :])


def rotate(vectors, cosine, sine_table, direction):
    row_count = vectors.shape[0]
    shaped = vectors.reshape(row_count, -1, HD)
    half_size = HD // 2
    front_half = shaped[..., :half_size]
    back_half = shaped[..., half_size:]
    turned = jnp.concatenate(
        [
            front_half * cosine - direction * back_half * sine_table,
            back_half * cosine + direction * front_half * sine_table,
        ],
        axis=-1,
    )
    return turned.reshape(row_count, -1)


def score_gradient(qk_student, qk_teacher):
    row_count = qk_student.shape[0]
    seq_count = row_count // SEQ
    group_size = HEADS // KVH
    inv_root = 1.0 / math.sqrt(HD)
    causal = jnp.arange(SEQ)[:, None] >= jnp.arange(SEQ)[None, :]

    def split_heads(packed):
        queries = packed[:, : HEADS * HD].reshape(seq_count, SEQ, KVH, group_size, HD)
        key_rows = packed[:, HEADS * HD :].reshape(seq_count, SEQ, KVH, HD)
        return (queries, key_rows)

    def log_probs(queries, key_rows):
        scores = (
            jnp.einsum("bikrd,bjkd->bkrij", queries, key_rows, preferred_element_type=jnp.float32)
            * inv_root
        )
        scores = jnp.where(causal, scores, MASKED)
        return jax.nn.log_softmax(scores, axis=-1)

    query_student, key_student = split_heads(qk_student)
    query_teacher, key_teacher = split_heads(qk_teacher)
    spread = jnp.exp(log_probs(query_student, key_student)) - jnp.exp(
        log_probs(query_teacher, key_teacher)
    )
    rounded = (jnp.where(causal, spread, 0.0) / HEADS).astype(jnp.bfloat16)
    query_grad = (
        jnp.einsum("bkrij,bjkd->bikrd", rounded, key_student, preferred_element_type=jnp.float32)
        * inv_root
    )
    key_grad = (
        jnp.einsum("bkrij,bikrd->bjkd", rounded, query_student, preferred_element_type=jnp.float32)
        * inv_root
    )
    return jnp.concatenate(
        [query_grad.reshape(row_count, HEADS * HD), key_grad.reshape(row_count, KVH * HD)], axis=1
    )


def project_with(rows_in, shard_rows):
    return lax.dot_general(
        rows_in, shard_rows, (((1,), (1,)), ((), ())), preferred_element_type=jnp.float32
    )


def per_device(tokens, student_weight, snapshot, moment_one, moment_two):
    own_tokens = tokens[0]
    master = student_weight[0]
    student_copy = master.astype(jnp.bfloat16)
    cosine, sine_table = rotary_tables(own_tokens.shape[0], SEQ, HD)
    teacher_piece = shifted(snapshot, "blk", 1)[0]
    raw_student = project_with(own_tokens, lax.all_gather(student_copy, "fsdp", axis=0, tiled=True))
    raw_teacher = project_with(
        own_tokens, lax.all_gather(teacher_piece, "fsdp", axis=0, tiled=True)
    )
    qk_teacher = rotate(raw_teacher, cosine, sine_table, 1.0).astype(jnp.bfloat16)
    qk_student = rotate(raw_student, cosine, sine_table, 1.0).astype(jnp.bfloat16)
    proj_grad = rotate(score_gradient(qk_student, qk_teacher), cosine, sine_table, -1.0).astype(
        jnp.bfloat16
    )
    gradient = lax.psum_scatter(
        lax.dot_general(
            proj_grad, own_tokens, (((0,), (0,)), ((), ())), preferred_element_type=jnp.float32
        ),
        "fsdp",
        scatter_dimension=0,
        tiled=True,
    )
    first_new = BETA_ONE * moment_one[0] + (1.0 - BETA_ONE) * gradient
    second_new = BETA_TWO * moment_two[0] + (1.0 - BETA_TWO) * gradient * gradient
    step_dir = (
        first_new
        / (1.0 - BETA_ONE**STEP)
        / (jnp.sqrt(second_new / (1.0 - BETA_TWO**STEP)) + EPSILON)
    )
    updated = master - LEARN_RATE * (step_dir + DECAY * master)
    return (updated[None], first_new[None], second_new[None])


def solution(mesh):
    return jax.shard_map(
        per_device,
        mesh=mesh,
        in_specs=(
            P("blk", "fsdp", None),
            P("blk", "fsdp", None),
            P("blk", "fsdp", None),
            P("blk", "fsdp", None),
            P("blk", "fsdp", None),
        ),
        out_specs=(P("blk", "fsdp", None), P("blk", "fsdp", None), P("blk", "fsdp", None)),
        check_vma=False,
    )
```

profile of v0, /device:TPU:1, one launch (start us, length us, event | category | flops | bytes accessed | tf_op | source)
XLA Modules:
  0.0 398.9 jit_solution(11334622367761333918)
XLA Ops:
  9.7 4.5 %collective-permute-start = (bf16[1,160,2048]{2,1,0:T(8,128)(2,1)S(1)}, bf16[1,160,2048]{2,1,0:T(8,128)(2,1)S(1)}, u32[]{:S(2)}, u32[]{:S(2)}) collective-permute-start(bf16[1,160,2048]{2,1,0:T(8,128)(2,1)S(1)} %copy-done.5), channel_id=1, source_target_pairs={{0,16},{16,32},{32,48},{48,64},{64,80},{80,96},{96,112},{112,0},{1... | collective-permute-start | bytes 1966088 | tf_op jit(solution)/shard_map/ppermute | solution.py:27
  14.2 18.2 %collective-permute-done = bf16[1,160,2048]{2,1,0:T(8,128)(2,1)S(1)} collective-permute-done((bf16[1,160,2048]{2,1,0:T(8,128)(2,1)S(1)}, bf16[1,160,2048]{2,1,0:T(8,128)(2,1)S(1)}, u32[]{:S(2)}, u32[]{:S(2)}) %collective-permute-start) | collective-permute-done | bytes 655392 | tf_op jit(solution)/shard_map/ppermute | solution.py:27
  33.9 47.4 %all-gather.4.cloned.1.call-done = bf16[2560,2048]{1,0:T(8,128)(2,1)} async-done(((bf16[160,2048]{1,0:T(8,128)(2,1)}), bf16[2560,2048]{1,0:T(8,128)(2,1)}) %all-gather.4.cloned.1.call-update) | async-done | bytes 10485776 | tf_op jit(solution)/shard_map/all_gather | solution.py:105
  81.3 9.8 %fusion.28 = f32[512,20,128]{0,2,1:T(8,128)} fusion(bf16[20,128,2048]{2,1,0:T(8,128)(2,1)} %bitcast.116, bf16[1,512,2048]{2,1,0:T(8,128)(2,1)S(1)} %copy-done), kind=kOutput, calls=%fused_computation.43 | convolution fusion | flops 5368709120 | bytes 17825792 | tf_op jit(solution)/shard_map/dot_general | solution.py:94
  91.1 54.6 %all-gather.6.cloned.1.call-done = bf16[1,2560,2048]{2,1,0:T(8,128)(2,1)} async-done(((bf16[1,160,2048]{2,1,0:T(8,128)(2,1)}), bf16[1,2560,2048]{2,1,0:T(8,128)(2,1)}) %all-gather.6.cloned.1.call-update) | async-done | bytes 10485776 | tf_op jit(solution)/shard_map/all_gather | solution.py:107
  145.8 8.6 %fusion.26 = f32[512,20,128]{0,2,1:T(8,128)S(1)} fusion(bf16[20,128,2048]{2,1,0:T(8,128)(2,1)} %bitcast.117, bf16[1,512,2048]{2,1,0:T(8,128)(2,1)S(1)} %copy-done), kind=kOutput, calls=%fused_computation.41 | convolution fusion | flops 5368709120 | bytes 17825792 | tf_op jit(solution)/shard_map/dot_general | solution.py:94
  160.1 4.0 reshape.133
  166.6 6.1 %fusion.24 = f32[2,4,256,256,4]{3,2,4,1,0:T(8,128)} fusion(bf16[2,256,4,4,128]{1,0,4,3,2:T(2,128)(2,1)} %reshape.133, bf16[2,256,4,128,1]{3,2,1,0,4:T(4,128)(2,1)S(1)} %bitcast.115), kind=kOutput, calls=%fused_computation.39 | convolution fusion | flops 536870912 | bytes 11010048 | tf_op jit(solution)/shard_map/bikrd,bjkd->bkrij/dot_general | solution.py:68
  172.7 12.7 %fusion = f32[2,4,4,256,256]{3,4,2,1,0:T(8,128)} fusion(f32[2,4,256,256,4]{3,2,4,1,0:T(8,128)} %fusion.24, pred[256,256]{0,1:T(8,128)(4,1)S(1)} %iota_compare_fusion), kind=kOutput, calls=%fused_computation | output fusion | flops 10502654 | bytes 16842752 | tf_op jit(solution)/shard_map/jit(log_softmax)/reduce_sum | solution.py:72
  185.5 11.6 %fusion.15 = f32[2,4,4,256,256]{3,4,2,1,0:T(8,128)} fusion(f32[2,4,256,256,4]{3,2,4,1,0:T(8,128)} %fusion.24, pred[256,256]{0,1:T(8,128)(4,1)S(1)} %iota_compare_fusion), kind=kOutput, calls=%fused_computation.21 | output fusion | flops 10494207 | bytes 16842752 | tf_op jit(solution)/shard_map/jit(log_softmax)/sub | solution.py:72
  197.1 4.0 %reshape.131 = bf16[2,256,4,4,128]{1,0,4,3,2:T(2,128)(2,1)} reshape(bf16[512,2048]{0,1:T(8,128)(2,1)} %slice.43) | data formatting | bytes 4194304 | tf_op jit(solution)/shard_map/reshape | solution.py:62
  203.9 2.9 fusion.32
  206.8 5.0 %fusion.13 = f32[2,4,4,256,256]{3,4,2,1,0:T(8,128)} fusion(f32[2,4,256,256,4]{3,2,4,1,0:T(8,128)S(1)} %fusion.32, pred[256,256]{0,1:T(8,128)(4,1)S(1)} %iota_compare_fusion), kind=kOutput, calls=%fused_computation.19 | output fusion | flops 10494207 | bytes 16842752 | tf_op jit(solution)/shard_map/jit(log_softmax)/sub | solution.py:72
  211.8 13.6 %fusion.8 = bf16[2,4,4,256,256]{3,4,2,1,0:T(8,128)(2,1)S(1)} fusion(f32[2,4,4,256,256]{3,4,2,1,0:T(8,128)} %fusion.15, f32[2,4,4,256,256]{3,4,2,1,0:T(8,128)} %fusion, f32[2,4,4,256,256]{3,4,2,1,0:T(8,128)} %fusion.13, pred[256,256]{0,1:T(8,128)(4,1)S(1)} %iota_compare_fusion), kind=kOutput, calls=%fused_computation.9 | output fusion | flops 12591359 | bytes 29425664 | tf_op jit(solution)/shard_map/jit(log_softmax)/reduce_sum | solution.py:72
  225.4 2.5 fusion.42
  227.9 2.8 multiply_bitcast_fusion
  230.6 5.4 %copy.22 = f32[2,256,4,4,128]{4,3,2,1,0:T(4,128)} copy(f32[2,256,4,4,128]{1,4,3,2,0:T(8,128)} %multiply_bitcast_fusion) | data formatting | bytes 8388608 | tf_op jit(solution)/shard_map/mul | solution.py:81
  236.1 5.6 %reshape.120 = f32[512,2048]{1,0:T(8,128)} reshape(f32[2,256,4,4,128]{4,3,2,1,0:T(4,128)} %copy.22) | data formatting | bytes 8388608 | tf_op jit(solution)/shard_map/reshape | solution.py:89
  244.3 4.9 %pad_maximum_fusion = f32[512,2560]{1,0:T(8,128)} fusion(f32[512,512]{1,0:T(8,128)S(1)} %bitcast.111, f32[512,2048]{1,0:T(8,128)} %reshape.120), kind=kLoop, calls=%fused_computation.22 | loop fusion | flops 1310720 | bytes 10485760 | tf_op jit(solution)/shard_map/concatenate | solution.py:88
  249.2 5.9 %copy.26 = f32[512,2560]{0,1:T(8,128)} copy(f32[512,2560]{1,0:T(8,128)} %pad_maximum_fusion) | data formatting | bytes 10485760 | tf_op jit(solution)/shard_map/concatenate | solution.py:88
  255.2 3.4 subtract_convert_fusion
  258.9 10.0 %fusion.30 = f32[2560,2048]{1,0:T(8,128)} fusion(bf16[512,2560]{0,1:T(8,128)(2,1)S(1)} %bitcast.113, bf16[1,512,2048]{2,1,0:T(8,128)(2,1)S(1)} %copy-done), kind=kOutput, calls=%fused_computation.45 | convolution fusion | flops 5368709120 | bytes 25690112 | tf_op jit(solution)/shard_map/dot_general | solution.py:115
  268.8 118.6 %reduce-scatter.2.cloned.1.call-done = f32[160,2048]{1,0:T(8,128)} async-done(((f32[2560,2048]{1,0:T(8,128)}), f32[160,2048]{1,0:T(8,128)}) %reduce-scatter.2.cloned.1.call-update) | async-done | bytes 1310736 | tf_op jit(solution)/shard_map/reduce_scatter | solution.py:114
  387.4 5.0 %fusion.51 = (f32[1,160,2048]{2,1,0:T(8,128)}, f32[1,160,2048]{2,1,0:T(8,128)}, f32[1,160,2048]{2,1,0:T(8,128)}) fusion(f32[160,2048]{1,0:T(8,128)} %reduce-scatter.2.cloned.1.call-done, f32[1,160,2048]{2,1,0:T(8,128)} %param.10, f32[1,160,2048]{2,1,0:T(8,128)} %param.9, f32[1,160,2048]{2,1,0:T(8,128)S(1)} %copy-done.2), kind=kLoop, calls=%fused_computation.66 | loop fusion | flops 4915200 | bytes 9175040 | tf_op jit(solution)/shard_map/broadcast_in_dim | solution.py:130
  (42 shorter events, 18.0 us)
Async XLA Ops:
  7.2 74.2 %copy-start = (bf16[1,512,2048]{2,1,0:T(8,128)(2,1)S(1)}, bf16[1,512,2048]{2,1,0:T(8,128)(2,1)}, u32[]{:S(2)}) copy-start(bf16[1,512,2048]{2,1,0:T(8,128)(2,1)} %param.6) | copy-start | bytes 6291460
  7.2 2.5 copy-start.5
  7.2 74.1 %all-gather.4.cloned.1.call-start = ((), (), s32[]{:S(2)}) async-start(), calls=%async_computation.1 | async-start | bytes 11141120 | tf_op jit(solution)/shard_map/all_gather | solution.py:105
  9.7 136.1 %all-gather.6.cloned.1.call-start = ((), (), s32[]{:S(2)}) async-start(), calls=%async_computation.3 | async-start | bytes 11141120 | tf_op jit(solution)/shard_map/all_gather | solution.py:107
  9.7 22.7 %collective-permute-start = (bf16[1,160,2048]{2,1,0:T(8,128)(2,1)S(1)}, bf16[1,160,2048]{2,1,0:T(8,128)(2,1)S(1)}, u32[]{:S(2)}, u32[]{:S(2)}) collective-permute-start(bf16[1,160,2048]{2,1,0:T(8,128)(2,1)S(1)} %copy-done.5), channel_id=1, source_target_pairs={{0,16},{16,32},{32,48},{48,64},{64,80},{80,96},{96,112},{112,0},{1... | collective-permute-start | bytes 1966088 | tf_op jit(solution)/shard_map/ppermute | solution.py:27
  32.4 0.8 copy-start.4
  33.3 354.1 %reduce-scatter.2.cloned.1.call-start = ((), (), s32[]{:S(2)}) async-start(), calls=%async_computation.2 | async-start | bytes 22282240 | tf_op jit(solution)/shard_map/reduce_scatter | solution.py:114
  145.8 8.6 %slice-start = ((s8[5242880]{0:T(1024)(128)(4,1)}), s8[4194304]{0:T(1024)(128)(4,1)S(1)}, s32[]{:S(2)}) async-start(s8[5242880]{0:T(1024)(128)(4,1)} %bitcast.109), calls=%async_computation.4 | async-start | bytes 8388608
  145.8 8.6 %slice-start.1 = ((s8[5242880]{0:T(1024)(128)(4,1)}), s8[1048576]{0:T(1024)(128)(4,1)S(1)}, s32[]{:S(2)}) async-start(s8[5242880]{0:T(1024)(128)(4,1)} %bitcast.109), calls=%async_computation.5 | async-start | bytes 2097152
  211.8 13.6 %copy-start.1 = (bf16[2,256,4,4,128]{1,0,4,3,2:T(2,128)(2,1)S(1)}, bf16[2,256,4,4,128]{1,0,4,3,2:T(2,128)(2,1)}, u32[]{:S(2)}) copy-start(bf16[2,256,4,4,128]{1,0,4,3,2:T(2,128)(2,1)} %reshape.131) | copy-start | bytes 6291460
  236.1 5.6 %copy-start.3 = (f32[2,256,4,128]{1,3,2,0:T(8,128)S(1)}, f32[2,256,4,128]{1,3,2,0:T(8,128)}, u32[]{:S(2)}) copy-start(f32[2,256,4,128]{1,3,2,0:T(8,128)} %fusion.42) | copy-start | bytes 3145732
  268.8 118.6 %copy-start.2 = (f32[1,160,2048]{2,1,0:T(8,128)S(1)}, f32[1,160,2048]{2,1,0:T(8,128)}, u32[]{:S(2)}) copy-start(f32[1,160,2048]{2,1,0:T(8,128)} %param.7) | copy-start | bytes 3932164
Sparse Core Ops, SparseCore 0:
  10.3 70.9 all-gather.3
  83.6 62.1 all-gather.5
  269.0 118.4 reduce-scatter.1
where the time goes:
time: 400 us; the launch traced here: 399 us
  waiting for transfers between devices  239 us (60%)
  other arithmetic  62 us (16%)
  matrix products  42.6 us (11%)
  local copies, waits for them, and re-layouts  36.9 us (9%)
  between operations  13.9 us (3%)
  starting transfers between devices  4.62 us (1%)
    reduce_scatter x1, waiting for transfers between devices, per_device(): lax.psum_scatter(lax.dot_general(proj_grad, own_tokens, (((0,), (0,)), ((...  119 us
    all_gather x1, waiting for transfers between devices, per_device(): lax.all_gather(teacher_piece, 'fsdp', axis=0, tiled=True)  54.6 us
    all_gather x1, waiting for transfers between devices, per_device(): lax.all_gather(student_copy, 'fsdp', axis=0, tiled=True)  47.4 us
    reduce_sum x2, other arithmetic, log_probs(): return jax.nn.log_softmax(scores, axis=-1)  26.3 us
    dot_general x2, matrix products, project_with(): lax.dot_general(rows_in, shard_rows, (((1,), (1,)), ((), ())), preferred_...  18.4 us
    ppermute x1, waiting for transfers between devices, shifted(): return lax.ppermute(value, axis, pairs)  18.2 us
    sub x2, other arithmetic, log_probs(): return jax.nn.log_softmax(scores, axis=-1)  16.6 us
    dot_general x1, matrix products, per_device(): lax.dot_general(proj_grad, own_tokens, (((0,), (0,)), ((), ())), preferre...  9.96 us
  transfers between devices with their start and end apart: 4, of which 4 were waited for; matrix products, arithmetic and copies ran while one was open for 3% of the time, Pallas kernels for 0%

commit v1 on v0

v1 whole, which is shorter than its diff:
```python
import math

import jax
import jax.numpy as jnp
import numpy as np
from jax import lax
from jax.experimental import pallas as pl
from jax.experimental.pallas import tpu as pltpu
from jax.sharding import PartitionSpec as P

HEADS = 16
KVH = 4
HD = 128
SEQ = 256
STEP = 100
D = 2048
THETA = 500000.0
BETA_ONE = 0.9
BETA_TWO = 0.95
LEARN_RATE = 0.002
DECAY = 0.1
EPSILON = 1e-08
MASKED = -1e30

BF = jnp.bfloat16
F32 = jnp.float32
SHARD = 160
UNIT = 32
HALF = HD // 2
KVROWS = 640
FAR = 96
INV_ROOT = 1.0 / math.sqrt(HD)

ARRANGED = [[5 * d + k for k in range(5)] for d in range(16)]
ARRANGED[12] = [60, 61, 64, 62, 63]
ARRANGED[14] = [72, 73, 74, 70, 71]
ALIGNED = [list(units) for units in ARRANGED]
ALIGNED[6] = [30, 31, 64, 70, 71]
ALIGNED[7] = [65, 66, 67, 68, 69]
ALIGNED[12] = [60, 61, 32, 62, 63]
ALIGNED[13] = [35, 36, 37, 38, 39]
ALIGNED[14] = [72, 73, 74, 33, 34]
OWNER = list(range(16))
OWNER[7], OWNER[13] = 13, 7


def head_position(unit, plane):
    if unit < 64:
        return (unit // 16 - 2 * plane) * 20 + unit % 16
    return ((unit - 64) // 4 - 2 * plane) * 20 + 16 + (unit - 64) % 4


def build_tables():
    order = np.array([[u - 5 * d for u in ARRANGED[d]] for d in range(16)], np.int32)
    inverse = np.argsort(order, axis=1).astype(np.int32)
    place = np.zeros((16, 40), np.int32)
    for d in range(16):
        z, y, c = d // 8, d % 8 // 2, d % 2
        row = []
        for r in range(2):
            for step in range(4):
                other = 8 * z + 2 * ((y + step) % 4) + (c ^ r)
                row += [head_position(u, z) for u in ALIGNED[other]]
        assert sorted(row) == list(range(40))
        place[d] = row
    return order, inverse, place


ORDER, INVERSE, PLACE = build_tables()


def pairs_of(function):
    out = []
    for d in range(16):
        z, y, c = function(d // 8, d % 8 // 2, d % 2)
        out.append((d, z % 2 * 8 + y % 4 * 2 + c % 2))
    return out


TO_CORE = pairs_of(lambda z, y, c: (z, y, c + 1))
TO_PLANE = pairs_of(lambda z, y, c: (z + 1, y, c))
UP = pairs_of(lambda z, y, c: (z, y + 1, c))
DOWN = pairs_of(lambda z, y, c: (z, y - 1, c))
SWAP_A = [(7, 13), (13, 7), (6, 14), (14, 6)]
SWAP_PART = [(6, 14), (14, 6)]
SWAP_B = [(6, 12), (12, 6)]


def send(value, pairs):
    return lax.ppermute(value, "fsdp", pairs)


def send_next(value, pairs):
    return lax.ppermute(
        value,
        ("blk", "fsdp"),
        [(g * 16 + a, (g + 1) % 8 * 16 + b) for g in range(8) for a, b in pairs],
    )


def params(mib):
    return pltpu.CompilerParams(vmem_limit_bytes=mib * 2**20)


def arrange_kernel(order, weight, snapshot, weight_out, snapshot_out):
    weight_out[...] = weight[...].astype(BF)
    snapshot_out[...] = snapshot[...]


def arrange(order, weight, snapshot):
    picked = pl.BlockSpec((UNIT, D), lambda k, order: (order[k], 0))
    straight = pl.BlockSpec((UNIT, D), lambda k, order: (k, 0))
    return pl.pallas_call(
        arrange_kernel,
        grid_spec=pltpu.PrefetchScalarGridSpec(
            num_scalar_prefetch=1, grid=(5,), in_specs=[picked, picked], out_specs=[straight, straight]
        ),
        out_shape=[jax.ShapeDtypeStruct((SHARD, D), BF)] * 2,
        compiler_params=params(32),
        name="arrange",
    )(order, weight, snapshot)


PIECES = ((0, SHARD, 0), (1, SHARD, 0), (2, SHARD, 0), (3, SHARD, 0))


def copies(place, arrays, held, sems):
    out = []
    for at, array in enumerate(arrays):
        for k in range(5):
            n = at * 5 + k
            row = pl.multiple_of(place[n] * UNIT, UNIT)
            out.append(
                pltpu.make_async_copy(
                    array.at[pl.ds(k * UNIT, UNIT)], held.at[pl.ds(row, UNIT)], sems.at[n]
                )
            )
    return out


def load_weight(place, arrays, held, sems):
    @pl.when(pl.program_id(0) == 0)
    def _():
        for copy in copies(place, arrays, held, sems):
            copy.start()
        for copy in copies(place, arrays, held, sems):
            copy.wait()


def rotated(raw, cosine, sine):
    front, back = raw[:HALF], raw[HALF:]
    return jnp.concatenate([front * cosine - back * sine, back * cosine + front * sine], axis=0)


def project(held, rows_in, cosine, sine, kv):
    raw = lax.dot_general(
        held[kv * KVROWS : (kv + 1) * KVROWS, :],
        rows_in,
        (((1,), (1,)), ((), ())),
        preferred_element_type=F32,
    )
    return [rotated(raw[h * HD : (h + 1) * HD], cosine, sine).astype(BF) for h in range(5)]


def student_kernel(place, x, cosine, sine, *rest):
    arrays, (out, held, sems) = rest[:8], rest[8:]
    load_weight(place, arrays, held, sems)
    for kv in range(2):
        for h, value in enumerate(project(held, x[...], cosine[...], sine[...], kv)):
            out[kv * KVROWS + h * HD : kv * KVROWS + (h + 1) * HD, :] = value


ANY = pl.BlockSpec(memory_space=pl.ANY)
TABLE = pl.BlockSpec((HALF, SEQ), lambda s, place: (0, 0))
ROWS = pl.BlockSpec((SEQ, D), lambda s, place: (s, 0))
COLUMNS = pl.BlockSpec((2 * KVROWS, SEQ), lambda s, place: (0, s))


def student_projection(place, x, cosine, sine, arrays):
    count = x.shape[0] // SEQ
    return pl.pallas_call(
        student_kernel,
        grid_spec=pltpu.PrefetchScalarGridSpec(
            num_scalar_prefetch=1,
            grid=(count,),
            in_specs=[ROWS, TABLE, TABLE] + [ANY] * 8,
            out_specs=COLUMNS,
            scratch_shapes=[pltpu.VMEM((2 * KVROWS, D), BF), pltpu.SemaphoreType.DMA((40,))],
        ),
        out_shape=jax.ShapeDtypeStruct((2 * KVROWS, x.shape[0]), BF),
        compiler_params=params(48),
        cost_estimate=pl.CostEstimate(
            flops=2 * x.shape[0] * 2 * KVROWS * D, bytes_accessed=9 * 2**20, transcendentals=0
        ),
        name="student_projection",
    )(place, x, cosine, sine, *arrays)


GRID_SCALE = INV_ROOT * math.log2(math.e)


def softmax_parts(scores, diagonal):
    scores = scores * GRID_SCALE
    low = scores.shape[0] - HD
    masked = jnp.where(diagonal, scores[low:], MASKED)
    if low:
        scores = jnp.concatenate([scores[:low], masked], axis=0)
    else:
        scores = masked
    power = jnp.exp2(scores - jnp.max(scores, axis=0, keepdims=True))
    return power, (1.0 / HEADS) / jnp.sum(power, axis=0, keepdims=True)


def dot(a, b, dims=((1,), (0,))):
    return lax.dot_general(a, b, (dims, ((), ())), preferred_element_type=F32)


def side_by_side(heads, half):
    return jnp.concatenate([q[:, half * HD : (half + 1) * HD] for q in heads], axis=1)


def attention_gradient(student, teacher, cosine, sine):
    key_s = student[4]
    rows_s, rows_t = key_s.T, teacher[4].T
    lane = lax.broadcasted_iota(jnp.int32, (HD, 4 * HD), 1) % HD
    diagonal = lax.broadcasted_iota(jnp.int32, (HD, 4 * HD), 0) <= lane
    query_parts, key_grad = [], None
    for half in range(2):
        extent = (half + 1) * HD
        q_s = side_by_side(student[:4], half)
        q_t = side_by_side(teacher[:4], half)
        power_s, inverse_s = softmax_parts(dot(rows_s[:extent], q_s), diagonal)
        power_t, inverse_t = softmax_parts(dot(rows_t[:extent], q_t), diagonal)
        spread = (power_s * inverse_s - power_t * inverse_t).astype(BF)
        query_parts.append(dot(key_s[:, :extent], spread))
        part = dot(q_s, spread, ((1,), (1,)))
        if half == 0:
            key_grad = part
        else:
            key_grad = jnp.concatenate([part[:, :HD] + key_grad, part[:, HD:]], axis=1)
    grads = [
        jnp.concatenate([p[:, h * HD : (h + 1) * HD] for p in query_parts], axis=1)
        for h in range(4)
    ] + [key_grad]
    return [rotated(g * INV_ROOT, cosine, -sine).astype(BF) for g in grads]


def gradient_kernel(place, x, qk_student, cosine, sine, *rest):
    arrays, (out, held, grads, sems) = rest[:8], rest[8:]
    load_weight(place, arrays, held, sems)
    for kv in range(2):
        teacher = project(held, x[...], cosine[...], sine[...], kv)
        base = kv * KVROWS
        student = [qk_student[base + h * HD : base + (h + 1) * HD, :] for h in range(5)]
        for h, value in enumerate(attention_gradient(student, teacher, cosine[...], sine[...])):
            grads[base + h * HD : base + (h + 1) * HD, :] = value
    for n in range(40):
        row = pl.multiple_of(place[n] * UNIT, UNIT)
        out[n * UNIT : (n + 1) * UNIT, :] = grads[pl.ds(row, UNIT), :]


def projection_gradient(place, x, qk_student, cosine, sine, arrays):
    count = x.shape[0] // SEQ
    return pl.pallas_call(
        gradient_kernel,
        grid_spec=pltpu.PrefetchScalarGridSpec(
            num_scalar_prefetch=1,
            grid=(count,),
            in_specs=[ROWS, COLUMNS, TABLE, TABLE] + [ANY] * 8,
            out_specs=COLUMNS,
            scratch_shapes=[
                pltpu.VMEM((2 * KVROWS, D), BF),
                pltpu.VMEM((2 * KVROWS, SEQ), BF),
                pltpu.SemaphoreType.DMA((40,)),
            ],
        ),
        out_shape=jax.ShapeDtypeStruct((2 * KVROWS, x.shape[0]), BF),
        compiler_params=params(56),
        cost_estimate=pl.CostEstimate(
            flops=6 * x.shape[0] * 2 * KVROWS * D, bytes_accessed=9 * 2**20, transcendentals=0
        ),
        name="projection_gradient",
    )(place, x, qk_student, cosine, sine, *arrays)


TILE = 512


def weight_kernel(first, count, own_a, own_b, other_a, other_b, xa, xb, ya, yb, *outs):
    lo, hi = first * SHARD, (first + count) * SHARD
    total = dot(own_a[lo:hi, :], xa[...])
    total += dot(own_b[lo:hi, :], xb[...])
    total += dot(other_a[lo:hi, :], ya[...])
    total += dot(other_b[lo:hi, :], yb[...])
    for n, out in enumerate(outs):
        out[...] = total[n * SHARD : (n + 1) * SHARD].astype(BF)


def weight_gradient(first, count, grads, tokens):
    whole = [pl.BlockSpec((KVROWS, 2 * SEQ), lambda t: (0, 0))] * 4
    return pl.pallas_call(
        lambda *refs: weight_kernel(first, count, *refs),
        grid=(D // TILE,),
        in_specs=whole + [pl.BlockSpec((2 * SEQ, TILE), lambda t: (0, t))] * 4,
        out_specs=[pl.BlockSpec((SHARD, TILE), lambda t: (0, t))] * count,
        out_shape=[jax.ShapeDtypeStruct((SHARD, D), BF)] * count,
        compiler_params=params(48),
        cost_estimate=pl.CostEstimate(
            flops=2 * count * SHARD * 8 * SEQ * D, bytes_accessed=12 * 2**20, transcendentals=0
        ),
        name="weight_gradient",
    )(*grads, *tokens)


def adam_kernel(table, b0, b1, b2, b3, part_a, part_b, weight, one, two, weight_out, one_out, two_out):
    k = pl.program_id(0)
    at = table[k]
    swapped = table[5]
    gradient = (b0[...].astype(F32) + b1[...].astype(F32)) + (
        b2[...].astype(F32) + b3[...].astype(F32)
    )
    take_a = jnp.logical_and(at >= 3, swapped % 2 == 1)
    take_b = jnp.logical_and(at == 2, swapped // 2 == 1)
    gradient = jnp.where(take_a, part_a[...], jnp.where(take_b, part_b[...], gradient))
    first_new = BETA_ONE * one[...] + (1.0 - BETA_ONE) * gradient
    second_new = BETA_TWO * two[...] + (1.0 - BETA_TWO) * gradient * gradient
    step_dir = (
        first_new
        / (1.0 - BETA_ONE**STEP)
        / (jnp.sqrt(second_new / (1.0 - BETA_TWO**STEP)) + EPSILON)
    )
    master = weight[...]
    weight_out[...] = master - LEARN_RATE * (step_dir + DECAY * master)
    one_out[...] = first_new
    two_out[...] = second_new


def adam(table, blocks, part_a, part_b, weight, one, two):
    picked = pl.BlockSpec((UNIT, D), lambda k, t: (t[k], 0))
    from_a = pl.BlockSpec((UNIT, D), lambda k, t: (jnp.maximum(t[k] - 3, 0), 0))
    from_b = pl.BlockSpec((UNIT, D), lambda k, t: (0, 0))
    straight = pl.BlockSpec((UNIT, D), lambda k, t: (k, 0))
    return pl.pallas_call(
        adam_kernel,
        grid_spec=pltpu.PrefetchScalarGridSpec(
            num_scalar_prefetch=1,
            grid=(5,),
            in_specs=[picked] * 4 + [from_a, from_b] + [straight] * 3,
            out_specs=[straight] * 3,
        ),
        out_shape=[jax.ShapeDtypeStruct((SHARD, D), F32)] * 3,
        compiler_params=params(32),
        name="adam",
    )(table, *blocks, part_a, part_b, weight, one, two)


def rotary_tables():
    positions = jnp.arange(SEQ).astype(F32)
    exponents = jnp.arange(HALF).astype(F32) * (2.0 / HD)
    frequency = THETA ** (-exponents)
    angles = frequency[:, None] * positions[None, :]
    return jnp.cos(angles), jnp.sin(angles)


def ring_gather(shard):
    below = send(shard, UP)
    above = send(shard, DOWN)
    far_low = send(below[:FAR], UP)
    far_high = send(above[FAR:], DOWN)
    far = jnp.concatenate([far_low, far_high], axis=0)
    own = [shard, above, far, below]
    return own + [send(piece, TO_CORE) for piece in own]


def per_device(tokens, student_weight, snapshot, moment_one, moment_two):
    own_tokens = tokens[0]
    master = student_weight[0]
    me = lax.axis_index("fsdp")
    order = jnp.asarray(ORDER)[me]
    place = jnp.asarray(PLACE)[me]
    cosine, sine = rotary_tables()

    student_shard, teacher_shard = arrange(order, master, snapshot[0])
    row = lax.broadcasted_iota(jnp.int32, (SHARD, 1), 0)
    whole = (me == 7) | (me == 13)
    mask_a = whole | (((me == 6) | (me == 14)) & (row >= 96))
    mask_b = ((me == 6) | (me == 12)) & (row >= 64) & (row < 96)

    main = send_next(teacher_shard, list(enumerate(OWNER)))
    tail = send_next(teacher_shard[96:], SWAP_PART)
    middle = send_next(teacher_shard[64:96], SWAP_B)
    swap_a = send(student_shard, SWAP_A)
    swap_b = send(student_shard[64:96], SWAP_B)

    def widen(part, low):
        return jnp.pad(part, ((low, SHARD - low - part.shape[0]), (0, 0)))

    student = jnp.where(mask_a, swap_a, jnp.where(mask_b, widen(swap_b, 64), student_shard))
    mask_tail = ((me == 6) | (me == 14)) & (row >= 96)
    teacher = jnp.where(mask_tail, widen(tail, 96), jnp.where(mask_b, widen(middle, 64), main))

    plane_tokens = send(own_tokens, TO_PLANE)
    student_rows = ring_gather(student)
    teacher_rows = ring_gather(teacher)
    core_tokens = send(own_tokens, TO_CORE)
    far_tokens = send(plane_tokens, TO_CORE)

    grads, others = [], []
    for x in (own_tokens, plane_tokens):
        qk_student = student_projection(place, x, cosine, sine, student_rows)
        grad = projection_gradient(place, x, qk_student, cosine, sine, teacher_rows)
        grads.append(grad)
        others.append(send(grad[KVROWS:], TO_CORE))

    parts = grads + others
    all_tokens = (own_tokens, plane_tokens, core_tokens, far_tokens)

    def to_owner(block, step):
        return send(
            block,
            [
                (d, OWNER[d // 8 * 8 + (d % 8 // 2 + step) % 4 * 2 + d % 2])
                for d in range(16)
            ],
        )

    (block_two,) = weight_gradient(2, 1, parts, all_tokens)
    got_two = to_owner(block_two, 2)
    block_zero, block_one = weight_gradient(0, 2, parts, all_tokens)
    (block_three,) = weight_gradient(3, 1, parts, all_tokens)
    got_one = to_owner(block_one, 1)
    got_three = to_owner(block_three, 3)
    got_zero = to_owner(block_zero, 0)
    blocks = [got_zero, got_one, got_two, got_three]

    reduced = sum(block[64:].astype(F32) for block in blocks)
    part_b = send(reduced[:32], SWAP_B)
    part_a = send(reduced[32:], SWAP_PART)
    in_a = ((me == 6) | (me == 14)).astype(jnp.int32)
    in_b = ((me == 6) | (me == 12)).astype(jnp.int32)
    table = jnp.concatenate([jnp.asarray(INVERSE)[me], (in_a + 2 * in_b)[None]])
    updated = adam(table, blocks, part_a, part_b, master, moment_one[0], moment_two[0])
    return tuple(value[None] for value in updated)


def solution(mesh):
    spec = P("blk", "fsdp", None)
    return jax.shard_map(
        per_device,
        mesh=mesh,
        in_specs=(spec,) * 5,
        out_specs=(spec,) * 3,
        check_vma=False,
    )
```

time: 400 us -> 230 us (0.57)
  the two profiles are of different devices: /device:TPU:1 before, /device:TPU:26 now
where the time goes in v1:
time: 230 us; the launch traced here: 229 us
  Pallas kernels  83.7 us (36%)
  waiting for transfers between devices  82.9 us (36%)
  starting transfers between devices  43.4 us (19%)
  local copies, waits for them, and re-layouts  17.2 us (7%)
    ppermute x29, waiting for transfers between devices, send(): return lax.ppermute(value, 'fsdp', pairs)  71.6 us
    ppermute x29, starting transfers between devices, send(): return lax.ppermute(value, 'fsdp', pairs)  35 us
    pallas_call x2, Pallas kernels, projection_gradient(): pl.pallas_call(gradient_kernel, grid_spec=pltpu.PrefetchScalarGridSpec(nu...  33.8 us
    pallas_call x2, Pallas kernels, student_projection(): pl.pallas_call(student_kernel, grid_spec=pltpu.PrefetchScalarGridSpec(num...  28.1 us
    pallas_call x3, Pallas kernels, weight_gradient(): pl.pallas_call(lambda *refs: weight_kernel(first, count, *refs), grid=(D...  15.7 us
    ppermute x3, waiting for transfers between devices, send_next(): lax.ppermute(value, ('blk', 'fsdp'), [(g * 16 + a, (g + 1) % 8 * 16 + b)...  11.3 us
    unnamed x48, local copies, waits for them, and re-layouts  9.49 us
    ppermute x3, starting transfers between devices, send_next(): lax.ppermute(value, ('blk', 'fsdp'), [(g * 16 + a, (g + 1) % 8 * 16 + b)...  8.41 us
  transfers between devices with their start and end apart: 32, of which 14 were waited for; matrix products, arithmetic and copies ran while one was open for 3% of the time, Pallas kernels for 31%

profile of v1, /device:TPU:26, one launch (start us, length us, event | category | flops | bytes accessed | tf_op | source)
XLA Modules:
  0.0 229.4 jit_solution(12625234768250186909)
XLA Ops:
  4.5 3.9 %collective-permute-start.12 = (bf16[160,2048]{1,0:T(8,128)(2,1)S(1)}, bf16[160,2048]{1,0:T(8,128)(2,1)S(1)}, u32[]{:S(2)}, u32[]{:S(2)}) collective-permute-start(bf16[160,2048]{1,0:T(8,128)(2,1)S(1)} %get-tuple-element.11), channel_id=1, source_target_pairs={{0,16},{1,17},{2,18},{3,19},{4,20},{5,21},{6,22},{7,29},{8,24},{9,... | collective-permute-start | bytes 1966088 | tf_op jit(solution)/shard_map/ppermute | solution.py:94
  8.4 2.9 %collective-permute-start = (bf16[160,2048]{1,0:T(8,128)(2,1)S(1)}, bf16[160,2048]{1,0:T(8,128)(2,1)S(1)}, u32[]{:S(2)}, u32[]{:S(2)}) collective-permute-start(bf16[160,2048]{1,0:T(8,128)(2,1)S(1)} %get-tuple-element.10), channel_id=1, source_target_pairs={{7,13},{13,7},{6,14},{14,6},{23,29},{29,23},{22,30},{30,22},{39,45... | collective-permute-start | bytes 1966088 | tf_op jit(solution)/shard_map/ppermute | solution.py:90
  11.4 2.5 %collective-permute-start.10 = (bf16[64,2048]{1,0:T(8,128)(2,1)S(1)}, bf16[64,2048]{1,0:T(8,128)(2,1)S(1)}, u32[]{:S(2)}, u32[]{:S(2)}) collective-permute-start(bf16[64,2048]{1,0:T(8,128)(2,1)S(1)} %slice.48), channel_id=1, source_target_pairs={{6,30},{14,22},{22,46},{30,38},{38,62},{46,54},{54,78},{62,70},{70... | collective-permute-start | bytes 786440 | tf_op jit(solution)/shard_map/ppermute | solution.py:94
  16.5 6.1 %collective-permute-start.1 = (bf16[32,2048]{1,0:T(8,128)(2,1)}, bf16[32,2048]{1,0:T(8,128)(2,1)S(1)}, u32[]{:S(2)}, u32[]{:S(2)}) collective-permute-start(bf16[32,2048]{1,0:T(8,128)(2,1)} %slice.45), channel_id=1, source_target_pairs={{6,12},{12,6},{22,28},{28,22},{38,44},{44,38},{54,60},{60,54},{70,... | collective-permute-start | bytes 393224 | tf_op jit(solution)/shard_map/ppermute | solution.py:90
  22.7 2.9 %collective-permute-done.11 = bf16[32,2048]{1,0:T(8,128)(2,1)S(1)} collective-permute-done((bf16[32,2048]{1,0:T(8,128)(2,1)S(1)}, bf16[32,2048]{1,0:T(8,128)(2,1)S(1)}, u32[]{:S(2)}, u32[]{:S(2)}) %collective-permute-start.11) | collective-permute-done | bytes 131104 | tf_op jit(solution)/shard_map/ppermute | solution.py:94
  27.3 8.5 %collective-permute-done.10 = bf16[64,2048]{1,0:T(8,128)(2,1)S(1)} collective-permute-done((bf16[64,2048]{1,0:T(8,128)(2,1)S(1)}, bf16[64,2048]{1,0:T(8,128)(2,1)S(1)}, u32[]{:S(2)}, u32[]{:S(2)}) %collective-permute-start.10) | collective-permute-done | bytes 262176 | tf_op jit(solution)/shard_map/ppermute | solution.py:94
  35.8 3.6 %collective-permute-done = bf16[160,2048]{1,0:T(8,128)(2,1)S(1)} collective-permute-done((bf16[160,2048]{1,0:T(8,128)(2,1)S(1)}, bf16[160,2048]{1,0:T(8,128)(2,1)S(1)}, u32[]{:S(2)}, u32[]{:S(2)}) %collective-permute-start) | collective-permute-done | bytes 655392 | tf_op jit(solution)/shard_map/ppermute | solution.py:90
  44.0 13.6 %collective-permute-done.3.rest_3_ = bf16[160,2048]{1,0:T(8,128)(2,1)S(1)} collective-permute-done((bf16[160,2048]{1,0:T(8,128)(2,1)S(1)}, bf16[160,2048]{1,0:T(8,128)(2,1)S(1)}, u32[]{:S(2)}, u32[]{:S(2)}) %collective-permute-start.3) | collective-permute-done | bytes 655392 | tf_op jit(solution)/shard_map/ppermute | solution.py:90
  59.8 8.2 %collective-permute-done.14.rest_3_ = bf16[160,2048]{1,0:T(8,128)(2,1)S(1)} collective-permute-done((bf16[160,2048]{1,0:T(8,128)(2,1)S(1)}, bf16[160,2048]{1,0:T(8,128)(2,1)S(1)}, u32[]{:S(2)}, u32[]{:S(2)}) %collective-permute-start.14) | collective-permute-done | bytes 655392 | tf_op jit(solution)/shard_map/ppermute | solution.py:90
  69.7 3.5 %collective-permute-done.4 = bf16[96,2048]{1,0:T(8,128)(2,1)S(1)} collective-permute-done((bf16[96,2048]{1,0:T(8,128)(2,1)S(1)}, bf16[96,2048]{1,0:T(8,128)(2,1)S(1)}, u32[]{:S(2)}, u32[]{:S(2)}) %collective-permute-start.4) | collective-permute-done | bytes 393248 | tf_op jit(solution)/shard_map/ppermute | solution.py:90
  73.3 7.4 %collective-permute-done.16 = bf16[64,2048]{1,0:T(8,128)(2,1)S(1)} collective-permute-done((bf16[64,2048]{1,0:T(8,128)(2,1)S(1)}, bf16[64,2048]{1,0:T(8,128)(2,1)S(1)}, u32[]{:S(2)}, u32[]{:S(2)}) %collective-permute-start.16) | collective-permute-done | bytes 262176 | tf_op jit(solution)/shard_map/ppermute | solution.py:90
  84.9 14.1 %student_projection.2.qk_student = bf16[1280,512]{1,0:T(8,128)(2,1)} custom-call(s32[40]{0:T(128)S(1)} %fusion.1.place, bf16[512,2048]{1,0:T(8,128)(2,1)} %bitcast.3.x.refs_4_, f32[64,256]{1,0:T(8,128)S(1)} %get-tuple-element.18.cosine, f32[64,256]{1,0:T(8,128)S(1)} %get-tuple-element.17.sine, bf16[160,2048]{1,0:T(8,128)(2,1)S(1)} %get-tuple-element.20.rest_0_, ...), custom_call_target="tpu_custom_call" | custom-call | flops 2684354560 | bytes 9437184 | tf_op jit(solution)/shard_map/student_projection/pallas_call | solution.py:181
  101.8 16.9 %projection_gradient.2.refs_0_ = bf16[1280,512]{1,0:T(8,128)(2,1)} custom-call(s32[40]{0:T(128)} %copy-done.13, bf16[512,2048]{1,0:T(8,128)(2,1)} %bitcast.3.x.refs_4_, bf16[1280,512]{1,0:T(8,128)(2,1)} %student_projection.2.qk_student, f32[64,256]{1,0:T(8,128)} %copy-done.11, f32[64,256]{1,0:T(8,128)} %copy-done.9, bf16[160,2048]{1,0:T(8,128)(2,1)} %copy-done.16, ...), custom_call_target="tpu_custom_call" | custom-call | flops 8053063680 | bytes 9437184 | tf_op jit(solution)/shard_map/projection_gradient/pallas_call | solution.py:264
  118.7 2.0 slice.64
  121.0 14.1 %student_projection.3.qk_student = bf16[1280,512]{1,0:T(8,128)(2,1)} custom-call(s32[40]{0:T(128)S(1)} %copy-done.14, bf16[512,2048]{1,0:T(8,128)(2,1)} %copy-done.15, f32[64,256]{1,0:T(8,128)S(1)} %copy-done.12, f32[64,256]{1,0:T(8,128)S(1)} %copy-done.10, bf16[160,2048]{1,0:T(8,128)(2,1)S(1)} %get-tuple-element.20.rest_0_, ...), custom_call_target="tpu_custom_call" | custom-call | flops 2684354560 | bytes 9437184 | tf_op jit(solution)/shard_map/student_projection/pallas_call | solution.py:181
  135.1 16.9 %projection_gradient.3.refs_1_ = bf16[1280,512]{1,0:T(8,128)(2,1)} custom-call(s32[40]{0:T(128)} %copy-done.13, bf16[512,2048]{1,0:T(8,128)(2,1)} %copy-done.15, bf16[1280,512]{1,0:T(8,128)(2,1)} %student_projection.3.qk_student, f32[64,256]{1,0:T(8,128)} %copy-done.11, f32[64,256]{1,0:T(8,128)} %copy-done.9, bf16[160,2048]{1,0:T(8,128)(2,1)} %copy-done.16, ...), custom_call_target="tpu_custom_call" | custom-call | flops 8053063680 | bytes 9437184 | tf_op jit(solution)/shard_map/projection_gradient/pallas_call | solution.py:264
  156.8 5.8 %weight_gradient.3 = (bf16[160,2048]{1,0:T(8,128)(2,1)S(1)}, bf16[160,2048]{1,0:T(8,128)(2,1)S(1)}) custom-call(bf16[1280,512]{1,0:T(8,128)(2,1)S(1)} %copy-done, bf16[1280,512]{1,0:T(8,128)(2,1)S(1)} %copy-done.1, bf16[640,512]{1,0:T(8,128)(2,1)S(1)} %collective-permute-done.22.refs_2_, bf16[640,512]{1,0:T(8,128)(2,1)S(1)} %collective-permute-done.23.refs_3_, ...), custom_call_target="tpu_custom_call" | custom-call | flops 2684354560 | bytes 12582912 | tf_op jit(solution)/shard_map/weight_gradient/pallas_call | solution.py:301
  164.1 4.9 %weight_gradient.4 = bf16[160,2048]{1,0:T(8,128)(2,1)S(1)} custom-call(bf16[1280,512]{1,0:T(8,128)(2,1)S(1)} %copy-done, bf16[1280,512]{1,0:T(8,128)(2,1)S(1)} %copy-done.1, bf16[640,512]{1,0:T(8,128)(2,1)S(1)} %collective-permute-done.22.refs_2_, bf16[640,512]{1,0:T(8,128)(2,1)S(1)} %collective-permute-done.23.refs_3_, bf16[512,2048]{1,0:T(8,128)(2,1)} %bitcast.3.x.refs_4_, ...), custom_call_target="tpu_custom_call" | custom-call | flops 1342177280 | bytes 12582912 | tf_op jit(solution)/shard_map/weight_gradient/pallas_call | solution.py:301
  170.4 4.9 %weight_gradient.5 = bf16[160,2048]{1,0:T(8,128)(2,1)S(1)} custom-call(bf16[1280,512]{1,0:T(8,128)(2,1)S(1)} %copy-done, bf16[1280,512]{1,0:T(8,128)(2,1)S(1)} %copy-done.1, bf16[640,512]{1,0:T(8,128)(2,1)S(1)} %collective-permute-done.22.refs_2_, bf16[640,512]{1,0:T(8,128)(2,1)S(1)} %collective-permute-done.23.refs_3_, bf16[512,2048]{1,0:T(8,128)(2,1)} %bitcast.3.x.refs_4_, ...), custom_call_target="tpu_custom_call" | custom-call | flops 1342177280 | bytes 12582912 | tf_op jit(solution)/shard_map/weight_gradient/pallas_call | solution.py:301
  176.5 16.0 %collective-permute-done.27.b1 = bf16[160,2048]{1,0:T(8,128)(2,1)S(1)} collective-permute-done((bf16[160,2048]{1,0:T(8,128)(2,1)S(1)}, bf16[160,2048]{1,0:T(8,128)(2,1)S(1)}, u32[]{:S(2)}, u32[]{:S(2)}) %collective-permute-start.27) | collective-permute-done | bytes 655392 | tf_op jit(solution)/shard_map/ppermute | solution.py:90
  192.5 7.2 %collective-permute-done.29.b3 = bf16[160,2048]{1,0:T(8,128)(2,1)S(1)} collective-permute-done((bf16[160,2048]{1,0:T(8,128)(2,1)S(1)}, bf16[160,2048]{1,0:T(8,128)(2,1)S(1)}, u32[]{:S(2)}, u32[]{:S(2)}) %collective-permute-start.29) | collective-permute-done | bytes 655392 | tf_op jit(solution)/shard_map/ppermute | solution.py:90
  200.8 9.4 %collective-permute-start.30 = (f32[64,2048]{1,0:T(8,128)}, f32[64,2048]{1,0:T(8,128)}, u32[]{:S(2)}, u32[]{:S(2)}) collective-permute-start(f32[64,2048]{1,0:T(8,128)} %slice.70), channel_id=1, source_target_pairs={{6,14},{14,6},{22,30},{30,22},{38,46},{46,38},{54,62},{62,54},{70,... | collective-permute-start | bytes 1572872 | tf_op jit(solution)/shard_map/ppermute | solution.py:90
  213.6 6.7 %collective-permute-done.31.part_b = f32[32,2048]{1,0:T(8,128)S(1)} collective-permute-done((f32[32,2048]{1,0:T(8,128)}, f32[32,2048]{1,0:T(8,128)S(1)}, u32[]{:S(2)}, u32[]{:S(2)}) %collective-permute-start.31) | collective-permute-done | bytes 262176 | tf_op jit(solution)/shard_map/ppermute | solution.py:90
  224.1 5.3 %adam.1 = (f32[160,2048]{1,0:T(8,128)}, f32[160,2048]{1,0:T(8,128)}, f32[160,2048]{1,0:T(8,128)}) custom-call(s32[6]{0:T(128)S(1)} %pad_add_fusion.table, bf16[160,2048]{1,0:T(8,128)(2,1)S(1)} %collective-permute-done.26.b0, bf16[160,2048]{1,0:T(8,128)(2,1)S(1)} %collective-permute-done.27.b1, bf16[160,2048]{1,0:T(8,128)(2,1)S(1)} %collective-permute-done.28.b2, ...), custom_call_target="tpu_custom_call" | custom-call | tf_op jit(solution)/shard_map/adam/pallas_call | solution.py:343
  (121 shorter events, 40.7 us)
Async XLA Ops:
  4.5 31.3 %collective-permute-start.12 = (bf16[160,2048]{1,0:T(8,128)(2,1)S(1)}, bf16[160,2048]{1,0:T(8,128)(2,1)S(1)}, u32[]{:S(2)}, u32[]{:S(2)}) collective-permute-start(bf16[160,2048]{1,0:T(8,128)(2,1)S(1)} %get-tuple-element.11), channel_id=1, source_target_pairs={{0,16},{1,17},{2,18},{3,19},{4,20},{5,21},{6,22},{7,29},{8,24},{9,... | collective-permute-start | bytes 1966088 | tf_op jit(solution)/shard_map/ppermute | solution.py:94
  8.4 31.0 %collective-permute-start = (bf16[160,2048]{1,0:T(8,128)(2,1)S(1)}, bf16[160,2048]{1,0:T(8,128)(2,1)S(1)}, u32[]{:S(2)}, u32[]{:S(2)}) collective-permute-start(bf16[160,2048]{1,0:T(8,128)(2,1)S(1)} %get-tuple-element.10), channel_id=1, source_target_pairs={{7,13},{13,7},{6,14},{14,6},{23,29},{29,23},{22,30},{30,22},{39,45... | collective-permute-start | bytes 1966088 | tf_op jit(solution)/shard_map/ppermute | solution.py:90
  11.4 24.4 %collective-permute-start.10 = (bf16[64,2048]{1,0:T(8,128)(2,1)S(1)}, bf16[64,2048]{1,0:T(8,128)(2,1)S(1)}, u32[]{:S(2)}, u32[]{:S(2)}) collective-permute-start(bf16[64,2048]{1,0:T(8,128)(2,1)S(1)} %slice.48), channel_id=1, source_target_pairs={{6,30},{14,22},{22,46},{30,38},{38,62},{46,54},{54,78},{62,70},{70... | collective-permute-start | bytes 786440 | tf_op jit(solution)/shard_map/ppermute | solution.py:94
  39.9 17.7 %collective-permute-start.3 = (bf16[160,2048]{1,0:T(8,128)(2,1)S(1)}, bf16[160,2048]{1,0:T(8,128)(2,1)S(1)}, u32[]{:S(2)}, u32[]{:S(2)}) collective-permute-start(bf16[160,2048]{1,0:T(8,128)(2,1)S(1)} %get-tuple-element.20.rest_0_), channel_id=1, source_target_pairs={{0,2},{1,3},{2,4},{3,5},{4,6},{5,7},{6,0},{7,1},{8,10},{9,11},{10,... | collective-permute-start | bytes 1966088 | tf_op jit(solution)/shard_map/ppermute | solution.py:90
  39.9 19.0 %collective-permute-start.2 = (bf16[160,2048]{1,0:T(8,128)(2,1)S(1)}, bf16[160,2048]{1,0:T(8,128)(2,1)S(1)}, u32[]{:S(2)}, u32[]{:S(2)}) collective-permute-start(bf16[160,2048]{1,0:T(8,128)(2,1)S(1)} %get-tuple-element.20.rest_0_), channel_id=1, source_target_pairs={{0,6},{1,7},{2,0},{3,1},{4,2},{5,3},{6,4},{7,5},{8,14},{9,15},{10,... | collective-permute-start | bytes 1966088 | tf_op jit(solution)/shard_map/ppermute | solution.py:90
  42.0 26.1 %collective-permute-start.14 = (bf16[160,2048]{1,0:T(8,128)(2,1)S(1)}, bf16[160,2048]{1,0:T(8,128)(2,1)S(1)}, u32[]{:S(2)}, u32[]{:S(2)}) collective-permute-start(bf16[160,2048]{1,0:T(8,128)(2,1)S(1)} %get-tuple-element.19.rest_0_), channel_id=1, source_target_pairs={{0,2},{1,3},{2,4},{3,5},{4,6},{5,7},{6,0},{7,1},{8,10},{9,11},{10,... | collective-permute-start | bytes 1966088 | tf_op jit(solution)/shard_map/ppermute | solution.py:90
  43.2 24.8 %collective-permute-start.13 = (bf16[160,2048]{1,0:T(8,128)(2,1)S(1)}, bf16[160,2048]{1,0:T(8,128)(2,1)S(1)}, u32[]{:S(2)}, u32[]{:S(2)}) collective-permute-start(bf16[160,2048]{1,0:T(8,128)(2,1)S(1)} %get-tuple-element.19.rest_0_), channel_id=1, source_target_pairs={{0,6},{1,7},{2,0},{3,1},{4,2},{5,3},{6,4},{7,5},{8,14},{9,15},{10,... | collective-permute-start | bytes 1966088 | tf_op jit(solution)/shard_map/ppermute | solution.py:90
  57.6 15.5 %collective-permute-start.4 = (bf16[96,2048]{1,0:T(8,128)(2,1)S(1)}, bf16[96,2048]{1,0:T(8,128)(2,1)S(1)}, u32[]{:S(2)}, u32[]{:S(2)}) collective-permute-start(bf16[96,2048]{1,0:T(8,128)(2,1)S(1)} %slice.60), channel_id=1, source_target_pairs={{0,2},{1,3},{2,4},{3,5},{4,6},{5,7},{6,0},{7,1},{8,10},{9,11},{10,... | collective-permute-start | bytes 1179656 | tf_op jit(solution)/shard_map/ppermute | solution.py:90
  58.9 40.6 %collective-permute-start.21 = (bf16[512,2048]{1,0:T(8,128)(2,1)}, bf16[512,2048]{1,0:T(8,128)(2,1)S(1)}, u32[]{:S(2)}, u32[]{:S(2)}) collective-permute-start(bf16[512,2048]{1,0:T(8,128)(2,1)} %bitcast.3.x.refs_4_), channel_id=1, source_target_pairs={{0,8},{1,9},{2,10},{3,11},{4,12},{5,13},{6,14},{7,15},{8,0},{9,1},... | collective-permute-start | bytes 6291464 | tf_op jit(solution)/shard_map/ppermute | solution.py:90
  58.9 14.2 %collective-permute-start.5 = (bf16[64,2048]{1,0:T(8,128)(2,1)S(1)}, bf16[64,2048]{1,0:T(8,128)(2,1)S(1)}, u32[]{:S(2)}, u32[]{:S(2)}) collective-permute-start(bf16[64,2048]{1,0:T(8,128)(2,1)S(1)} %slice.61), channel_id=1, source_target_pairs={{0,6},{1,7},{2,0},{3,1},{4,2},{5,3},{6,4},{7,5},{8,14},{9,15},{10,... | collective-permute-start | bytes 786440 | tf_op jit(solution)/shard_map/ppermute | solution.py:90
  68.0 13.3 %collective-permute-start.6 = (bf16[160,2048]{1,0:T(8,128)(2,1)S(1)}, bf16[160,2048]{1,0:T(8,128)(2,1)S(1)}, u32[]{:S(2)}, u32[]{:S(2)}) collective-permute-start(bf16[160,2048]{1,0:T(8,128)(2,1)S(1)} %get-tuple-element.20.rest_0_), channel_id=1, source_target_pairs={{0,1},{1,0},{2,3},{3,2},{4,5},{5,4},{6,7},{7,6},{8,9},{9,8},{10,11... | collective-permute-start | bytes 1966088 | tf_op jit(solution)/shard_map/ppermute | solution.py:90
  68.1 12.7 %collective-permute-start.15 = (bf16[96,2048]{1,0:T(8,128)(2,1)S(1)}, bf16[96,2048]{1,0:T(8,128)(2,1)S(1)}, u32[]{:S(2)}, u32[]{:S(2)}) collective-permute-start(bf16[96,2048]{1,0:T(8,128)(2,1)S(1)} %slice.62), channel_id=1, source_target_pairs={{0,2},{1,3},{2,4},{3,5},{4,6},{5,7},{6,0},{7,1},{8,10},{9,11},{10,... | collective-permute-start | bytes 1179656 | tf_op jit(solution)/shard_map/ppermute | solution.py:90
  81.3 17.7 %collective-permute-start.17 = (bf16[160,2048]{1,0:T(8,128)(2,1)S(1)}, bf16[160,2048]{1,0:T(8,128)(2,1)S(1)}, u32[]{:S(2)}, u32[]{:S(2)}) collective-permute-start(bf16[160,2048]{1,0:T(8,128)(2,1)S(1)} %get-tuple-element.19.rest_0_), channel_id=1, source_target_pairs={{0,1},{1,0},{2,3},{3,2},{4,5},{5,4},{6,7},{7,6},{8,9},{9,8},{10,11... | collective-permute-start | bytes 1966088 | tf_op jit(solution)/shard_map/ppermute | solution.py:90
  81.4 18.4 %collective-permute-start.18 = (bf16[160,2048]{1,0:T(8,128)(2,1)S(1)}, bf16[160,2048]{1,0:T(8,128)(2,1)S(1)}, u32[]{:S(2)}, u32[]{:S(2)}) collective-permute-start(bf16[160,2048]{1,0:T(8,128)(2,1)S(1)} %collective-permute-done.13.rest_1_), channel_id=1, source_target_pairs={{0,1},{1,0},{2,3},{3,2},{4,5},{5,4},{6,7},{7,6},{8,9},{9,8},{10,11... | collective-permute-start | bytes 1966088 | tf_op jit(solution)/shard_map/ppermute | solution.py:90
  82.8 17.0 %collective-permute-start.20 = (bf16[160,2048]{1,0:T(8,128)(2,1)S(1)}, bf16[160,2048]{1,0:T(8,128)(2,1)S(1)}, u32[]{:S(2)}, u32[]{:S(2)}) collective-permute-start(bf16[160,2048]{1,0:T(8,128)(2,1)S(1)} %collective-permute-done.14.rest_3_), channel_id=1, source_target_pairs={{0,1},{1,0},{2,3},{3,2},{4,5},{5,4},{6,7},{7,6},{8,9},{9,8},{10,11... | collective-permute-start | bytes 1966088 | tf_op jit(solution)/shard_map/ppermute | solution.py:90
  83.8 18.0 %collective-permute-start.19 = (bf16[160,2048]{1,0:T(8,128)(2,1)S(1)}, bf16[160,2048]{1,0:T(8,128)(2,1)}, u32[]{:S(2)}, u32[]{:S(2)}) collective-permute-start(bf16[160,2048]{1,0:T(8,128)(2,1)S(1)} %constant_dynamic-update-slice_fusion.2.rest_2_), channel_id=1, source_target_pairs={{0,1},{1,0},{2,3},{3,2},{4,5},{5,4},{6,7},{7,6},{8,9},{9,8},{10,11... | collective-permute-start | bytes 1966088 | tf_op jit(solution)/shard_map/ppermute | solution.py:90
  99.1 54.5 %collective-permute-start.24 = (bf16[512,2048]{1,0:T(8,128)(2,1)}, bf16[512,2048]{1,0:T(8,128)(2,1)}, u32[]{:S(2)}, u32[]{:S(2)}) collective-permute-start(bf16[512,2048]{1,0:T(8,128)(2,1)} %bitcast.3.x.refs_4_), channel_id=1, source_target_pairs={{0,1},{1,0},{2,3},{3,2},{4,5},{5,4},{6,7},{7,6},{8,9},{9,8},{10,11... | collective-permute-start | bytes 6291464 | tf_op jit(solution)/shard_map/ppermute | solution.py:90
  99.5 55.9 %collective-permute-start.25 = (bf16[512,2048]{1,0:T(8,128)(2,1)S(1)}, bf16[512,2048]{1,0:T(8,128)(2,1)}, u32[]{:S(2)}, u32[]{:S(2)}) collective-permute-start(bf16[512,2048]{1,0:T(8,128)(2,1)S(1)} %collective-permute-done.21.x.refs_5_), channel_id=1, source_target_pairs={{0,1},{1,0},{2,3},{3,2},{4,5},{5,4},{6,7},{7,6},{8,9},{9,8},{10,11... | collective-permute-start | bytes 6291464 | tf_op jit(solution)/shard_map/ppermute | solution.py:90
  120.7 32.9 %collective-permute-start.22 = (bf16[640,512]{1,0:T(8,128)(2,1)}, bf16[640,512]{1,0:T(8,128)(2,1)S(1)}, u32[]{:S(2)}, u32[]{:S(2)}) collective-permute-start(bf16[640,512]{1,0:T(8,128)(2,1)} %slice.64), channel_id=1, source_target_pairs={{0,1},{1,0},{2,3},{3,2},{4,5},{5,4},{6,7},{7,6},{8,9},{9,8},{10,11... | collective-permute-start | bytes 1966088 | tf_op jit(solution)/shard_map/ppermute | solution.py:90
  162.6 13.9 %collective-permute-start.26 = (bf16[160,2048]{1,0:T(8,128)(2,1)S(1)}, bf16[160,2048]{1,0:T(8,128)(2,1)S(1)}, u32[]{:S(2)}, u32[]{:S(2)}) collective-permute-start(bf16[160,2048]{1,0:T(8,128)(2,1)S(1)} %get-tuple-element.12), channel_id=1, source_target_pairs={{0,0},{1,1},{2,2},{3,3},{4,4},{5,5},{6,6},{7,13},{8,8},{9,9},{10,1... | collective-permute-start | bytes 1966088 | tf_op jit(solution)/shard_map/ppermute | solution.py:90
  163.3 29.2 %collective-permute-start.27 = (bf16[160,2048]{1,0:T(8,128)(2,1)S(1)}, bf16[160,2048]{1,0:T(8,128)(2,1)S(1)}, u32[]{:S(2)}, u32[]{:S(2)}) collective-permute-start(bf16[160,2048]{1,0:T(8,128)(2,1)S(1)} %get-tuple-element.13), channel_id=1, source_target_pairs={{0,2},{1,3},{2,4},{3,5},{4,6},{5,13},{6,0},{7,1},{8,10},{9,11},{10... | collective-permute-start | bytes 1966088 | tf_op jit(solution)/shard_map/ppermute | solution.py:90
  169.0 23.5 %collective-permute-start.28 = (bf16[160,2048]{1,0:T(8,128)(2,1)S(1)}, bf16[160,2048]{1,0:T(8,128)(2,1)S(1)}, u32[]{:S(2)}, u32[]{:S(2)}) collective-permute-start(bf16[160,2048]{1,0:T(8,128)(2,1)S(1)} %weight_gradient.4), channel_id=1, source_target_pairs={{0,4},{1,5},{2,6},{3,13},{4,0},{5,1},{6,2},{7,3},{8,12},{9,7},{10,... | collective-permute-start | bytes 1966088 | tf_op jit(solution)/shard_map/ppermute | solution.py:90
  175.4 24.3 %collective-permute-start.29 = (bf16[160,2048]{1,0:T(8,128)(2,1)S(1)}, bf16[160,2048]{1,0:T(8,128)(2,1)S(1)}, u32[]{:S(2)}, u32[]{:S(2)}) collective-permute-start(bf16[160,2048]{1,0:T(8,128)(2,1)S(1)} %weight_gradient.5), channel_id=1, source_target_pairs={{0,6},{1,13},{2,0},{3,1},{4,2},{5,3},{6,4},{7,5},{8,14},{9,15},{10... | collective-permute-start | bytes 1966088 | tf_op jit(solution)/shard_map/ppermute | solution.py:90
  200.8 19.6 %collective-permute-start.30 = (f32[64,2048]{1,0:T(8,128)}, f32[64,2048]{1,0:T(8,128)}, u32[]{:S(2)}, u32[]{:S(2)}) collective-permute-start(f32[64,2048]{1,0:T(8,128)} %slice.70), channel_id=1, source_target_pairs={{6,14},{14,6},{22,30},{30,22},{38,46},{46,38},{54,62},{62,54},{70,... | collective-permute-start | bytes 1572872 | tf_op jit(solution)/shard_map/ppermute | solution.py:90
  (31 other events, 246.2 us)

commit v2 on v1

--- a/solution.py
+++ b/solution.py
@@ -28,7 +28,6 @@
 UNIT = 32
 HALF = HD // 2
 KVROWS = 640
-FAR = 96
 INV_ROOT = 1.0 / math.sqrt(HD)
 
 ARRANGED = [[5 * d + k for k in range(5)] for d in range(16)]
@@ -42,6 +41,10 @@
 ALIGNED[14] = [72, 73, 74, 33, 34]
 OWNER = list(range(16))
 OWNER[7], OWNER[13] = 13, 7
+PARTS = ((0, 64), (64, 96), (96, 160))
+PART_OWNER = [list(OWNER) for _ in PARTS]
+PART_OWNER[1][6], PART_OWNER[1][12] = 12, 6
+PART_OWNER[2][6], PART_OWNER[2][14] = 14, 6
 
 
 def head_position(unit, plane):
@@ -52,7 +55,6 @@
 
 def build_tables():
     order = np.array([[u - 5 * d for u in ARRANGED[d]] for d in range(16)], np.int32)
-    inverse = np.argsort(order, axis=1).astype(np.int32)
     place = np.zeros((16, 40), np.int32)
     for d in range(16):
         z, y, c = d // 8, d % 8 // 2, d % 2
@@ -63,10 +65,10 @@
                 row += [head_position(u, z) for u in ALIGNED[other]]
         assert sorted(row) == list(range(40))
         place[d] = row
-    return order, inverse, place
-
-
-ORDER, INVERSE, PLACE = build_tables()
+    return order, place
+
+
+ORDER, PLACE = build_tables()
 
 
 def pairs_of(function):
@@ -116,12 +118,9 @@
             num_scalar_prefetch=1, grid=(5,), in_specs=[picked, picked], out_specs=[straight, straight]
         ),
         out_shape=[jax.ShapeDtypeStruct((SHARD, D), BF)] * 2,
-        compiler_params=params(32),
+        compiler_params=params(56),
         name="arrange",
     )(order, weight, snapshot)
-
-
-PIECES = ((0, SHARD, 0), (1, SHARD, 0), (2, SHARD, 0), (3, SHARD, 0))
 
 
 def copies(place, arrays, held, sems):
@@ -174,6 +173,7 @@
 TABLE = pl.BlockSpec((HALF, SEQ), lambda s, place: (0, 0))
 ROWS = pl.BlockSpec((SEQ, D), lambda s, place: (s, 0))
 COLUMNS = pl.BlockSpec((2 * KVROWS, SEQ), lambda s, place: (0, s))
+HALF_COLUMNS = pl.BlockSpec((KVROWS, SEQ), lambda s, place: (0, s))
 
 
 def student_projection(place, x, cosine, sine, arrays):
@@ -188,7 +188,7 @@
             scratch_shapes=[pltpu.VMEM((2 * KVROWS, D), BF), pltpu.SemaphoreType.DMA((40,))],
         ),
         out_shape=jax.ShapeDtypeStruct((2 * KVROWS, x.shape[0]), BF),
-        compiler_params=params(48),
+        compiler_params=params(56),
         cost_estimate=pl.CostEstimate(
             flops=2 * x.shape[0] * 2 * KVROWS * D, bytes_accessed=9 * 2**20, transcendentals=0
         ),
@@ -246,7 +246,7 @@
 
 
 def gradient_kernel(place, x, qk_student, cosine, sine, *rest):
-    arrays, (out, held, grads, sems) = rest[:8], rest[8:]
+    arrays, (out, out_other, held, grads, sems) = rest[:8], rest[8:]
     load_weight(place, arrays, held, sems)
     for kv in range(2):
         teacher = project(held, x[...], cosine[...], sine[...], kv)
@@ -256,7 +256,8 @@
             grads[base + h * HD : base + (h + 1) * HD, :] = value
     for n in range(40):
         row = pl.multiple_of(place[n] * UNIT, UNIT)
-        out[n * UNIT : (n + 1) * UNIT, :] = grads[pl.ds(row, UNIT), :]
+        target, at = (out, n) if n < 20 else (out_other, n - 20)
+        target[at * UNIT : (at + 1) * UNIT, :] = grads[pl.ds(row, UNIT), :]
 
 
 def projection_gradient(place, x, qk_student, cosine, sine, arrays):
@@ -267,14 +268,14 @@
             num_scalar_prefetch=1,
             grid=(count,),
             in_specs=[ROWS, COLUMNS, TABLE, TABLE] + [ANY] * 8,
-            out_specs=COLUMNS,
+            out_specs=[HALF_COLUMNS] * 2,
             scratch_shapes=[
                 pltpu.VMEM((2 * KVROWS, D), BF),
                 pltpu.VMEM((2 * KVROWS, SEQ), BF),
                 pltpu.SemaphoreType.DMA((40,)),
             ],
         ),
-        out_shape=jax.ShapeDtypeStruct((2 * KVROWS, x.shape[0]), BF),
+        out_shape=[jax.ShapeDtypeStruct((KVROWS, x.shape[0]), BF)] * 2,
         compiler_params=params(56),
         cost_estimate=pl.CostEstimate(
             flops=6 * x.shape[0] * 2 * KVROWS * D, bytes_accessed=9 * 2**20, transcendentals=0
@@ -286,42 +287,42 @@
 TILE = 512
 
 
-def weight_kernel(first, count, own_a, own_b, other_a, other_b, xa, xb, ya, yb, *outs):
-    lo, hi = first * SHARD, (first + count) * SHARD
-    total = dot(own_a[lo:hi, :], xa[...])
-    total += dot(own_b[lo:hi, :], xb[...])
-    total += dot(other_a[lo:hi, :], ya[...])
-    total += dot(other_b[lo:hi, :], yb[...])
-    for n, out in enumerate(outs):
-        out[...] = total[n * SHARD : (n + 1) * SHARD].astype(BF)
-
-
-def weight_gradient(first, count, grads, tokens):
+def weight_kernel(steps, own_a, own_b, other_a, other_b, xa, xb, ya, yb, *outs):
+    for at, step in enumerate(steps):
+        rows = slice(step * SHARD, (step + 1) * SHARD)
+        total = dot(own_a[rows, :], xa[...])
+        total += dot(own_b[rows, :], xb[...])
+        total += dot(other_a[rows, :], ya[...])
+        total += dot(other_b[rows, :], yb[...])
+        total = total.astype(BF)
+        for n, (low, high) in enumerate(PARTS):
+            outs[at * 3 + n][...] = total[low:high]
+
+
+def weight_gradient(steps, grads, tokens):
     whole = [pl.BlockSpec((KVROWS, 2 * SEQ), lambda t: (0, 0))] * 4
     return pl.pallas_call(
-        lambda *refs: weight_kernel(first, count, *refs),
+        lambda *refs: weight_kernel(steps, *refs),
         grid=(D // TILE,),
         in_specs=whole + [pl.BlockSpec((2 * SEQ, TILE), lambda t: (0, t))] * 4,
-        out_specs=[pl.BlockSpec((SHARD, TILE), lambda t: (0, t))] * count,
-        out_shape=[jax.ShapeDtypeStruct((SHARD, D), BF)] * count,
-        compiler_params=params(48),
+        out_specs=[pl.BlockSpec((h - l, TILE), lambda t: (0, t)) for l, h in PARTS] * len(steps),
+        out_shape=[jax.ShapeDtypeStruct((h - l, D), BF) for l, h in PARTS] * len(steps),
+        compiler_params=params(56),
         cost_estimate=pl.CostEstimate(
-            flops=2 * count * SHARD * 8 * SEQ * D, bytes_accessed=12 * 2**20, transcendentals=0
+            flops=2 * len(steps) * SHARD * 8 * SEQ * D, bytes_accessed=12 * 2**20, transcendentals=0
         ),
         name="weight_gradient",
     )(*grads, *tokens)
 
 
-def adam_kernel(table, b0, b1, b2, b3, part_a, part_b, weight, one, two, weight_out, one_out, two_out):
-    k = pl.program_id(0)
-    at = table[k]
-    swapped = table[5]
-    gradient = (b0[...].astype(F32) + b1[...].astype(F32)) + (
-        b2[...].astype(F32) + b3[...].astype(F32)
-    )
-    take_a = jnp.logical_and(at >= 3, swapped % 2 == 1)
-    take_b = jnp.logical_and(at == 2, swapped // 2 == 1)
-    gradient = jnp.where(take_a, part_a[...], jnp.where(take_b, part_b[...], gradient))
+def adam_kernel(table, *refs):
+    position = pl.program_id(0)
+    pieces, (weight, one, two, weight_out, one_out, two_out) = refs[:12], refs[12:]
+    sums = []
+    for n in range(3):
+        a, b, c, d = (pieces[4 * n + s][...].astype(F32) for s in range(4))
+        sums.append((a + b) + (c + d))
+    gradient = jnp.where(position < 2, sums[0], jnp.where(position == 2, sums[1], sums[2]))
     first_new = BETA_ONE * one[...] + (1.0 - BETA_ONE) * gradient
     second_new = BETA_TWO * two[...] + (1.0 - BETA_TWO) * gradient * gradient
     step_dir = (
@@ -335,23 +336,25 @@
     two_out[...] = second_new
 
 
-def adam(table, blocks, part_a, part_b, weight, one, two):
-    picked = pl.BlockSpec((UNIT, D), lambda k, t: (t[k], 0))
-    from_a = pl.BlockSpec((UNIT, D), lambda k, t: (jnp.maximum(t[k] - 3, 0), 0))
-    from_b = pl.BlockSpec((UNIT, D), lambda k, t: (0, 0))
-    straight = pl.BlockSpec((UNIT, D), lambda k, t: (k, 0))
+def adam(order, pieces, weight, one, two):
+    native = pl.BlockSpec((UNIT, D), lambda k, order: (order[k], 0))
+    parts = [
+        pl.BlockSpec((UNIT, D), lambda k, order: (jnp.minimum(k, 1), 0)),
+        pl.BlockSpec((UNIT, D), lambda k, order: (0, 0)),
+        pl.BlockSpec((UNIT, D), lambda k, order: (jnp.maximum(k - 3, 0), 0)),
+    ]
     return pl.pallas_call(
         adam_kernel,
         grid_spec=pltpu.PrefetchScalarGridSpec(
             num_scalar_prefetch=1,
             grid=(5,),
-            in_specs=[picked] * 4 + [from_a, from_b] + [straight] * 3,
-            out_specs=[straight] * 3,
+            in_specs=[part for part in parts for _ in range(4)] + [native] * 3,
+            out_specs=[native] * 3,
         ),
         out_shape=[jax.ShapeDtypeStruct((SHARD, D), F32)] * 3,
-        compiler_params=params(32),
+        compiler_params=params(56),
         name="adam",
-    )(table, *blocks, part_a, part_b, weight, one, two)
+    )(order, *pieces, weight, one, two)
 
 
 def rotary_tables():
@@ -362,14 +365,15 @@
     return jnp.cos(angles), jnp.sin(angles)
 
 
-def ring_gather(shard):
+def ring_gather(shard, up_again):
     below = send(shard, UP)
     above = send(shard, DOWN)
-    far_low = send(below[:FAR], UP)
-    far_high = send(above[FAR:], DOWN)
-    far = jnp.concatenate([far_low, far_high], axis=0)
-    own = [shard, above, far, below]
-    return own + [send(piece, TO_CORE) for piece in own]
+    far = send(below, UP) if up_again else send(above, DOWN)
+    return [shard, above, far, below]
+
+
+def both_cores(pieces):
+    return pieces + [send(piece, TO_CORE) for piece in pieces]
 
 
 def per_device(tokens, student_weight, snapshot, moment_one, moment_two):
@@ -383,63 +387,56 @@
     student_shard, teacher_shard = arrange(order, master, snapshot[0])
     row = lax.broadcasted_iota(jnp.int32, (SHARD, 1), 0)
     whole = (me == 7) | (me == 13)
-    mask_a = whole | (((me == 6) | (me == 14)) & (row >= 96))
+    mask_a = ((me == 6) | (me == 14)) & (row >= 96)
     mask_b = ((me == 6) | (me == 12)) & (row >= 64) & (row < 96)
 
-    main = send_next(teacher_shard, list(enumerate(OWNER)))
-    tail = send_next(teacher_shard[96:], SWAP_PART)
-    middle = send_next(teacher_shard[64:96], SWAP_B)
+    def widen(part, low):
+        return jnp.pad(part, ((low, SHARD - low - part.shape[0]), (0, 0)))
+
     swap_a = send(student_shard, SWAP_A)
     swap_b = send(student_shard[64:96], SWAP_B)
-
-    def widen(part, low):
-        return jnp.pad(part, ((low, SHARD - low - part.shape[0]), (0, 0)))
-
-    student = jnp.where(mask_a, swap_a, jnp.where(mask_b, widen(swap_b, 64), student_shard))
-    mask_tail = ((me == 6) | (me == 14)) & (row >= 96)
-    teacher = jnp.where(mask_tail, widen(tail, 96), jnp.where(mask_b, widen(middle, 64), main))
-
+    main = send_next(teacher_shard, list(enumerate(OWNER)))
     plane_tokens = send(own_tokens, TO_PLANE)
-    student_rows = ring_gather(student)
-    teacher_rows = ring_gather(teacher)
+    student = jnp.where(whole | mask_a, swap_a, jnp.where(mask_b, widen(swap_b, 64), student_shard))
+    tail = send(main[96:], SWAP_PART)
+    middle = send(main[64:96], SWAP_B)
+    teacher = jnp.where(mask_a, widen(tail, 96), jnp.where(mask_b, widen(middle, 64), main))
+
+    student_rows = both_cores(ring_gather(student, True))
+    qk_own = student_projection(place, own_tokens, cosine, sine, student_rows)
+    teacher_own = ring_gather(teacher, False)
+    teacher_own[2], qk_own = lax.optimization_barrier((teacher_own[2], qk_own))
+    teacher_rows = both_cores(teacher_own)
+    qk_plane = student_projection(place, plane_tokens, cosine, sine, student_rows)
     core_tokens = send(own_tokens, TO_CORE)
     far_tokens = send(plane_tokens, TO_CORE)
 
     grads, others = [], []
-    for x in (own_tokens, plane_tokens):
-        qk_student = student_projection(place, x, cosine, sine, student_rows)
-        grad = projection_gradient(place, x, qk_student, cosine, sine, teacher_rows)
+    for x, qk_student in ((own_tokens, qk_own), (plane_tokens, qk_plane)):
+        grad, other = projection_gradient(place, x, qk_student, cosine, sine, teacher_rows)
         grads.append(grad)
-        others.append(send(grad[KVROWS:], TO_CORE))
+        others.append(send(other, TO_CORE))
 
     parts = grads + others
     all_tokens = (own_tokens, plane_tokens, core_tokens, far_tokens)
 
-    def to_owner(block, step):
-        return send(
-            block,
-            [
-                (d, OWNER[d // 8 * 8 + (d % 8 // 2 + step) % 4 * 2 + d % 2])
-                for d in range(16)
-            ],
-        )
-
-    (block_two,) = weight_gradient(2, 1, parts, all_tokens)
-    got_two = to_owner(block_two, 2)
-    block_zero, block_one = weight_gradient(0, 2, parts, all_tokens)
-    (block_three,) = weight_gradient(3, 1, parts, all_tokens)
-    got_one = to_owner(block_one, 1)
-    got_three = to_owner(block_three, 3)
-    got_zero = to_owner(block_zero, 0)
-    blocks = [got_zero, got_one, got_two, got_three]
-
-    reduced = sum(block[64:].astype(F32) for block in blocks)
-    part_b = send(reduced[:32], SWAP_B)
-    part_a = send(reduced[32:], SWAP_PART)
-    in_a = ((me == 6) | (me == 14)).astype(jnp.int32)
-    in_b = ((me == 6) | (me == 12)).astype(jnp.int32)
-    table = jnp.concatenate([jnp.asarray(INVERSE)[me], (in_a + 2 * in_b)[None]])
-    updated = adam(table, blocks, part_a, part_b, master, moment_one[0], moment_two[0])
+    def to_owner(blocks, step):
+        out = []
+        for part, block in enumerate(blocks):
+            pairs = []
+            for d in range(16):
+                aligned = d // 8 * 8 + (d % 8 // 2 + step) % 4 * 2 + d % 2
+                pairs.append((d, PART_OWNER[part][aligned]))
+            out.append(send(block, pairs))
+        return out
+
+    two = weight_gradient((2,), parts, all_tokens)
+    got = {2: to_owner(two, 2)}
+    rest = weight_gradient((1, 3, 0), parts, all_tokens)
+    for at, step in enumerate((1, 3, 0)):
+        got[step] = to_owner(rest[at * 3 : at * 3 + 3], step)
+    pieces = [got[step][part] for part in range(3) for step in range(4)]
+    updated = adam(order, pieces, master, moment_one[0], moment_two[0])
     return tuple(value[None] for value in updated)
 
 

time: 230 us -> 233 us (1.013)
  the two profiles are of different devices: /device:TPU:26 before, /device:TPU:1 now
where the time goes in v2:
time: 233 us; the launch traced here: 229 us
  starting transfers between devices  104 us (45%)
  Pallas kernels  79.1 us (34%)
  waiting for transfers between devices  34.7 us (15%)
  local copies, waits for them, and re-layouts  8.98 us (4%)
    ppermute x35, starting transfers between devices, send(): return lax.ppermute(value, 'fsdp', pairs)  99.5 us
    pallas_call x2, Pallas kernels, projection_gradient(): pl.pallas_call(gradient_kernel, grid_spec=pltpu.PrefetchScalarGridSpec(nu...  33.9 us
    ppermute x35, waiting for transfers between devices, send(): return lax.ppermute(value, 'fsdp', pairs)  18.5 us
    pallas_call x2, Pallas kernels, student_projection(): pl.pallas_call(student_kernel, grid_spec=pltpu.PrefetchScalarGridSpec(num...  17.6 us
    ppermute x1, waiting for transfers between devices, send_next(): lax.ppermute(value, ('blk', 'fsdp'), [(g * 16 + a, (g + 1) % 8 * 16 + b)...  16.2 us
    pallas_call x2, Pallas kernels, weight_gradient(): pl.pallas_call(lambda *refs: weight_kernel(steps, *refs), grid=(D // TILE...  15.1 us
    pallas_call x1, Pallas kernels, adam(): pl.pallas_call(adam_kernel, grid_spec=pltpu.PrefetchScalarGridSpec(num_sc...  7.75 us
    unnamed x64, local copies, waits for them, and re-layouts  5.52 us
  transfers between devices with their start and end apart: 36, of which 7 were waited for; matrix products, arithmetic and copies ran while one was open for 1% of the time, Pallas kernels for 26%

profile of v2, /device:TPU:1, one launch (start us, length us, event | category | flops | bytes accessed | tf_op | source)
XLA Modules:
  0.0 229.3 jit_solution(8580526032602050145)
XLA Ops:
  1.9 4.8 %arrange.1 = (bf16[160,2048]{1,0:T(8,128)(2,1)}, bf16[160,2048]{1,0:T(8,128)(2,1)}) custom-call(s32[5]{0:T(128)} %dynamic-slice_bitcast_fusion.1.order.table, f32[160,2048]{1,0:T(8,128)} %bitcast.12, bf16[160,2048]{1,0:T(8,128)(2,1)} %bitcast.16), custom_call_target="tpu_custom_call" | custom-call | tf_op jit(solution)/shard_map/arrange/pallas_call | solution.py:115
  6.7 4.4 %collective-permute-start = (bf16[160,2048]{1,0:T(8,128)(2,1)}, bf16[160,2048]{1,0:T(8,128)(2,1)S(1)}, u32[]{:S(2)}, u32[]{:S(2)}) collective-permute-start(bf16[160,2048]{1,0:T(8,128)(2,1)} %get-tuple-element.26), channel_id=1, source_target_pairs={{0,16},{1,17},{2,18},{3,19},{4,20},{5,21},{6,22},{7,29},{8,24},{9,... | collective-permute-start | bytes 1966088 | tf_op jit(solution)/shard_map/ppermute | solution.py:96
  11.8 16.2 %collective-permute-done = bf16[160,2048]{1,0:T(8,128)(2,1)S(1)} collective-permute-done((bf16[160,2048]{1,0:T(8,128)(2,1)}, bf16[160,2048]{1,0:T(8,128)(2,1)S(1)}, u32[]{:S(2)}, u32[]{:S(2)}) %collective-permute-start) | collective-permute-done | bytes 655392 | tf_op jit(solution)/shard_map/ppermute | solution.py:96
  32.9 2.3 %collective-permute-start.7 = (bf16[160,2048]{1,0:T(8,128)(2,1)S(1)}, bf16[160,2048]{1,0:T(8,128)(2,1)S(1)}, u32[]{:S(2)}, u32[]{:S(2)}) collective-permute-start(bf16[160,2048]{1,0:T(8,128)(2,1)S(1)} %get-tuple-element.51.rest_0_), channel_id=1, source_target_pairs={{0,6},{1,7},{2,0},{3,1},{4,2},{5,3},{6,4},{7,5},{8,14},{9,15},{10,... | collective-permute-start | bytes 1966088 | tf_op jit(solution)/shard_map/ppermute | solution.py:92
  35.2 6.6 %collective-permute-start.19 = (bf16[512,2048]{1,0:T(8,128)(2,1)}, bf16[512,2048]{1,0:T(8,128)(2,1)S(1)}, u32[]{:S(2)}, u32[]{:S(2)}) collective-permute-start(bf16[512,2048]{1,0:T(8,128)(2,1)} %bitcast.2.x.refs_4_), channel_id=1, source_target_pairs={{0,8},{1,9},{2,10},{3,11},{4,12},{5,13},{6,14},{7,15},{8,0},{9,1},... | collective-permute-start | bytes 6291464 | tf_op jit(solution)/shard_map/ppermute | solution.py:92
  41.9 13.6 %collective-permute-start.10 = (bf16[160,2048]{1,0:T(8,128)(2,1)S(1)}, bf16[160,2048]{1,0:T(8,128)(2,1)S(1)}, u32[]{:S(2)}, u32[]{:S(2)}) collective-permute-start(bf16[160,2048]{1,0:T(8,128)(2,1)S(1)} %get-tuple-element.51.rest_0_), channel_id=1, source_target_pairs={{0,1},{1,0},{2,3},{3,2},{4,5},{5,4},{6,7},{7,6},{8,9},{9,8},{10,11... | collective-permute-start | bytes 1966088 | tf_op jit(solution)/shard_map/ppermute | solution.py:92
  58.2 12.4 %collective-permute-start.11 = (bf16[160,2048]{1,0:T(8,128)(2,1)S(1)}, bf16[160,2048]{1,0:T(8,128)(2,1)S(1)}, u32[]{:S(2)}, u32[]{:S(2)}) collective-permute-start(bf16[160,2048]{1,0:T(8,128)(2,1)S(1)} %collective-permute-done.7.rest_1_), channel_id=1, source_target_pairs={{0,1},{1,0},{2,3},{3,2},{4,5},{5,4},{6,7},{7,6},{8,9},{9,8},{10,11... | collective-permute-start | bytes 1966088 | tf_op jit(solution)/shard_map/ppermute | solution.py:92
  71.8 5.8 %collective-permute-start.13 = (bf16[160,2048]{1,0:T(8,128)(2,1)S(1)}, bf16[160,2048]{1,0:T(8,128)(2,1)S(1)}, u32[]{:S(2)}, u32[]{:S(2)}) collective-permute-start(bf16[160,2048]{1,0:T(8,128)(2,1)S(1)} %collective-permute-done.8.rest_3_), channel_id=1, source_target_pairs={{0,1},{1,0},{2,3},{3,2},{4,5},{5,4},{6,7},{7,6},{8,9},{9,8},{10,11... | collective-permute-start | bytes 1966088 | tf_op jit(solution)/shard_map/ppermute | solution.py:92
  77.6 7.4 %collective-permute-start.12 = (bf16[160,2048]{1,0:T(8,128)(2,1)S(1)}, bf16[160,2048]{1,0:T(8,128)(2,1)S(1)}, u32[]{:S(2)}, u32[]{:S(2)}) collective-permute-start(bf16[160,2048]{1,0:T(8,128)(2,1)S(1)} %collective-permute-done.9.rest_2_), channel_id=1, source_target_pairs={{0,1},{1,0},{2,3},{3,2},{4,5},{5,4},{6,7},{7,6},{8,9},{9,8},{10,11... | collective-permute-start | bytes 1966088 | tf_op jit(solution)/shard_map/ppermute | solution.py:92
  89.1 7.2 %collective-permute-start.15 = (bf16[160,2048]{1,0:T(8,128)(2,1)S(1)}, bf16[160,2048]{1,0:T(8,128)(2,1)}, u32[]{:S(2)}, u32[]{:S(2)}) collective-permute-start(bf16[160,2048]{1,0:T(8,128)(2,1)S(1)} %get-tuple-element.52.rest_0_), channel_id=1, source_target_pairs={{0,1},{1,0},{2,3},{3,2},{4,5},{5,4},{6,7},{7,6},{8,9},{9,8},{10,11... | collective-permute-start | bytes 1966088 | tf_op jit(solution)/shard_map/ppermute | solution.py:92
  98.0 8.8 %student_projection.2.qk_student = bf16[1280,512]{1,0:T(8,128)(2,1)} custom-call(s32[40]{0:T(128)} %dynamic-slice_bitcast_fusion.place, bf16[512,2048]{1,0:T(8,128)(2,1)} %bitcast.2.x.refs_4_, f32[64,256]{1,0:T(8,128)} %get-tuple-element.50.cosine, f32[64,256]{1,0:T(8,128)} %get-tuple-element.49.sine, bf16[160,2048]{1,0:T(8,128)(2,1)} %copy-done.5, ...), custom_call_target="tpu_custom_call" | custom-call | flops 2684354560 | bytes 9437184 | tf_op jit(solution)/shard_map/student_projection/pallas_call | solution.py:181
  108.3 8.8 %student_projection.3.qk_student = bf16[1280,512]{1,0:T(8,128)(2,1)} custom-call(s32[40]{0:T(128)} %dynamic-slice_bitcast_fusion.place, bf16[512,2048]{1,0:T(8,128)(2,1)} %copy-done, f32[64,256]{1,0:T(8,128)} %get-tuple-element.50.cosine, f32[64,256]{1,0:T(8,128)} %get-tuple-element.49.sine, bf16[160,2048]{1,0:T(8,128)(2,1)} %copy-done.5, ...), custom_call_target="tpu_custom_call" | custom-call | flops 2684354560 | bytes 9437184 | tf_op jit(solution)/shard_map/student_projection/pallas_call | solution.py:181
  118.7 16.9 %projection_gradient.3 = (bf16[640,512]{1,0:T(8,128)(2,1)}, bf16[640,512]{1,0:T(8,128)(2,1)}) custom-call(s32[40]{0:T(128)} %dynamic-slice_bitcast_fusion.place, bf16[512,2048]{1,0:T(8,128)(2,1)} %copy-done, bf16[1280,512]{1,0:T(8,128)(2,1)} %student_projection.3.qk_student, f32[64,256]{1,0:T(8,128)} %get-tuple-element.50.cosine, ...), custom_call_target="tpu_custom_call" | custom-call | flops 8053063680 | bytes 9437184 | tf_op jit(solution)/shard_map/projection_gradient/pallas_call | solution.py:265
  135.8 16.9 %projection_gradient.2 = (bf16[640,512]{1,0:T(8,128)(2,1)}, bf16[640,512]{1,0:T(8,128)(2,1)}) custom-call(s32[40]{0:T(128)} %dynamic-slice_bitcast_fusion.place, bf16[512,2048]{1,0:T(8,128)(2,1)} %bitcast.2.x.refs_4_, bf16[1280,512]{1,0:T(8,128)(2,1)} %student_projection.2.qk_student, f32[64,256]{1,0:T(8,128)} %get-tuple-element.50.cosine, ...), custom_call_target="tpu_custom_call" | custom-call | flops 8053063680 | bytes 9437184 | tf_op jit(solution)/shard_map/projection_gradient/pallas_call | solution.py:265
  156.8 6.6 %weight_gradient.3 = (bf16[64,2048]{1,0:T(8,128)(2,1)}, bf16[32,2048]{1,0:T(8,128)(2,1)}, bf16[64,2048]{1,0:T(8,128)(2,1)}) custom-call(bf16[640,512]{1,0:T(8,128)(2,1)} %get-tuple-element.30.refs_0_, bf16[640,512]{1,0:T(8,128)(2,1)} %get-tuple-element.31.refs_1_, bf16[640,512]{1,0:T(8,128)(2,1)} %copy-done.7, bf16[640,512]{1,0:T(8,128)(2,1)} %copy-done.6, ...), custom_call_target="tpu_custom_call" | custom-call | flops 1342177280 | bytes 12582912 | tf_op jit(solution)/shard_map/weight_gradient/pallas_call | solution.py:304
  163.5 8.5 %weight_gradient.2 = (bf16[64,2048]{1,0:T(8,128)(2,1)}, bf16[32,2048]{1,0:T(8,128)(2,1)}, bf16[64,2048]{1,0:T(8,128)(2,1)}, bf16[64,2048]{1,0:T(8,128)(2,1)}, bf...) custom-call(bf16[640,512]{1,0:T(8,128)(2,1)} %get-tuple-element.30.r, ...), custom_call_target="tpu_custom_call" | custom-call | flops 4026531840 | bytes 12582912 | tf_op jit(solution)/shard_map/weight_gradient/pallas_call | solution.py:304
  173.6 2.9 %collective-permute-start.26 = (bf16[64,2048]{1,0:T(8,128)(2,1)S(1)}, bf16[64,2048]{1,0:T(8,128)(2,1)S(1)}, u32[]{:S(2)}, u32[]{:S(2)}) collective-permute-start(bf16[64,2048]{1,0:T(8,128)(2,1)S(1)} %copy-done.31), channel_id=1, source_target_pairs={{0,4},{1,5},{2,6},{3,13},{4,0},{5,1},{6,2},{7,3},{8,12},{9,7},{10,... | collective-permute-start | bytes 786440 | tf_op jit(solution)/shard_map/ppermute | solution.py:92
  179.5 4.9 %collective-permute-start.31 = (bf16[32,2048]{1,0:T(8,128)(2,1)}, bf16[32,2048]{1,0:T(8,128)(2,1)S(1)}, u32[]{:S(2)}, u32[]{:S(2)}) collective-permute-start(bf16[32,2048]{1,0:T(8,128)(2,1)} %get-tuple-element.41), channel_id=1, source_target_pairs={{0,12},{1,13},{2,0},{3,1},{4,2},{5,3},{6,4},{7,5},{8,14},{9,15},{1... | collective-permute-start | bytes 393224 | tf_op jit(solution)/shard_map/ppermute | solution.py:92
  184.4 7.4 %collective-permute-done.29.refs_5_ = bf16[32,2048]{1,0:T(8,128)(2,1)S(1)} collective-permute-done((bf16[32,2048]{1,0:T(8,128)(2,1)}, bf16[32,2048]{1,0:T(8,128)(2,1)S(1)}, u32[]{:S(2)}, u32[]{:S(2)}) %collective-permute-start.29) | collective-permute-done | bytes 131104 | tf_op jit(solution)/shard_map/ppermute | solution.py:92
  191.8 14.0 %collective-permute-start.25 = (bf16[64,2048]{1,0:T(8,128)(2,1)}, bf16[64,2048]{1,0:T(8,128)(2,1)S(1)}, u32[]{:S(2)}, u32[]{:S(2)}) collective-permute-start(bf16[64,2048]{1,0:T(8,128)(2,1)} %get-tuple-element.35), channel_id=1, source_target_pairs={{0,2},{1,3},{2,4},{3,5},{4,6},{5,13},{6,0},{7,1},{8,10},{9,11},{10... | collective-permute-start | bytes 786440 | tf_op jit(solution)/shard_map/ppermute | solution.py:92
  209.6 3.2 %collective-permute-start.35 = (bf16[64,2048]{1,0:T(8,128)(2,1)}, bf16[64,2048]{1,0:T(8,128)(2,1)S(1)}, u32[]{:S(2)}, u32[]{:S(2)}) collective-permute-start(bf16[64,2048]{1,0:T(8,128)(2,1)} %get-tuple-element.45), channel_id=1, source_target_pairs={{0,14},{1,13},{2,0},{3,1},{4,2},{5,3},{6,4},{7,5},{8,6},{9,15},{10... | collective-permute-start | bytes 786440 | tf_op jit(solution)/shard_map/ppermute | solution.py:92
  215.1 2.8 %collective-permute-done.33.refs_9_ = bf16[64,2048]{1,0:T(8,128)(2,1)S(1)} collective-permute-done((bf16[64,2048]{1,0:T(8,128)(2,1)}, bf16[64,2048]{1,0:T(8,128)(2,1)S(1)}, u32[]{:S(2)}, u32[]{:S(2)}) %collective-permute-start.33) | collective-permute-done | bytes 262176 | tf_op jit(solution)/shard_map/ppermute | solution.py:92
  217.9 2.8 %collective-permute-done.35.refs_11_ = bf16[64,2048]{1,0:T(8,128)(2,1)S(1)} collective-permute-done((bf16[64,2048]{1,0:T(8,128)(2,1)}, bf16[64,2048]{1,0:T(8,128)(2,1)S(1)}, u32[]{:S(2)}, u32[]{:S(2)}) %collective-permute-start.35) | collective-permute-done | bytes 262176 | tf_op jit(solution)/shard_map/ppermute | solution.py:92
  221.4 7.7 %adam.1 = (f32[160,2048]{1,0:T(8,128)}, f32[160,2048]{1,0:T(8,128)}, f32[160,2048]{1,0:T(8,128)}) custom-call(s32[5]{0:T(128)} %dynamic-slice_bitcast_fusion.1.order.table, bf16[64,2048]{1,0:T(8,128)(2,1)} %copy-done.10, bf16[64,2048]{1,0:T(8,128)(2,1)} %copy-done.11, bf16[64,2048]{1,0:T(8,128)(2,1)} %copy-done.8, bf16[64,2048]{1,0:T(8,128)(2,1)} %copy-done.12, ...), custom_call_target="tpu_custom_call" | custom-call | tf_op jit(solution)/shard_map/adam/pallas_call | solution.py:346
  (131 shorter events, 34.9 us)
Async XLA Ops:
  6.7 21.3 %collective-permute-start = (bf16[160,2048]{1,0:T(8,128)(2,1)}, bf16[160,2048]{1,0:T(8,128)(2,1)S(1)}, u32[]{:S(2)}, u32[]{:S(2)}) collective-permute-start(bf16[160,2048]{1,0:T(8,128)(2,1)} %get-tuple-element.26), channel_id=1, source_target_pairs={{0,16},{1,17},{2,18},{3,19},{4,20},{5,21},{6,22},{7,29},{8,24},{9,... | collective-permute-start | bytes 1966088 | tf_op jit(solution)/shard_map/ppermute | solution.py:96
  11.1 19.9 %collective-permute-start.5 = (bf16[160,2048]{1,0:T(8,128)(2,1)}, bf16[160,2048]{1,0:T(8,128)(2,1)S(1)}, u32[]{:S(2)}, u32[]{:S(2)}) collective-permute-start(bf16[160,2048]{1,0:T(8,128)(2,1)} %get-tuple-element.27), channel_id=1, source_target_pairs={{7,13},{13,7},{6,14},{14,6},{23,29},{29,23},{22,30},{30,22},{39,45... | collective-permute-start | bytes 1966088 | tf_op jit(solution)/shard_map/ppermute | solution.py:92
  31.6 25.6 %collective-permute-start.8 = (bf16[160,2048]{1,0:T(8,128)(2,1)S(1)}, bf16[160,2048]{1,0:T(8,128)(2,1)S(1)}, u32[]{:S(2)}, u32[]{:S(2)}) collective-permute-start(bf16[160,2048]{1,0:T(8,128)(2,1)S(1)} %get-tuple-element.51.rest_0_), channel_id=1, source_target_pairs={{0,2},{1,3},{2,4},{3,5},{4,6},{5,7},{6,0},{7,1},{8,10},{9,11},{10,... | collective-permute-start | bytes 1966088 | tf_op jit(solution)/shard_map/ppermute | solution.py:92
  32.9 24.2 %collective-permute-start.7 = (bf16[160,2048]{1,0:T(8,128)(2,1)S(1)}, bf16[160,2048]{1,0:T(8,128)(2,1)S(1)}, u32[]{:S(2)}, u32[]{:S(2)}) collective-permute-start(bf16[160,2048]{1,0:T(8,128)(2,1)S(1)} %get-tuple-element.51.rest_0_), channel_id=1, source_target_pairs={{0,6},{1,7},{2,0},{3,1},{4,2},{5,3},{6,4},{7,5},{8,14},{9,15},{10,... | collective-permute-start | bytes 1966088 | tf_op jit(solution)/shard_map/ppermute | solution.py:92
  35.2 71.8 %collective-permute-start.19 = (bf16[512,2048]{1,0:T(8,128)(2,1)}, bf16[512,2048]{1,0:T(8,128)(2,1)S(1)}, u32[]{:S(2)}, u32[]{:S(2)}) collective-permute-start(bf16[512,2048]{1,0:T(8,128)(2,1)} %bitcast.2.x.refs_4_), channel_id=1, source_target_pairs={{0,8},{1,9},{2,10},{3,11},{4,12},{5,13},{6,14},{7,15},{8,0},{9,1},... | collective-permute-start | bytes 6291464 | tf_op jit(solution)/shard_map/ppermute | solution.py:92
  41.9 16.3 %collective-permute-start.10 = (bf16[160,2048]{1,0:T(8,128)(2,1)S(1)}, bf16[160,2048]{1,0:T(8,128)(2,1)S(1)}, u32[]{:S(2)}, u32[]{:S(2)}) collective-permute-start(bf16[160,2048]{1,0:T(8,128)(2,1)S(1)} %get-tuple-element.51.rest_0_), channel_id=1, source_target_pairs={{0,1},{1,0},{2,3},{3,2},{4,5},{5,4},{6,7},{7,6},{8,9},{9,8},{10,11... | collective-permute-start | bytes 1966088 | tf_op jit(solution)/shard_map/ppermute | solution.py:92
  55.5 16.4 %collective-permute-start.3 = (bf16[160,2048]{1,0:T(8,128)(2,1)S(1)}, bf16[160,2048]{1,0:T(8,128)(2,1)S(1)}, u32[]{:S(2)}, u32[]{:S(2)}) collective-permute-start(bf16[160,2048]{1,0:T(8,128)(2,1)S(1)} %get-tuple-element.52.rest_0_), channel_id=1, source_target_pairs={{0,6},{1,7},{2,0},{3,1},{4,2},{5,3},{6,4},{7,5},{8,14},{9,15},{10,... | collective-permute-start | bytes 1966088 | tf_op jit(solution)/shard_map/ppermute | solution.py:92
  57.2 20.5 %collective-permute-start.9 = (bf16[160,2048]{1,0:T(8,128)(2,1)S(1)}, bf16[160,2048]{1,0:T(8,128)(2,1)S(1)}, u32[]{:S(2)}, u32[]{:S(2)}) collective-permute-start(bf16[160,2048]{1,0:T(8,128)(2,1)S(1)} %collective-permute-done.8.rest_3_), channel_id=1, source_target_pairs={{0,2},{1,3},{2,4},{3,5},{4,6},{5,7},{6,0},{7,1},{8,10},{9,11},{10,... | collective-permute-start | bytes 1966088 | tf_op jit(solution)/shard_map/ppermute | solution.py:92
  57.2 27.9 %collective-permute-start.14 = (bf16[160,2048]{1,0:T(8,128)(2,1)S(1)}, bf16[160,2048]{1,0:T(8,128)(2,1)S(1)}, u32[]{:S(2)}, u32[]{:S(2)}) collective-permute-start(bf16[160,2048]{1,0:T(8,128)(2,1)S(1)} %get-tuple-element.52.rest_0_), channel_id=1, source_target_pairs={{0,2},{1,3},{2,4},{3,5},{4,6},{5,7},{6,0},{7,1},{8,10},{9,11},{10,... | collective-permute-start | bytes 1966088 | tf_op jit(solution)/shard_map/ppermute | solution.py:92
  58.2 30.8 %collective-permute-start.11 = (bf16[160,2048]{1,0:T(8,128)(2,1)S(1)}, bf16[160,2048]{1,0:T(8,128)(2,1)S(1)}, u32[]{:S(2)}, u32[]{:S(2)}) collective-permute-start(bf16[160,2048]{1,0:T(8,128)(2,1)S(1)} %collective-permute-done.7.rest_1_), channel_id=1, source_target_pairs={{0,1},{1,0},{2,3},{3,2},{4,5},{5,4},{6,7},{7,6},{8,9},{9,8},{10,11... | collective-permute-start | bytes 1966088 | tf_op jit(solution)/shard_map/ppermute | solution.py:92
  71.8 24.4 %collective-permute-start.13 = (bf16[160,2048]{1,0:T(8,128)(2,1)S(1)}, bf16[160,2048]{1,0:T(8,128)(2,1)S(1)}, u32[]{:S(2)}, u32[]{:S(2)}) collective-permute-start(bf16[160,2048]{1,0:T(8,128)(2,1)S(1)} %collective-permute-done.8.rest_3_), channel_id=1, source_target_pairs={{0,1},{1,0},{2,3},{3,2},{4,5},{5,4},{6,7},{7,6},{8,9},{9,8},{10,11... | collective-permute-start | bytes 1966088 | tf_op jit(solution)/shard_map/ppermute | solution.py:92
  77.6 18.8 %collective-permute-start.12 = (bf16[160,2048]{1,0:T(8,128)(2,1)S(1)}, bf16[160,2048]{1,0:T(8,128)(2,1)S(1)}, u32[]{:S(2)}, u32[]{:S(2)}) collective-permute-start(bf16[160,2048]{1,0:T(8,128)(2,1)S(1)} %collective-permute-done.9.rest_2_), channel_id=1, source_target_pairs={{0,1},{1,0},{2,3},{3,2},{4,5},{5,4},{6,7},{7,6},{8,9},{9,8},{10,11... | collective-permute-start | bytes 1966088 | tf_op jit(solution)/shard_map/ppermute | solution.py:92
  85.1 21.8 %collective-permute-start.4 = (bf16[160,2048]{1,0:T(8,128)(2,1)S(1)}, bf16[160,2048]{1,0:T(8,128)(2,1)}, u32[]{:S(2)}, u32[]{:S(2)}) collective-permute-start(bf16[160,2048]{1,0:T(8,128)(2,1)S(1)} %collective-permute-done.3.rest_1_), channel_id=1, source_target_pairs={{0,6},{1,7},{2,0},{3,1},{4,2},{5,3},{6,4},{7,5},{8,14},{9,15},{10,... | collective-permute-start | bytes 1966088 | tf_op jit(solution)/shard_map/ppermute | solution.py:92
  89.1 28.1 %collective-permute-start.15 = (bf16[160,2048]{1,0:T(8,128)(2,1)S(1)}, bf16[160,2048]{1,0:T(8,128)(2,1)}, u32[]{:S(2)}, u32[]{:S(2)}) collective-permute-start(bf16[160,2048]{1,0:T(8,128)(2,1)S(1)} %get-tuple-element.52.rest_0_), channel_id=1, source_target_pairs={{0,1},{1,0},{2,3},{3,2},{4,5},{5,4},{6,7},{7,6},{8,9},{9,8},{10,11... | collective-permute-start | bytes 1966088 | tf_op jit(solution)/shard_map/ppermute | solution.py:92
  96.3 21.6 %collective-permute-start.16 = (bf16[160,2048]{1,0:T(8,128)(2,1)S(1)}, bf16[160,2048]{1,0:T(8,128)(2,1)}, u32[]{:S(2)}, u32[]{:S(2)}) collective-permute-start(bf16[160,2048]{1,0:T(8,128)(2,1)S(1)} %collective-permute-done.3.rest_1_), channel_id=1, source_target_pairs={{0,1},{1,0},{2,3},{3,2},{4,5},{5,4},{6,7},{7,6},{8,9},{9,8},{10,11... | collective-permute-start | bytes 1966088 | tf_op jit(solution)/shard_map/ppermute | solution.py:92
  97.1 20.7 %collective-permute-start.18 = (bf16[160,2048]{1,0:T(8,128)(2,1)S(1)}, bf16[160,2048]{1,0:T(8,128)(2,1)}, u32[]{:S(2)}, u32[]{:S(2)}) collective-permute-start(bf16[160,2048]{1,0:T(8,128)(2,1)S(1)} %collective-permute-done.14.rest_3_), channel_id=1, source_target_pairs={{0,1},{1,0},{2,3},{3,2},{4,5},{5,4},{6,7},{7,6},{8,9},{9,8},{10,11... | collective-permute-start | bytes 1966088 | tf_op jit(solution)/shard_map/ppermute | solution.py:92
  107.0 46.2 %collective-permute-start.22 = (bf16[512,2048]{1,0:T(8,128)(2,1)}, bf16[512,2048]{1,0:T(8,128)(2,1)S(1)}, u32[]{:S(2)}, u32[]{:S(2)}) collective-permute-start(bf16[512,2048]{1,0:T(8,128)(2,1)} %bitcast.2.x.refs_4_), channel_id=1, source_target_pairs={{0,1},{1,0},{2,3},{3,2},{4,5},{5,4},{6,7},{7,6},{8,9},{9,8},{10,11... | collective-permute-start | bytes 6291464 | tf_op jit(solution)/shard_map/ppermute | solution.py:92
  117.1 38.0 %collective-permute-start.23 = (bf16[512,2048]{1,0:T(8,128)(2,1)}, bf16[512,2048]{1,0:T(8,128)(2,1)S(1)}, u32[]{:S(2)}, u32[]{:S(2)}) collective-permute-start(bf16[512,2048]{1,0:T(8,128)(2,1)} %copy-done), channel_id=1, source_target_pairs={{0,1},{1,0},{2,3},{3,2},{4,5},{5,4},{6,7},{7,6},{8,9},{9,8},{10,11... | collective-permute-start | bytes 6291464 | tf_op jit(solution)/shard_map/ppermute | solution.py:92
  135.6 17.6 %collective-permute-start.21 = (bf16[640,512]{1,0:T(8,128)(2,1)}, bf16[640,512]{1,0:T(8,128)(2,1)S(1)}, u32[]{:S(2)}, u32[]{:S(2)}) collective-permute-start(bf16[640,512]{1,0:T(8,128)(2,1)} %get-tuple-element.33), channel_id=1, source_target_pairs={{0,1},{1,0},{2,3},{3,2},{4,5},{5,4},{6,7},{7,6},{8,9},{9,8},{10,11... | collective-permute-start | bytes 1966088 | tf_op jit(solution)/shard_map/ppermute | solution.py:92
  173.6 32.3 %collective-permute-start.26 = (bf16[64,2048]{1,0:T(8,128)(2,1)S(1)}, bf16[64,2048]{1,0:T(8,128)(2,1)S(1)}, u32[]{:S(2)}, u32[]{:S(2)}) collective-permute-start(bf16[64,2048]{1,0:T(8,128)(2,1)S(1)} %copy-done.31), channel_id=1, source_target_pairs={{0,4},{1,5},{2,6},{3,13},{4,0},{5,1},{6,2},{7,3},{8,12},{9,7},{10,... | collective-permute-start | bytes 786440 | tf_op jit(solution)/shard_map/ppermute | solution.py:92
  176.5 31.0 %collective-permute-start.34 = (bf16[64,2048]{1,0:T(8,128)(2,1)S(1)}, bf16[64,2048]{1,0:T(8,128)(2,1)S(1)}, u32[]{:S(2)}, u32[]{:S(2)}) collective-permute-start(bf16[64,2048]{1,0:T(8,128)(2,1)S(1)} %copy-done.30), channel_id=1, source_target_pairs={{0,4},{1,5},{2,14},{3,13},{4,0},{5,1},{6,2},{7,3},{8,12},{9,7},{10... | collective-permute-start | bytes 786440 | tf_op jit(solution)/shard_map/ppermute | solution.py:92
  176.6 33.0 %collective-permute-start.24 = (bf16[64,2048]{1,0:T(8,128)(2,1)}, bf16[64,2048]{1,0:T(8,128)(2,1)S(1)}, u32[]{:S(2)}, u32[]{:S(2)}) collective-permute-start(bf16[64,2048]{1,0:T(8,128)(2,1)} %get-tuple-element.34), channel_id=1, source_target_pairs={{0,0},{1,1},{2,2},{3,3},{4,4},{5,5},{6,6},{7,13},{8,8},{9,9},{10,1... | collective-permute-start | bytes 786440 | tf_op jit(solution)/shard_map/ppermute | solution.py:92
  179.5 26.3 %collective-permute-start.31 = (bf16[32,2048]{1,0:T(8,128)(2,1)}, bf16[32,2048]{1,0:T(8,128)(2,1)S(1)}, u32[]{:S(2)}, u32[]{:S(2)}) collective-permute-start(bf16[32,2048]{1,0:T(8,128)(2,1)} %get-tuple-element.41), channel_id=1, source_target_pairs={{0,12},{1,13},{2,0},{3,1},{4,2},{5,3},{6,4},{7,5},{8,14},{9,15},{1... | collective-permute-start | bytes 393224 | tf_op jit(solution)/shard_map/ppermute | solution.py:92
  191.8 21.0 %collective-permute-start.25 = (bf16[64,2048]{1,0:T(8,128)(2,1)}, bf16[64,2048]{1,0:T(8,128)(2,1)S(1)}, u32[]{:S(2)}, u32[]{:S(2)}) collective-permute-start(bf16[64,2048]{1,0:T(8,128)(2,1)} %get-tuple-element.35), channel_id=1, source_target_pairs={{0,2},{1,3},{2,4},{3,5},{4,6},{5,13},{6,0},{7,1},{8,10},{9,11},{10... | collective-permute-start | bytes 786440 | tf_op jit(solution)/shard_map/ppermute | solution.py:92
  (44 other events, 691.5 us)

commit v3 on v2

--- a/solution.py
+++ b/solution.py
@@ -41,10 +41,7 @@
 ALIGNED[14] = [72, 73, 74, 33, 34]
 OWNER = list(range(16))
 OWNER[7], OWNER[13] = 13, 7
-PARTS = ((0, 64), (64, 96), (96, 160))
-PART_OWNER = [list(OWNER) for _ in PARTS]
-PART_OWNER[1][6], PART_OWNER[1][12] = 12, 6
-PART_OWNER[2][6], PART_OWNER[2][14] = 14, 6
+MIXED = [[64, 70, 71], [32, 33, 34]]
 
 
 def head_position(unit, plane):
@@ -55,7 +52,8 @@
 
 def build_tables():
     order = np.array([[u - 5 * d for u in ARRANGED[d]] for d in range(16)], np.int32)
-    place = np.zeros((16, 40), np.int32)
+    place = np.zeros((16, 43), np.int32)
+    slot = np.full((16, 3), -1, np.int32)
     for d in range(16):
         z, y, c = d // 8, d % 8 // 2, d % 2
         row = []
@@ -64,11 +62,18 @@
                 other = 8 * z + 2 * ((y + step) % 4) + (c ^ r)
                 row += [head_position(u, z) for u in ALIGNED[other]]
         assert sorted(row) == list(range(40))
-        place[d] = row
-    return order, place
-
-
-ORDER, PLACE = build_tables()
+        place[d] = row + [head_position(u, z) for u in MIXED[z]]
+        if c == 0:
+            for n, u in enumerate(MIXED[z]):
+                (other,) = [e for e in range(16) if u in ALIGNED[e]]
+                assert other // 8 == z and other % 2 == 0
+                at = ALIGNED[other].index(u)
+                assert ARRANGED[other][at] == MIXED[1 - z][n]
+                slot[d, n] = (other % 8 // 2 - y) % 4 * SHARD + at * UNIT
+    return order, place, slot
+
+
+ORDER, PLACE, SLOT = build_tables()
 
 
 def pairs_of(function):
@@ -174,6 +179,7 @@
 ROWS = pl.BlockSpec((SEQ, D), lambda s, place: (s, 0))
 COLUMNS = pl.BlockSpec((2 * KVROWS, SEQ), lambda s, place: (0, s))
 HALF_COLUMNS = pl.BlockSpec((KVROWS, SEQ), lambda s, place: (0, s))
+MIXED_COLUMNS = pl.BlockSpec((3 * UNIT, SEQ), lambda s, place: (0, s))
 
 
 def student_projection(place, x, cosine, sine, arrays):
@@ -246,7 +252,7 @@
 
 
 def gradient_kernel(place, x, qk_student, cosine, sine, *rest):
-    arrays, (out, out_other, held, grads, sems) = rest[:8], rest[8:]
+    arrays, (out, out_other, out_mixed, held, grads, sems) = rest[:8], rest[8:]
     load_weight(place, arrays, held, sems)
     for kv in range(2):
         teacher = project(held, x[...], cosine[...], sine[...], kv)
@@ -254,9 +260,9 @@
         student = [qk_student[base + h * HD : base + (h + 1) * HD, :] for h in range(5)]
         for h, value in enumerate(attention_gradient(student, teacher, cosine[...], sine[...])):
             grads[base + h * HD : base + (h + 1) * HD, :] = value
-    for n in range(40):
+    for n in range(43):
         row = pl.multiple_of(place[n] * UNIT, UNIT)
-        target, at = (out, n) if n < 20 else (out_other, n - 20)
+        target, at = ((out, n), (out_other, n - 20), (out_mixed, n - 40))[n // 20]
         target[at * UNIT : (at + 1) * UNIT, :] = grads[pl.ds(row, UNIT), :]
 
 
@@ -268,14 +274,14 @@
             num_scalar_prefetch=1,
             grid=(count,),
             in_specs=[ROWS, COLUMNS, TABLE, TABLE] + [ANY] * 8,
-            out_specs=[HALF_COLUMNS] * 2,
+            out_specs=[HALF_COLUMNS] * 2 + [MIXED_COLUMNS],
             scratch_shapes=[
                 pltpu.VMEM((2 * KVROWS, D), BF),
                 pltpu.VMEM((2 * KVROWS, SEQ), BF),
                 pltpu.SemaphoreType.DMA((40,)),
             ],
         ),
-        out_shape=[jax.ShapeDtypeStruct((KVROWS, x.shape[0]), BF)] * 2,
+        out_shape=[jax.ShapeDtypeStruct((rows, x.shape[0]), BF) for rows in (KVROWS, KVROWS, 3 * UNIT)],
         compiler_params=params(56),
         cost_estimate=pl.CostEstimate(
             flops=6 * x.shape[0] * 2 * KVROWS * D, bytes_accessed=9 * 2**20, transcendentals=0
@@ -287,42 +293,55 @@
 TILE = 512
 
 
-def weight_kernel(steps, own_a, own_b, other_a, other_b, xa, xb, ya, yb, *outs):
-    for at, step in enumerate(steps):
+def weight_kernel(steps, slot, *refs):
+    grads, mixed, tokens, outs, held = refs[:4], refs[4:8], refs[8:12], refs[12:-1], refs[-1]
+    span = 2 * SEQ
+
+    @pl.when(pl.program_id(0) == 0)
+    def _():
+        for n in range(4):
+            held[:, n * span : (n + 1) * span] = grads[n][...]
+
+        @pl.when(slot[0] >= 0)
+        def _():
+            for u in range(3):
+                row = pl.multiple_of(slot[u], UNIT)
+                for n in range(4):
+                    unit = mixed[n][u * UNIT : (u + 1) * UNIT, :]
+                    held[pl.ds(row, UNIT), n * span : (n + 1) * span] = unit
+
+    for step, out in zip(steps, outs):
         rows = slice(step * SHARD, (step + 1) * SHARD)
-        total = dot(own_a[rows, :], xa[...])
-        total += dot(own_b[rows, :], xb[...])
-        total += dot(other_a[rows, :], ya[...])
-        total += dot(other_b[rows, :], yb[...])
-        total = total.astype(BF)
-        for n, (low, high) in enumerate(PARTS):
-            outs[at * 3 + n][...] = total[low:high]
-
-
-def weight_gradient(steps, grads, tokens):
-    whole = [pl.BlockSpec((KVROWS, 2 * SEQ), lambda t: (0, 0))] * 4
+        total = dot(held[rows, :span], tokens[0][...])
+        for n in range(1, 4):
+            total += dot(held[rows, n * span : (n + 1) * span], tokens[n][...])
+        out[...] = total.astype(BF)
+
+
+def weight_gradient(steps, slot, grads, mixed, tokens):
+    span = 2 * SEQ
     return pl.pallas_call(
         lambda *refs: weight_kernel(steps, *refs),
-        grid=(D // TILE,),
-        in_specs=whole + [pl.BlockSpec((2 * SEQ, TILE), lambda t: (0, t))] * 4,
-        out_specs=[pl.BlockSpec((h - l, TILE), lambda t: (0, t)) for l, h in PARTS] * len(steps),
-        out_shape=[jax.ShapeDtypeStruct((h - l, D), BF) for l, h in PARTS] * len(steps),
+        grid_spec=pltpu.PrefetchScalarGridSpec(
+            num_scalar_prefetch=1,
+            grid=(D // TILE,),
+            in_specs=[pl.BlockSpec((KVROWS, span), lambda t, slot: (0, 0))] * 4
+            + [pl.BlockSpec((3 * UNIT, span), lambda t, slot: (0, 0))] * 4
+            + [pl.BlockSpec((span, TILE), lambda t, slot: (0, t))] * 4,
+            out_specs=[pl.BlockSpec((SHARD, TILE), lambda t, slot: (0, t))] * len(steps),
+            scratch_shapes=[pltpu.VMEM((KVROWS, 4 * span), BF)],
+        ),
+        out_shape=[jax.ShapeDtypeStruct((SHARD, D), BF)] * len(steps),
         compiler_params=params(56),
         cost_estimate=pl.CostEstimate(
             flops=2 * len(steps) * SHARD * 8 * SEQ * D, bytes_accessed=12 * 2**20, transcendentals=0
         ),
         name="weight_gradient",
-    )(*grads, *tokens)
-
-
-def adam_kernel(table, *refs):
-    position = pl.program_id(0)
-    pieces, (weight, one, two, weight_out, one_out, two_out) = refs[:12], refs[12:]
-    sums = []
-    for n in range(3):
-        a, b, c, d = (pieces[4 * n + s][...].astype(F32) for s in range(4))
-        sums.append((a + b) + (c + d))
-    gradient = jnp.where(position < 2, sums[0], jnp.where(position == 2, sums[1], sums[2]))
+    )(slot, *grads, *mixed, *tokens)
+
+
+def adam_kernel(order, a, b, c, d, weight, one, two, weight_out, one_out, two_out):
+    gradient = (a[...].astype(F32) + b[...].astype(F32)) + (c[...].astype(F32) + d[...].astype(F32))
     first_new = BETA_ONE * one[...] + (1.0 - BETA_ONE) * gradient
     second_new = BETA_TWO * two[...] + (1.0 - BETA_TWO) * gradient * gradient
     step_dir = (
@@ -336,25 +355,21 @@
     two_out[...] = second_new
 
 
-def adam(order, pieces, weight, one, two):
-    native = pl.BlockSpec((UNIT, D), lambda k, order: (order[k], 0))
-    parts = [
-        pl.BlockSpec((UNIT, D), lambda k, order: (jnp.minimum(k, 1), 0)),
-        pl.BlockSpec((UNIT, D), lambda k, order: (0, 0)),
-        pl.BlockSpec((UNIT, D), lambda k, order: (jnp.maximum(k - 3, 0), 0)),
-    ]
+def adam(order, blocks, weight, one, two):
+    native = pl.BlockSpec((UNIT, D // 2), lambda k, h, order: (order[k], h))
+    straight = pl.BlockSpec((UNIT, D // 2), lambda k, h, order: (k, h))
     return pl.pallas_call(
         adam_kernel,
         grid_spec=pltpu.PrefetchScalarGridSpec(
             num_scalar_prefetch=1,
-            grid=(5,),
-            in_specs=[part for part in parts for _ in range(4)] + [native] * 3,
+            grid=(5, 2),
+            in_specs=[straight] * 4 + [native] * 3,
             out_specs=[native] * 3,
         ),
         out_shape=[jax.ShapeDtypeStruct((SHARD, D), F32)] * 3,
         compiler_params=params(56),
         name="adam",
-    )(order, *pieces, weight, one, two)
+    )(order, *blocks, weight, one, two)
 
 
 def rotary_tables():
@@ -382,6 +397,7 @@
     me = lax.axis_index("fsdp")
     order = jnp.asarray(ORDER)[me]
     place = jnp.asarray(PLACE)[me]
+    slot = jnp.asarray(SLOT)[me]
     cosine, sine = rotary_tables()
 
     student_shard, teacher_shard = arrange(order, master, snapshot[0])
@@ -396,13 +412,15 @@
     swap_a = send(student_shard, SWAP_A)
     swap_b = send(student_shard[64:96], SWAP_B)
     main = send_next(teacher_shard, list(enumerate(OWNER)))
+    tail = send_next(teacher_shard[96:], SWAP_PART)
+    middle = send_next(teacher_shard[64:96], SWAP_B)
     plane_tokens = send(own_tokens, TO_PLANE)
     student = jnp.where(whole | mask_a, swap_a, jnp.where(mask_b, widen(swap_b, 64), student_shard))
-    tail = send(main[96:], SWAP_PART)
-    middle = send(main[64:96], SWAP_B)
+    student_too, main, tail, middle = lax.optimization_barrier((student, main, tail, middle))
     teacher = jnp.where(mask_a, widen(tail, 96), jnp.where(mask_b, widen(middle, 64), main))
 
-    student_rows = both_cores(ring_gather(student, True))
+    student_own = ring_gather(student, True)
+    student_rows = student_own + [send(p, TO_CORE) for p in [student_too] + student_own[1:]]
     qk_own = student_projection(place, own_tokens, cosine, sine, student_rows)
     teacher_own = ring_gather(teacher, False)
     teacher_own[2], qk_own = lax.optimization_barrier((teacher_own[2], qk_own))
@@ -411,32 +429,28 @@
     core_tokens = send(own_tokens, TO_CORE)
     far_tokens = send(plane_tokens, TO_CORE)
 
-    grads, others = [], []
+    grads, others, given = [], [], []
     for x, qk_student in ((own_tokens, qk_own), (plane_tokens, qk_plane)):
-        grad, other = projection_gradient(place, x, qk_student, cosine, sine, teacher_rows)
+        grad, other, mixed = projection_gradient(place, x, qk_student, cosine, sine, teacher_rows)
         grads.append(grad)
         others.append(send(other, TO_CORE))
-
+        given.append(send(mixed, TO_PLANE))
+    received = given[::-1]
     parts = grads + others
+    mixed_parts = received + [send(value, TO_CORE) for value in received]
     all_tokens = (own_tokens, plane_tokens, core_tokens, far_tokens)
 
-    def to_owner(blocks, step):
-        out = []
-        for part, block in enumerate(blocks):
-            pairs = []
-            for d in range(16):
-                aligned = d // 8 * 8 + (d % 8 // 2 + step) % 4 * 2 + d % 2
-                pairs.append((d, PART_OWNER[part][aligned]))
-            out.append(send(block, pairs))
-        return out
-
-    two = weight_gradient((2,), parts, all_tokens)
-    got = {2: to_owner(two, 2)}
-    rest = weight_gradient((1, 3, 0), parts, all_tokens)
-    for at, step in enumerate((1, 3, 0)):
-        got[step] = to_owner(rest[at * 3 : at * 3 + 3], step)
-    pieces = [got[step][part] for part in range(3) for step in range(4)]
-    updated = adam(order, pieces, master, moment_one[0], moment_two[0])
+    def to_owner(block, step):
+        pairs = []
+        for d in range(16):
+            pairs.append((d, OWNER[d // 8 * 8 + (d % 8 // 2 + step) % 4 * 2 + d % 2]))
+        return send(block, pairs)
+
+    blocks = []
+    for steps in ((2,), (1, 3, 0)):
+        made = weight_gradient(steps, slot, parts, mixed_parts, all_tokens)
+        blocks += [to_owner(block, step) for block, step in zip(made, steps)]
+    updated = adam(order, blocks, master, moment_one[0], moment_two[0])
     return tuple(value[None] for value in updated)
 
 

time: 233 us -> 236 us (1.013)
  the two profiles are of different devices: /device:TPU:1 before, /device:TPU:25 now
where the time goes in v3:
time: 236 us; the launch traced here: 235 us
  Pallas kernels  82.3 us (35%)
  starting transfers between devices  79.2 us (34%)
  waiting for transfers between devices  55.6 us (24%)
  local copies, waits for them, and re-layouts  12.6 us (5%)
  other arithmetic  3.85 us (2%)
    ppermute x29, starting transfers between devices, send(): return lax.ppermute(value, 'fsdp', pairs)  74.1 us
    ppermute x29, waiting for transfers between devices, send(): return lax.ppermute(value, 'fsdp', pairs)  49.6 us
    pallas_call x2, Pallas kernels, projection_gradient(): pl.pallas_call(gradient_kernel, grid_spec=pltpu.PrefetchScalarGridSpec(nu...  33.9 us
    pallas_call x2, Pallas kernels, student_projection(): pl.pallas_call(student_kernel, grid_spec=pltpu.PrefetchScalarGridSpec(num...  17.7 us
    pallas_call x2, Pallas kernels, weight_gradient(): pl.pallas_call(lambda *refs: weight_kernel(steps, *refs), grid_spec=pltpu...  16.9 us
    pallas_call x1, Pallas kernels, adam(): pl.pallas_call(adam_kernel, grid_spec=pltpu.PrefetchScalarGridSpec(num_sc...  8.98 us
    ppermute x3, waiting for transfers between devices, send_next(): lax.ppermute(value, ('blk', 'fsdp'), [(g * 16 + a, (g + 1) % 8 * 16 + b)...  5.95 us
    ppermute x3, starting transfers between devices, send_next(): lax.ppermute(value, ('blk', 'fsdp'), [(g * 16 + a, (g + 1) % 8 * 16 + b)...  5.14 us
  transfers between devices with their start and end apart: 32, of which 9 were waited for; matrix products, arithmetic and copies ran while one was open for 5% of the time, Pallas kernels for 25%

profile of v3, /device:TPU:25, one launch (start us, length us, event | category | flops | bytes accessed | tf_op | source)
XLA Modules:
  0.0 234.5 jit_solution(9950265108120066388)
XLA Ops:
  1.8 4.8 %arrange.1 = (bf16[160,2048]{1,0:T(8,128)(2,1)}, bf16[160,2048]{1,0:T(8,128)(2,1)}) custom-call(s32[5]{0:T(128)} %fusion.order, f32[160,2048]{1,0:T(8,128)} %bitcast.14, bf16[160,2048]{1,0:T(8,128)(2,1)} %bitcast.24), custom_call_target="tpu_custom_call" | custom-call | tf_op jit(solution)/shard_map/arrange/pallas_call | solution.py:120
  6.6 3.7 %collective-permute-start = (bf16[160,2048]{1,0:T(8,128)(2,1)}, bf16[160,2048]{1,0:T(8,128)(2,1)S(1)}, u32[]{:S(2)}, u32[]{:S(2)}) collective-permute-start(bf16[160,2048]{1,0:T(8,128)(2,1)} %get-tuple-element.23), channel_id=1, source_target_pairs={{7,13},{13,7},{6,14},{14,6},{23,29},{29,23},{22,30},{30,22},{39,45... | collective-permute-start | bytes 1966088 | tf_op jit(solution)/shard_map/ppermute | solution.py:97
  13.2 3.0 %collective-permute-start.2 = (bf16[160,2048]{1,0:T(8,128)(2,1)}, bf16[160,2048]{1,0:T(8,128)(2,1)S(1)}, u32[]{:S(2)}, u32[]{:S(2)}) collective-permute-start(bf16[160,2048]{1,0:T(8,128)(2,1)} %get-tuple-element.24), channel_id=1, source_target_pairs={{0,16},{1,17},{2,18},{3,19},{4,20},{5,21},{6,22},{7,29},{8,24},{9,... | collective-permute-start | bytes 1966088 | tf_op jit(solution)/shard_map/ppermute | solution.py:101
  23.4 2.7 %collective-permute-start.7 = (bf16[160,2048]{1,0:T(8,128)(2,1)S(1)}, bf16[160,2048]{1,0:T(8,128)(2,1)S(1)}, u32[]{:S(2)}, u32[]{:S(2)}) collective-permute-start(bf16[160,2048]{1,0:T(8,128)(2,1)S(1)} %select_select_fusion.1.rest_0_), channel_id=1, source_target_pairs={{0,6},{1,7},{2,0},{3,1},{4,2},{5,3},{6,4},{7,5},{8,14},{9,15},{10,... | collective-permute-start | bytes 1966088 | tf_op jit(solution)/shard_map/ppermute | solution.py:97
  26.2 5.9 %collective-permute-done.2 = bf16[160,2048]{1,0:T(8,128)(2,1)S(1)} collective-permute-done((bf16[160,2048]{1,0:T(8,128)(2,1)}, bf16[160,2048]{1,0:T(8,128)(2,1)S(1)}, u32[]{:S(2)}, u32[]{:S(2)}) %collective-permute-start.2) | collective-permute-done | bytes 655392 | tf_op jit(solution)/shard_map/ppermute | solution.py:101
  32.1 27.9 %collective-permute-start.10 = (bf16[160,2048]{1,0:T(8,128)(2,1)S(1)}, bf16[160,2048]{1,0:T(8,128)(2,1)S(1)}, u32[]{:S(2)}, u32[]{:S(2)}) collective-permute-start(bf16[160,2048]{1,0:T(8,128)(2,1)S(1)} %select_select_fusion.1.rest_0_), channel_id=1, source_target_pairs={{0,1},{1,0},{2,3},{3,2},{4,5},{5,4},{6,7},{7,6},{8,9},{9,8},{10,11... | collective-permute-start | bytes 1966088 | tf_op jit(solution)/shard_map/ppermute | solution.py:97
  61.5 2.9 %collective-permute-start.9 = (bf16[160,2048]{1,0:T(8,128)(2,1)S(1)}, bf16[160,2048]{1,0:T(8,128)(2,1)S(1)}, u32[]{:S(2)}, u32[]{:S(2)}) collective-permute-start(bf16[160,2048]{1,0:T(8,128)(2,1)S(1)} %collective-permute-done.8.rest_3_), channel_id=1, source_target_pairs={{0,2},{1,3},{2,4},{3,5},{4,6},{5,7},{6,0},{7,1},{8,10},{9,11},{10,... | collective-permute-start | bytes 1966088 | tf_op jit(solution)/shard_map/ppermute | solution.py:97
  65.8 11.7 %collective-permute-start.11 = (bf16[160,2048]{1,0:T(8,128)(2,1)S(1)}, bf16[160,2048]{1,0:T(8,128)(2,1)S(1)}, u32[]{:S(2)}, u32[]{:S(2)}) collective-permute-start(bf16[160,2048]{1,0:T(8,128)(2,1)S(1)} %collective-permute-done.7.rest_1_), channel_id=1, source_target_pairs={{0,1},{1,0},{2,3},{3,2},{4,5},{5,4},{6,7},{7,6},{8,9},{9,8},{10,11... | collective-permute-start | bytes 1966088 | tf_op jit(solution)/shard_map/ppermute | solution.py:97
  77.5 2.2 collective-permute-done.5.rest_1_
  79.7 6.1 %collective-permute-start.13 = (bf16[160,2048]{1,0:T(8,128)(2,1)S(1)}, bf16[160,2048]{1,0:T(8,128)(2,1)S(1)}, u32[]{:S(2)}, u32[]{:S(2)}) collective-permute-start(bf16[160,2048]{1,0:T(8,128)(2,1)S(1)} %collective-permute-done.8.rest_3_), channel_id=1, source_target_pairs={{0,1},{1,0},{2,3},{3,2},{4,5},{5,4},{6,7},{7,6},{8,9},{9,8},{10,11... | collective-permute-start | bytes 1966088 | tf_op jit(solution)/shard_map/ppermute | solution.py:97
  85.9 6.7 %collective-permute-done.14.rest_3_ = bf16[160,2048]{1,0:T(8,128)(2,1)} collective-permute-done((bf16[160,2048]{1,0:T(8,128)(2,1)S(1)}, bf16[160,2048]{1,0:T(8,128)(2,1)}, u32[]{:S(2)}, u32[]{:S(2)}) %collective-permute-start.14) | collective-permute-done | bytes 655392 | tf_op jit(solution)/shard_map/ppermute | solution.py:97
  98.6 8.9 %student_projection.2.qk_student = bf16[1280,512]{1,0:T(8,128)(2,1)} custom-call(s32[43]{0:T(128)} %fusion.2.place, bf16[512,2048]{1,0:T(8,128)(2,1)} %bitcast.16, f32[64,256]{1,0:T(8,128)} %get-tuple-element.44.cosine, f32[64,256]{1,0:T(8,128)} %get-tuple-element.43.sine, bf16[160,2048]{1,0:T(8,128)(2,1)} %copy-done.8, bf16[160,2048]{1,0:T(8,128)(2,1)} %copy-done.19, ...), custom_call_target="tpu_custom_call" | custom-call | flops 2684354560 | bytes 9437184 | tf_op jit(solution)/shard_map/student_projection/pallas_call | solution.py:187
  107.6 3.0 %collective-permute-done.6.rest_2_ = bf16[160,2048]{1,0:T(8,128)(2,1)} collective-permute-done((bf16[160,2048]{1,0:T(8,128)(2,1)S(1)}, bf16[160,2048]{1,0:T(8,128)(2,1)}, u32[]{:S(2)}, u32[]{:S(2)}) %collective-permute-start.6) | collective-permute-done | bytes 655392 | tf_op jit(solution)/shard_map/ppermute | solution.py:97
  113.3 8.8 %student_projection.3.qk_student = bf16[1280,512]{1,0:T(8,128)(2,1)} custom-call(s32[43]{0:T(128)} %fusion.2.place, bf16[512,2048]{1,0:T(8,128)(2,1)} %copy-done.2, f32[64,256]{1,0:T(8,128)} %get-tuple-element.44.cosine, f32[64,256]{1,0:T(8,128)} %get-tuple-element.43.sine, bf16[160,2048]{1,0:T(8,128)(2,1)} %copy-done.8, bf16[160,2048]{1,0:T(8,128)(2,1)} %copy-done.19, ...), custom_call_target="tpu_custom_call" | custom-call | flops 2684354560 | bytes 9437184 | tf_op jit(solution)/shard_map/student_projection/pallas_call | solution.py:187
  122.4 17.0 %projection_gradient.3 = (bf16[640,512]{1,0:T(8,128)(2,1)}, bf16[640,512]{1,0:T(8,128)(2,1)}, bf16[96,512]{1,0:T(8,128)(2,1)}) custom-call(s32[43]{0:T(128)} %fusion.2.place, bf16[512,2048]{1,0:T(8,128)(2,1)} %copy-done.2, bf16[1280,512]{1,0:T(8,128)(2,1)} %student_projection.3.qk_student, f32[64,256]{1,0:T(8,128)} %get-tuple-element.44.cosine, ...), custom_call_target="tpu_custom_call" | custom-call | flops 8053063680 | bytes 9437184 | tf_op jit(solution)/shard_map/projection_gradient/pallas_call | solution.py:271
  140.0 16.9 %projection_gradient.2 = (bf16[640,512]{1,0:T(8,128)(2,1)}, bf16[640,512]{1,0:T(8,128)(2,1)}, bf16[96,512]{1,0:T(8,128)(2,1)}) custom-call(s32[43]{0:T(128)} %fusion.2.place, bf16[512,2048]{1,0:T(8,128)(2,1)} %bitcast.17, bf16[1280,512]{1,0:T(8,128)(2,1)} %student_projection.2.qk_student, f32[64,256]{1,0:T(8,128)} %get-tuple-element.44.cosine, ...), custom_call_target="tpu_custom_call" | custom-call | flops 8053063680 | bytes 9437184 | tf_op jit(solution)/shard_map/projection_gradient/pallas_call | solution.py:271
  158.6 2.5 %collective-permute-done.22.refs_5_ = bf16[96,512]{1,0:T(8,128)(2,1)S(1)} collective-permute-done((bf16[96,512]{1,0:T(8,128)(2,1)S(1)}, bf16[96,512]{1,0:T(8,128)(2,1)S(1)}, u32[]{:S(2)}, u32[]{:S(2)}) %collective-permute-start.22) | collective-permute-done | bytes 98336 | tf_op jit(solution)/shard_map/ppermute | solution.py:97
  161.1 2.1 collective-permute-start.24
  167.7 9.5 %weight_gradient.3 = (bf16[160,2048]{1,0:T(8,128)(2,1)}, bf16[160,2048]{1,0:T(8,128)(2,1)}, bf16[160,2048]{1,0:T(8,128)(2,1)}) custom-call(s32[3]{0:T(128)} %fusion.1.refs_0_, bf16[640,512]{1,0:T(8,128)(2,1)} %get-tuple-element.31.refs_1_, bf16[640,512]{1,0:T(8,128)(2,1)} %get-tuple-element.32.refs_2_, bf16[640,512]{1,0:T(8,128)(2,1)} %copy-done.6, ...), custom_call_target="tpu_custom_call" | custom-call | flops 4026531840 | bytes 12582912 | tf_op jit(solution)/shard_map/weight_gradient/pallas_call | solution.py:323
  178.6 4.0 %collective-permute-start.31 = (bf16[160,2048]{1,0:T(8,128)(2,1)}, bf16[160,2048]{1,0:T(8,128)(2,1)S(1)}, u32[]{:S(2)}, u32[]{:S(2)}) collective-permute-start(bf16[160,2048]{1,0:T(8,128)(2,1)} %get-tuple-element.39), channel_id=1, source_target_pairs={{0,0},{1,1},{2,2},{3,3},{4,4},{5,5},{6,6},{7,13},{8,8},{9,9},{10,1... | collective-permute-start | bytes 1966088 | tf_op jit(solution)/shard_map/ppermute | solution.py:97
  182.6 7.5 %weight_gradient.2 = bf16[160,2048]{1,0:T(8,128)(2,1)} custom-call(s32[3]{0:T(128)} %fusion.1.refs_0_, bf16[640,512]{1,0:T(8,128)(2,1)} %get-tuple-element.31.refs_1_, bf16[640,512]{1,0:T(8,128)(2,1)} %get-tuple-element.32.refs_2_, bf16[640,512]{1,0:T(8,128)(2,1)} %copy-done.6, bf16[640,512]{1,0:T(8,128)(2,1)} %copy-done.5, bf16[96,512]{1,0:T(8,128)(2,1)} %copy-done.13, ...), custom_call_target="tpu_custom_call" | custom-call | flops 1342177280 | bytes 12582912 | tf_op jit(solution)/shard_map/weight_gradient/pallas_call | solution.py:323
  190.0 16.9 %collective-permute-done.29.b = bf16[160,2048]{1,0:T(8,128)(2,1)S(1)} collective-permute-done((bf16[160,2048]{1,0:T(8,128)(2,1)}, bf16[160,2048]{1,0:T(8,128)(2,1)S(1)}, u32[]{:S(2)}, u32[]{:S(2)}) %collective-permute-start.29) | collective-permute-done | bytes 655392 | tf_op jit(solution)/shard_map/ppermute | solution.py:97
  208.0 16.7 %collective-permute-done.28.a = bf16[160,2048]{1,0:T(8,128)(2,1)S(1)} collective-permute-done((bf16[160,2048]{1,0:T(8,128)(2,1)}, bf16[160,2048]{1,0:T(8,128)(2,1)S(1)}, u32[]{:S(2)}, u32[]{:S(2)}) %collective-permute-start.28) | collective-permute-done | bytes 655392 | tf_op jit(solution)/shard_map/ppermute | solution.py:97
  225.5 9.0 %adam.1 = (f32[160,2048]{1,0:T(8,128)}, f32[160,2048]{1,0:T(8,128)}, f32[160,2048]{1,0:T(8,128)}) custom-call(s32[5]{0:T(128)} %fusion.order, bf16[160,2048]{1,0:T(8,128)(2,1)} %copy-done.12, bf16[160,2048]{1,0:T(8,128)(2,1)} %copy-done.9, bf16[160,2048]{1,0:T(8,128)(2,1)} %copy-done.10, bf16[160,2048]{1,0:T(8,128)(2,1)} %copy-done.11, ...), custom_call_target="tpu_custom_call" | custom-call | tf_op jit(solution)/shard_map/adam/pallas_call | solution.py:361
  (113 shorter events, 33.1 us)
Async XLA Ops:
  6.6 13.3 %collective-permute-start = (bf16[160,2048]{1,0:T(8,128)(2,1)}, bf16[160,2048]{1,0:T(8,128)(2,1)S(1)}, u32[]{:S(2)}, u32[]{:S(2)}) collective-permute-start(bf16[160,2048]{1,0:T(8,128)(2,1)} %get-tuple-element.23), channel_id=1, source_target_pairs={{7,13},{13,7},{6,14},{14,6},{23,29},{29,23},{22,30},{30,22},{39,45... | collective-permute-start | bytes 1966088 | tf_op jit(solution)/shard_map/ppermute | solution.py:97
  13.2 18.9 %collective-permute-start.2 = (bf16[160,2048]{1,0:T(8,128)(2,1)}, bf16[160,2048]{1,0:T(8,128)(2,1)S(1)}, u32[]{:S(2)}, u32[]{:S(2)}) collective-permute-start(bf16[160,2048]{1,0:T(8,128)(2,1)} %get-tuple-element.24), channel_id=1, source_target_pairs={{0,16},{1,17},{2,18},{3,19},{4,20},{5,21},{6,22},{7,29},{8,24},{9,... | collective-permute-start | bytes 1966088 | tf_op jit(solution)/shard_map/ppermute | solution.py:101
  21.5 40.0 %collective-permute-start.8 = (bf16[160,2048]{1,0:T(8,128)(2,1)S(1)}, bf16[160,2048]{1,0:T(8,128)(2,1)S(1)}, u32[]{:S(2)}, u32[]{:S(2)}) collective-permute-start(bf16[160,2048]{1,0:T(8,128)(2,1)S(1)} %select_select_fusion.1.rest_0_), channel_id=1, source_target_pairs={{0,2},{1,3},{2,4},{3,5},{4,6},{5,7},{6,0},{7,1},{8,10},{9,11},{10,... | collective-permute-start | bytes 1966088 | tf_op jit(solution)/shard_map/ppermute | solution.py:97
  23.3 88.7 %collective-permute-start.19 = (bf16[512,2048]{1,0:T(8,128)(2,1)S(1)}, bf16[512,2048]{1,0:T(8,128)(2,1)S(1)}, u32[]{:S(2)}, u32[]{:S(2)}) collective-permute-start(bf16[512,2048]{1,0:T(8,128)(2,1)S(1)} %bitcast.20), channel_id=1, source_target_pairs={{0,8},{1,9},{2,10},{3,11},{4,12},{5,13},{6,14},{7,15},{8,0},{9,1},... | collective-permute-start | bytes 6291464 | tf_op jit(solution)/shard_map/ppermute | solution.py:97
  23.4 42.4 %collective-permute-start.7 = (bf16[160,2048]{1,0:T(8,128)(2,1)S(1)}, bf16[160,2048]{1,0:T(8,128)(2,1)S(1)}, u32[]{:S(2)}, u32[]{:S(2)}) collective-permute-start(bf16[160,2048]{1,0:T(8,128)(2,1)S(1)} %select_select_fusion.1.rest_0_), channel_id=1, source_target_pairs={{0,6},{1,7},{2,0},{3,1},{4,2},{5,3},{6,4},{7,5},{8,14},{9,15},{10,... | collective-permute-start | bytes 1966088 | tf_op jit(solution)/shard_map/ppermute | solution.py:97
  32.1 32.3 %collective-permute-start.10 = (bf16[160,2048]{1,0:T(8,128)(2,1)S(1)}, bf16[160,2048]{1,0:T(8,128)(2,1)S(1)}, u32[]{:S(2)}, u32[]{:S(2)}) collective-permute-start(bf16[160,2048]{1,0:T(8,128)(2,1)S(1)} %select_select_fusion.1.rest_0_), channel_id=1, source_target_pairs={{0,1},{1,0},{2,3},{3,2},{4,5},{5,4},{6,7},{7,6},{8,9},{9,8},{10,11... | collective-permute-start | bytes 1966088 | tf_op jit(solution)/shard_map/ppermute | solution.py:97
  61.4 18.3 %collective-permute-start.5 = (bf16[160,2048]{1,0:T(8,128)(2,1)S(1)}, bf16[160,2048]{1,0:T(8,128)(2,1)S(1)}, u32[]{:S(2)}, u32[]{:S(2)}) collective-permute-start(bf16[160,2048]{1,0:T(8,128)(2,1)S(1)} %select_select_fusion.rest_0_), channel_id=1, source_target_pairs={{0,6},{1,7},{2,0},{3,1},{4,2},{5,3},{6,4},{7,5},{8,14},{9,15},{10,... | collective-permute-start | bytes 1966088 | tf_op jit(solution)/shard_map/ppermute | solution.py:97
  61.5 24.3 %collective-permute-start.9 = (bf16[160,2048]{1,0:T(8,128)(2,1)S(1)}, bf16[160,2048]{1,0:T(8,128)(2,1)S(1)}, u32[]{:S(2)}, u32[]{:S(2)}) collective-permute-start(bf16[160,2048]{1,0:T(8,128)(2,1)S(1)} %collective-permute-done.8.rest_3_), channel_id=1, source_target_pairs={{0,2},{1,3},{2,4},{3,5},{4,6},{5,7},{6,0},{7,1},{8,10},{9,11},{10,... | collective-permute-start | bytes 1966088 | tf_op jit(solution)/shard_map/ppermute | solution.py:97
  64.5 28.2 %collective-permute-start.14 = (bf16[160,2048]{1,0:T(8,128)(2,1)S(1)}, bf16[160,2048]{1,0:T(8,128)(2,1)}, u32[]{:S(2)}, u32[]{:S(2)}) collective-permute-start(bf16[160,2048]{1,0:T(8,128)(2,1)S(1)} %select_select_fusion.rest_0_), channel_id=1, source_target_pairs={{0,2},{1,3},{2,4},{3,5},{4,6},{5,7},{6,0},{7,1},{8,10},{9,11},{10,... | collective-permute-start | bytes 1966088 | tf_op jit(solution)/shard_map/ppermute | solution.py:97
  65.8 30.6 %collective-permute-start.11 = (bf16[160,2048]{1,0:T(8,128)(2,1)S(1)}, bf16[160,2048]{1,0:T(8,128)(2,1)S(1)}, u32[]{:S(2)}, u32[]{:S(2)}) collective-permute-start(bf16[160,2048]{1,0:T(8,128)(2,1)S(1)} %collective-permute-done.7.rest_1_), channel_id=1, source_target_pairs={{0,1},{1,0},{2,3},{3,2},{4,5},{5,4},{6,7},{7,6},{8,9},{9,8},{10,11... | collective-permute-start | bytes 1966088 | tf_op jit(solution)/shard_map/ppermute | solution.py:97
  79.7 17.8 %collective-permute-start.13 = (bf16[160,2048]{1,0:T(8,128)(2,1)S(1)}, bf16[160,2048]{1,0:T(8,128)(2,1)S(1)}, u32[]{:S(2)}, u32[]{:S(2)}) collective-permute-start(bf16[160,2048]{1,0:T(8,128)(2,1)S(1)} %collective-permute-done.8.rest_3_), channel_id=1, source_target_pairs={{0,1},{1,0},{2,3},{3,2},{4,5},{5,4},{6,7},{7,6},{8,9},{9,8},{10,11... | collective-permute-start | bytes 1966088 | tf_op jit(solution)/shard_map/ppermute | solution.py:97
  85.8 11.8 %collective-permute-start.12 = (bf16[160,2048]{1,0:T(8,128)(2,1)S(1)}, bf16[160,2048]{1,0:T(8,128)(2,1)S(1)}, u32[]{:S(2)}, u32[]{:S(2)}) collective-permute-start(bf16[160,2048]{1,0:T(8,128)(2,1)S(1)} %collective-permute-done.9.rest_2_), channel_id=1, source_target_pairs={{0,1},{1,0},{2,3},{3,2},{4,5},{5,4},{6,7},{7,6},{8,9},{9,8},{10,11... | collective-permute-start | bytes 1966088 | tf_op jit(solution)/shard_map/ppermute | solution.py:97
  92.7 17.9 %collective-permute-start.6 = (bf16[160,2048]{1,0:T(8,128)(2,1)S(1)}, bf16[160,2048]{1,0:T(8,128)(2,1)}, u32[]{:S(2)}, u32[]{:S(2)}) collective-permute-start(bf16[160,2048]{1,0:T(8,128)(2,1)S(1)} %collective-permute-done.5.rest_1_), channel_id=1, source_target_pairs={{0,6},{1,7},{2,0},{3,1},{4,2},{5,3},{6,4},{7,5},{8,14},{9,15},{10,... | collective-permute-start | bytes 1966088 | tf_op jit(solution)/shard_map/ppermute | solution.py:97
  96.5 25.7 %collective-permute-start.15 = (bf16[160,2048]{1,0:T(8,128)(2,1)S(1)}, bf16[160,2048]{1,0:T(8,128)(2,1)}, u32[]{:S(2)}, u32[]{:S(2)}) collective-permute-start(bf16[160,2048]{1,0:T(8,128)(2,1)S(1)} %select_select_fusion.rest_0_), channel_id=1, source_target_pairs={{0,1},{1,0},{2,3},{3,2},{4,5},{5,4},{6,7},{7,6},{8,9},{9,8},{10,11... | collective-permute-start | bytes 1966088 | tf_op jit(solution)/shard_map/ppermute | solution.py:97
  97.5 24.9 %collective-permute-start.16 = (bf16[160,2048]{1,0:T(8,128)(2,1)S(1)}, bf16[160,2048]{1,0:T(8,128)(2,1)}, u32[]{:S(2)}, u32[]{:S(2)}) collective-permute-start(bf16[160,2048]{1,0:T(8,128)(2,1)S(1)} %collective-permute-done.5.rest_1_), channel_id=1, source_target_pairs={{0,1},{1,0},{2,3},{3,2},{4,5},{5,4},{6,7},{7,6},{8,9},{9,8},{10,11... | collective-permute-start | bytes 1966088 | tf_op jit(solution)/shard_map/ppermute | solution.py:97
  97.6 24.8 %collective-permute-start.18 = (bf16[160,2048]{1,0:T(8,128)(2,1)}, bf16[160,2048]{1,0:T(8,128)(2,1)}, u32[]{:S(2)}, u32[]{:S(2)}) collective-permute-start(bf16[160,2048]{1,0:T(8,128)(2,1)} %collective-permute-done.14.rest_3_), channel_id=1, source_target_pairs={{0,1},{1,0},{2,3},{3,2},{4,5},{5,4},{6,7},{7,6},{8,9},{9,8},{10,11... | collective-permute-start | bytes 1966088 | tf_op jit(solution)/shard_map/ppermute | solution.py:97
  110.6 11.8 %collective-permute-start.17 = (bf16[160,2048]{1,0:T(8,128)(2,1)}, bf16[160,2048]{1,0:T(8,128)(2,1)}, u32[]{:S(2)}, u32[]{:S(2)}) collective-permute-start(bf16[160,2048]{1,0:T(8,128)(2,1)} %collective-permute-done.6.rest_2_), channel_id=1, source_target_pairs={{0,1},{1,0},{2,3},{3,2},{4,5},{5,4},{6,7},{7,6},{8,9},{9,8},{10,11... | collective-permute-start | bytes 1966088 | tf_op jit(solution)/shard_map/ppermute | solution.py:97
  112.0 46.0 %collective-permute-start.26 = (bf16[512,2048]{1,0:T(8,128)(2,1)S(1)}, bf16[512,2048]{1,0:T(8,128)(2,1)S(1)}, u32[]{:S(2)}, u32[]{:S(2)}) collective-permute-start(bf16[512,2048]{1,0:T(8,128)(2,1)S(1)} %bitcast.21), channel_id=1, source_target_pairs={{0,1},{1,0},{2,3},{3,2},{4,5},{5,4},{6,7},{7,6},{8,9},{9,8},{10,11... | collective-permute-start | bytes 6291464 | tf_op jit(solution)/shard_map/ppermute | solution.py:97
  122.1 43.7 %collective-permute-start.27 = (bf16[512,2048]{1,0:T(8,128)(2,1)}, bf16[512,2048]{1,0:T(8,128)(2,1)S(1)}, u32[]{:S(2)}, u32[]{:S(2)}) collective-permute-start(bf16[512,2048]{1,0:T(8,128)(2,1)} %copy-done.2), channel_id=1, source_target_pairs={{0,1},{1,0},{2,3},{3,2},{4,5},{5,4},{6,7},{7,6},{8,9},{9,8},{10,11... | collective-permute-start | bytes 6291464 | tf_op jit(solution)/shard_map/ppermute | solution.py:97
  139.5 26.3 %collective-permute-start.21 = (bf16[640,512]{1,0:T(8,128)(2,1)}, bf16[640,512]{1,0:T(8,128)(2,1)S(1)}, u32[]{:S(2)}, u32[]{:S(2)}) collective-permute-start(bf16[640,512]{1,0:T(8,128)(2,1)} %get-tuple-element.34), channel_id=1, source_target_pairs={{0,1},{1,0},{2,3},{3,2},{4,5},{5,4},{6,7},{7,6},{8,9},{9,8},{10,11... | collective-permute-start | bytes 1966088 | tf_op jit(solution)/shard_map/ppermute | solution.py:97
  177.1 29.8 %collective-permute-start.29 = (bf16[160,2048]{1,0:T(8,128)(2,1)}, bf16[160,2048]{1,0:T(8,128)(2,1)S(1)}, u32[]{:S(2)}, u32[]{:S(2)}) collective-permute-start(bf16[160,2048]{1,0:T(8,128)(2,1)} %get-tuple-element.37), channel_id=1, source_target_pairs={{0,2},{1,3},{2,4},{3,5},{4,6},{5,13},{6,0},{7,1},{8,10},{9,11},{10... | collective-permute-start | bytes 1966088 | tf_op jit(solution)/shard_map/ppermute | solution.py:97
  178.6 28.3 %collective-permute-start.30 = (bf16[160,2048]{1,0:T(8,128)(2,1)}, bf16[160,2048]{1,0:T(8,128)(2,1)S(1)}, u32[]{:S(2)}, u32[]{:S(2)}) collective-permute-start(bf16[160,2048]{1,0:T(8,128)(2,1)} %get-tuple-element.38), channel_id=1, source_target_pairs={{0,6},{1,13},{2,0},{3,1},{4,2},{5,3},{6,4},{7,5},{8,14},{9,15},{10... | collective-permute-start | bytes 1966088 | tf_op jit(solution)/shard_map/ppermute | solution.py:97
  178.6 29.4 %collective-permute-start.31 = (bf16[160,2048]{1,0:T(8,128)(2,1)}, bf16[160,2048]{1,0:T(8,128)(2,1)S(1)}, u32[]{:S(2)}, u32[]{:S(2)}) collective-permute-start(bf16[160,2048]{1,0:T(8,128)(2,1)} %get-tuple-element.39), channel_id=1, source_target_pairs={{0,0},{1,1},{2,2},{3,3},{4,4},{5,5},{6,6},{7,13},{8,8},{9,9},{10,1... | collective-permute-start | bytes 1966088 | tf_op jit(solution)/shard_map/ppermute | solution.py:97
  190.0 34.7 %collective-permute-start.28 = (bf16[160,2048]{1,0:T(8,128)(2,1)}, bf16[160,2048]{1,0:T(8,128)(2,1)S(1)}, u32[]{:S(2)}, u32[]{:S(2)}) collective-permute-start(bf16[160,2048]{1,0:T(8,128)(2,1)} %weight_gradient.2), channel_id=1, source_target_pairs={{0,4},{1,5},{2,6},{3,13},{4,0},{5,1},{6,2},{7,3},{8,12},{9,7},{10,... | collective-permute-start | bytes 1966088 | tf_op jit(solution)/shard_map/ppermute | solution.py:97
  (34 other events, 421.7 us)

commit v4 on v3

v4 whole, which is shorter than its diff:
```python
import math

import jax
import jax.numpy as jnp
import numpy as np
from jax import lax
from jax.experimental import pallas as pl
from jax.experimental.pallas import tpu as pltpu
from jax.sharding import PartitionSpec as P

HEADS = 16
KVH = 4
HD = 128
SEQ = 256
STEP = 100
D = 2048
THETA = 500000.0
BETA_ONE = 0.9
BETA_TWO = 0.95
LEARN_RATE = 0.002
DECAY = 0.1
EPSILON = 1e-08
MASKED = -1e30

BF = jnp.bfloat16
F32 = jnp.float32
SHARD = 160
ROWS = 8 * SHARD
UNIT = 32
HALF = HD // 2
CORE = 4 * SHARD
EXCHANGED = 2 * HD
INV_ROOT = 1.0 / math.sqrt(HD)

AT_WEIGHT, AT_GIVEN, AT_QUERY, AT_KEY, AT_CORE, AT_STEP, AT_FILL = 0, 8, 9, 17, 19, 27, 31
GIVEN = (1024, 768)
QUERY = (tuple(range(8)), (10, 11, 0, 1, 2, 3, 4, 5))
KEY = ((10, 11), (8, 9))


def build_table():
    table = np.zeros((16, 39), np.int32)
    for d in range(16):
        z, y, c = d // 8, d % 8 // 2, d % 2
        gathered = [320 * ((y + s) % 4) + 160 * (c ^ r) for r in range(2) for s in range(4)]
        cores = [320 * k + 160 * (c ^ r) for r in range(2) for k in range(4)]
        steps = [160 * ((y + s) % 4) for s in range(4)]
        fill = []
        for unit in range(8):
            row = GIVEN[z] + UNIT * unit
            mine = row % 320 // 160 == c
            fill.append(row // 320 * 160 + row % 160 if mine else -1)
        table[d] = gathered + [GIVEN[z], *QUERY[z], *KEY[z]] + cores + steps + fill
    return table


TABLE = build_table()


def pairs_of(function):
    out = []
    for d in range(16):
        z, y, c = function(d // 8, d % 8 // 2, d % 2)
        out.append((d, z % 2 * 8 + y % 4 * 2 + c % 2))
    return out


TO_CORE = pairs_of(lambda z, y, c: (z, y, c + 1))
TO_PLANE = pairs_of(lambda z, y, c: (z + 1, y, c))
ALONG_Y = [pairs_of(lambda z, y, c, s=s: (z, y + s, c)) for s in range(4)]


def send(value, pairs):
    return lax.ppermute(value, "fsdp", pairs)


def params(mib):
    return pltpu.CompilerParams(vmem_limit_bytes=mib * 2**20)


def cost(flops, mib):
    return pl.CostEstimate(flops=flops, bytes_accessed=mib * 2**20, transcendentals=0)


def dot(a, b, dims=((1,), (0,))):
    return lax.dot_general(a, b, (dims, ((), ())), preferred_element_type=F32)


def rotated(raw, cosine, sine):
    front, back = raw[:HALF], raw[HALF:]
    return jnp.concatenate([front * cosine - back * sine, back * cosine + front * sine], axis=0)


ANY = pl.BlockSpec(memory_space=pl.ANY)
ANGLES = pl.BlockSpec((HALF, SEQ), lambda s, table: (0, 0))
TOKENS = pl.BlockSpec((SEQ, D), lambda s, table: (s, 0))


def columns(rows):
    return pl.BlockSpec((rows, SEQ), lambda s, table: (0, s))


def project_kernel(table, x, cosine, sine, *rest):
    arrays, (out, given, held, raw, sems) = rest[:8], rest[8:]
    first = pl.program_id(0) == 0

    def copy(n):
        rows = pl.ds(n * SHARD, SHARD)
        return pltpu.make_async_copy(arrays[n], held.at[rows], sems.at[n])

    @pl.when(first)
    def _():
        for n in range(8):
            copy(n).start()

    for half in range(2):

        @pl.when(first)
        def _():
            for n in range(4):
                copy(half * 4 + n).wait()

        part = dot(held[half * CORE : (half + 1) * CORE, :], x[...], ((1,), (1,)))
        for n in range(4):
            row = pl.multiple_of(table[AT_WEIGHT + half * 4 + n], SHARD)
            raw[pl.ds(row, SHARD), :] = part[n * SHARD : (n + 1) * SHARD]
    for h in range(10):
        rows = slice(h * HD, (h + 1) * HD)
        out[rows, :] = rotated(raw[rows, :], cosine[...], sine[...]).astype(BF)
    given[...] = out[pl.ds(pl.multiple_of(table[AT_GIVEN], EXCHANGED), EXCHANGED), :]


def project(table, x, cosine, sine, arrays):
    count = x.shape[0]
    return pl.pallas_call(
        project_kernel,
        grid_spec=pltpu.PrefetchScalarGridSpec(
            num_scalar_prefetch=1,
            grid=(count // SEQ,),
            in_specs=[TOKENS, ANGLES, ANGLES] + [ANY] * 8,
            out_specs=[columns(ROWS), columns(EXCHANGED)],
            scratch_shapes=[
                pltpu.VMEM((ROWS, D), BF),
                pltpu.VMEM((ROWS, SEQ), F32),
                pltpu.SemaphoreType.DMA((8,)),
            ],
        ),
        out_shape=[jax.ShapeDtypeStruct((rows, count), BF) for rows in (ROWS, EXCHANGED)],
        compiler_params=params(56),
        cost_estimate=cost(2 * count * ROWS * D, 9),
        name="project",
    )(table, x, cosine, sine, *arrays)


SCALE = INV_ROOT * math.log2(math.e)


def softmax_parts(scores, diagonal):
    scores = scores * SCALE
    low = scores.shape[0] - HD
    masked = jnp.where(diagonal, scores[low:], MASKED)
    if low:
        scores = jnp.concatenate([scores[:low], masked], axis=0)
    else:
        scores = masked
    power = jnp.exp2(scores - jnp.max(scores, axis=0, keepdims=True))
    return power, (1.0 / HEADS) / jnp.sum(power, axis=0, keepdims=True)


def side_by_side(heads, half):
    return jnp.concatenate([q[:, half * HD : (half + 1) * HD] for q in heads], axis=1)


def attention_gradient(student, teacher, cosine, sine):
    key_s = student[4]
    rows_s, rows_t = key_s.T, teacher[4].T
    lane = lax.broadcasted_iota(jnp.int32, (HD, 4 * HD), 1) % HD
    diagonal = lax.broadcasted_iota(jnp.int32, (HD, 4 * HD), 0) <= lane
    query_parts, key_grad = [], None
    for half in range(2):
        extent = (half + 1) * HD
        q_s = side_by_side(student[:4], half)
        q_t = side_by_side(teacher[:4], half)
        power_s, inverse_s = softmax_parts(dot(rows_s[:extent], q_s), diagonal)
        power_t, inverse_t = softmax_parts(dot(rows_t[:extent], q_t), diagonal)
        spread = (power_s * inverse_s - power_t * inverse_t).astype(BF)
        query_parts.append(dot(key_s[:, :extent], spread))
        part = dot(q_s, spread, ((1,), (1,)))
        if half == 0:
            key_grad = part
        else:
            key_grad = jnp.concatenate([part[:, :HD] + key_grad, part[:, HD:]], axis=1)
    grads = [
        jnp.concatenate([p[:, h * HD : (h + 1) * HD] for p in query_parts], axis=1)
        for h in range(4)
    ] + [key_grad]
    return [rotated(g * INV_ROOT, cosine, -sine).astype(BF) for g in grads]


def attend_kernel(table, own_s, got_s, own_t, got_t, cosine, sine, out, other, back, both_s, both_t, grads):
    for both, own, got in ((both_s, own_s, got_s), (both_t, own_t, got_t)):
        both[:ROWS, :] = own[...]
        both[ROWS:, :] = got[...]
    for kv in range(2):
        blocks = [table[AT_QUERY + 4 * kv + h] for h in range(4)] + [table[AT_KEY + kv]]
        rows = [pl.ds(pl.multiple_of(block * HD, HD), HD) for block in blocks]
        student = [both_s[at, :] for at in rows]
        teacher = [both_t[at, :] for at in rows]
        for at, value in zip(rows, attention_gradient(student, teacher, cosine[...], sine[...])):
            grads[at, :] = value
    for n in range(8):
        row = pl.multiple_of(table[AT_CORE + n], SHARD)
        target = out if n < 4 else other
        target[n % 4 * SHARD : (n % 4 + 1) * SHARD, :] = grads[pl.ds(row, SHARD), :]
    back[...] = grads[ROWS:, :]


def attend(table, student, teacher, cosine, sine):
    count = student[0].shape[1]
    wide = ROWS + EXCHANGED
    return pl.pallas_call(
        attend_kernel,
        grid_spec=pltpu.PrefetchScalarGridSpec(
            num_scalar_prefetch=1,
            grid=(count // SEQ,),
            in_specs=[columns(ROWS), columns(EXCHANGED)] * 2 + [ANGLES, ANGLES],
            out_specs=[columns(CORE), columns(CORE), columns(EXCHANGED)],
            scratch_shapes=[pltpu.VMEM((wide, SEQ), BF)] * 3,
        ),
        out_shape=[jax.ShapeDtypeStruct((rows, count), BF) for rows in (CORE, CORE, EXCHANGED)],
        compiler_params=params(56),
        cost_estimate=cost(12 * count * SEQ * HD * 8, 8),
        name="attend",
    )(table, *student, *teacher, cosine, sine)


TILE = 512
SPAN = 2 * SEQ


def weight_kernel(steps, table, *refs):
    grads, backs, tokens, outs, held = refs[:4], refs[4:8], refs[8:12], refs[12:-1], refs[-1]

    @pl.when(pl.program_id(0) == 0)
    def _():
        for n in range(4):
            held[:, n * SPAN : (n + 1) * SPAN] = grads[n][...]
        for unit in range(8):
            row = table[AT_FILL + unit]

            @pl.when(row >= 0)
            def _():
                at = pl.ds(pl.multiple_of(row, UNIT), UNIT)
                for n in range(4):
                    value = backs[n][unit * UNIT : (unit + 1) * UNIT, :]
                    held[at, n * SPAN : (n + 1) * SPAN] = value

    for step, out in zip(steps, outs):
        rows = pl.ds(pl.multiple_of(table[AT_STEP + step], SHARD), SHARD)
        total = dot(held[rows, :SPAN], tokens[0][...])
        for n in range(1, 4):
            total += dot(held[rows, n * SPAN : (n + 1) * SPAN], tokens[n][...])
        out[...] = total.astype(BF)


def weight_gradient(steps, table, grads, backs, tokens):
    return pl.pallas_call(
        lambda *refs: weight_kernel(steps, *refs),
        grid_spec=pltpu.PrefetchScalarGridSpec(
            num_scalar_prefetch=1,
            grid=(D // TILE,),
            in_specs=[pl.BlockSpec((CORE, SPAN), lambda t, table: (0, 0))] * 4
            + [pl.BlockSpec((EXCHANGED, SPAN), lambda t, table: (0, 0))] * 4
            + [pl.BlockSpec((SPAN, TILE), lambda t, table: (0, t))] * 4,
            out_specs=[pl.BlockSpec((SHARD, TILE), lambda t, table: (0, t))] * len(steps),
            scratch_shapes=[pltpu.VMEM((CORE, 4 * SPAN), BF)],
        ),
        out_shape=[jax.ShapeDtypeStruct((SHARD, D), BF)] * len(steps),
        compiler_params=params(56),
        cost_estimate=cost(2 * len(steps) * SHARD * 4 * SPAN * D, 12),
        name="weight_gradient",
    )(table, *grads, *backs, *tokens)


def adam_kernel(a, b, c, d, weight, one, two, weight_out, one_out, two_out):
    gradient = (a[...].astype(F32) + b[...].astype(F32)) + (c[...].astype(F32) + d[...].astype(F32))
    first_new = BETA_ONE * one[...] + (1.0 - BETA_ONE) * gradient
    second_new = BETA_TWO * two[...] + (1.0 - BETA_TWO) * gradient * gradient
    step_dir = (
        first_new
        / (1.0 - BETA_ONE**STEP)
        / (jnp.sqrt(second_new / (1.0 - BETA_TWO**STEP)) + EPSILON)
    )
    master = weight[...]
    weight_out[...] = master - LEARN_RATE * (step_dir + DECAY * master)
    one_out[...] = first_new
    two_out[...] = second_new


def adam(blocks, weight, one, two):
    block = pl.BlockSpec((UNIT, D), lambda k: (k, 0))
    return pl.pallas_call(
        adam_kernel,
        grid=(SHARD // UNIT,),
        in_specs=[block] * 7,
        out_specs=[block] * 3,
        out_shape=[jax.ShapeDtypeStruct((SHARD, D), F32)] * 3,
        compiler_params=params(56),
        name="adam",
    )(*blocks, weight, one, two)


def rotary_tables():
    positions = jnp.arange(SEQ).astype(F32)
    exponents = jnp.arange(HALF).astype(F32) * (2.0 / HD)
    frequency = THETA ** (-exponents)
    angles = frequency[:, None] * positions[None, :]
    return jnp.cos(angles), jnp.sin(angles)


def ring_gather(shard, up_again):
    below = send(shard, ALONG_Y[1])
    above = send(shard, ALONG_Y[3])
    far = send(below, ALONG_Y[1]) if up_again else send(above, ALONG_Y[3])
    return [shard, above, far, below]


def both_cores(pieces):
    return pieces + [send(piece, TO_CORE) for piece in pieces]


def per_device(tokens, student_weight, snapshot, moment_one, moment_two):
    own_tokens = tokens[0]
    master = student_weight[0]
    table = jnp.asarray(TABLE)[lax.axis_index("fsdp")]
    cosine, sine = rotary_tables()

    teacher = lax.ppermute(snapshot[0], "blk", [(g, (g + 1) % 8) for g in range(8)])
    plane_tokens = send(own_tokens, TO_PLANE)
    halves = (own_tokens, plane_tokens)
    student_rows = both_cores(ring_gather(master.astype(BF), True))
    teacher_own = ring_gather(teacher, False)
    core_tokens = send(own_tokens, TO_CORE)
    far_tokens = send(plane_tokens, TO_CORE)

    def crossed(both):
        received = [send(given, TO_PLANE) for _, given in both]
        return [(both[half][0], received[1 - half]) for half in range(2)]

    student = [project(table, own_tokens, cosine, sine, student_rows)]
    teacher_own[2], _ = lax.optimization_barrier((teacher_own[2], student[0][0]))
    teacher_rows = both_cores(teacher_own)
    student.append(project(table, plane_tokens, cosine, sine, student_rows))
    student = crossed(student)
    teacher = crossed([project(table, x, cosine, sine, teacher_rows) for x in halves])

    grads, others, backs = [], [], []
    for half in range(2):
        grad, other, back = attend(table, student[half], teacher[half], cosine, sine)
        grads.append(grad)
        others.append(send(other, TO_CORE))
        backs.append(send(back, TO_PLANE))
    backs = backs[::-1]
    parts = grads + others
    backs += [send(value, TO_CORE) for value in backs]
    all_tokens = (own_tokens, plane_tokens, core_tokens, far_tokens)

    blocks = []
    for steps in ((2,), (1, 3, 0)):
        made = weight_gradient(steps, table, parts, backs, all_tokens)
        blocks += [send(block, ALONG_Y[s]) if s else block for block, s in zip(made, steps)]
    updated = adam(blocks, master, moment_one[0], moment_two[0])
    return tuple(value[None] for value in updated)


def solution(mesh):
    spec = P("blk", "fsdp", None)
    return jax.shard_map(
        per_device,
        mesh=mesh,
        in_specs=(spec,) * 5,
        out_specs=(spec,) * 3,
        check_vma=False,
    )
```

time: 236 us -> 196 us (0.83)
  the two profiles are of different devices: /device:TPU:25 before, /device:TPU:1 now
where the time goes in v4:
time: 196 us; the launch traced here: 195 us
  Pallas kernels  84.8 us (43%)
  waiting for transfers between devices  64.3 us (33%)
  starting transfers between devices  35.4 us (18%)
  local copies, waits for them, and re-layouts  7.21 us (4%)
  other arithmetic  2.43 us (1%)
    ppermute x30, waiting for transfers between devices, send(): return lax.ppermute(value, 'fsdp', pairs)  58.3 us
    pallas_call x4, Pallas kernels, project(): pl.pallas_call(project_kernel, grid_spec=pltpu.PrefetchScalarGridSpec(num...  45.2 us
    ppermute x30, starting transfers between devices, send(): return lax.ppermute(value, 'fsdp', pairs)  31.7 us
    pallas_call x2, Pallas kernels, weight_gradient(): pl.pallas_call(lambda *refs: weight_kernel(steps, *refs), grid_spec=pltpu...  17.7 us
    pallas_call x2, Pallas kernels, attend(): pl.pallas_call(attend_kernel, grid_spec=pltpu.PrefetchScalarGridSpec(num_...  15.2 us
    pallas_call x1, Pallas kernels, adam(): pl.pallas_call(adam_kernel, grid=(SHARD // UNIT,), in_specs=[block] * 7,...  6.75 us
    ppermute x1, waiting for transfers between devices, per_device(): lax.ppermute(snapshot[0], 'blk', [(g, (g + 1) % 8) for g in range(8)])  6.01 us
    unnamed x60, local copies, waits for them, and re-layouts  6 us
  transfers between devices with their start and end apart: 31, of which 10 were waited for; matrix products, arithmetic and copies ran while one was open for 1% of the time, Pallas kernels for 36%

profile of v4, /device:TPU:1, one launch (start us, length us, event | category | flops | bytes accessed | tf_op | source)
XLA Modules:
  0.0 195.1 jit_solution(9634662770253616185)
XLA Ops:
  2.1 2.2 %collective-permute-start.1 = (bf16[160,2048]{1,0:T(8,128)(2,1)S(1)}, bf16[160,2048]{1,0:T(8,128)(2,1)S(1)}, u32[]{:S(2)}, u32[]{:S(2)}) collective-permute-start(bf16[160,2048]{1,0:T(8,128)(2,1)S(1)} %bitcast_convert_fusion.rest_0_), channel_id=1, source_target_pairs={{0,2},{1,3},{2,4},{3,5},{4,6},{5,7},{6,0},{7,1},{8,10},{9,11},{10,... | collective-permute-start | bytes 1966088 | tf_op jit(solution)/shard_map/ppermute | solution.py:74
  6.8 3.7 %collective-permute-start.9 = (bf16[160,2048]{1,0:T(8,128)(2,1)S(1)}, bf16[160,2048]{1,0:T(8,128)(2,1)S(1)}, u32[]{:S(2)}, u32[]{:S(2)}) collective-permute-start(bf16[160,2048]{1,0:T(8,128)(2,1)S(1)} %bitcast.23), channel_id=1, source_target_pairs={{0,16},{16,32},{32,48},{48,64},{64,80},{80,96},{96,112},{112,0},{1... | collective-permute-start | bytes 1966088 | tf_op jit(solution)/shard_map/ppermute | solution.py:338
  11.3 8.8 %collective-permute-done.1.rest_3_ = bf16[160,2048]{1,0:T(8,128)(2,1)S(1)} collective-permute-done((bf16[160,2048]{1,0:T(8,128)(2,1)S(1)}, bf16[160,2048]{1,0:T(8,128)(2,1)S(1)}, u32[]{:S(2)}, u32[]{:S(2)}) %collective-permute-start.1) | collective-permute-done | bytes 655392 | tf_op jit(solution)/shard_map/ppermute | solution.py:74
  21.9 6.0 %collective-permute-done.9.rest_0_ = bf16[160,2048]{1,0:T(8,128)(2,1)S(1)} collective-permute-done((bf16[160,2048]{1,0:T(8,128)(2,1)S(1)}, bf16[160,2048]{1,0:T(8,128)(2,1)S(1)}, u32[]{:S(2)}, u32[]{:S(2)}) %collective-permute-start.9) | collective-permute-done | bytes 655392 | tf_op jit(solution)/shard_map/ppermute | solution.py:338
  29.4 6.7 %collective-permute-done.2.rest_2_ = bf16[160,2048]{1,0:T(8,128)(2,1)S(1)} collective-permute-done((bf16[160,2048]{1,0:T(8,128)(2,1)S(1)}, bf16[160,2048]{1,0:T(8,128)(2,1)S(1)}, u32[]{:S(2)}, u32[]{:S(2)}) %collective-permute-start.2) | collective-permute-done | bytes 655392 | tf_op jit(solution)/shard_map/ppermute | solution.py:74
  36.1 2.3 %collective-permute-start.5 = (bf16[160,2048]{1,0:T(8,128)(2,1)S(1)}, bf16[160,2048]{1,0:T(8,128)(2,1)S(1)}, u32[]{:S(2)}, u32[]{:S(2)}) collective-permute-start(bf16[160,2048]{1,0:T(8,128)(2,1)S(1)} %collective-permute-done.2.rest_2_), channel_id=1, source_target_pairs={{0,1},{1,0},{2,3},{3,2},{4,5},{5,4},{6,7},{7,6},{8,9},{9,8},{10,11... | collective-permute-start | bytes 1966088 | tf_op jit(solution)/shard_map/ppermute | solution.py:74
  38.6 5.0 %collective-permute-done.10.rest_1_ = bf16[160,2048]{1,0:T(8,128)(2,1)} collective-permute-done((bf16[160,2048]{1,0:T(8,128)(2,1)S(1)}, bf16[160,2048]{1,0:T(8,128)(2,1)}, u32[]{:S(2)}, u32[]{:S(2)}) %collective-permute-start.10) | collective-permute-done | bytes 655392 | tf_op jit(solution)/shard_map/ppermute | solution.py:74
  43.6 2.7 %collective-permute-start.11 = (bf16[160,2048]{1,0:T(8,128)(2,1)}, bf16[160,2048]{1,0:T(8,128)(2,1)}, u32[]{:S(2)}, u32[]{:S(2)}) collective-permute-start(bf16[160,2048]{1,0:T(8,128)(2,1)} %collective-permute-done.10.rest_1_), channel_id=1, source_target_pairs={{0,6},{1,7},{2,0},{3,1},{4,2},{5,3},{6,4},{7,5},{8,14},{9,15},{10,... | collective-permute-start | bytes 1966088 | tf_op jit(solution)/shard_map/ppermute | solution.py:74
  50.5 11.3 %project.4 = (bf16[1280,512]{1,0:T(8,128)(2,1)}, bf16[256,512]{1,0:T(8,128)(2,1)}) custom-call(s32[39]{0:T(128)} %dynamic-slice_bitcast_fusion.table.refs_0_, bf16[512,2048]{1,0:T(8,128)(2,1)} %bitcast.14, f32[64,256]{1,0:T(8,128)} %get-tuple-element.46.cosine, f32[64,256]{1,0:T(8,128)} %get-tuple-element.45.sine, bf16[160,2048]{1,0:T(8,128)(2,1)} %copy-done.7, ...), custom_call_target="tpu_custom_call" | custom-call | flops 2684354560 | bytes 9437184 | tf_op jit(solution)/shard_map/project/pallas_call | solution.py:135
  62.5 8.6 %collective-permute-done.7.x.refs_10_ = bf16[512,2048]{1,0:T(8,128)(2,1)S(1)} collective-permute-done((bf16[512,2048]{1,0:T(8,128)(2,1)}, bf16[512,2048]{1,0:T(8,128)(2,1)S(1)}, u32[]{:S(2)}, u32[]{:S(2)}) %collective-permute-start.7) | collective-permute-done | bytes 2097184 | tf_op jit(solution)/shard_map/ppermute | solution.py:74
  72.4 11.3 %project.5 = (bf16[1280,512]{1,0:T(8,128)(2,1)}, bf16[256,512]{1,0:T(8,128)(2,1)}) custom-call(s32[39]{0:T(128)} %dynamic-slice_bitcast_fusion.table.refs_0_, bf16[512,2048]{1,0:T(8,128)(2,1)} %copy-done, f32[64,256]{1,0:T(8,128)} %get-tuple-element.46.cosine, f32[64,256]{1,0:T(8,128)} %get-tuple-element.45.sine, bf16[160,2048]{1,0:T(8,128)(2,1)} %copy-done.7, ...), custom_call_target="tpu_custom_call" | custom-call | flops 2684354560 | bytes 9437184 | tf_op jit(solution)/shard_map/project/pallas_call | solution.py:135
  86.3 11.3 %project.7 = (bf16[1280,512]{1,0:T(8,128)(2,1)}, bf16[256,512]{1,0:T(8,128)(2,1)}) custom-call(s32[39]{0:T(128)} %dynamic-slice_bitcast_fusion.table.refs_0_, bf16[512,2048]{1,0:T(8,128)(2,1)} %copy-done, f32[64,256]{1,0:T(8,128)} %get-tuple-element.46.cosine, f32[64,256]{1,0:T(8,128)} %get-tuple-element.45.sine, bf16[160,2048]{1,0:T(8,128)(2,1)} %copy-done.13, ...), custom_call_target="tpu_custom_call" | custom-call | flops 2684354560 | bytes 9437184 | tf_op jit(solution)/shard_map/project/pallas_call | solution.py:135
  98.4 11.3 %project.6 = (bf16[1280,512]{1,0:T(8,128)(2,1)}, bf16[256,512]{1,0:T(8,128)(2,1)}) custom-call(s32[39]{0:T(128)} %dynamic-slice_bitcast_fusion.table.refs_0_, bf16[512,2048]{1,0:T(8,128)(2,1)} %bitcast.15, f32[64,256]{1,0:T(8,128)} %get-tuple-element.46.cosine, f32[64,256]{1,0:T(8,128)} %get-tuple-element.45.sine, bf16[160,2048]{1,0:T(8,128)(2,1)} %copy-done.13, ...), custom_call_target="tpu_custom_call" | custom-call | flops 2684354560 | bytes 9437184 | tf_op jit(solution)/shard_map/project/pallas_call | solution.py:135
  111.3 7.6 %attend.2 = (bf16[640,512]{1,0:T(8,128)(2,1)}, bf16[640,512]{1,0:T(8,128)(2,1)}, bf16[256,512]{1,0:T(8,128)(2,1)}) custom-call(s32[39]{0:T(128)} %dynamic-slice_bitcast_fusion.table.refs_0_, bf16[1280,512]{1,0:T(8,128)(2,1)} %get-tuple-element.24.own_s, bf16[256,512]{1,0:T(8,128)(2,1)} %copy-done.27, bf16[1280,512]{1,0:T(8,128)(2,1)} %get-tuple-element.27.own_t, ...), custom_call_target="tpu_custom_call" | custom-call | flops 1610612736 | bytes 8388608 | tf_op jit(solution)/shard_map/attend/pallas_call | solution.py:221
  121.6 7.7 %attend.3 = (bf16[640,512]{1,0:T(8,128)(2,1)}, bf16[640,512]{1,0:T(8,128)(2,1)}, bf16[256,512]{1,0:T(8,128)(2,1)}) custom-call(s32[39]{0:T(128)} %dynamic-slice_bitcast_fusion.table.refs_0_, bf16[1280,512]{1,0:T(8,128)(2,1)} %get-tuple-element.30.own_s, bf16[256,512]{1,0:T(8,128)(2,1)} %copy-done.25, bf16[1280,512]{1,0:T(8,128)(2,1)} %get-tuple-element.32.own_t, ...), custom_call_target="tpu_custom_call" | custom-call | flops 1610612736 | bytes 8388608 | tf_op jit(solution)/shard_map/attend/pallas_call | solution.py:221
  130.8 6.2 %collective-permute-done.22.refs_5_ = bf16[256,512]{1,0:T(8,128)(2,1)S(1)} collective-permute-done((bf16[256,512]{1,0:T(8,128)(2,1)}, bf16[256,512]{1,0:T(8,128)(2,1)S(1)}, u32[]{:S(2)}, u32[]{:S(2)}) %collective-permute-start.22) | collective-permute-done | bytes 262176 | tf_op jit(solution)/shard_map/ppermute | solution.py:74
  137.0 2.1 %collective-permute-start.24 = (bf16[256,512]{1,0:T(8,128)(2,1)S(1)}, bf16[256,512]{1,0:T(8,128)(2,1)S(1)}, u32[]{:S(2)}, u32[]{:S(2)}) collective-permute-start(bf16[256,512]{1,0:T(8,128)(2,1)S(1)} %collective-permute-done.22.refs_5_), channel_id=1, source_target_pairs={{0,1},{1,0},{2,3},{3,2},{4,5},{5,4},{6,7},{7,6},{8,9},{9,8},{10,11... | collective-permute-start | bytes 786440 | tf_op jit(solution)/shard_map/ppermute | solution.py:74
  139.1 3.5 %collective-permute-done.23.refs_6_ = bf16[256,512]{1,0:T(8,128)(2,1)S(1)} collective-permute-done((bf16[256,512]{1,0:T(8,128)(2,1)S(1)}, bf16[256,512]{1,0:T(8,128)(2,1)S(1)}, u32[]{:S(2)}, u32[]{:S(2)}) %collective-permute-start.23) | collective-permute-done | bytes 262176 | tf_op jit(solution)/shard_map/ppermute | solution.py:74
  146.9 7.9 %weight_gradient.2 = bf16[160,2048]{1,0:T(8,128)(2,1)} custom-call(s32[39]{0:T(128)} %dynamic-slice_bitcast_fusion.table.refs_0_, bf16[640,512]{1,0:T(8,128)(2,1)} %get-tuple-element.29.refs_1_, bf16[640,512]{1,0:T(8,128)(2,1)} %get-tuple-element.34.refs_2_, bf16[640,512]{1,0:T(8,128)(2,1)} %copy-done.2, bf16[640,512]{1,0:T(8,128)(2,1)} %copy-done.3, ...), custom_call_target="tpu_custom_call" | custom-call | flops 1342177280 | bytes 12582912 | tf_op jit(solution)/shard_map/weight_gradient/pallas_call | solution.py:267
  156.6 9.8 %weight_gradient.3 = (bf16[160,2048]{1,0:T(8,128)(2,1)}, bf16[160,2048]{1,0:T(8,128)(2,1)}, bf16[160,2048]{1,0:T(8,128)(2,1)}) custom-call(s32[39]{0:T(128)} %dynamic-slice_bitcast_fusion.table.refs_0_, bf16[640,512]{1,0:T(8,128)(2,1)} %get-tuple-element.29.refs_1_, bf16[640,512]{1,0:T(8,128)(2,1)} %get-tuple-element.34.refs_2_, bf16[640,512]{1,0:T(8,128)(2,1)} %copy-done.2, ...), custom_call_target="tpu_custom_call" | custom-call | flops 4026531840 | bytes 12582912 | tf_op jit(solution)/shard_map/weight_gradient/pallas_call | solution.py:267
  166.7 2.3 %collective-permute-start.30 = (bf16[160,2048]{1,0:T(8,128)(2,1)}, bf16[160,2048]{1,0:T(8,128)(2,1)S(1)}, u32[]{:S(2)}, u32[]{:S(2)}) collective-permute-start(bf16[160,2048]{1,0:T(8,128)(2,1)} %get-tuple-element.40), channel_id=1, source_target_pairs={{0,6},{1,7},{2,0},{3,1},{4,2},{5,3},{6,4},{7,5},{8,14},{9,15},{10,... | collective-permute-start | bytes 1966088 | tf_op jit(solution)/shard_map/ppermute | solution.py:74
  169.0 3.6 %collective-permute-done.28.a = bf16[160,2048]{1,0:T(8,128)(2,1)S(1)} collective-permute-done((bf16[160,2048]{1,0:T(8,128)(2,1)}, bf16[160,2048]{1,0:T(8,128)(2,1)S(1)}, u32[]{:S(2)}, u32[]{:S(2)}) %collective-permute-start.28) | collective-permute-done | bytes 655392 | tf_op jit(solution)/shard_map/ppermute | solution.py:74
  172.6 14.7 %collective-permute-done.29.b = bf16[160,2048]{1,0:T(8,128)(2,1)S(1)} collective-permute-done((bf16[160,2048]{1,0:T(8,128)(2,1)}, bf16[160,2048]{1,0:T(8,128)(2,1)S(1)}, u32[]{:S(2)}, u32[]{:S(2)}) %collective-permute-start.29) | collective-permute-done | bytes 655392 | tf_op jit(solution)/shard_map/ppermute | solution.py:74
  188.3 6.7 %adam.1 = (f32[160,2048]{1,0:T(8,128)}, f32[160,2048]{1,0:T(8,128)}, f32[160,2048]{1,0:T(8,128)}) custom-call(bf16[160,2048]{1,0:T(8,128)(2,1)} %copy-done.4, bf16[160,2048]{1,0:T(8,128)(2,1)} %copy-done.5, bf16[160,2048]{1,0:T(8,128)(2,1)} %copy-done.6, bf16[160,2048]{1,0:T(8,128)(2,1)} %get-tuple-element.41.d, f32[160,2048]{1,0:T(8,128)} %bitcast.11, ...), custom_call_target="tpu_custom_call" | custom-call | tf_op jit(solution)/shard_map/adam/pallas_call | solution.py:302
  (112 shorter events, 30.9 us)
Async XLA Ops:
  2.1 17.9 %collective-permute-start.1 = (bf16[160,2048]{1,0:T(8,128)(2,1)S(1)}, bf16[160,2048]{1,0:T(8,128)(2,1)S(1)}, u32[]{:S(2)}, u32[]{:S(2)}) collective-permute-start(bf16[160,2048]{1,0:T(8,128)(2,1)S(1)} %bitcast_convert_fusion.rest_0_), channel_id=1, source_target_pairs={{0,2},{1,3},{2,4},{3,5},{4,6},{5,7},{6,0},{7,1},{8,10},{9,11},{10,... | collective-permute-start | bytes 1966088 | tf_op jit(solution)/shard_map/ppermute | solution.py:74
  4.3 15.8 %collective-permute-start = (bf16[160,2048]{1,0:T(8,128)(2,1)S(1)}, bf16[160,2048]{1,0:T(8,128)(2,1)S(1)}, u32[]{:S(2)}, u32[]{:S(2)}) collective-permute-start(bf16[160,2048]{1,0:T(8,128)(2,1)S(1)} %bitcast_convert_fusion.rest_0_), channel_id=1, source_target_pairs={{0,6},{1,7},{2,0},{3,1},{4,2},{5,3},{6,4},{7,5},{8,14},{9,15},{10,... | collective-permute-start | bytes 1966088 | tf_op jit(solution)/shard_map/ppermute | solution.py:74
  5.8 15.9 %collective-permute-start.3 = (bf16[160,2048]{1,0:T(8,128)(2,1)S(1)}, bf16[160,2048]{1,0:T(8,128)(2,1)S(1)}, u32[]{:S(2)}, u32[]{:S(2)}) collective-permute-start(bf16[160,2048]{1,0:T(8,128)(2,1)S(1)} %bitcast_convert_fusion.rest_0_), channel_id=1, source_target_pairs={{0,1},{1,0},{2,3},{3,2},{4,5},{5,4},{6,7},{7,6},{8,9},{9,8},{10,11... | collective-permute-start | bytes 1966088 | tf_op jit(solution)/shard_map/ppermute | solution.py:74
  6.8 21.0 %collective-permute-start.9 = (bf16[160,2048]{1,0:T(8,128)(2,1)S(1)}, bf16[160,2048]{1,0:T(8,128)(2,1)S(1)}, u32[]{:S(2)}, u32[]{:S(2)}) collective-permute-start(bf16[160,2048]{1,0:T(8,128)(2,1)S(1)} %bitcast.23), channel_id=1, source_target_pairs={{0,16},{16,32},{32,48},{48,64},{64,80},{80,96},{96,112},{112,0},{1... | collective-permute-start | bytes 1966088 | tf_op jit(solution)/shard_map/ppermute | solution.py:338
  10.5 60.6 %collective-permute-start.7 = (bf16[512,2048]{1,0:T(8,128)(2,1)}, bf16[512,2048]{1,0:T(8,128)(2,1)S(1)}, u32[]{:S(2)}, u32[]{:S(2)}) collective-permute-start(bf16[512,2048]{1,0:T(8,128)(2,1)} %bitcast.12), channel_id=1, source_target_pairs={{0,8},{1,9},{2,10},{3,11},{4,12},{5,13},{6,14},{7,15},{8,0},{9,1},... | collective-permute-start | bytes 6291464 | tf_op jit(solution)/shard_map/ppermute | solution.py:74
  20.1 16.1 %collective-permute-start.2 = (bf16[160,2048]{1,0:T(8,128)(2,1)S(1)}, bf16[160,2048]{1,0:T(8,128)(2,1)S(1)}, u32[]{:S(2)}, u32[]{:S(2)}) collective-permute-start(bf16[160,2048]{1,0:T(8,128)(2,1)S(1)} %collective-permute-done.1.rest_3_), channel_id=1, source_target_pairs={{0,2},{1,3},{2,4},{3,5},{4,6},{5,7},{6,0},{7,1},{8,10},{9,11},{10,... | collective-permute-start | bytes 1966088 | tf_op jit(solution)/shard_map/ppermute | solution.py:74
  20.1 18.3 %collective-permute-start.4 = (bf16[160,2048]{1,0:T(8,128)(2,1)S(1)}, bf16[160,2048]{1,0:T(8,128)(2,1)S(1)}, u32[]{:S(2)}, u32[]{:S(2)}) collective-permute-start(bf16[160,2048]{1,0:T(8,128)(2,1)S(1)} %collective-permute-done.rest_1_), channel_id=1, source_target_pairs={{0,1},{1,0},{2,3},{3,2},{4,5},{5,4},{6,7},{7,6},{8,9},{9,8},{10,11... | collective-permute-start | bytes 1966088 | tf_op jit(solution)/shard_map/ppermute | solution.py:74
  21.8 16.8 %collective-permute-start.6 = (bf16[160,2048]{1,0:T(8,128)(2,1)S(1)}, bf16[160,2048]{1,0:T(8,128)(2,1)S(1)}, u32[]{:S(2)}, u32[]{:S(2)}) collective-permute-start(bf16[160,2048]{1,0:T(8,128)(2,1)S(1)} %collective-permute-done.1.rest_3_), channel_id=1, source_target_pairs={{0,1},{1,0},{2,3},{3,2},{4,5},{5,4},{6,7},{7,6},{8,9},{9,8},{10,11... | collective-permute-start | bytes 1966088 | tf_op jit(solution)/shard_map/ppermute | solution.py:74
  27.9 15.7 %collective-permute-start.10 = (bf16[160,2048]{1,0:T(8,128)(2,1)S(1)}, bf16[160,2048]{1,0:T(8,128)(2,1)}, u32[]{:S(2)}, u32[]{:S(2)}) collective-permute-start(bf16[160,2048]{1,0:T(8,128)(2,1)S(1)} %collective-permute-done.9.rest_0_), channel_id=1, source_target_pairs={{0,6},{1,7},{2,0},{3,1},{4,2},{5,3},{6,4},{7,5},{8,14},{9,15},{10,... | collective-permute-start | bytes 1966088 | tf_op jit(solution)/shard_map/ppermute | solution.py:74
  38.4 23.3 %collective-permute-start.12 = (bf16[160,2048]{1,0:T(8,128)(2,1)S(1)}, bf16[160,2048]{1,0:T(8,128)(2,1)}, u32[]{:S(2)}, u32[]{:S(2)}) collective-permute-start(bf16[160,2048]{1,0:T(8,128)(2,1)S(1)} %collective-permute-done.9.rest_0_), channel_id=1, source_target_pairs={{0,2},{1,3},{2,4},{3,5},{4,6},{5,7},{6,0},{7,1},{8,10},{9,11},{10,... | collective-permute-start | bytes 1966088 | tf_op jit(solution)/shard_map/ppermute | solution.py:74
  38.5 23.8 %collective-permute-start.13 = (bf16[160,2048]{1,0:T(8,128)(2,1)S(1)}, bf16[160,2048]{1,0:T(8,128)(2,1)}, u32[]{:S(2)}, u32[]{:S(2)}) collective-permute-start(bf16[160,2048]{1,0:T(8,128)(2,1)S(1)} %collective-permute-done.9.rest_0_), channel_id=1, source_target_pairs={{0,1},{1,0},{2,3},{3,2},{4,5},{5,4},{6,7},{7,6},{8,9},{9,8},{10,11... | collective-permute-start | bytes 1966088 | tf_op jit(solution)/shard_map/ppermute | solution.py:74
  43.6 18.2 %collective-permute-start.11 = (bf16[160,2048]{1,0:T(8,128)(2,1)}, bf16[160,2048]{1,0:T(8,128)(2,1)}, u32[]{:S(2)}, u32[]{:S(2)}) collective-permute-start(bf16[160,2048]{1,0:T(8,128)(2,1)} %collective-permute-done.10.rest_1_), channel_id=1, source_target_pairs={{0,6},{1,7},{2,0},{3,1},{4,2},{5,3},{6,4},{7,5},{8,14},{9,15},{10,... | collective-permute-start | bytes 1966088 | tf_op jit(solution)/shard_map/ppermute | solution.py:74
  46.4 83.7 %collective-permute-start.26 = (bf16[512,2048]{1,0:T(8,128)(2,1)}, bf16[512,2048]{1,0:T(8,128)(2,1)}, u32[]{:S(2)}, u32[]{:S(2)}) collective-permute-start(bf16[512,2048]{1,0:T(8,128)(2,1)} %bitcast.13), channel_id=1, source_target_pairs={{0,1},{1,0},{2,3},{3,2},{4,5},{5,4},{6,7},{7,6},{8,9},{9,8},{10,11... | collective-permute-start | bytes 6291464 | tf_op jit(solution)/shard_map/ppermute | solution.py:74
  61.8 22.0 %collective-permute-start.14 = (bf16[160,2048]{1,0:T(8,128)(2,1)}, bf16[160,2048]{1,0:T(8,128)(2,1)S(1)}, u32[]{:S(2)}, u32[]{:S(2)}) collective-permute-start(bf16[160,2048]{1,0:T(8,128)(2,1)} %collective-permute-done.10.rest_1_), channel_id=1, source_target_pairs={{0,1},{1,0},{2,3},{3,2},{4,5},{5,4},{6,7},{7,6},{8,9},{9,8},{10,11... | collective-permute-start | bytes 1966088 | tf_op jit(solution)/shard_map/ppermute | solution.py:74
  61.9 22.8 %collective-permute-start.16 = (bf16[160,2048]{1,0:T(8,128)(2,1)}, bf16[160,2048]{1,0:T(8,128)(2,1)S(1)}, u32[]{:S(2)}, u32[]{:S(2)}) collective-permute-start(bf16[160,2048]{1,0:T(8,128)(2,1)} %collective-permute-done.12.rest_3_), channel_id=1, source_target_pairs={{0,1},{1,0},{2,3},{3,2},{4,5},{5,4},{6,7},{7,6},{8,9},{9,8},{10,11... | collective-permute-start | bytes 1966088 | tf_op jit(solution)/shard_map/ppermute | solution.py:74
  62.4 23.0 %collective-permute-start.15 = (bf16[160,2048]{1,0:T(8,128)(2,1)}, bf16[160,2048]{1,0:T(8,128)(2,1)S(1)}, u32[]{:S(2)}, u32[]{:S(2)}) collective-permute-start(bf16[160,2048]{1,0:T(8,128)(2,1)} %collective-permute-done.11.rest_2_), channel_id=1, source_target_pairs={{0,1},{1,0},{2,3},{3,2},{4,5},{5,4},{6,7},{7,6},{8,9},{9,8},{10,11... | collective-permute-start | bytes 1966088 | tf_op jit(solution)/shard_map/ppermute | solution.py:74
  71.1 74.0 %collective-permute-start.27 = (bf16[512,2048]{1,0:T(8,128)(2,1)S(1)}, bf16[512,2048]{1,0:T(8,128)(2,1)S(1)}, u32[]{:S(2)}, u32[]{:S(2)}) collective-permute-start(bf16[512,2048]{1,0:T(8,128)(2,1)S(1)} %collective-permute-done.7.x.refs_10_), channel_id=1, source_target_pairs={{0,1},{1,0},{2,3},{3,2},{4,5},{5,4},{6,7},{7,6},{8,9},{9,8},{10,11... | collective-permute-start | bytes 6291464 | tf_op jit(solution)/shard_map/ppermute | solution.py:74
  83.8 36.9 %collective-permute-start.18 = (bf16[256,512]{1,0:T(8,128)(2,1)S(1)}, bf16[256,512]{1,0:T(8,128)(2,1)S(1)}, u32[]{:S(2)}, u32[]{:S(2)}) collective-permute-start(bf16[256,512]{1,0:T(8,128)(2,1)S(1)} %copy-done.24), channel_id=1, source_target_pairs={{0,8},{1,9},{2,10},{3,11},{4,12},{5,13},{6,14},{7,15},{8,0},{9,1},... | collective-permute-start | bytes 786440 | tf_op jit(solution)/shard_map/ppermute | solution.py:74
  84.6 25.1 %collective-permute-start.8 = (bf16[256,512]{1,0:T(8,128)(2,1)}, bf16[256,512]{1,0:T(8,128)(2,1)S(1)}, u32[]{:S(2)}, u32[]{:S(2)}) collective-permute-start(bf16[256,512]{1,0:T(8,128)(2,1)} %get-tuple-element.25), channel_id=1, source_target_pairs={{0,8},{1,9},{2,10},{3,11},{4,12},{5,13},{6,14},{7,15},{8,0},{9,1},... | collective-permute-start | bytes 786440 | tf_op jit(solution)/shard_map/ppermute | solution.py:74
  118.9 26.2 %collective-permute-start.20 = (bf16[640,512]{1,0:T(8,128)(2,1)}, bf16[640,512]{1,0:T(8,128)(2,1)S(1)}, u32[]{:S(2)}, u32[]{:S(2)}) collective-permute-start(bf16[640,512]{1,0:T(8,128)(2,1)} %get-tuple-element.35), channel_id=1, source_target_pairs={{0,1},{1,0},{2,3},{3,2},{4,5},{5,4},{6,7},{7,6},{8,9},{9,8},{10,11... | collective-permute-start | bytes 1966088 | tf_op jit(solution)/shard_map/ppermute | solution.py:74
  129.2 15.9 %collective-permute-start.21 = (bf16[640,512]{1,0:T(8,128)(2,1)}, bf16[640,512]{1,0:T(8,128)(2,1)S(1)}, u32[]{:S(2)}, u32[]{:S(2)}) collective-permute-start(bf16[640,512]{1,0:T(8,128)(2,1)} %get-tuple-element.36), channel_id=1, source_target_pairs={{0,1},{1,0},{2,3},{3,2},{4,5},{5,4},{6,7},{7,6},{8,9},{9,8},{10,11... | collective-permute-start | bytes 1966088 | tf_op jit(solution)/shard_map/ppermute | solution.py:74
  154.9 17.7 %collective-permute-start.28 = (bf16[160,2048]{1,0:T(8,128)(2,1)}, bf16[160,2048]{1,0:T(8,128)(2,1)S(1)}, u32[]{:S(2)}, u32[]{:S(2)}) collective-permute-start(bf16[160,2048]{1,0:T(8,128)(2,1)} %weight_gradient.2), channel_id=1, source_target_pairs={{0,4},{1,5},{2,6},{3,7},{4,0},{5,1},{6,2},{7,3},{8,12},{9,13},{10,... | collective-permute-start | bytes 1966088 | tf_op jit(solution)/shard_map/ppermute | solution.py:74
  166.3 21.0 %collective-permute-start.29 = (bf16[160,2048]{1,0:T(8,128)(2,1)}, bf16[160,2048]{1,0:T(8,128)(2,1)S(1)}, u32[]{:S(2)}, u32[]{:S(2)}) collective-permute-start(bf16[160,2048]{1,0:T(8,128)(2,1)} %get-tuple-element.39), channel_id=1, source_target_pairs={{0,2},{1,3},{2,4},{3,5},{4,6},{5,7},{6,0},{7,1},{8,10},{9,11},{10,... | collective-permute-start | bytes 1966088 | tf_op jit(solution)/shard_map/ppermute | solution.py:74
  166.7 20.5 %collective-permute-start.30 = (bf16[160,2048]{1,0:T(8,128)(2,1)}, bf16[160,2048]{1,0:T(8,128)(2,1)S(1)}, u32[]{:S(2)}, u32[]{:S(2)}) collective-permute-start(bf16[160,2048]{1,0:T(8,128)(2,1)} %get-tuple-element.40), channel_id=1, source_target_pairs={{0,6},{1,7},{2,0},{3,1},{4,2},{5,3},{6,4},{7,5},{8,14},{9,15},{10,... | collective-permute-start | bytes 1966088 | tf_op jit(solution)/shard_map/ppermute | solution.py:74
  (37 other events, 340.5 us)

commit v5 on v4

v5 whole, which is shorter than its diff:
```python
import math

import jax
import jax.numpy as jnp
import numpy as np
from jax import lax
from jax.experimental import pallas as pl
from jax.experimental.pallas import tpu as pltpu
from jax.sharding import PartitionSpec as P

HEADS = 16
KVH = 4
HD = 128
SEQ = 256
STEP = 100
D = 2048
THETA = 500000.0
BETA_ONE = 0.9
BETA_TWO = 0.95
LEARN_RATE = 0.002
DECAY = 0.1
EPSILON = 1e-08
MASKED = -1e30

BF = jnp.bfloat16
F32 = jnp.float32
SHARD = 160
ROWS = 8 * SHARD
UNIT = 32
HALF = HD // 2
CORE = 4 * SHARD
EXCHANGED = 2 * HD
INV_ROOT = 1.0 / math.sqrt(HD)

AT_WEIGHT, AT_GIVEN, AT_QUERY, AT_KEY, AT_CORE, AT_STEP, AT_FILL = 0, 8, 9, 17, 19, 27, 31
GIVEN = (1024, 768)
QUERY = (tuple(range(8)), (10, 11, 0, 1, 2, 3, 4, 5))
KEY = ((10, 11), (8, 9))


def build_table():
    table = np.zeros((16, 39), np.int32)
    for d in range(16):
        z, y, c = d // 8, d % 8 // 2, d % 2
        gathered = [320 * ((y + s) % 4) + 160 * (c ^ r) for r in range(2) for s in range(4)]
        cores = [320 * k + 160 * (c ^ r) for r in range(2) for k in range(4)]
        steps = [160 * ((y + s) % 4) for s in range(4)]
        fill = []
        for unit in range(8):
            row = GIVEN[z] + UNIT * unit
            mine = row % 320 // 160 == c
            fill.append(row // 320 * 160 + row % 160 if mine else -1)
        table[d] = gathered + [GIVEN[z], *QUERY[z], *KEY[z]] + cores + steps + fill
    return table


TABLE = build_table()


def pairs_of(function):
    out = []
    for d in range(16):
        z, y, c = function(d // 8, d % 8 // 2, d % 2)
        out.append((d, z % 2 * 8 + y % 4 * 2 + c % 2))
    return out


TO_CORE = pairs_of(lambda z, y, c: (z, y, c + 1))
TO_PLANE = pairs_of(lambda z, y, c: (z + 1, y, c))
ALONG_Y = [pairs_of(lambda z, y, c, s=s: (z, y + s, c)) for s in range(4)]


def send(value, pairs):
    return lax.ppermute(value, "fsdp", pairs)


def params(mib):
    return pltpu.CompilerParams(vmem_limit_bytes=mib * 2**20)


def cost(microseconds):
    return pl.CostEstimate(flops=int(microseconds * 1e9), bytes_accessed=2**20, transcendentals=0)


def dot(a, b, dims=((1,), (0,))):
    return lax.dot_general(a, b, (dims, ((), ())), preferred_element_type=F32)


def rotated(raw, cosine, sine):
    front, back = raw[:HALF], raw[HALF:]
    return jnp.concatenate([front * cosine - back * sine, back * cosine + front * sine], axis=0)


ANY = pl.BlockSpec(memory_space=pl.ANY)


def block(shape, row=0, column=0):
    return pl.BlockSpec(shape, lambda s, table: (row, column))


def call(kernel, name, operands, outs, scratch, microseconds):
    return pl.pallas_call(
        kernel,
        grid_spec=pltpu.PrefetchScalarGridSpec(
            num_scalar_prefetch=1,
            grid=(1,),
            in_specs=[spec for _, spec in operands[1:]],
            out_specs=[block(shape) for shape, _ in outs],
            scratch_shapes=scratch,
        ),
        out_shape=[jax.ShapeDtypeStruct(shape, dtype) for shape, dtype in outs],
        compiler_params=params(56),
        cost_estimate=cost(microseconds),
        name=name,
    )(*[value for value, _ in operands])


def project_kernel(jobs, groups, x_count, set_count, table, *refs):
    refs = list(refs)
    carried, refs = refs[0], refs[1:]
    xs, refs = refs[:x_count], refs[x_count:]
    cosine, sine, refs = refs[0], refs[1], refs[2:]
    arrays, refs = refs[: 8 * set_count], refs[8 * set_count :]
    outs, refs = refs[: len(jobs)], refs[len(jobs) :]
    givens, refs = refs[: len(groups)], refs[len(groups) :]
    held, sems = refs[:-1], refs[-1]

    def copy(at, n):
        rows = pl.ds(pl.multiple_of(table[AT_WEIGHT + n], SHARD), SHARD)
        return pltpu.make_async_copy(arrays[8 * at + n], held[at].at[rows], sems.at[8 * at + n])

    for at in range(set_count):
        for n in range(8):
            copy(at, n).start()
    for at in range(set_count):
        for n in range(8):
            copy(at, n).wait()
        for job, (x, own_set) in enumerate(jobs):
            if own_set != at:
                continue
            for half in range(2):
                part = dot(held[at][half * CORE : (half + 1) * CORE, :], xs[x][...], ((1,), (1,)))
                for h in range(5):
                    row = half * CORE + h * HD
                    value = rotated(part[h * HD : (h + 1) * HD], cosine[...], sine[...])
                    outs[job][row : row + HD, :] = value.astype(BF)
    rows = pl.ds(pl.multiple_of(table[AT_GIVEN], EXCHANGED), EXCHANGED)
    for given, group in zip(givens, groups):
        for n, job in enumerate(group):
            lanes = slice(n * SEQ, (n + 1) * SEQ)
            given[:, lanes] = outs[job][rows, :] if job >= 0 else carried[:, lanes]


def project(table, angles, xs, sets, jobs, groups, carried=None):
    if carried is None:
        carried = jnp.zeros((16, 128), BF)
    operands = [(table, None), (carried, block(carried.shape))]
    operands += [(x, block((SEQ, D), at)) for x, at in xs]
    operands += [(value, block((HALF, SEQ))) for value in angles]
    operands += [(array, ANY) for arrays in sets for array in arrays]
    return call(
        lambda *refs: project_kernel(jobs, groups, len(xs), len(sets), *refs),
        "project",
        operands,
        [((ROWS, SEQ), BF)] * len(jobs) + [((EXCHANGED, SEQ * len(group)), BF) for group in groups],
        [pltpu.VMEM((ROWS, D), BF)] * len(sets) + [pltpu.SemaphoreType.DMA((8 * len(sets),))],
        0.5 if len(sets) == 1 else 8.0,
    )


SCALE = INV_ROOT * math.log2(math.e)


def softmax_parts(scores, diagonal):
    scores = scores * SCALE
    low = scores.shape[0] - HD
    masked = jnp.where(diagonal, scores[low:], MASKED)
    if low:
        scores = jnp.concatenate([scores[:low], masked], axis=0)
    else:
        scores = masked
    power = jnp.exp2(scores - jnp.max(scores, axis=0, keepdims=True))
    return power, (1.0 / HEADS) / jnp.sum(power, axis=0, keepdims=True)


def side_by_side(heads, half):
    return jnp.concatenate([q[:, half * HD : (half + 1) * HD] for q in heads], axis=1)


def attention_gradient(student, teacher, cosine, sine):
    key_s = student[4]
    rows_s, rows_t = key_s.T, teacher[4].T
    lane = lax.broadcasted_iota(jnp.int32, (HD, 4 * HD), 1) % HD
    diagonal = lax.broadcasted_iota(jnp.int32, (HD, 4 * HD), 0) <= lane
    query_parts, key_grad = [], None
    for half in range(2):
        extent = (half + 1) * HD
        q_s = side_by_side(student[:4], half)
        q_t = side_by_side(teacher[:4], half)
        power_s, inverse_s = softmax_parts(dot(rows_s[:extent], q_s), diagonal)
        power_t, inverse_t = softmax_parts(dot(rows_t[:extent], q_t), diagonal)
        spread = (power_s * inverse_s - power_t * inverse_t).astype(BF)
        query_parts.append(dot(key_s[:, :extent], spread))
        part = dot(q_s, spread, ((1,), (1,)))
        if half == 0:
            key_grad = part
        else:
            key_grad = jnp.concatenate([part[:, :HD] + key_grad, part[:, HD:]], axis=1)
    grads = [
        jnp.concatenate([p[:, h * HD : (h + 1) * HD] for p in query_parts], axis=1)
        for h in range(4)
    ] + [key_grad]
    return [rotated(g * INV_ROOT, cosine, -sine).astype(BF) for g in grads]


def attend_kernel(count, table, *refs):
    inputs, (cosine, sine, out, other, back, both_s, both_t, grads) = refs[: 4 * count], refs[4 * count :]
    for seq in range(count):
        own_s, got_s, own_t, got_t = inputs[4 * seq : 4 * seq + 4]
        lanes = slice(seq * SEQ, (seq + 1) * SEQ)
        for both, own, got in ((both_s, own_s, got_s), (both_t, own_t, got_t)):
            both[:ROWS, lanes] = own[...]
            both[ROWS:, lanes] = got[...]
    for seq in range(count):
        lanes = slice(seq * SEQ, (seq + 1) * SEQ)
        for kv in range(2):
            blocks = [table[AT_QUERY + 4 * kv + h] for h in range(4)] + [table[AT_KEY + kv]]
            rows = [pl.ds(pl.multiple_of(n * HD, HD), HD) for n in blocks]
            student = [both_s[at, lanes] for at in rows]
            teacher = [both_t[at, lanes] for at in rows]
            made = attention_gradient(student, teacher, cosine[...], sine[...])
            for at, value in zip(rows, made):
                grads[at, lanes] = value
    for n in range(8):
        row = pl.multiple_of(table[AT_CORE + n], SHARD)
        target = out if n < 4 else other
        target[n % 4 * SHARD : (n % 4 + 1) * SHARD, :] = grads[pl.ds(row, SHARD), :]
    back[...] = grads[ROWS:, :]


def attend(table, angles, sequences):
    count = len(sequences)
    operands = [(table, None)]
    for sequence in sequences:
        for own, (got, at) in sequence:
            operands += [(own, block((ROWS, SEQ))), (got, block((EXCHANGED, SEQ), 0, at))]
    operands += [(value, block((HALF, SEQ))) for value in angles]
    return call(
        lambda *refs: attend_kernel(count, *refs),
        "attend",
        operands,
        [((rows, count * SEQ), BF) for rows in (CORE, CORE, EXCHANGED)],
        [pltpu.VMEM((ROWS + EXCHANGED, count * SEQ), BF)] * 3,
        1.0 + 3.5 * count,
    )


TILE = 512
SPAN = 2 * SEQ


def fill(table, held, grads, backs):
    for n in range(2):
        held[:, n * SPAN : (n + 1) * SPAN] = grads[n][...]
    for unit in range(8):
        row = table[AT_FILL + unit]

        @pl.when(row >= 0)
        def _():
            at = pl.ds(pl.multiple_of(row, UNIT), UNIT)
            for n in range(2):
                held[at, n * SPAN : (n + 1) * SPAN] = backs[n][unit * UNIT : (unit + 1) * UNIT, :]


def first_kernel(table, *refs):
    grads, backs, tokens, out, held = refs[:2], refs[2:4], refs[4:6], refs[6], refs[7]

    @pl.when(pl.program_id(0) == 0)
    def _():
        fill(table, held, grads, backs)

    out[...] = dot(held[:, :SPAN], tokens[0][...]) + dot(held[:, SPAN:], tokens[1][...])


def second_kernel(steps, table, *refs):
    grads, backs, tokens, before, outs, held = refs[:2], refs[2:4], refs[4:6], refs[6], refs[7:-1], refs[-1]

    @pl.when(pl.program_id(0) == 0)
    def _():
        fill(table, held, grads, backs)

    for step, out in zip(steps, outs):
        rows = pl.ds(pl.multiple_of(table[AT_STEP + step], SHARD), SHARD)
        total = before[rows, :] + dot(held[rows, :SPAN], tokens[0][...])
        total += dot(held[rows, SPAN:], tokens[1][...])
        out[...] = total.astype(BF)


def weight_call(kernel, table, grads, backs, tokens, more, outs, microseconds):
    tile = lambda t, table: (0, t)
    return pl.pallas_call(
        kernel,
        grid_spec=pltpu.PrefetchScalarGridSpec(
            num_scalar_prefetch=1,
            grid=(D // TILE,),
            in_specs=[block((CORE, SPAN))] * 2
            + [block((EXCHANGED, SPAN))] * 2
            + [pl.BlockSpec((x.shape[0], TILE), tile) for x in tokens + more],
            out_specs=[pl.BlockSpec((rows, TILE), tile) for rows, _ in outs],
            scratch_shapes=[pltpu.VMEM((CORE, 2 * SPAN), BF)],
        ),
        out_shape=[jax.ShapeDtypeStruct((rows, D), dtype) for rows, dtype in outs],
        compiler_params=params(56),
        cost_estimate=cost(microseconds),
        name="weight_gradient",
    )(table, *grads, *backs, *tokens, *more)


def adam_kernel(a, b, c, d, weight, one, two, weight_out, one_out, two_out):
    gradient = (a[...].astype(F32) + b[...].astype(F32)) + (c[...].astype(F32) + d[...].astype(F32))
    first_new = BETA_ONE * one[...] + (1.0 - BETA_ONE) * gradient
    second_new = BETA_TWO * two[...] + (1.0 - BETA_TWO) * gradient * gradient
    step_dir = (
        first_new
        / (1.0 - BETA_ONE**STEP)
        / (jnp.sqrt(second_new / (1.0 - BETA_TWO**STEP)) + EPSILON)
    )
    master = weight[...]
    weight_out[...] = master - LEARN_RATE * (step_dir + DECAY * master)
    one_out[...] = first_new
    two_out[...] = second_new


def adam(blocks, weight, one, two):
    block = pl.BlockSpec((UNIT, D), lambda k: (k, 0))
    return pl.pallas_call(
        adam_kernel,
        grid=(SHARD // UNIT,),
        in_specs=[block] * 7,
        out_specs=[block] * 3,
        out_shape=[jax.ShapeDtypeStruct((SHARD, D), F32)] * 3,
        compiler_params=params(56),
        name="adam",
    )(*blocks, weight, one, two)


def rotary_tables():
    positions = jnp.arange(SEQ).astype(F32)
    exponents = jnp.arange(HALF).astype(F32) * (2.0 / HD)
    frequency = THETA ** (-exponents)
    angles = frequency[:, None] * positions[None, :]
    return jnp.cos(angles), jnp.sin(angles)


def ring_gather(shard, up_again):
    below = send(shard, ALONG_Y[1])
    above = send(shard, ALONG_Y[3])
    far = send(below, ALONG_Y[1]) if up_again else send(above, ALONG_Y[3])
    return [shard, above, far, below]


def both_cores(pieces):
    return pieces + [send(piece, TO_CORE) for piece in pieces]


def per_device(tokens, student_weight, snapshot, moment_one, moment_two):
    own = tokens[0]
    master = student_weight[0]
    table = jnp.asarray(TABLE)[lax.axis_index("fsdp")]
    angles = rotary_tables()

    teacher = lax.ppermute(snapshot[0], "blk", [(g, (g + 1) % 8) for g in range(8)])
    plane = send(own, TO_PLANE)
    student_rows = both_cores(ring_gather(master.astype(BF), True))
    teacher_own = ring_gather(teacher, False)

    own_two, plane_two = [(own, 0), (own, 1)], [(plane, 0), (plane, 1)]
    two = [(0, 0), (1, 0)]
    *own_s, given = project(table, angles, own_two, [student_rows], two, [[0, 1]])
    teacher_own[2], given = lax.optimization_barrier((teacher_own[2], given))
    teacher_rows = both_cores(teacher_own)
    *own_t, given = project(table, angles, own_two, [teacher_rows], two, [[-1, -1, 0, 1]], given)
    got_own = send(given, TO_PLANE)
    plane_after, _ = lax.optimization_barrier((plane, own_t[0]))
    plane_two = [(plane_after, 0), (plane_after, 1)]
    *made, given_s, given_t = project(
        table,
        angles,
        plane_two,
        [student_rows, teacher_rows],
        two + [(0, 1), (1, 1)],
        [[0, 1], [2, 3]],
    )
    plane_s, plane_t = made[:2], made[2:]
    got_s, got_t = send(given_s, TO_PLANE), send(given_t, TO_PLANE)

    second = attend(
        table,
        angles,
        [[(plane_s[n], (got_own, n)), (plane_t[n], (got_own, 2 + n))] for n in range(2)],
    )
    got_s, got_t, _ = lax.optimization_barrier((got_s, got_t, second[2]))
    first = attend(
        table, angles, [[(own_s[n], (got_s, n)), (own_t[n], (got_t, n))] for n in range(2)]
    )
    back_first = send(second[2], TO_PLANE)
    back_second = send(first[2], TO_PLANE)
    core_first = [first[0], send(first[1], TO_CORE)], [back_first, send(back_first, TO_CORE)]
    core_second = [second[0], send(second[1], TO_CORE)], [back_second, send(back_second, TO_CORE)]

    planes = [plane, send(plane, TO_CORE)]
    cores = [own, send(own, TO_CORE)]
    (before,) = weight_call(first_kernel, table, *core_first, cores, [], [(CORE, F32)], 6.0)
    blocks = []
    for steps in ((2,), (1, 3, 0)):
        made = weight_call(
            lambda *refs: second_kernel(steps, *refs),
            table,
            *core_second,
            planes,
            [before],
            [(SHARD, BF)] * len(steps),
            5.0,
        )
        blocks += [send(value, ALONG_Y[s]) if s else value for value, s in zip(made, steps)]
    updated = adam(blocks, master, moment_one[0], moment_two[0])
    return tuple(value[None] for value in updated)


def solution(mesh):
    spec = P("blk", "fsdp", None)
    return jax.shard_map(
        per_device,
        mesh=mesh,
        in_specs=(spec,) * 5,
        out_specs=(spec,) * 3,
        check_vma=False,
    )
```

time: 196 us -> 191 us (0.974)
  Pallas kernels: 84.8 us -> 75.8 us
  starting transfers between devices: 35.4 us -> 39 us
    pallas_call x8, Pallas kernels: 78.1 us -> 69.1 us  [the longest x5 46 us: call(): pl.pallas_call(kernel, grid_spec=pltpu.PrefetchScalarGridSpec(num_scalar_...]
    ppermute x30 -> x29, starting transfers between devices: 31.7 us -> 35.4 us  [send(): return lax.ppermute(value, 'fsdp', pairs)]
    ppermute x1, waiting for transfers between devices: 6.01 us -> 3.89 us  [per_device(): lax.ppermute(snapshot[0], 'blk', [(g, (g + 1) % 8) for g in range(8)])]
    ppermute x30 -> x29, waiting for transfers between devices: 58.3 us -> 59.7 us  [send(): return lax.ppermute(value, 'fsdp', pairs)]
    unnamed x60 -> x54, local copies, waits for them, and re-layouts: 6 us -> 6.85 us
  transfers between devices with their start and end apart: 31 -> 30, of which waited for: 10 -> 12; matrix products, arithmetic and copies ran while one was open for 1% -> 1% of each run, Pallas kernels for 36% -> 32%
where the time goes in v5:
time: 191 us; the launch traced here: 190 us
  Pallas kernels  75.8 us (40%)
  waiting for transfers between devices  63.6 us (33%)
  starting transfers between devices  39 us (20%)
  local copies, waits for them, and re-layouts  8.72 us (5%)
  other arithmetic  2.43 us (1%)
    ppermute x29, waiting for transfers between devices, send(): return lax.ppermute(value, 'fsdp', pairs)  59.7 us
    pallas_call x5, Pallas kernels, call(): pl.pallas_call(kernel, grid_spec=pltpu.PrefetchScalarGridSpec(num_scalar_...  46 us
    ppermute x29, starting transfers between devices, send(): return lax.ppermute(value, 'fsdp', pairs)  35.4 us
    pallas_call x3, Pallas kernels, weight_call(): pl.pallas_call(kernel, grid_spec=pltpu.PrefetchScalarGridSpec(num_scalar_...  23.1 us
    unnamed x54, local copies, waits for them, and re-layouts  6.85 us
    pallas_call x1, Pallas kernels, adam(): pl.pallas_call(adam_kernel, grid=(SHARD // UNIT,), in_specs=[block] * 7,...  6.75 us
    ppermute x1, waiting for transfers between devices, per_device(): lax.ppermute(snapshot[0], 'blk', [(g, (g + 1) % 8) for g in range(8)])  3.89 us
  transfers between devices with their start and end apart: 30, of which 12 were waited for; matrix products, arithmetic and copies ran while one was open for 1% of the time, Pallas kernels for 32%

profile of v5, /device:TPU:1, one launch (start us, length us, event | category | flops | bytes accessed | tf_op | source)
XLA Modules:
  0.0 190.5 jit_solution(10095224900571549028)
XLA Ops:
  5.8 3.6 %collective-permute-start.1 = (bf16[160,2048]{1,0:T(8,128)(2,1)S(1)}, bf16[160,2048]{1,0:T(8,128)(2,1)S(1)}, u32[]{:S(2)}, u32[]{:S(2)}) collective-permute-start(bf16[160,2048]{1,0:T(8,128)(2,1)S(1)} %bitcast.24), channel_id=1, source_target_pairs={{0,16},{16,32},{32,48},{48,64},{64,80},{80,96},{96,112},{112,0},{1... | collective-permute-start | bytes 1966088 | tf_op jit(solution)/shard_map/ppermute | solution.py:372
  11.8 8.2 %collective-permute-done.5.refs_9_ = bf16[160,2048]{1,0:T(8,128)(2,1)S(1)} collective-permute-done((bf16[160,2048]{1,0:T(8,128)(2,1)S(1)}, bf16[160,2048]{1,0:T(8,128)(2,1)S(1)}, u32[]{:S(2)}, u32[]{:S(2)}) %collective-permute-start.5) | collective-permute-done | bytes 655392 | tf_op jit(solution)/shard_map/ppermute | solution.py:74
  21.8 3.9 %collective-permute-done.1.refs_6_.refs_14_ = bf16[160,2048]{1,0:T(8,128)(2,1)S(1)} collective-permute-done((bf16[160,2048]{1,0:T(8,128)(2,1)S(1)}, bf16[160,2048]{1,0:T(8,128)(2,1)S(1)}, u32[]{:S(2)}, u32[]{:S(2)}) %collective-permute-start.1) | collective-permute-done | bytes 655392 | tf_op jit(solution)/shard_map/ppermute | solution.py:372
  29.1 7.1 %collective-permute-done.6.refs_8_ = bf16[160,2048]{1,0:T(8,128)(2,1)} collective-permute-done((bf16[160,2048]{1,0:T(8,128)(2,1)S(1)}, bf16[160,2048]{1,0:T(8,128)(2,1)}, u32[]{:S(2)}, u32[]{:S(2)}) %collective-permute-start.6) | collective-permute-done | bytes 655392 | tf_op jit(solution)/shard_map/ppermute | solution.py:74
  36.2 2.4 %collective-permute-start.9 = (bf16[160,2048]{1,0:T(8,128)(2,1)}, bf16[160,2048]{1,0:T(8,128)(2,1)}, u32[]{:S(2)}, u32[]{:S(2)}) collective-permute-start(bf16[160,2048]{1,0:T(8,128)(2,1)} %collective-permute-done.6.refs_8_), channel_id=1, source_target_pairs={{0,1},{1,0},{2,3},{3,2},{4,5},{5,4},{6,7},{7,6},{8,9},{9,8},{10,11... | collective-permute-start | bytes 1966088 | tf_op jit(solution)/shard_map/ppermute | solution.py:74
  44.7 3.1 %collective-permute-start.12 = (bf16[160,2048]{1,0:T(8,128)(2,1)S(1)}, bf16[160,2048]{1,0:T(8,128)(2,1)S(1)}, u32[]{:S(2)}, u32[]{:S(2)}) collective-permute-start(bf16[160,2048]{1,0:T(8,128)(2,1)S(1)} %collective-permute-done.1.refs_6_.refs_14_), channel_id=1, source_target_pairs={{0,1},{1,0},{2,3},{3,2},{4,5},{5,4},{6,7},{7,6},{8,9},{9,8},{10,11... | collective-permute-start | bytes 1966088 | tf_op jit(solution)/shard_map/ppermute | solution.py:74
  47.9 3.6 %collective-permute-done.11.refs_9_.refs_17_ = bf16[160,2048]{1,0:T(8,128)(2,1)} collective-permute-done((bf16[160,2048]{1,0:T(8,128)(2,1)S(1)}, bf16[160,2048]{1,0:T(8,128)(2,1)}, u32[]{:S(2)}, u32[]{:S(2)}) %collective-permute-start.11) | collective-permute-done | bytes 655392 | tf_op jit(solution)/shard_map/ppermute | solution.py:74
  51.5 3.2 %collective-permute-start.13 = (bf16[160,2048]{1,0:T(8,128)(2,1)}, bf16[160,2048]{1,0:T(8,128)(2,1)S(1)}, u32[]{:S(2)}, u32[]{:S(2)}) collective-permute-start(bf16[160,2048]{1,0:T(8,128)(2,1)} %collective-permute-done.2.refs_7_.refs_15_), channel_id=1, source_target_pairs={{0,1},{1,0},{2,3},{3,2},{4,5},{5,4},{6,7},{7,6},{8,9},{9,8},{10,11... | collective-permute-start | bytes 1966088 | tf_op jit(solution)/shard_map/ppermute | solution.py:74
  55.3 8.8 %project.3 = (bf16[1280,256]{1,0:T(8,128)(2,1)}, bf16[1280,256]{1,0:T(8,128)(2,1)}, bf16[256,512]{1,0:T(8,128)(2,1)}) custom-call(s32[39]{0:T(128)} %dynamic-slice_bitcast_fusion.refs_0_.table, bf16[16,128]{1,0:T(8,128)(2,1)} %broadcast_1_refs_1_.2.refs_1_, bf16[512,2048]{1,0:T(8,128)(2,1)} %bitcast.12, bf16[512,2048]{1,0:T(8,128)(2,1)} %bitcast.13, ...), custom_call_target="tpu_custom_call" | custom-call | flops 500000000 | bytes 1048576 | tf_op jit(solution)/shard_map/project/pallas_call | solution.py:102
  64.9 4.0 %collective-permute-done.refs_2_.refs_3_.refs_5_ = bf16[512,2048]{1,0:T(8,128)(2,1)} collective-permute-done((bf16[512,2048]{1,0:T(8,128)(2,1)}, bf16[512,2048]{1,0:T(8,128)(2,1)}, u32[]{:S(2)}, u32[]{:S(2)}) %collective-permute-start) | collective-permute-done | bytes 2097184 | tf_op jit(solution)/shard_map/ppermute | solution.py:74
  72.8 8.9 %project.4 = (bf16[1280,256]{1,0:T(8,128)(2,1)}, bf16[1280,256]{1,0:T(8,128)(2,1)}, bf16[256,1024]{1,0:T(8,128)(2,1)}) custom-call(s32[39]{0:T(128)} %dynamic-slice_bitcast_fusion.refs_0_.table, bf16[256,512]{1,0:T(8,128)(2,1)} %get-tuple-element.33.refs_1_, bf16[512,2048]{1,0:T(8,128)(2,1)} %bitcast.14, bf16[512,2048]{1,0:T(8,128)(2,1)} %bitcast.15, ...), custom_call_target="tpu_custom_call" | custom-call | flops 500000000 | bytes 1048576 | tf_op jit(solution)/shard_map/project/pallas_call | solution.py:102
  82.7 11.9 %project.5 = (bf16[1280,256]{1,0:T(8,128)(2,1)}, bf16[1280,256]{1,0:T(8,128)(2,1)}, bf16[1280,256]{1,0:T(8,128)(2,1)}, bf16[1280,256]{1,0:T(8,128)(2,1)}, bf16[2...) custom-call(s32[39]{0:T(128)} %dynamic-slice_bitcast_fusion.refs_0_.table, bf16[16,128]{1,0:T(8,128)(2,1)} %broadcast_1_refs_1_.2.refs_1_, ...), custom_call_target="tpu_custom_call" | custom-call | flops 8000000000 | bytes 1048576 | tf_op jit(solution)/shard_map/project/pallas_call | solution.py:102
  96.9 8.1 %attend.2 = (bf16[640,512]{1,0:T(8,128)(2,1)}, bf16[640,512]{1,0:T(8,128)(2,1)}, bf16[256,512]{1,0:T(8,128)(2,1)}) custom-call(s32[39]{0:T(128)} %dynamic-slice_bitcast_fusion.refs_0_.table, bf16[1280,256]{1,0:T(8,128)(2,1)} %get-tuple-element.37.refs_1_, bf16[256,1024]{1,0:T(8,128)(2,1)} %copy-done.19, bf16[1280,256]{1,0:T(8,128)(2,1)} %get-tuple-element.39.refs_3_, ...), custom_call_target="tpu_custom_call" | custom-call | flops 8000000000 | bytes 1048576 | tf_op jit(solution)/shard_map/attend/pallas_call | solution.py:102
  105.1 3.0 %collective-permute-done.19.refs_4_.refs_8_ = bf16[256,512]{1,0:T(8,128)(2,1)S(1)} collective-permute-done((bf16[256,512]{1,0:T(8,128)(2,1)}, bf16[256,512]{1,0:T(8,128)(2,1)S(1)}, u32[]{:S(2)}, u32[]{:S(2)}) %collective-permute-start.19) | collective-permute-done | bytes 262176 | tf_op jit(solution)/shard_map/ppermute | solution.py:74
  108.8 8.2 %attend.3 = (bf16[640,512]{1,0:T(8,128)(2,1)}, bf16[640,512]{1,0:T(8,128)(2,1)}, bf16[256,512]{1,0:T(8,128)(2,1)}) custom-call(s32[39]{0:T(128)} %dynamic-slice_bitcast_fusion.refs_0_.table, bf16[1280,256]{1,0:T(8,128)(2,1)} %get-tuple-element.44.refs_1_, bf16[256,512]{1,0:T(8,128)(2,1)} %copy-done.24, bf16[1280,256]{1,0:T(8,128)(2,1)} %get-tuple-element.35.refs_3_, ...), custom_call_target="tpu_custom_call" | custom-call | flops 8000000000 | bytes 1048576 | tf_op jit(solution)/shard_map/attend/pallas_call | solution.py:102
  119.7 6.4 %collective-permute-done.24.refs_2_ = bf16[256,512]{1,0:T(8,128)(2,1)S(1)} collective-permute-done((bf16[256,512]{1,0:T(8,128)(2,1)S(1)}, bf16[256,512]{1,0:T(8,128)(2,1)S(1)}, u32[]{:S(2)}, u32[]{:S(2)}) %collective-permute-start.24) | collective-permute-done | bytes 262176 | tf_op jit(solution)/shard_map/ppermute | solution.py:74
  127.5 4.2 %collective-permute-done.20.refs_3_ = bf16[256,512]{1,0:T(8,128)(2,1)S(1)} collective-permute-done((bf16[256,512]{1,0:T(8,128)(2,1)}, bf16[256,512]{1,0:T(8,128)(2,1)S(1)}, u32[]{:S(2)}, u32[]{:S(2)}) %collective-permute-start.20) | collective-permute-done | bytes 262176 | tf_op jit(solution)/shard_map/ppermute | solution.py:74
  133.5 8.0 %weight_gradient.3.refs_7_ = f32[640,2048]{1,0:T(8,128)} custom-call(s32[39]{0:T(128)} %dynamic-slice_bitcast_fusion.refs_0_.table, bf16[640,512]{1,0:T(8,128)(2,1)} %get-tuple-element.53.refs_0_, bf16[640,512]{1,0:T(8,128)(2,1)} %copy-done.18, bf16[256,512]{1,0:T(8,128)(2,1)} %copy-done.23, bf16[256,512]{1,0:T(8,128)(2,1)} %copy-done.26, ...), custom_call_target="tpu_custom_call" | custom-call | flops 6000000000 | bytes 1048576 | tf_op jit(solution)/shard_map/weight_gradient/pallas_call | solution.py:301
  143.2 8.0 %weight_gradient.5 = (bf16[160,2048]{1,0:T(8,128)(2,1)}, bf16[160,2048]{1,0:T(8,128)(2,1)}, bf16[160,2048]{1,0:T(8,128)(2,1)}) custom-call(s32[39]{0:T(128)} %dynamic-slice_bitcast_fusion.refs_0_.table, bf16[640,512]{1,0:T(8,128)(2,1)} %get-tuple-element.42.refs_1_, bf16[640,512]{1,0:T(8,128)(2,1)} %copy-done.17, bf16[256,512]{1,0:T(8,128)(2,1)} %copy-done.20, ...), custom_call_target="tpu_custom_call" | custom-call | flops 5000000000 | bytes 1048576 | tf_op jit(solution)/shard_map/weight_gradient/pallas_call | solution.py:301
  151.2 2.7 %collective-permute-start.29 = (bf16[160,2048]{1,0:T(8,128)(2,1)}, bf16[160,2048]{1,0:T(8,128)(2,1)S(1)}, u32[]{:S(2)}, u32[]{:S(2)}) collective-permute-start(bf16[160,2048]{1,0:T(8,128)(2,1)} %get-tuple-element.56), channel_id=1, source_target_pairs={{0,6},{1,7},{2,0},{3,1},{4,2},{5,3},{6,4},{7,5},{8,14},{9,15},{10,... | collective-permute-start | bytes 1966088 | tf_op jit(solution)/shard_map/ppermute | solution.py:74
  153.8 7.1 %weight_gradient.4 = bf16[160,2048]{1,0:T(8,128)(2,1)} custom-call(s32[39]{0:T(128)} %dynamic-slice_bitcast_fusion.refs_0_.table, bf16[640,512]{1,0:T(8,128)(2,1)} %get-tuple-element.42.refs_1_, bf16[640,512]{1,0:T(8,128)(2,1)} %copy-done.17, bf16[256,512]{1,0:T(8,128)(2,1)} %copy-done.20, bf16[256,512]{1,0:T(8,128)(2,1)} %copy-done.21, ...), custom_call_target="tpu_custom_call" | custom-call | flops 5000000000 | bytes 1048576 | tf_op jit(solution)/shard_map/weight_gradient/pallas_call | solution.py:301
  161.3 7.7 %collective-permute-done.28.b = bf16[160,2048]{1,0:T(8,128)(2,1)S(1)} collective-permute-done((bf16[160,2048]{1,0:T(8,128)(2,1)}, bf16[160,2048]{1,0:T(8,128)(2,1)S(1)}, u32[]{:S(2)}, u32[]{:S(2)}) %collective-permute-start.28) | collective-permute-done | bytes 655392 | tf_op jit(solution)/shard_map/ppermute | solution.py:74
  169.0 12.8 %collective-permute-done.29.c = bf16[160,2048]{1,0:T(8,128)(2,1)S(1)} collective-permute-done((bf16[160,2048]{1,0:T(8,128)(2,1)}, bf16[160,2048]{1,0:T(8,128)(2,1)S(1)}, u32[]{:S(2)}, u32[]{:S(2)}) %collective-permute-start.29) | collective-permute-done | bytes 655392 | tf_op jit(solution)/shard_map/ppermute | solution.py:74
  183.7 6.7 %adam.1 = (f32[160,2048]{1,0:T(8,128)}, f32[160,2048]{1,0:T(8,128)}, f32[160,2048]{1,0:T(8,128)}) custom-call(bf16[160,2048]{1,0:T(8,128)(2,1)} %copy-done.13, bf16[160,2048]{1,0:T(8,128)(2,1)} %copy-done.11, bf16[160,2048]{1,0:T(8,128)(2,1)} %copy-done.12, bf16[160,2048]{1,0:T(8,128)(2,1)} %get-tuple-element.57.d, f32[160,2048]{1,0:T(8,128)} %bitcast.18, ...), custom_call_target="tpu_custom_call" | custom-call | tf_op jit(solution)/shard_map/adam/pallas_call | solution.py:336
  (105 shorter events, 37.8 us)
Async XLA Ops:
  2.1 17.9 %collective-permute-start.5 = (bf16[160,2048]{1,0:T(8,128)(2,1)S(1)}, bf16[160,2048]{1,0:T(8,128)(2,1)S(1)}, u32[]{:S(2)}, u32[]{:S(2)}) collective-permute-start(bf16[160,2048]{1,0:T(8,128)(2,1)S(1)} %bitcast_convert_fusion.refs_6_), channel_id=1, source_target_pairs={{0,2},{1,3},{2,4},{3,5},{4,6},{5,7},{6,0},{7,1},{8,10},{9,11},{10,... | collective-permute-start | bytes 1966088 | tf_op jit(solution)/shard_map/ppermute | solution.py:74
  4.3 15.8 %collective-permute-start.4 = (bf16[160,2048]{1,0:T(8,128)(2,1)S(1)}, bf16[160,2048]{1,0:T(8,128)(2,1)S(1)}, u32[]{:S(2)}, u32[]{:S(2)}) collective-permute-start(bf16[160,2048]{1,0:T(8,128)(2,1)S(1)} %bitcast_convert_fusion.refs_6_), channel_id=1, source_target_pairs={{0,6},{1,7},{2,0},{3,1},{4,2},{5,3},{6,4},{7,5},{8,14},{9,15},{10,... | collective-permute-start | bytes 1966088 | tf_op jit(solution)/shard_map/ppermute | solution.py:74
  5.8 19.8 %collective-permute-start.1 = (bf16[160,2048]{1,0:T(8,128)(2,1)S(1)}, bf16[160,2048]{1,0:T(8,128)(2,1)S(1)}, u32[]{:S(2)}, u32[]{:S(2)}) collective-permute-start(bf16[160,2048]{1,0:T(8,128)(2,1)S(1)} %bitcast.24), channel_id=1, source_target_pairs={{0,16},{16,32},{32,48},{48,64},{64,80},{80,96},{96,112},{112,0},{1... | collective-permute-start | bytes 1966088 | tf_op jit(solution)/shard_map/ppermute | solution.py:372
  9.4 59.4 %collective-permute-start = (bf16[512,2048]{1,0:T(8,128)(2,1)}, bf16[512,2048]{1,0:T(8,128)(2,1)}, u32[]{:S(2)}, u32[]{:S(2)}) collective-permute-start(bf16[512,2048]{1,0:T(8,128)(2,1)} %bitcast.11), channel_id=1, source_target_pairs={{0,8},{1,9},{2,10},{3,11},{4,12},{5,13},{6,14},{7,15},{8,0},{9,1},... | collective-permute-start | bytes 6291464 | tf_op jit(solution)/shard_map/ppermute | solution.py:74
  10.2 16.7 %collective-permute-start.7 = (bf16[160,2048]{1,0:T(8,128)(2,1)S(1)}, bf16[160,2048]{1,0:T(8,128)(2,1)S(1)}, u32[]{:S(2)}, u32[]{:S(2)}) collective-permute-start(bf16[160,2048]{1,0:T(8,128)(2,1)S(1)} %bitcast_convert_fusion.refs_6_), channel_id=1, source_target_pairs={{0,1},{1,0},{2,3},{3,2},{4,5},{5,4},{6,7},{7,6},{8,9},{9,8},{10,11... | collective-permute-start | bytes 1966088 | tf_op jit(solution)/shard_map/ppermute | solution.py:74
  20.1 16.2 %collective-permute-start.6 = (bf16[160,2048]{1,0:T(8,128)(2,1)S(1)}, bf16[160,2048]{1,0:T(8,128)(2,1)}, u32[]{:S(2)}, u32[]{:S(2)}) collective-permute-start(bf16[160,2048]{1,0:T(8,128)(2,1)S(1)} %collective-permute-done.5.refs_9_), channel_id=1, source_target_pairs={{0,2},{1,3},{2,4},{3,5},{4,6},{5,7},{6,0},{7,1},{8,10},{9,11},{10,... | collective-permute-start | bytes 1966088 | tf_op jit(solution)/shard_map/ppermute | solution.py:74
  20.1 16.1 %collective-permute-start.10 = (bf16[160,2048]{1,0:T(8,128)(2,1)S(1)}, bf16[160,2048]{1,0:T(8,128)(2,1)S(1)}, u32[]{:S(2)}, u32[]{:S(2)}) collective-permute-start(bf16[160,2048]{1,0:T(8,128)(2,1)S(1)} %collective-permute-done.5.refs_9_), channel_id=1, source_target_pairs={{0,1},{1,0},{2,3},{3,2},{4,5},{5,4},{6,7},{7,6},{8,9},{9,8},{10,11... | collective-permute-start | bytes 1966088 | tf_op jit(solution)/shard_map/ppermute | solution.py:74
  25.6 14.6 %collective-permute-start.2 = (bf16[160,2048]{1,0:T(8,128)(2,1)S(1)}, bf16[160,2048]{1,0:T(8,128)(2,1)}, u32[]{:S(2)}, u32[]{:S(2)}) collective-permute-start(bf16[160,2048]{1,0:T(8,128)(2,1)S(1)} %collective-permute-done.1.refs_6_.refs_14_), channel_id=1, source_target_pairs={{0,6},{1,7},{2,0},{3,1},{4,2},{5,3},{6,4},{7,5},{8,14},{9,15},{10,... | collective-permute-start | bytes 1966088 | tf_op jit(solution)/shard_map/ppermute | solution.py:74
  26.9 17.9 %collective-permute-start.8 = (bf16[160,2048]{1,0:T(8,128)(2,1)S(1)}, bf16[160,2048]{1,0:T(8,128)(2,1)}, u32[]{:S(2)}, u32[]{:S(2)}) collective-permute-start(bf16[160,2048]{1,0:T(8,128)(2,1)S(1)} %collective-permute-done.4.refs_7_), channel_id=1, source_target_pairs={{0,1},{1,0},{2,3},{3,2},{4,5},{5,4},{6,7},{7,6},{8,9},{9,8},{10,11... | collective-permute-start | bytes 1966088 | tf_op jit(solution)/shard_map/ppermute | solution.py:74
  36.2 15.2 %collective-permute-start.11 = (bf16[160,2048]{1,0:T(8,128)(2,1)S(1)}, bf16[160,2048]{1,0:T(8,128)(2,1)}, u32[]{:S(2)}, u32[]{:S(2)}) collective-permute-start(bf16[160,2048]{1,0:T(8,128)(2,1)S(1)} %collective-permute-done.1.refs_6_.refs_14_), channel_id=1, source_target_pairs={{0,2},{1,3},{2,4},{3,5},{4,6},{5,7},{6,0},{7,1},{8,10},{9,11},{10,... | collective-permute-start | bytes 1966088 | tf_op jit(solution)/shard_map/ppermute | solution.py:74
  36.2 18.5 %collective-permute-start.9 = (bf16[160,2048]{1,0:T(8,128)(2,1)}, bf16[160,2048]{1,0:T(8,128)(2,1)}, u32[]{:S(2)}, u32[]{:S(2)}) collective-permute-start(bf16[160,2048]{1,0:T(8,128)(2,1)} %collective-permute-done.6.refs_8_), channel_id=1, source_target_pairs={{0,1},{1,0},{2,3},{3,2},{4,5},{5,4},{6,7},{7,6},{8,9},{9,8},{10,11... | collective-permute-start | bytes 1966088 | tf_op jit(solution)/shard_map/ppermute | solution.py:74
  40.2 24.0 %collective-permute-start.3 = (bf16[160,2048]{1,0:T(8,128)(2,1)}, bf16[160,2048]{1,0:T(8,128)(2,1)}, u32[]{:S(2)}, u32[]{:S(2)}) collective-permute-start(bf16[160,2048]{1,0:T(8,128)(2,1)} %collective-permute-done.2.refs_7_.refs_15_), channel_id=1, source_target_pairs={{0,6},{1,7},{2,0},{3,1},{4,2},{5,3},{6,4},{7,5},{8,14},{9,15},{10,... | collective-permute-start | bytes 1966088 | tf_op jit(solution)/shard_map/ppermute | solution.py:74
  44.7 20.0 %collective-permute-start.12 = (bf16[160,2048]{1,0:T(8,128)(2,1)S(1)}, bf16[160,2048]{1,0:T(8,128)(2,1)S(1)}, u32[]{:S(2)}, u32[]{:S(2)}) collective-permute-start(bf16[160,2048]{1,0:T(8,128)(2,1)S(1)} %collective-permute-done.1.refs_6_.refs_14_), channel_id=1, source_target_pairs={{0,1},{1,0},{2,3},{3,2},{4,5},{5,4},{6,7},{7,6},{8,9},{9,8},{10,11... | collective-permute-start | bytes 1966088 | tf_op jit(solution)/shard_map/ppermute | solution.py:74
  51.5 19.4 %collective-permute-start.13 = (bf16[160,2048]{1,0:T(8,128)(2,1)}, bf16[160,2048]{1,0:T(8,128)(2,1)S(1)}, u32[]{:S(2)}, u32[]{:S(2)}) collective-permute-start(bf16[160,2048]{1,0:T(8,128)(2,1)} %collective-permute-done.2.refs_7_.refs_15_), channel_id=1, source_target_pairs={{0,1},{1,0},{2,3},{3,2},{4,5},{5,4},{6,7},{7,6},{8,9},{9,8},{10,11... | collective-permute-start | bytes 1966088 | tf_op jit(solution)/shard_map/ppermute | solution.py:74
  54.7 16.2 %collective-permute-start.15 = (bf16[160,2048]{1,0:T(8,128)(2,1)}, bf16[160,2048]{1,0:T(8,128)(2,1)S(1)}, u32[]{:S(2)}, u32[]{:S(2)}) collective-permute-start(bf16[160,2048]{1,0:T(8,128)(2,1)} %collective-permute-done.11.refs_9_.refs_17_), channel_id=1, source_target_pairs={{0,1},{1,0},{2,3},{3,2},{4,5},{5,4},{6,7},{7,6},{8,9},{9,8},{10,11... | collective-permute-start | bytes 1966088 | tf_op jit(solution)/shard_map/ppermute | solution.py:74
  64.8 62.6 %collective-permute-start.26 = (bf16[512,2048]{1,0:T(8,128)(2,1)S(1)}, bf16[512,2048]{1,0:T(8,128)(2,1)}, u32[]{:S(2)}, u32[]{:S(2)}) collective-permute-start(bf16[512,2048]{1,0:T(8,128)(2,1)S(1)} %bitcast.17), channel_id=1, source_target_pairs={{0,1},{1,0},{2,3},{3,2},{4,5},{5,4},{6,7},{7,6},{8,9},{9,8},{10,11... | collective-permute-start | bytes 6291464 | tf_op jit(solution)/shard_map/ppermute | solution.py:74
  68.9 72.7 %collective-permute-start.22 = (bf16[512,2048]{1,0:T(8,128)(2,1)}, bf16[512,2048]{1,0:T(8,128)(2,1)S(1)}, u32[]{:S(2)}, u32[]{:S(2)}) collective-permute-start(bf16[512,2048]{1,0:T(8,128)(2,1)} %collective-permute-done.refs_2_.refs_3_.refs_5_), channel_id=1, source_target_pairs={{0,1},{1,0},{2,3},{3,2},{4,5},{5,4},{6,7},{7,6},{8,9},{9,8},{10,11... | collective-permute-start | bytes 6291464 | tf_op jit(solution)/shard_map/ppermute | solution.py:74
  81.7 14.4 %collective-permute-start.16 = (bf16[256,1024]{1,0:T(8,128)(2,1)}, bf16[256,1024]{1,0:T(8,128)(2,1)S(1)}, u32[]{:S(2)}, u32[]{:S(2)}) collective-permute-start(bf16[256,1024]{1,0:T(8,128)(2,1)} %get-tuple-element.38), channel_id=1, source_target_pairs={{0,8},{1,9},{2,10},{3,11},{4,12},{5,13},{6,14},{7,15},{8,0},{9,1},... | collective-permute-start | bytes 1572872 | tf_op jit(solution)/shard_map/ppermute | solution.py:74
  117.1 15.5 %collective-permute-start.23 = (bf16[640,512]{1,0:T(8,128)(2,1)}, bf16[640,512]{1,0:T(8,128)(2,1)S(1)}, u32[]{:S(2)}, u32[]{:S(2)}) collective-permute-start(bf16[640,512]{1,0:T(8,128)(2,1)} %get-tuple-element.54), channel_id=1, source_target_pairs={{0,1},{1,0},{2,3},{3,2},{4,5},{5,4},{6,7},{7,6},{8,9},{9,8},{10,11... | collective-permute-start | bytes 1966088 | tf_op jit(solution)/shard_map/ppermute | solution.py:74
  118.9 12.7 %collective-permute-start.20 = (bf16[256,512]{1,0:T(8,128)(2,1)}, bf16[256,512]{1,0:T(8,128)(2,1)S(1)}, u32[]{:S(2)}, u32[]{:S(2)}) collective-permute-start(bf16[256,512]{1,0:T(8,128)(2,1)} %get-tuple-element.52), channel_id=1, source_target_pairs={{0,8},{1,9},{2,10},{3,11},{4,12},{5,13},{6,14},{7,15},{8,0},{9,1},... | collective-permute-start | bytes 786440 | tf_op jit(solution)/shard_map/ppermute | solution.py:74
  127.4 14.1 %collective-permute-start.17 = (bf16[640,512]{1,0:T(8,128)(2,1)S(1)}, bf16[640,512]{1,0:T(8,128)(2,1)S(1)}, u32[]{:S(2)}, u32[]{:S(2)}) collective-permute-start(bf16[640,512]{1,0:T(8,128)(2,1)S(1)} %copy-done.16), channel_id=1, source_target_pairs={{0,1},{1,0},{2,3},{3,2},{4,5},{5,4},{6,7},{7,6},{8,9},{9,8},{10,11... | collective-permute-start | bytes 1966088 | tf_op jit(solution)/shard_map/ppermute | solution.py:74
  151.2 17.8 %collective-permute-start.28 = (bf16[160,2048]{1,0:T(8,128)(2,1)}, bf16[160,2048]{1,0:T(8,128)(2,1)S(1)}, u32[]{:S(2)}, u32[]{:S(2)}) collective-permute-start(bf16[160,2048]{1,0:T(8,128)(2,1)} %get-tuple-element.55), channel_id=1, source_target_pairs={{0,2},{1,3},{2,4},{3,5},{4,6},{5,7},{6,0},{7,1},{8,10},{9,11},{10,... | collective-permute-start | bytes 1966088 | tf_op jit(solution)/shard_map/ppermute | solution.py:74
  151.2 30.7 %collective-permute-start.29 = (bf16[160,2048]{1,0:T(8,128)(2,1)}, bf16[160,2048]{1,0:T(8,128)(2,1)S(1)}, u32[]{:S(2)}, u32[]{:S(2)}) collective-permute-start(bf16[160,2048]{1,0:T(8,128)(2,1)} %get-tuple-element.56), channel_id=1, source_target_pairs={{0,6},{1,7},{2,0},{3,1},{4,2},{5,3},{6,4},{7,5},{8,14},{9,15},{10,... | collective-permute-start | bytes 1966088 | tf_op jit(solution)/shard_map/ppermute | solution.py:74
  161.0 21.9 %collective-permute-start.27 = (bf16[160,2048]{1,0:T(8,128)(2,1)}, bf16[160,2048]{1,0:T(8,128)(2,1)S(1)}, u32[]{:S(2)}, u32[]{:S(2)}) collective-permute-start(bf16[160,2048]{1,0:T(8,128)(2,1)} %weight_gradient.4), channel_id=1, source_target_pairs={{0,4},{1,5},{2,6},{3,7},{4,0},{5,1},{6,2},{7,3},{8,12},{9,13},{10,... | collective-permute-start | bytes 1966088 | tf_op jit(solution)/shard_map/ppermute | solution.py:74
  (33 other events, 341.8 us)

commit v6 on v5

--- a/solution.py
+++ b/solution.py
@@ -32,25 +32,29 @@
 EXCHANGED = 2 * HD
 INV_ROOT = 1.0 / math.sqrt(HD)
 
-AT_WEIGHT, AT_GIVEN, AT_QUERY, AT_KEY, AT_CORE, AT_STEP, AT_FILL = 0, 8, 9, 17, 19, 27, 31
+AT_WEIGHT, AT_GIVEN, AT_QUERY, AT_KEY, AT_CORE, AT_STEP, AT_FILL, AT_BACK = 0, 8, 9, 17, 19, 27, 31, 36
 GIVEN = (1024, 768)
 QUERY = (tuple(range(8)), (10, 11, 0, 1, 2, 3, 4, 5))
 KEY = ((10, 11), (8, 9))
 
 
+def given_units(plane, core):
+    rows = [GIVEN[plane] + UNIT * unit for unit in range(8)]
+    return [(u, r // 320 * 160 + r % 160) for u, r in enumerate(rows) if r % 320 // 160 == core]
+
+
 def build_table():
-    table = np.zeros((16, 39), np.int32)
+    table = np.zeros((16, 46), np.int32)
     for d in range(16):
         z, y, c = d // 8, d % 8 // 2, d % 2
         gathered = [320 * ((y + s) % 4) + 160 * (c ^ r) for r in range(2) for s in range(4)]
         cores = [320 * k + 160 * (c ^ r) for r in range(2) for k in range(4)]
         steps = [160 * ((y + s) % 4) for s in range(4)]
-        fill = []
-        for unit in range(8):
-            row = GIVEN[z] + UNIT * unit
-            mine = row % 320 // 160 == c
-            fill.append(row // 320 * 160 + row % 160 if mine else -1)
-        table[d] = gathered + [GIVEN[z], *QUERY[z], *KEY[z]] + cores + steps + fill
+        fill = ([row for _, row in given_units(z, c)] + [-1] * 5)[:5]
+        back = []
+        for r in range(2):
+            back += ([unit for unit, _ in given_units(1 - z, c ^ r)] + [0] * 5)[:5]
+        table[d] = gathered + [GIVEN[z], *QUERY[z], *KEY[z]] + cores + steps + fill + back
     return table
 
 
@@ -67,6 +71,7 @@
 
 TO_CORE = pairs_of(lambda z, y, c: (z, y, c + 1))
 TO_PLANE = pairs_of(lambda z, y, c: (z + 1, y, c))
+TO_BOTH = pairs_of(lambda z, y, c: (z + 1, y, c + 1))
 ALONG_Y = [pairs_of(lambda z, y, c, s=s: (z, y + s, c)) for s in range(4)]
 
 
@@ -213,8 +218,9 @@
     return [rotated(g * INV_ROOT, cosine, -sine).astype(BF) for g in grads]
 
 
-def attend_kernel(count, table, *refs):
-    inputs, (cosine, sine, out, other, back, both_s, both_t, grads) = refs[: 4 * count], refs[4 * count :]
+def attend_kernel(count, carry_count, table, *refs):
+    carried, refs = refs[:carry_count], refs[carry_count:]
+    inputs, (cosine, sine, out, other, back, back_other, both_s, both_t, grads) = refs[: 4 * count], refs[4 * count :]
     for seq in range(count):
         own_s, got_s, own_t, got_t = inputs[4 * seq : 4 * seq + 4]
         lanes = slice(seq * SEQ, (seq + 1) * SEQ)
@@ -235,21 +241,28 @@
         row = pl.multiple_of(table[AT_CORE + n], SHARD)
         target = out if n < 4 else other
         target[n % 4 * SHARD : (n % 4 + 1) * SHARD, :] = grads[pl.ds(row, SHARD), :]
-    back[...] = grads[ROWS:, :]
-
-
-def attend(table, angles, sequences):
+    for n in range(10):
+        row = pl.multiple_of(ROWS + table[AT_BACK + n] * UNIT, UNIT)
+        target = back if n < 5 else back_other
+        unit = slice(n % 5 * UNIT, (n % 5 + 1) * UNIT)
+        target[unit, target.shape[1] - count * SEQ :] = grads[pl.ds(row, UNIT), :]
+    for value, target in zip(carried, (back, back_other)):
+        target[:, : value.shape[1]] = value[...]
+
+
+def attend(table, angles, sequences, carried=()):
     count = len(sequences)
-    operands = [(table, None)]
+    operands = [(table, None)] + [(value, block(value.shape)) for value in carried]
+    wide = count * SEQ + (carried[0].shape[1] if carried else 0)
     for sequence in sequences:
         for own, (got, at) in sequence:
             operands += [(own, block((ROWS, SEQ))), (got, block((EXCHANGED, SEQ), 0, at))]
     operands += [(value, block((HALF, SEQ))) for value in angles]
     return call(
-        lambda *refs: attend_kernel(count, *refs),
+        lambda *refs: attend_kernel(count, len(carried), *refs),
         "attend",
         operands,
-        [((rows, count * SEQ), BF) for rows in (CORE, CORE, EXCHANGED)],
+        [((CORE, count * SEQ), BF)] * 2 + [((SHARD, wide), BF)] * 2,
         [pltpu.VMEM((ROWS + EXCHANGED, count * SEQ), BF)] * 3,
         1.0 + 3.5 * count,
     )
@@ -257,23 +270,36 @@
 
 TILE = 512
 SPAN = 2 * SEQ
+PART = SHARD // 2
 
 
 def fill(table, held, grads, backs):
-    for n in range(2):
-        held[:, n * SPAN : (n + 1) * SPAN] = grads[n][...]
-    for unit in range(8):
+    first = 0
+    for grad in grads:
+        held[:, first : first + grad.shape[1]] = grad[...]
+        first += grad.shape[1]
+    for unit in range(5):
         row = table[AT_FILL + unit]
 
         @pl.when(row >= 0)
         def _():
-            at = pl.ds(pl.multiple_of(row, UNIT), UNIT)
-            for n in range(2):
-                held[at, n * SPAN : (n + 1) * SPAN] = backs[n][unit * UNIT : (unit + 1) * UNIT, :]
-
-
-def first_kernel(table, *refs):
-    grads, backs, tokens, out, held = refs[:2], refs[2:4], refs[4:6], refs[6], refs[7]
+            at, first = pl.ds(pl.multiple_of(row, UNIT), UNIT), 0
+            for back in backs:
+                lanes = slice(first, first + back.shape[1])
+                held[at, lanes] = back[unit * UNIT : (unit + 1) * UNIT, :]
+                first = lanes.stop
+
+
+def split(refs, counts):
+    out, refs = [], list(refs)
+    for count in counts:
+        out.append(refs[:count])
+        refs = refs[count:]
+    return out + [refs]
+
+
+def first_kernel(counts, table, *refs):
+    grads, backs, tokens, (out, held) = split(refs, counts)
 
     @pl.when(pl.program_id(0) == 0)
     def _():
@@ -282,29 +308,30 @@
     out[...] = dot(held[:, :SPAN], tokens[0][...]) + dot(held[:, SPAN:], tokens[1][...])
 
 
-def second_kernel(steps, table, *refs):
-    grads, backs, tokens, before, outs, held = refs[:2], refs[2:4], refs[4:6], refs[6], refs[7:-1], refs[-1]
+def second_kernel(steps, counts, table, *refs):
+    grads, backs, tokens, (before, *outs, held) = split(refs, counts)
 
     @pl.when(pl.program_id(0) == 0)
     def _():
         fill(table, held, grads, backs)
 
-    for step, out in zip(steps, outs):
+    for at, step in enumerate(steps):
         rows = pl.ds(pl.multiple_of(table[AT_STEP + step], SHARD), SHARD)
         total = before[rows, :] + dot(held[rows, :SPAN], tokens[0][...])
         total += dot(held[rows, SPAN:], tokens[1][...])
-        out[...] = total.astype(BF)
+        total = total.astype(BF)
+        outs[2 * at][...] = total[:PART]
+        outs[2 * at + 1][...] = total[PART:]
 
 
 def weight_call(kernel, table, grads, backs, tokens, more, outs, microseconds):
     tile = lambda t, table: (0, t)
     return pl.pallas_call(
-        kernel,
+        lambda *refs: kernel((len(grads), len(backs), len(tokens)), *refs),
         grid_spec=pltpu.PrefetchScalarGridSpec(
             num_scalar_prefetch=1,
             grid=(D // TILE,),
-            in_specs=[block((CORE, SPAN))] * 2
-            + [block((EXCHANGED, SPAN))] * 2
+            in_specs=[block(value.shape) for value in grads + backs]
             + [pl.BlockSpec((x.shape[0], TILE), tile) for x in tokens + more],
             out_specs=[pl.BlockSpec((rows, TILE), tile) for rows, _ in outs],
             scratch_shapes=[pltpu.VMEM((CORE, 2 * SPAN), BF)],
@@ -316,8 +343,8 @@
     )(table, *grads, *backs, *tokens, *more)
 
 
-def adam_kernel(a, b, c, d, weight, one, two, weight_out, one_out, two_out):
-    gradient = (a[...].astype(F32) + b[...].astype(F32)) + (c[...].astype(F32) + d[...].astype(F32))
+def adam_kernel(a, b, c, weight, one, two, weight_out, one_out, two_out):
+    gradient = a[...].astype(F32) + (b[...].astype(F32) + c[...].astype(F32))
     first_new = BETA_ONE * one[...] + (1.0 - BETA_ONE) * gradient
     second_new = BETA_TWO * two[...] + (1.0 - BETA_TWO) * gradient * gradient
     step_dir = (
@@ -331,17 +358,33 @@
     two_out[...] = second_new
 
 
-def adam(blocks, weight, one, two):
-    block = pl.BlockSpec((UNIT, D), lambda k: (k, 0))
+def adam_body(*refs):
+    pairs, rest = refs[:6], refs[6:]
+    half = pl.program_id(0) // (PART // ADAM_ROWS)
+    for at in range(2):
+
+        @pl.when(half == at)
+        def _():
+            adam_kernel(*pairs[at::2], *rest)
+
+
+ADAM_ROWS = 16
+
+
+def adam(pairs, weight, one, two):
+    steps = PART // ADAM_ROWS
+    straight = pl.BlockSpec((ADAM_ROWS, D), lambda k: (k, 0))
+    low = pl.BlockSpec((ADAM_ROWS, D), lambda k: (jnp.minimum(k, steps - 1), 0))
+    high = pl.BlockSpec((ADAM_ROWS, D), lambda k: (jnp.maximum(k - steps, 0), 0))
     return pl.pallas_call(
-        adam_kernel,
-        grid=(SHARD // UNIT,),
-        in_specs=[block] * 7,
-        out_specs=[block] * 3,
+        adam_body,
+        grid=(2 * steps,),
+        in_specs=[low, high] * 3 + [straight] * 3,
+        out_specs=[straight] * 3,
         out_shape=[jax.ShapeDtypeStruct((SHARD, D), F32)] * 3,
         compiler_params=params(56),
         name="adam",
-    )(*blocks, weight, one, two)
+    )(*[value for pair in pairs for value in pair], weight, one, two)
 
 
 def rotary_tables():
@@ -377,7 +420,9 @@
     own_two, plane_two = [(own, 0), (own, 1)], [(plane, 0), (plane, 1)]
     two = [(0, 0), (1, 0)]
     *own_s, given = project(table, angles, own_two, [student_rows], two, [[0, 1]])
-    teacher_own[2], given = lax.optimization_barrier((teacher_own[2], given))
+    teacher_own[2], teacher_own[3], given = lax.optimization_barrier(
+        (teacher_own[2], teacher_own[3], given)
+    )
     teacher_rows = both_cores(teacher_own)
     *own_t, given = project(table, angles, own_two, [teacher_rows], two, [[-1, -1, 0, 1]], given)
     got_own = send(given, TO_PLANE)
@@ -400,30 +445,54 @@
         [[(plane_s[n], (got_own, n)), (plane_t[n], (got_own, 2 + n))] for n in range(2)],
     )
     got_s, got_t, _ = lax.optimization_barrier((got_s, got_t, second[2]))
-    first = attend(
-        table, angles, [[(own_s[n], (got_s, n)), (own_t[n], (got_t, n))] for n in range(2)]
-    )
-    back_first = send(second[2], TO_PLANE)
-    back_second = send(first[2], TO_PLANE)
-    core_first = [first[0], send(first[1], TO_CORE)], [back_first, send(back_first, TO_CORE)]
-    core_second = [second[0], send(second[1], TO_CORE)], [back_second, send(back_second, TO_CORE)]
-
-    planes = [plane, send(plane, TO_CORE)]
-    cores = [own, send(own, TO_CORE)]
-    (before,) = weight_call(first_kernel, table, *core_first, cores, [], [(CORE, F32)], 6.0)
-    blocks = []
-    for steps in ((2,), (1, 3, 0)):
-        made = weight_call(
+    first = [attend(table, angles, [[(own_s[0], (got_s, 0)), (own_t[0], (got_t, 0))]])]
+    back_first = [send(second[2], TO_PLANE), send(second[3], TO_PLANE)]
+    got_s, got_t, *back_first, carried = lax.optimization_barrier(
+        (got_s, got_t, *back_first, first[0][2])
+    )
+    back_first[1] = send(back_first[1], TO_CORE)
+    first.append(
+        attend(
+            table,
+            angles,
+            [[(own_s[1], (got_s, 1)), (own_t[1], (got_t, 1))]],
+            (carried, first[0][3]),
+        )
+    )
+    back_second = [send(first[1][2], TO_PLANE), send(first[1][3], TO_BOTH)]
+    (before,) = weight_call(
+        first_kernel,
+        table,
+        [part[0] for part in first] + [send(part[1], TO_CORE) for part in first],
+        back_first,
+        [own, send(own, TO_CORE)],
+        [],
+        [(CORE, F32)],
+        6.0,
+    )
+
+    def weight_blocks(steps):
+        return weight_call(
             lambda *refs: second_kernel(steps, *refs),
             table,
-            *core_second,
-            planes,
+            [second[0], send(second[1], TO_CORE)],
+            back_second,
+            [plane_after, send(plane_after, TO_CORE)],
             [before],
-            [(SHARD, BF)] * len(steps),
+            [(PART, BF)] * (2 * len(steps)),
             5.0,
         )
-        blocks += [send(value, ALONG_Y[s]) if s else value for value, s in zip(made, steps)]
-    updated = adam(blocks, master, moment_one[0], moment_two[0])
+
+    up, down = ALONG_Y[1], ALONG_Y[3]
+    far_low, far_high = weight_blocks((2,))
+    far_low, far_high = send(far_low, up), send(far_high, down)
+    next_low, next_high, last_low, last_high, own_low, own_high = weight_blocks((1, 3, 0))
+    from_below = [None, send(next_high, up)]
+    from_above = [send(last_low, down), None]
+    from_below[0] = send((next_low.astype(F32) + far_low.astype(F32)).astype(BF), up)
+    from_above[1] = send((last_high.astype(F32) + far_high.astype(F32)).astype(BF), down)
+    pairs = [(own_low, own_high), from_below, from_above]
+    updated = adam(pairs, master, moment_one[0], moment_two[0])
     return tuple(value[None] for value in updated)
 
 

time: 191 us -> 170 us (0.89)
  waiting for transfers between devices: 63.6 us -> 37.2 us
  Pallas kernels: 75.8 us -> 79.8 us
  local copies, waits for them, and re-layouts: 8.72 us -> 6.61 us
  other arithmetic: 2.43 us -> 4.54 us
    ppermute x29 -> x34, waiting for transfers between devices: 59.7 us -> 33.4 us  [send(): return lax.ppermute(value, 'fsdp', pairs)]
    pallas_call x5 -> x6, Pallas kernels: 46 us -> 48.5 us  [call(): pl.pallas_call(kernel, grid_spec=pltpu.PrefetchScalarGridSpec(num_scalar_...]
    convert_element_type x0 -> x2, other arithmetic: none -> 2.1 us  [the longest x1 1.05 us: per_device(): (last_high.astype(F32) + far_high.astype(F32)).astype(BF)]
    unnamed x54 -> x58, local copies, waits for them, and re-layouts: 6.85 us -> 4.79 us
    ppermute x29 -> x34, starting transfers between devices: 35.4 us -> 36.5 us  [send(): return lax.ppermute(value, 'fsdp', pairs)]
  transfers between devices with their start and end apart: 30 -> 35, of which waited for: 12 -> 11; matrix products, arithmetic and copies ran while one was open for 1% -> 3% of each run, Pallas kernels for 32% -> 38%
where the time goes in v6:
time: 170 us; the launch traced here: 169 us
  Pallas kernels  79.8 us (47%)
  starting transfers between devices  40.1 us (24%)
  waiting for transfers between devices  37.2 us (22%)
  local copies, waits for them, and re-layouts  6.61 us (4%)
  other arithmetic  4.54 us (3%)
    pallas_call x6, Pallas kernels, call(): pl.pallas_call(kernel, grid_spec=pltpu.PrefetchScalarGridSpec(num_scalar_...  48.5 us
    ppermute x34, starting transfers between devices, send(): return lax.ppermute(value, 'fsdp', pairs)  36.5 us
    ppermute x34, waiting for transfers between devices, send(): return lax.ppermute(value, 'fsdp', pairs)  33.4 us
    pallas_call x3, Pallas kernels, weight_call(): pl.pallas_call(lambda *refs: kernel((len(grads), len(backs), len(tokens))...  23 us
    pallas_call x1, Pallas kernels, adam(): pl.pallas_call(adam_body, grid=(2 * steps,), in_specs=[low, high] * 3 + [...  8.38 us
    unnamed x58, local copies, waits for them, and re-layouts  4.79 us
    ppermute x1, waiting for transfers between devices, per_device(): lax.ppermute(snapshot[0], 'blk', [(g, (g + 1) % 8) for g in range(8)])  3.89 us
    ppermute x1, starting transfers between devices, per_device(): lax.ppermute(snapshot[0], 'blk', [(g, (g + 1) % 8) for g in range(8)])  3.6 us
  transfers between devices with their start and end apart: 35, of which 11 were waited for; matrix products, arithmetic and copies ran while one was open for 3% of the time, Pallas kernels for 38%

profile of v6, /device:TPU:1, one launch (start us, length us, event | category | flops | bytes accessed | tf_op | source)
XLA Modules:
  0.0 169.4 jit_solution(17547780033252734978)
XLA Ops:
  2.1 2.2 %collective-permute-start.6 = (bf16[160,2048]{1,0:T(8,128)(2,1)S(1)}, bf16[160,2048]{1,0:T(8,128)(2,1)S(1)}, u32[]{:S(2)}, u32[]{:S(2)}) collective-permute-start(bf16[160,2048]{1,0:T(8,128)(2,1)S(1)} %bitcast_convert_fusion.refs_6_), channel_id=1, source_target_pairs={{0,2},{1,3},{2,4},{3,5},{4,6},{5,7},{6,0},{7,1},{8,10},{9,11},{10,... | collective-permute-start | bytes 1966088 | tf_op jit(solution)/shard_map/ppermute | solution.py:79
  5.8 3.6 %collective-permute-start.1 = (bf16[160,2048]{1,0:T(8,128)(2,1)S(1)}, bf16[160,2048]{1,0:T(8,128)(2,1)S(1)}, u32[]{:S(2)}, u32[]{:S(2)}) collective-permute-start(bf16[160,2048]{1,0:T(8,128)(2,1)S(1)} %bitcast.24), channel_id=1, source_target_pairs={{0,16},{16,32},{32,48},{48,64},{64,80},{80,96},{96,112},{112,0},{1... | collective-permute-start | bytes 1966088 | tf_op jit(solution)/shard_map/ppermute | solution.py:415
  11.8 8.2 %collective-permute-done.6.refs_9_ = bf16[160,2048]{1,0:T(8,128)(2,1)S(1)} collective-permute-done((bf16[160,2048]{1,0:T(8,128)(2,1)S(1)}, bf16[160,2048]{1,0:T(8,128)(2,1)S(1)}, u32[]{:S(2)}, u32[]{:S(2)}) %collective-permute-start.6) | collective-permute-done | bytes 655392 | tf_op jit(solution)/shard_map/ppermute | solution.py:79
  21.8 3.9 %collective-permute-done.1.refs_6_.refs_14_ = bf16[160,2048]{1,0:T(8,128)(2,1)S(1)} collective-permute-done((bf16[160,2048]{1,0:T(8,128)(2,1)S(1)}, bf16[160,2048]{1,0:T(8,128)(2,1)S(1)}, u32[]{:S(2)}, u32[]{:S(2)}) %collective-permute-start.1) | collective-permute-done | bytes 655392 | tf_op jit(solution)/shard_map/ppermute | solution.py:415
  26.9 2.2 %collective-permute-start.9 = (bf16[160,2048]{1,0:T(8,128)(2,1)S(1)}, bf16[160,2048]{1,0:T(8,128)(2,1)}, u32[]{:S(2)}, u32[]{:S(2)}) collective-permute-start(bf16[160,2048]{1,0:T(8,128)(2,1)S(1)} %collective-permute-done.5.refs_7_), channel_id=1, source_target_pairs={{0,1},{1,0},{2,3},{3,2},{4,5},{5,4},{6,7},{7,6},{8,9},{9,8},{10,11... | collective-permute-start | bytes 1966088 | tf_op jit(solution)/shard_map/ppermute | solution.py:79
  29.1 7.1 %collective-permute-done.7.refs_8_ = bf16[160,2048]{1,0:T(8,128)(2,1)} collective-permute-done((bf16[160,2048]{1,0:T(8,128)(2,1)S(1)}, bf16[160,2048]{1,0:T(8,128)(2,1)}, u32[]{:S(2)}, u32[]{:S(2)}) %collective-permute-start.7) | collective-permute-done | bytes 655392 | tf_op jit(solution)/shard_map/ppermute | solution.py:79
  36.2 2.3 %collective-permute-start.10 = (bf16[160,2048]{1,0:T(8,128)(2,1)}, bf16[160,2048]{1,0:T(8,128)(2,1)}, u32[]{:S(2)}, u32[]{:S(2)}) collective-permute-start(bf16[160,2048]{1,0:T(8,128)(2,1)} %collective-permute-done.7.refs_8_), channel_id=1, source_target_pairs={{0,1},{1,0},{2,3},{3,2},{4,5},{5,4},{6,7},{7,6},{8,9},{9,8},{10,11... | collective-permute-start | bytes 1966088 | tf_op jit(solution)/shard_map/ppermute | solution.py:79
  40.2 2.3 %collective-permute-start.3 = (bf16[160,2048]{1,0:T(8,128)(2,1)}, bf16[160,2048]{1,0:T(8,128)(2,1)}, u32[]{:S(2)}, u32[]{:S(2)}) collective-permute-start(bf16[160,2048]{1,0:T(8,128)(2,1)} %collective-permute-done.2.refs_7_.refs_15_), channel_id=1, source_target_pairs={{0,6},{1,7},{2,0},{3,1},{4,2},{5,3},{6,4},{7,5},{8,14},{9,15},{10,... | collective-permute-start | bytes 1966088 | tf_op jit(solution)/shard_map/ppermute | solution.py:79
  44.7 3.1 %collective-permute-start.12 = (bf16[160,2048]{1,0:T(8,128)(2,1)S(1)}, bf16[160,2048]{1,0:T(8,128)(2,1)S(1)}, u32[]{:S(2)}, u32[]{:S(2)}) collective-permute-start(bf16[160,2048]{1,0:T(8,128)(2,1)S(1)} %collective-permute-done.1.refs_6_.refs_14_), channel_id=1, source_target_pairs={{0,1},{1,0},{2,3},{3,2},{4,5},{5,4},{6,7},{7,6},{8,9},{9,8},{10,11... | collective-permute-start | bytes 1966088 | tf_op jit(solution)/shard_map/ppermute | solution.py:79
  48.5 8.9 %project.3 = (bf16[1280,256]{1,0:T(8,128)(2,1)}, bf16[1280,256]{1,0:T(8,128)(2,1)}, bf16[256,512]{1,0:T(8,128)(2,1)}) custom-call(s32[46]{0:T(128)} %dynamic-slice_bitcast_fusion.refs_0_, bf16[16,128]{1,0:T(8,128)(2,1)} %broadcast_1_refs_1_.2.refs_1_, bf16[512,2048]{1,0:T(8,128)(2,1)} %bitcast.12, bf16[512,2048]{1,0:T(8,128)(2,1)} %bitcast.13, ...), custom_call_target="tpu_custom_call" | custom-call | flops 500000000 | bytes 1048576 | tf_op jit(solution)/shard_map/project/pallas_call | solution.py:107
  62.6 8.9 %project.4 = (bf16[1280,256]{1,0:T(8,128)(2,1)}, bf16[1280,256]{1,0:T(8,128)(2,1)}, bf16[256,1024]{1,0:T(8,128)(2,1)}) custom-call(s32[46]{0:T(128)} %dynamic-slice_bitcast_fusion.refs_0_, bf16[256,512]{1,0:T(8,128)(2,1)} %get-tuple-element.50.refs_1_, bf16[512,2048]{1,0:T(8,128)(2,1)} %bitcast.14, bf16[512,2048]{1,0:T(8,128)(2,1)} %bitcast.15, ...), custom_call_target="tpu_custom_call" | custom-call | flops 500000000 | bytes 1048576 | tf_op jit(solution)/shard_map/project/pallas_call | solution.py:107
  72.9 11.9 %project.5 = (bf16[1280,256]{1,0:T(8,128)(2,1)}, bf16[1280,256]{1,0:T(8,128)(2,1)}, bf16[1280,256]{1,0:T(8,128)(2,1)}, bf16[1280,256]{1,0:T(8,128)(2,1)}, bf16[2...) custom-call(s32[46]{0:T(128)} %dynamic-slice_bitcast_fusion.refs_0_, bf16[16,128]{1,0:T(8,128)(2,1)} %broadcast_1_refs_1_.2.refs_1_, ...), custom_call_target="tpu_custom_call" | custom-call | flops 8000000000 | bytes 1048576 | tf_op jit(solution)/shard_map/project/pallas_call | solution.py:107
  87.1 8.2 %attend.3 = (bf16[640,512]{1,0:T(8,128)(2,1)}, bf16[640,512]{1,0:T(8,128)(2,1)}, bf16[160,512]{1,0:T(8,128)(2,1)}, bf16[160,512]{1,0:T(8,128)(2,1)}) custom-call(s32[46]{0:T(128)} %dynamic-slice_bitcast_fusion.refs_0_, bf16[1280,256]{1,0:T(8,128)(2,1)} %get-tuple-element.55.refs_1_, bf16[256,1024]{1,0:T(8,128)(2,1)} %copy-done.20, ...), custom_call_target="tpu_custom_call" | custom-call | flops 8000000000 | bytes 1048576 | tf_op jit(solution)/shard_map/attend/pallas_call | solution.py:107
  96.1 2.5 %collective-permute-done.19.refs_4_.refs_6_ = bf16[256,512]{1,0:T(8,128)(2,1)S(1)} collective-permute-done((bf16[256,512]{1,0:T(8,128)(2,1)}, bf16[256,512]{1,0:T(8,128)(2,1)S(1)}, u32[]{:S(2)}, u32[]{:S(2)}) %collective-permute-start.19) | collective-permute-done | bytes 262176 | tf_op jit(solution)/shard_map/ppermute | solution.py:79
  99.5 5.2 %attend.4 = (bf16[640,256]{1,0:T(8,128)(2,1)}, bf16[640,256]{1,0:T(8,128)(2,1)}, bf16[160,256]{1,0:T(8,128)(2,1)}, bf16[160,256]{1,0:T(8,128)(2,1)}) custom-call(s32[46]{0:T(128)} %dynamic-slice_bitcast_fusion.refs_0_, bf16[1280,256]{1,0:T(8,128)(2,1)} %get-tuple-element.68.refs_1_, bf16[256,512]{1,0:T(8,128)(2,1)} %copy-done.23, ...), custom_call_target="tpu_custom_call" | custom-call | flops 4499999744 | bytes 1048576 | tf_op jit(solution)/shard_map/attend/pallas_call | solution.py:107
  106.1 5.5 %attend.5 = (bf16[640,256]{1,0:T(8,128)(2,1)}, bf16[640,256]{1,0:T(8,128)(2,1)}, bf16[160,512]{1,0:T(8,128)(2,1)}, bf16[160,512]{1,0:T(8,128)(2,1)}) custom-call(s32[46]{0:T(128)} %dynamic-slice_bitcast_fusion.refs_0_, bf16[160,256]{1,0:T(8,128)(2,1)} %get-tuple-element.70.refs_1_, bf16[160,256]{1,0:T(8,128)(2,1)} %get-tuple-element.71.refs_2_, ...), custom_call_target="tpu_custom_call" | custom-call | flops 4499999744 | bytes 1048576 | tf_op jit(solution)/shard_map/attend/pallas_call | solution.py:107
  115.3 8.1 %weight_gradient.3.refs_7_ = f32[640,2048]{1,0:T(8,128)} custom-call(s32[46]{0:T(128)} %dynamic-slice_bitcast_fusion.refs_0_, bf16[640,256]{1,0:T(8,128)(2,1)} %get-tuple-element.78.refs_1_, bf16[640,256]{1,0:T(8,128)(2,1)} %get-tuple-element.79.refs_2_, bf16[640,256]{1,0:T(8,128)(2,1)} %copy-done.21, bf16[640,256]{1,0:T(8,128)(2,1)} %copy-done.22, ...), custom_call_target="tpu_custom_call" | custom-call | flops 6000000000 | bytes 1048576 | tf_op jit(solution)/shard_map/weight_gradient/pallas_call | solution.py:329
  125.0 7.0 %weight_gradient.5 = (bf16[80,2048]{1,0:T(8,128)(2,1)}, bf16[80,2048]{1,0:T(8,128)(2,1)}) custom-call(s32[46]{0:T(128)} %dynamic-slice_bitcast_fusion.refs_0_, bf16[640,512]{1,0:T(8,128)(2,1)} %get-tuple-element.60.refs_1_, bf16[640,512]{1,0:T(8,128)(2,1)} %copy-done.19, bf16[160,512]{1,0:T(8,128)(2,1)} %copy-done.26, bf16[160,512]{1,0:T(8,128)(2,1)} %copy-done.27, ...), custom_call_target="tpu_custom_call" | custom-call | flops 5000000000 | bytes 1048576 | tf_op jit(solution)/shard_map/weight_gradient/pallas_call | solution.py:329
  132.1 3.2 %collective-permute-start.33 = (bf16[80,2048]{1,0:T(8,128)(2,1)}, bf16[80,2048]{1,0:T(8,128)(2,1)S(1)}, u32[]{:S(2)}, u32[]{:S(2)}) collective-permute-start(bf16[80,2048]{1,0:T(8,128)(2,1)} %get-tuple-element.91), channel_id=1, source_target_pairs={{0,6},{1,7},{2,0},{3,1},{4,2},{5,3},{6,4},{7,5},{8,14},{9,15},{10,... | collective-permute-start | bytes 983048 | tf_op jit(solution)/shard_map/ppermute | solution.py:79
  135.3 7.9 %weight_gradient.4 = (bf16[80,2048]{1,0:T(8,128)(2,1)}, bf16[80,2048]{1,0:T(8,128)(2,1)}, bf16[80,2048]{1,0:T(8,128)(2,1)}, bf16[80,2048]{1,0:T(8,128)(2,1)}, bf...) custom-call(s32[46]{0:T(128)} %dynamic-slice_bitcast_fusion.refs_0_, bf16[640,512]{1,0:T(8,128)(2,1)} %get-tuple-element.60.refs_1_, ...), custom_call_target="tpu_custom_call" | custom-call | flops 5000000000 | bytes 1048576 | tf_op jit(solution)/shard_map/weight_gradient/pallas_call | solution.py:329
  143.2 2.7 %collective-permute-start.32 = (bf16[80,2048]{1,0:T(8,128)(2,1)}, bf16[80,2048]{1,0:T(8,128)(2,1)S(1)}, u32[]{:S(2)}, u32[]{:S(2)}) collective-permute-start(bf16[80,2048]{1,0:T(8,128)(2,1)} %get-tuple-element.89), channel_id=1, source_target_pairs={{0,6},{1,7},{2,0},{3,1},{4,2},{5,3},{6,4},{7,5},{8,14},{9,15},{10,... | collective-permute-start | bytes 983048 | tf_op jit(solution)/shard_map/ppermute | solution.py:79
  149.7 3.8 %collective-permute-done.31.refs_3_ = bf16[80,2048]{1,0:T(8,128)(2,1)S(1)} collective-permute-done((bf16[80,2048]{1,0:T(8,128)(2,1)}, bf16[80,2048]{1,0:T(8,128)(2,1)S(1)}, u32[]{:S(2)}, u32[]{:S(2)}) %collective-permute-start.31) | collective-permute-done | bytes 327712 | tf_op jit(solution)/shard_map/ppermute | solution.py:79
  153.5 6.0 %collective-permute-done.34.refs_5_ = bf16[80,2048]{1,0:T(8,128)(2,1)S(1)} collective-permute-done((bf16[80,2048]{1,0:T(8,128)(2,1)S(1)}, bf16[80,2048]{1,0:T(8,128)(2,1)S(1)}, u32[]{:S(2)}, u32[]{:S(2)}) %collective-permute-start.34) | collective-permute-done | bytes 327712 | tf_op jit(solution)/shard_map/ppermute | solution.py:79
  160.9 8.4 %adam.1 = (f32[160,2048]{1,0:T(8,128)}, f32[160,2048]{1,0:T(8,128)}, f32[160,2048]{1,0:T(8,128)}) custom-call(bf16[80,2048]{1,0:T(8,128)(2,1)} %get-tuple-element.84.refs_0_, bf16[80,2048]{1,0:T(8,128)(2,1)} %get-tuple-element.85.refs_1_, bf16[80,2048]{1,0:T(8,128)(2,1)} %copy-done.14, bf16[80,2048]{1,0:T(8,128)(2,1)} %copy-done.11, ...), custom_call_target="tpu_custom_call" | custom-call | tf_op jit(solution)/shard_map/adam/pallas_call | solution.py:379
  (122 shorter events, 35.3 us)
Async XLA Ops:
  2.1 17.9 %collective-permute-start.6 = (bf16[160,2048]{1,0:T(8,128)(2,1)S(1)}, bf16[160,2048]{1,0:T(8,128)(2,1)S(1)}, u32[]{:S(2)}, u32[]{:S(2)}) collective-permute-start(bf16[160,2048]{1,0:T(8,128)(2,1)S(1)} %bitcast_convert_fusion.refs_6_), channel_id=1, source_target_pairs={{0,2},{1,3},{2,4},{3,5},{4,6},{5,7},{6,0},{7,1},{8,10},{9,11},{10,... | collective-permute-start | bytes 1966088 | tf_op jit(solution)/shard_map/ppermute | solution.py:79
  4.3 15.8 %collective-permute-start.5 = (bf16[160,2048]{1,0:T(8,128)(2,1)S(1)}, bf16[160,2048]{1,0:T(8,128)(2,1)S(1)}, u32[]{:S(2)}, u32[]{:S(2)}) collective-permute-start(bf16[160,2048]{1,0:T(8,128)(2,1)S(1)} %bitcast_convert_fusion.refs_6_), channel_id=1, source_target_pairs={{0,6},{1,7},{2,0},{3,1},{4,2},{5,3},{6,4},{7,5},{8,14},{9,15},{10,... | collective-permute-start | bytes 1966088 | tf_op jit(solution)/shard_map/ppermute | solution.py:79
  5.8 19.8 %collective-permute-start.1 = (bf16[160,2048]{1,0:T(8,128)(2,1)S(1)}, bf16[160,2048]{1,0:T(8,128)(2,1)S(1)}, u32[]{:S(2)}, u32[]{:S(2)}) collective-permute-start(bf16[160,2048]{1,0:T(8,128)(2,1)S(1)} %bitcast.24), channel_id=1, source_target_pairs={{0,16},{16,32},{32,48},{48,64},{64,80},{80,96},{96,112},{112,0},{1... | collective-permute-start | bytes 1966088 | tf_op jit(solution)/shard_map/ppermute | solution.py:415
  9.4 62.1 %collective-permute-start = (bf16[512,2048]{1,0:T(8,128)(2,1)}, bf16[512,2048]{1,0:T(8,128)(2,1)}, u32[]{:S(2)}, u32[]{:S(2)}) collective-permute-start(bf16[512,2048]{1,0:T(8,128)(2,1)} %bitcast.11), channel_id=1, source_target_pairs={{0,8},{1,9},{2,10},{3,11},{4,12},{5,13},{6,14},{7,15},{8,0},{9,1},... | collective-permute-start | bytes 6291464 | tf_op jit(solution)/shard_map/ppermute | solution.py:79
  10.2 16.7 %collective-permute-start.8 = (bf16[160,2048]{1,0:T(8,128)(2,1)S(1)}, bf16[160,2048]{1,0:T(8,128)(2,1)S(1)}, u32[]{:S(2)}, u32[]{:S(2)}) collective-permute-start(bf16[160,2048]{1,0:T(8,128)(2,1)S(1)} %bitcast_convert_fusion.refs_6_), channel_id=1, source_target_pairs={{0,1},{1,0},{2,3},{3,2},{4,5},{5,4},{6,7},{7,6},{8,9},{9,8},{10,11... | collective-permute-start | bytes 1966088 | tf_op jit(solution)/shard_map/ppermute | solution.py:79
  20.1 16.2 %collective-permute-start.7 = (bf16[160,2048]{1,0:T(8,128)(2,1)S(1)}, bf16[160,2048]{1,0:T(8,128)(2,1)}, u32[]{:S(2)}, u32[]{:S(2)}) collective-permute-start(bf16[160,2048]{1,0:T(8,128)(2,1)S(1)} %collective-permute-done.6.refs_9_), channel_id=1, source_target_pairs={{0,2},{1,3},{2,4},{3,5},{4,6},{5,7},{6,0},{7,1},{8,10},{9,11},{10,... | collective-permute-start | bytes 1966088 | tf_op jit(solution)/shard_map/ppermute | solution.py:79
  20.1 18.4 %collective-permute-start.11 = (bf16[160,2048]{1,0:T(8,128)(2,1)S(1)}, bf16[160,2048]{1,0:T(8,128)(2,1)S(1)}, u32[]{:S(2)}, u32[]{:S(2)}) collective-permute-start(bf16[160,2048]{1,0:T(8,128)(2,1)S(1)} %collective-permute-done.6.refs_9_), channel_id=1, source_target_pairs={{0,1},{1,0},{2,3},{3,2},{4,5},{5,4},{6,7},{7,6},{8,9},{9,8},{10,11... | collective-permute-start | bytes 1966088 | tf_op jit(solution)/shard_map/ppermute | solution.py:79
  25.6 14.6 %collective-permute-start.2 = (bf16[160,2048]{1,0:T(8,128)(2,1)S(1)}, bf16[160,2048]{1,0:T(8,128)(2,1)}, u32[]{:S(2)}, u32[]{:S(2)}) collective-permute-start(bf16[160,2048]{1,0:T(8,128)(2,1)S(1)} %collective-permute-done.1.refs_6_.refs_14_), channel_id=1, source_target_pairs={{0,6},{1,7},{2,0},{3,1},{4,2},{5,3},{6,4},{7,5},{8,14},{9,15},{10,... | collective-permute-start | bytes 1966088 | tf_op jit(solution)/shard_map/ppermute | solution.py:79
  26.9 17.8 %collective-permute-start.9 = (bf16[160,2048]{1,0:T(8,128)(2,1)S(1)}, bf16[160,2048]{1,0:T(8,128)(2,1)}, u32[]{:S(2)}, u32[]{:S(2)}) collective-permute-start(bf16[160,2048]{1,0:T(8,128)(2,1)S(1)} %collective-permute-done.5.refs_7_), channel_id=1, source_target_pairs={{0,1},{1,0},{2,3},{3,2},{4,5},{5,4},{6,7},{7,6},{8,9},{9,8},{10,11... | collective-permute-start | bytes 1966088 | tf_op jit(solution)/shard_map/ppermute | solution.py:79
  36.2 11.6 %collective-permute-start.10 = (bf16[160,2048]{1,0:T(8,128)(2,1)}, bf16[160,2048]{1,0:T(8,128)(2,1)}, u32[]{:S(2)}, u32[]{:S(2)}) collective-permute-start(bf16[160,2048]{1,0:T(8,128)(2,1)} %collective-permute-done.7.refs_8_), channel_id=1, source_target_pairs={{0,1},{1,0},{2,3},{3,2},{4,5},{5,4},{6,7},{7,6},{8,9},{9,8},{10,11... | collective-permute-start | bytes 1966088 | tf_op jit(solution)/shard_map/ppermute | solution.py:79
  38.5 18.9 %collective-permute-start.4 = (bf16[160,2048]{1,0:T(8,128)(2,1)S(1)}, bf16[160,2048]{1,0:T(8,128)(2,1)}, u32[]{:S(2)}, u32[]{:S(2)}) collective-permute-start(bf16[160,2048]{1,0:T(8,128)(2,1)S(1)} %collective-permute-done.1.refs_6_.refs_14_), channel_id=1, source_target_pairs={{0,2},{1,3},{2,4},{3,5},{4,6},{5,7},{6,0},{7,1},{8,10},{9,11},{10,... | collective-permute-start | bytes 1966088 | tf_op jit(solution)/shard_map/ppermute | solution.py:79
  40.2 17.2 %collective-permute-start.3 = (bf16[160,2048]{1,0:T(8,128)(2,1)}, bf16[160,2048]{1,0:T(8,128)(2,1)}, u32[]{:S(2)}, u32[]{:S(2)}) collective-permute-start(bf16[160,2048]{1,0:T(8,128)(2,1)} %collective-permute-done.2.refs_7_.refs_15_), channel_id=1, source_target_pairs={{0,6},{1,7},{2,0},{3,1},{4,2},{5,3},{6,4},{7,5},{8,14},{9,15},{10,... | collective-permute-start | bytes 1966088 | tf_op jit(solution)/shard_map/ppermute | solution.py:79
  44.7 13.3 %collective-permute-start.12 = (bf16[160,2048]{1,0:T(8,128)(2,1)S(1)}, bf16[160,2048]{1,0:T(8,128)(2,1)S(1)}, u32[]{:S(2)}, u32[]{:S(2)}) collective-permute-start(bf16[160,2048]{1,0:T(8,128)(2,1)S(1)} %collective-permute-done.1.refs_6_.refs_14_), channel_id=1, source_target_pairs={{0,1},{1,0},{2,3},{3,2},{4,5},{5,4},{6,7},{7,6},{8,9},{9,8},{10,11... | collective-permute-start | bytes 1966088 | tf_op jit(solution)/shard_map/ppermute | solution.py:79
  58.0 54.1 %collective-permute-start.28 = (bf16[512,2048]{1,0:T(8,128)(2,1)S(1)}, bf16[512,2048]{1,0:T(8,128)(2,1)S(1)}, u32[]{:S(2)}, u32[]{:S(2)}) collective-permute-start(bf16[512,2048]{1,0:T(8,128)(2,1)S(1)} %bitcast.17), channel_id=1, source_target_pairs={{0,1},{1,0},{2,3},{3,2},{4,5},{5,4},{6,7},{7,6},{8,9},{9,8},{10,11... | collective-permute-start | bytes 6291464 | tf_op jit(solution)/shard_map/ppermute | solution.py:79
  71.5 14.8 %collective-permute-start.16 = (bf16[256,1024]{1,0:T(8,128)(2,1)}, bf16[256,1024]{1,0:T(8,128)(2,1)S(1)}, u32[]{:S(2)}, u32[]{:S(2)}) collective-permute-start(bf16[256,1024]{1,0:T(8,128)(2,1)} %get-tuple-element.56), channel_id=1, source_target_pairs={{0,8},{1,9},{2,10},{3,11},{4,12},{5,13},{6,14},{7,15},{8,0},{9,1},... | collective-permute-start | bytes 1572872 | tf_op jit(solution)/shard_map/ppermute | solution.py:79
  72.2 51.2 %collective-permute-start.24 = (bf16[512,2048]{1,0:T(8,128)(2,1)}, bf16[512,2048]{1,0:T(8,128)(2,1)S(1)}, u32[]{:S(2)}, u32[]{:S(2)}) collective-permute-start(bf16[512,2048]{1,0:T(8,128)(2,1)} %collective-permute-done.refs_2_.refs_3_.refs_5_), channel_id=1, source_target_pairs={{0,1},{1,0},{2,3},{3,2},{4,5},{5,4},{6,7},{7,6},{8,9},{9,8},{10,11... | collective-permute-start | bytes 6291464 | tf_op jit(solution)/shard_map/ppermute | solution.py:79
  84.8 11.3 %collective-permute-start.18 = (bf16[256,512]{1,0:T(8,128)(2,1)}, bf16[256,512]{1,0:T(8,128)(2,1)S(1)}, u32[]{:S(2)}, u32[]{:S(2)}) collective-permute-start(bf16[256,512]{1,0:T(8,128)(2,1)} %get-tuple-element.62), channel_id=1, source_target_pairs={{0,8},{1,9},{2,10},{3,11},{4,12},{5,13},{6,14},{7,15},{8,0},{9,1},... | collective-permute-start | bytes 786440 | tf_op jit(solution)/shard_map/ppermute | solution.py:79
  85.7 12.9 %collective-permute-start.19 = (bf16[256,512]{1,0:T(8,128)(2,1)}, bf16[256,512]{1,0:T(8,128)(2,1)S(1)}, u32[]{:S(2)}, u32[]{:S(2)}) collective-permute-start(bf16[256,512]{1,0:T(8,128)(2,1)} %get-tuple-element.63), channel_id=1, source_target_pairs={{0,8},{1,9},{2,10},{3,11},{4,12},{5,13},{6,14},{7,15},{8,0},{9,1},... | collective-permute-start | bytes 786440 | tf_op jit(solution)/shard_map/ppermute | solution.py:79
  95.3 10.9 %collective-permute-start.20 = (bf16[160,512]{1,0:T(8,128)(2,1)}, bf16[160,512]{1,0:T(8,128)(2,1)S(1)}, u32[]{:S(2)}, u32[]{:S(2)}) collective-permute-start(bf16[160,512]{1,0:T(8,128)(2,1)} %get-tuple-element.64), channel_id=1, source_target_pairs={{0,8},{1,9},{2,10},{3,11},{4,12},{5,13},{6,14},{7,15},{8,0},{9,1},... | collective-permute-start | bytes 491528 | tf_op jit(solution)/shard_map/ppermute | solution.py:79
  112.2 11.2 %collective-permute-start.17 = (bf16[640,512]{1,0:T(8,128)(2,1)S(1)}, bf16[640,512]{1,0:T(8,128)(2,1)S(1)}, u32[]{:S(2)}, u32[]{:S(2)}) collective-permute-start(bf16[640,512]{1,0:T(8,128)(2,1)S(1)} %copy-done.18), channel_id=1, source_target_pairs={{0,1},{1,0},{2,3},{3,2},{4,5},{5,4},{6,7},{7,6},{8,9},{9,8},{10,11... | collective-permute-start | bytes 1966088 | tf_op jit(solution)/shard_map/ppermute | solution.py:79
  112.5 10.8 %collective-permute-start.22 = (bf16[160,512]{1,0:T(8,128)(2,1)}, bf16[160,512]{1,0:T(8,128)(2,1)S(1)}, u32[]{:S(2)}, u32[]{:S(2)}) collective-permute-start(bf16[160,512]{1,0:T(8,128)(2,1)} %get-tuple-element.76), channel_id=1, source_target_pairs={{0,8},{1,9},{2,10},{3,11},{4,12},{5,13},{6,14},{7,15},{8,0},{9,1},... | collective-permute-start | bytes 491528 | tf_op jit(solution)/shard_map/ppermute | solution.py:79
  132.1 13.9 %collective-permute-start.33 = (bf16[80,2048]{1,0:T(8,128)(2,1)}, bf16[80,2048]{1,0:T(8,128)(2,1)S(1)}, u32[]{:S(2)}, u32[]{:S(2)}) collective-permute-start(bf16[80,2048]{1,0:T(8,128)(2,1)} %get-tuple-element.91), channel_id=1, source_target_pairs={{0,6},{1,7},{2,0},{3,1},{4,2},{5,3},{6,4},{7,5},{8,14},{9,15},{10,... | collective-permute-start | bytes 983048 | tf_op jit(solution)/shard_map/ppermute | solution.py:79
  135.3 13.2 %collective-permute-start.29 = (bf16[80,2048]{1,0:T(8,128)(2,1)}, bf16[80,2048]{1,0:T(8,128)(2,1)S(1)}, u32[]{:S(2)}, u32[]{:S(2)}) collective-permute-start(bf16[80,2048]{1,0:T(8,128)(2,1)} %get-tuple-element.87), channel_id=1, source_target_pairs={{0,2},{1,3},{2,4},{3,5},{4,6},{5,7},{6,0},{7,1},{8,10},{9,11},{10,... | collective-permute-start | bytes 983048 | tf_op jit(solution)/shard_map/ppermute | solution.py:79
  147.0 12.5 %collective-permute-start.34 = (bf16[80,2048]{1,0:T(8,128)(2,1)S(1)}, bf16[80,2048]{1,0:T(8,128)(2,1)S(1)}, u32[]{:S(2)}, u32[]{:S(2)}) collective-permute-start(bf16[80,2048]{1,0:T(8,128)(2,1)S(1)} %add_convert_fusion), channel_id=1, source_target_pairs={{0,6},{1,7},{2,0},{3,1},{4,2},{5,3},{6,4},{7,5},{8,14},{9,15},{10,... | collective-permute-start | bytes 983048 | tf_op jit(solution)/shard_map/ppermute | solution.py:79
  (40 other events, 302.1 us)

commit v7 on v6

--- a/solution.py
+++ b/solution.py
@@ -27,6 +27,8 @@
 SHARD = 160
 ROWS = 8 * SHARD
 UNIT = 32
+PART = SHARD // 2
+GATHERED = ((0, 0, SHARD), (1, 0, SHARD), (2, 0, PART), (2, PART, PART), (3, 0, SHARD))
 HALF = HD // 2
 CORE = 4 * SHARD
 EXCHANGED = 2 * HD
@@ -96,6 +98,14 @@
     return jnp.concatenate([front * cosine - back * sine, back * cosine + front * sine], axis=0)
 
 
+def split(refs, counts):
+    out, refs = [], list(refs)
+    for count in counts:
+        out.append(refs[:count])
+        refs = refs[count:]
+    return out + [refs]
+
+
 ANY = pl.BlockSpec(memory_space=pl.ANY)
 
 
@@ -110,70 +120,95 @@
             num_scalar_prefetch=1,
             grid=(1,),
             in_specs=[spec for _, spec in operands[1:]],
-            out_specs=[block(shape) for shape, _ in outs],
+            out_specs=[spec[0] if spec else block(shape) for shape, _, *spec in outs],
             scratch_shapes=scratch,
         ),
-        out_shape=[jax.ShapeDtypeStruct(shape, dtype) for shape, dtype in outs],
+        out_shape=[jax.ShapeDtypeStruct(shape, dtype) for shape, dtype, *_ in outs],
         compiler_params=params(56),
         cost_estimate=cost(microseconds),
         name=name,
     )(*[value for value, _ in operands])
 
 
-def project_kernel(jobs, groups, x_count, set_count, table, *refs):
-    refs = list(refs)
-    carried, refs = refs[0], refs[1:]
-    xs, refs = refs[:x_count], refs[x_count:]
-    cosine, sine, refs = refs[0], refs[1], refs[2:]
-    arrays, refs = refs[: 8 * set_count], refs[8 * set_count :]
-    outs, refs = refs[: len(jobs)], refs[len(jobs) :]
-    givens, refs = refs[: len(groups)], refs[len(groups) :]
-    held, sems = refs[:-1], refs[-1]
-
-    def copy(at, n):
-        rows = pl.ds(pl.multiple_of(table[AT_WEIGHT + n], SHARD), SHARD)
-        return pltpu.make_async_copy(arrays[8 * at + n], held[at].at[rows], sems.at[8 * at + n])
-
+def project_kernel(jobs, groups, x_places, set_count, table, *refs):
+    pieces = 2 * len(GATHERED)
+    (carried, cosine, sine), xs, arrays, outs, givens, (tokens, made, sems, *held) = split(
+        refs, (3, len(x_places), pieces * set_count, len(jobs), len(groups))
+    )
+    x_count = len(x_places)
+
+    def token_copy(n):
+        rows = pl.ds(x_places[n] * SEQ, SEQ)
+        return pltpu.make_async_copy(xs[n].at[rows], tokens.at[n], sems.at[n])
+
+    def weight_copy(at, n):
+        step, first, rows = GATHERED[n % len(GATHERED)]
+        row = table[AT_WEIGHT + n // len(GATHERED) * 4 + step] + first
+        place = held[at].at[pl.ds(pl.multiple_of(row, 16), rows)]
+        n += at * pieces
+        return pltpu.make_async_copy(arrays[n], place, sems.at[x_count + n])
+
+    def result_copy(job):
+        sem = sems.at[x_count + pieces * set_count + job]
+        return pltpu.make_async_copy(made.at[job], outs[job], sem)
+
+    for n in range(x_count):
+        token_copy(n).start()
     for at in range(set_count):
-        for n in range(8):
-            copy(at, n).start()
+        for n in range(pieces):
+            weight_copy(at, n).start()
+    for n in range(x_count):
+        token_copy(n).wait()
     for at in range(set_count):
-        for n in range(8):
-            copy(at, n).wait()
+        for n in range(pieces):
+            weight_copy(at, n).wait()
         for job, (x, own_set) in enumerate(jobs):
             if own_set != at:
                 continue
             for half in range(2):
-                part = dot(held[at][half * CORE : (half + 1) * CORE, :], xs[x][...], ((1,), (1,)))
+                part = dot(held[at][half * CORE : (half + 1) * CORE, :], tokens[x], ((1,), (1,)))
                 for h in range(5):
                     row = half * CORE + h * HD
                     value = rotated(part[h * HD : (h + 1) * HD], cosine[...], sine[...])
-                    outs[job][row : row + HD, :] = value.astype(BF)
+                    made[job, row : row + HD, :] = value.astype(BF)
+            result_copy(job).start()
     rows = pl.ds(pl.multiple_of(table[AT_GIVEN], EXCHANGED), EXCHANGED)
     for given, group in zip(givens, groups):
         for n, job in enumerate(group):
             lanes = slice(n * SEQ, (n + 1) * SEQ)
-            given[:, lanes] = outs[job][rows, :] if job >= 0 else carried[:, lanes]
+            given[:, lanes] = made[job, rows, :] if job >= 0 else carried[:, lanes]
+    for job in range(len(jobs)):
+        result_copy(job).wait()
 
 
 def project(table, angles, xs, sets, jobs, groups, carried=None):
     if carried is None:
         carried = jnp.zeros((16, 128), BF)
+    pieces = 2 * len(GATHERED)
     operands = [(table, None), (carried, block(carried.shape))]
-    operands += [(x, block((SEQ, D), at)) for x, at in xs]
     operands += [(value, block((HALF, SEQ))) for value in angles]
+    operands += [(x, ANY) for x, _ in xs]
     operands += [(array, ANY) for arrays in sets for array in arrays]
+    places = tuple(at for _, at in xs)
+    count = len(xs) + pieces * len(sets) + len(jobs)
     return call(
-        lambda *refs: project_kernel(jobs, groups, len(xs), len(sets), *refs),
+        lambda *refs: project_kernel(jobs, groups, places, len(sets), *refs),
         "project",
         operands,
-        [((ROWS, SEQ), BF)] * len(jobs) + [((EXCHANGED, SEQ * len(group)), BF) for group in groups],
-        [pltpu.VMEM((ROWS, D), BF)] * len(sets) + [pltpu.SemaphoreType.DMA((8 * len(sets),))],
+        [((ROWS, SEQ), BF, ANY)] * len(jobs)
+        + [((EXCHANGED, SEQ * len(group)), BF) for group in groups],
+        [
+            pltpu.VMEM((len(xs), SEQ, D), BF),
+            pltpu.VMEM((len(jobs), ROWS, SEQ), BF),
+            pltpu.SemaphoreType.DMA((count,)),
+        ]
+        + [pltpu.VMEM((ROWS, D), BF)] * len(sets),
         0.5 if len(sets) == 1 else 8.0,
     )
 
 
 SCALE = INV_ROOT * math.log2(math.e)
+SPAN = 2 * SEQ
 
 
 def softmax_parts(scores, diagonal):
@@ -269,8 +304,6 @@
 
 
 TILE = 512
-SPAN = 2 * SEQ
-PART = SHARD // 2
 
 
 def fill(table, held, grads, backs):
@@ -290,14 +323,6 @@
                 first = lanes.stop
 
 
-def split(refs, counts):
-    out, refs = [], list(refs)
-    for count in counts:
-        out.append(refs[:count])
-        refs = refs[count:]
-    return out + [refs]
-
-
 def first_kernel(counts, table, *refs):
     grads, backs, tokens, (out, held) = split(refs, counts)
 
@@ -308,20 +333,19 @@
     out[...] = dot(held[:, :SPAN], tokens[0][...]) + dot(held[:, SPAN:], tokens[1][...])
 
 
-def second_kernel(steps, counts, table, *refs):
-    grads, backs, tokens, (before, *outs, held) = split(refs, counts)
+def second_kernel(parts, counts, table, *refs):
+    grads, backs, tokens, befores, rest = split(refs, (*counts, len(parts)))
+    outs, held = rest[:-1], rest[-1]
 
     @pl.when(pl.program_id(0) == 0)
     def _():
         fill(table, held, grads, backs)
 
-    for at, step in enumerate(steps):
-        rows = pl.ds(pl.multiple_of(table[AT_STEP + step], SHARD), SHARD)
-        total = before[rows, :] + dot(held[rows, :SPAN], tokens[0][...])
+    for (step, first, _), before, out in zip(parts, befores, outs):
+        rows = pl.ds(pl.multiple_of(table[AT_STEP + step] + first, 16), PART)
+        total = before[...] + dot(held[rows, :SPAN], tokens[0][...])
         total += dot(held[rows, SPAN:], tokens[1][...])
-        total = total.astype(BF)
-        outs[2 * at][...] = total[:PART]
-        outs[2 * at + 1][...] = total[PART:]
+        out[...] = total.astype(out.dtype)
 
 
 def weight_call(kernel, table, grads, backs, tokens, more, outs, microseconds):
@@ -332,7 +356,8 @@
             num_scalar_prefetch=1,
             grid=(D // TILE,),
             in_specs=[block(value.shape) for value in grads + backs]
-            + [pl.BlockSpec((x.shape[0], TILE), tile) for x in tokens + more],
+            + [pl.BlockSpec((x.shape[0], TILE), tile) for x in tokens]
+            + [pl.BlockSpec((PART, TILE), index) for _, index in more],
             out_specs=[pl.BlockSpec((rows, TILE), tile) for rows, _ in outs],
             scratch_shapes=[pltpu.VMEM((CORE, 2 * SPAN), BF)],
         ),
@@ -340,7 +365,11 @@
         compiler_params=params(56),
         cost_estimate=cost(microseconds),
         name="weight_gradient",
-    )(table, *grads, *backs, *tokens, *more)
+    )(table, *grads, *backs, *tokens, *[value for value, _ in more])
+
+
+def part_index(step, first):
+    return lambda t, table: (table[AT_STEP + step] // PART + first // PART, t)
 
 
 def adam_kernel(a, b, c, weight, one, two, weight_out, one_out, two_out):
@@ -360,25 +389,24 @@
 
 def adam_body(*refs):
     pairs, rest = refs[:6], refs[6:]
-    half = pl.program_id(0) // (PART // ADAM_ROWS)
     for at in range(2):
 
-        @pl.when(half == at)
+        @pl.when(pl.program_id(0) == at)
         def _():
             adam_kernel(*pairs[at::2], *rest)
 
 
-ADAM_ROWS = 16
+ADAM_TILE = 1024
 
 
 def adam(pairs, weight, one, two):
-    steps = PART // ADAM_ROWS
-    straight = pl.BlockSpec((ADAM_ROWS, D), lambda k: (k, 0))
-    low = pl.BlockSpec((ADAM_ROWS, D), lambda k: (jnp.minimum(k, steps - 1), 0))
-    high = pl.BlockSpec((ADAM_ROWS, D), lambda k: (jnp.maximum(k - steps, 0), 0))
+    straight = pl.BlockSpec((PART, ADAM_TILE), lambda k, t: (k, t))
+    last = D // ADAM_TILE - 1
+    low = pl.BlockSpec((PART, ADAM_TILE), lambda k, t: (0, jnp.where(k == 0, t, last)))
+    high = pl.BlockSpec((PART, ADAM_TILE), lambda k, t: (0, jnp.where(k == 0, 0, t)))
     return pl.pallas_call(
         adam_body,
-        grid=(2 * steps,),
+        grid=(2, D // ADAM_TILE),
         in_specs=[low, high] * 3 + [straight] * 3,
         out_specs=[straight] * 3,
         out_shape=[jax.ShapeDtypeStruct((SHARD, D), F32)] * 3,
@@ -395,11 +423,10 @@
     return jnp.cos(angles), jnp.sin(angles)
 
 
-def ring_gather(shard, up_again):
-    below = send(shard, ALONG_Y[1])
-    above = send(shard, ALONG_Y[3])
-    far = send(below, ALONG_Y[1]) if up_again else send(above, ALONG_Y[3])
-    return [shard, above, far, below]
+def ring_gather(shard):
+    up, down = ALONG_Y[1], ALONG_Y[3]
+    below, above = send(shard, up), send(shard, down)
+    return [shard, above, send(below[:PART], up), send(above[PART:], down), below]
 
 
 def both_cores(pieces):
@@ -414,15 +441,13 @@
 
     teacher = lax.ppermute(snapshot[0], "blk", [(g, (g + 1) % 8) for g in range(8)])
     plane = send(own, TO_PLANE)
-    student_rows = both_cores(ring_gather(master.astype(BF), True))
-    teacher_own = ring_gather(teacher, False)
+    student_rows = both_cores(ring_gather(master.astype(BF)))
+    teacher_own = ring_gather(teacher)
 
     own_two, plane_two = [(own, 0), (own, 1)], [(plane, 0), (plane, 1)]
     two = [(0, 0), (1, 0)]
     *own_s, given = project(table, angles, own_two, [student_rows], two, [[0, 1]])
-    teacher_own[2], teacher_own[3], given = lax.optimization_barrier(
-        (teacher_own[2], teacher_own[3], given)
-    )
+    *teacher_own[2:], given = lax.optimization_barrier((*teacher_own[2:], given))
     teacher_rows = both_cores(teacher_own)
     *own_t, given = project(table, angles, own_two, [teacher_rows], two, [[-1, -1, 0, 1]], given)
     got_own = send(given, TO_PLANE)
@@ -471,27 +496,30 @@
         6.0,
     )
 
-    def weight_blocks(steps):
+    def weight_blocks(parts):
         return weight_call(
-            lambda *refs: second_kernel(steps, *refs),
+            lambda *refs: second_kernel(parts, *refs),
             table,
             [second[0], send(second[1], TO_CORE)],
             back_second,
             [plane_after, send(plane_after, TO_CORE)],
-            [before],
-            [(PART, BF)] * (2 * len(steps)),
+            [(before, part_index(step, first)) for step, first, _ in parts],
+            [(PART, dtype) for _, _, dtype in parts],
             5.0,
         )
 
     up, down = ALONG_Y[1], ALONG_Y[3]
-    far_low, far_high = weight_blocks((2,))
+    far_low, far_high, next_high, last_low = weight_blocks(
+        ((2, 0, BF), (2, PART, BF), (1, PART, BF), (3, 0, BF))
+    )
     far_low, far_high = send(far_low, up), send(far_high, down)
-    next_low, next_high, last_low, last_high, own_low, own_high = weight_blocks((1, 3, 0))
-    from_below = [None, send(next_high, up)]
-    from_above = [send(last_low, down), None]
-    from_below[0] = send((next_low.astype(F32) + far_low.astype(F32)).astype(BF), up)
-    from_above[1] = send((last_high.astype(F32) + far_high.astype(F32)).astype(BF), down)
-    pairs = [(own_low, own_high), from_below, from_above]
+    from_below, from_above = [None, send(next_high, up)], [send(last_low, down), None]
+    next_low, last_high, *own_parts = weight_blocks(
+        ((1, 0, F32), (3, PART, F32), (0, 0, F32), (0, PART, F32))
+    )
+    from_below[0] = send((next_low + far_low.astype(F32)).astype(BF), up)
+    from_above[1] = send((last_high + far_high.astype(F32)).astype(BF), down)
+    pairs = [own_parts, from_below, from_above]
     updated = adam(pairs, master, moment_one[0], moment_two[0])
     return tuple(value[None] for value in updated)
 

time: 170 us -> 181 us (1.065)
  local copies, waits for them, and re-layouts: 6.61 us -> 15.6 us
  starting transfers between devices: 40.1 us -> 42.7 us
    ppermute x1, waiting for transfers between devices: 3.89 us -> 10.5 us  [per_device(): lax.ppermute(snapshot[0], 'blk', [(g, (g + 1) % 8) for g in range(8)])]
    ppermute x34 -> x38, waiting for transfers between devices: 33.4 us -> 27.1 us  [send(): return lax.ppermute(value, 'fsdp', pairs)]
    slice x0 -> x4, local copies, waits for them, and re-layouts: none -> 4.6 us  [the longest x2 2.86 us: ring_gather(): above[PART:]]
    unnamed x58 -> x70, local copies, waits for them, and re-layouts: 4.79 us -> 9.15 us
    pallas_call x1, Pallas kernels: 8.38 us -> 5.62 us  [adam(): pl.pallas_call(adam_body, grid=(2, D // ADAM_TILE), in_specs=[low, high]...]
    pallas_call x6, Pallas kernels: 48.5 us -> 50.4 us  [call(): pl.pallas_call(kernel, grid_spec=pltpu.PrefetchScalarGridSpec(num_scalar_...]
    ppermute x34 -> x38, starting transfers between devices: 36.5 us -> 38.2 us  [send(): return lax.ppermute(value, 'fsdp', pairs)]
  transfers between devices with their start and end apart: 35 -> 39, of which waited for: 11 -> 11; matrix products, arithmetic and copies ran while one was open for 3% -> 6% of each run, Pallas kernels for 38% -> 37%
where the time goes in v7:
time: 181 us; the launch traced here: 180 us
  Pallas kernels  79.4 us (44%)
  starting transfers between devices  42.7 us (24%)
  waiting for transfers between devices  37.6 us (21%)
  local copies, waits for them, and re-layouts  15.6 us (9%)
  other arithmetic  3.64 us (2%)
    pallas_call x6, Pallas kernels, call(): pl.pallas_call(kernel, grid_spec=pltpu.PrefetchScalarGridSpec(num_scalar_...  50.4 us
    ppermute x38, starting transfers between devices, send(): return lax.ppermute(value, 'fsdp', pairs)  38.2 us
    ppermute x38, waiting for transfers between devices, send(): return lax.ppermute(value, 'fsdp', pairs)  27.1 us
    pallas_call x3, Pallas kernels, weight_call(): pl.pallas_call(lambda *refs: kernel((len(grads), len(backs), len(tokens))...  23.4 us
    ppermute x1, waiting for transfers between devices, per_device(): lax.ppermute(snapshot[0], 'blk', [(g, (g + 1) % 8) for g in range(8)])  10.5 us
    unnamed x70, local copies, waits for them, and re-layouts  9.15 us
    pallas_call x1, Pallas kernels, adam(): pl.pallas_call(adam_body, grid=(2, D // ADAM_TILE), in_specs=[low, high]...  5.62 us
    ppermute x1, starting transfers between devices, per_device(): lax.ppermute(snapshot[0], 'blk', [(g, (g + 1) % 8) for g in range(8)])  4.49 us
  transfers between devices with their start and end apart: 39, of which 11 were waited for; matrix products, arithmetic and copies ran while one was open for 6% of the time, Pallas kernels for 37%

profile of v7, /device:TPU:1, one launch (start us, length us, event | category | flops | bytes accessed | tf_op | source)
XLA Modules:
  0.0 179.9 jit_solution(1214670364985949044)
XLA Ops:
  0.6 4.5 %collective-permute-start.1 = (bf16[160,2048]{1,0:T(8,128)(2,1)}, bf16[160,2048]{1,0:T(8,128)(2,1)S(1)}, u32[]{:S(2)}, u32[]{:S(2)}) collective-permute-start(bf16[160,2048]{1,0:T(8,128)(2,1)} %bitcast.24), channel_id=1, source_target_pairs={{0,16},{16,32},{32,48},{48,64},{64,80},{80,96},{96,112},{112,0},{1... | collective-permute-start | bytes 1966088 | tf_op jit(solution)/shard_map/ppermute | solution.py:442
  11.5 10.5 %collective-permute-done.1.refs_6_.refs_16_ = bf16[160,2048]{1,0:T(8,128)(2,1)S(1)} collective-permute-done((bf16[160,2048]{1,0:T(8,128)(2,1)}, bf16[160,2048]{1,0:T(8,128)(2,1)S(1)}, u32[]{:S(2)}, u32[]{:S(2)}) %collective-permute-start.1) | collective-permute-done | bytes 655392 | tf_op jit(solution)/shard_map/ppermute | solution.py:442
  22.0 2.7 %collective-permute-start.4 = (bf16[160,2048]{1,0:T(8,128)(2,1)S(1)}, bf16[160,2048]{1,0:T(8,128)(2,1)S(1)}, u32[]{:S(2)}, u32[]{:S(2)}) collective-permute-start(bf16[160,2048]{1,0:T(8,128)(2,1)S(1)} %collective-permute-done.1.refs_6_.refs_16_), channel_id=1, source_target_pairs={{0,6},{1,7},{2,0},{3,1},{4,2},{5,3},{6,4},{7,5},{8,14},{9,15},{10,... | collective-permute-start | bytes 1966088 | tf_op jit(solution)/shard_map/ppermute | solution.py:81
  26.0 2.7 %collective-permute-start.9 = (bf16[80,2048]{1,0:T(8,128)(2,1)S(1)}, bf16[80,2048]{1,0:T(8,128)(2,1)}, u32[]{:S(2)}, u32[]{:S(2)}) collective-permute-start(bf16[80,2048]{1,0:T(8,128)(2,1)S(1)} %slice.19), channel_id=1, source_target_pairs={{0,6},{1,7},{2,0},{3,1},{4,2},{5,3},{6,4},{7,5},{8,14},{9,15},{10,... | collective-permute-start | bytes 983048 | tf_op jit(solution)/shard_map/ppermute | solution.py:81
  28.7 5.1 %collective-permute-done.8.refs_8_ = bf16[80,2048]{1,0:T(8,128)(2,1)} collective-permute-done((bf16[80,2048]{1,0:T(8,128)(2,1)S(1)}, bf16[80,2048]{1,0:T(8,128)(2,1)}, u32[]{:S(2)}, u32[]{:S(2)}) %collective-permute-start.8) | collective-permute-done | bytes 327712 | tf_op jit(solution)/shard_map/ppermute | solution.py:81
  33.8 4.6 %collective-permute-start.11 = (bf16[160,2048]{1,0:T(8,128)(2,1)}, bf16[160,2048]{1,0:T(8,128)(2,1)}, u32[]{:S(2)}, u32[]{:S(2)}) collective-permute-start(bf16[160,2048]{1,0:T(8,128)(2,1)} %collective-permute-done.6.refs_7_), channel_id=1, source_target_pairs={{0,1},{1,0},{2,3},{3,2},{4,5},{5,4},{6,7},{7,6},{8,9},{9,8},{10,11... | collective-permute-start | bytes 1966088 | tf_op jit(solution)/shard_map/ppermute | solution.py:81
  38.4 6.1 %collective-permute-done.9.refs_9_ = bf16[80,2048]{1,0:T(8,128)(2,1)} collective-permute-done((bf16[80,2048]{1,0:T(8,128)(2,1)S(1)}, bf16[80,2048]{1,0:T(8,128)(2,1)}, u32[]{:S(2)}, u32[]{:S(2)}) %collective-permute-start.9) | collective-permute-done | bytes 327712 | tf_op jit(solution)/shard_map/ppermute | solution.py:81
  48.6 2.5 %collective-permute-start.14 = (bf16[160,2048]{1,0:T(8,128)(2,1)S(1)}, bf16[160,2048]{1,0:T(8,128)(2,1)}, u32[]{:S(2)}, u32[]{:S(2)}) collective-permute-start(bf16[160,2048]{1,0:T(8,128)(2,1)S(1)} %collective-permute-done.7.refs_10_), channel_id=1, source_target_pairs={{0,1},{1,0},{2,3},{3,2},{4,5},{5,4},{6,7},{7,6},{8,9},{9,8},{10,11... | collective-permute-start | bytes 1966088 | tf_op jit(solution)/shard_map/ppermute | solution.py:81
  60.1 9.5 %project.3 = (bf16[1280,256]{1,0:T(8,128)(2,1)}, bf16[1280,256]{1,0:T(8,128)(2,1)}, bf16[256,512]{1,0:T(8,128)(2,1)}) custom-call(s32[46]{0:T(128)} %dynamic-slice_bitcast_fusion.refs_0_, bf16[16,128]{1,0:T(8,128)(2,1)} %broadcast_1_refs_1_.2.refs_1_, f32[64,256]{1,0:T(8,128)} %get-tuple-element.98.refs_2_.refs_9_.refs_5_.refs_7_, ...), custom_call_target="tpu_custom_call" | custom-call | flops 500000000 | bytes 1048576 | tf_op jit(solution)/shard_map/project/pallas_call | solution.py:117
  76.2 9.5 %project.4 = (bf16[1280,256]{1,0:T(8,128)(2,1)}, bf16[1280,256]{1,0:T(8,128)(2,1)}, bf16[256,1024]{1,0:T(8,128)(2,1)}) custom-call(s32[46]{0:T(128)} %dynamic-slice_bitcast_fusion.refs_0_, bf16[256,512]{1,0:T(8,128)(2,1)} %get-tuple-element.51.refs_1_, f32[64,256]{1,0:T(8,128)} %get-tuple-element.98.refs_2_.refs_9_.refs_5_.refs_7_, ...), custom_call_target="tpu_custom_call" | custom-call | flops 500000000 | bytes 1048576 | tf_op jit(solution)/shard_map/project/pallas_call | solution.py:117
  87.1 12.5 %project.5 = (bf16[1280,256]{1,0:T(8,128)(2,1)}, bf16[1280,256]{1,0:T(8,128)(2,1)}, bf16[1280,256]{1,0:T(8,128)(2,1)}, bf16[1280,256]{1,0:T(8,128)(2,1)}, bf16[2...) custom-call(s32[46]{0:T(128)} %dynamic-slice_bitcast_fusion.refs_0_, bf16[16,128]{1,0:T(8,128)(2,1)} %broadcast_1_refs_1_.2.refs_1_, ...), custom_call_target="tpu_custom_call" | custom-call | flops 8000000000 | bytes 1048576 | tf_op jit(solution)/shard_map/project/pallas_call | solution.py:117
  102.0 8.1 %attend.3 = (bf16[640,512]{1,0:T(8,128)(2,1)}, bf16[640,512]{1,0:T(8,128)(2,1)}, bf16[160,512]{1,0:T(8,128)(2,1)}, bf16[160,512]{1,0:T(8,128)(2,1)}) custom-call(s32[46]{0:T(128)} %dynamic-slice_bitcast_fusion.refs_0_, bf16[1280,256]{1,0:T(8,128)(2,1)} %get-tuple-element.57.refs_1_, bf16[256,1024]{1,0:T(8,128)(2,1)} %copy-done.28, ...), custom_call_target="tpu_custom_call" | custom-call | flops 8000000000 | bytes 1048576 | tf_op jit(solution)/shard_map/attend/pallas_call | solution.py:117
  110.8 2.5 %collective-permute-done.23.refs_4_.refs_6_ = bf16[256,512]{1,0:T(8,128)(2,1)S(1)} collective-permute-done((bf16[256,512]{1,0:T(8,128)(2,1)}, bf16[256,512]{1,0:T(8,128)(2,1)S(1)}, u32[]{:S(2)}, u32[]{:S(2)}) %collective-permute-start.23) | collective-permute-done | bytes 262176 | tf_op jit(solution)/shard_map/ppermute | solution.py:81
  114.0 5.2 %attend.4 = (bf16[640,256]{1,0:T(8,128)(2,1)}, bf16[640,256]{1,0:T(8,128)(2,1)}, bf16[160,256]{1,0:T(8,128)(2,1)}, bf16[160,256]{1,0:T(8,128)(2,1)}) custom-call(s32[46]{0:T(128)} %dynamic-slice_bitcast_fusion.refs_0_, bf16[1280,256]{1,0:T(8,128)(2,1)} %get-tuple-element.70.refs_1_, bf16[256,512]{1,0:T(8,128)(2,1)} %copy-done.31, ...), custom_call_target="tpu_custom_call" | custom-call | flops 4499999744 | bytes 1048576 | tf_op jit(solution)/shard_map/attend/pallas_call | solution.py:117
  121.0 5.5 %attend.5 = (bf16[640,256]{1,0:T(8,128)(2,1)}, bf16[640,256]{1,0:T(8,128)(2,1)}, bf16[160,512]{1,0:T(8,128)(2,1)}, bf16[160,512]{1,0:T(8,128)(2,1)}) custom-call(s32[46]{0:T(128)} %dynamic-slice_bitcast_fusion.refs_0_, bf16[160,256]{1,0:T(8,128)(2,1)} %get-tuple-element.72.refs_1_, bf16[160,256]{1,0:T(8,128)(2,1)} %get-tuple-element.73.refs_2_, ...), custom_call_target="tpu_custom_call" | custom-call | flops 4499999744 | bytes 1048576 | tf_op jit(solution)/shard_map/attend/pallas_call | solution.py:117
  130.0 8.0 %weight_gradient.3.refs_7_.refs_8_.refs_9_.refs_10_ = f32[640,2048]{1,0:T(8,128)} custom-call(s32[46]{0:T(128)} %dynamic-slice_bitcast_fusion.refs_0_, bf16[640,256]{1,0:T(8,128)(2,1)} %get-tuple-element.80.refs_1_, bf16[640,256]{1,0:T(8,128)(2,1)} %get-tuple-element.81.refs_2_, bf16[640,256]{1,0:T(8,128)(2,1)} %copy-done.29, bf16[640,256]{1,0:T(8,128)(2,1)} %copy-done.30, ...), custom_call_target="tpu_custom_call" | custom-call | flops 6000000000 | bytes 1048576 | tf_op jit(solution)/shard_map/weight_gradient/pallas_call | solution.py:353
  139.7 7.7 %weight_gradient.5 = (bf16[80,2048]{1,0:T(8,128)(2,1)}, bf16[80,2048]{1,0:T(8,128)(2,1)}, bf16[80,2048]{1,0:T(8,128)(2,1)}, bf16[80,2048]{1,0:T(8,128)(2,1)}) custom-call(s32[46]{0:T(128)} %dynamic-slice_bitcast_fusion.refs_0_, bf16[640,512]{1,0:T(8,128)(2,1)} %get-tuple-element.62.refs_1_, bf16[640,512]{1,0:T(8,128)(2,1)} %copy-done.3, ...), custom_call_target="tpu_custom_call" | custom-call | flops 5000000000 | bytes 1048576 | tf_op jit(solution)/shard_map/weight_gradient/pallas_call | solution.py:353
  147.4 2.2 %collective-permute-start.37 = (bf16[80,2048]{1,0:T(8,128)(2,1)}, bf16[80,2048]{1,0:T(8,128)(2,1)S(1)}, u32[]{:S(2)}, u32[]{:S(2)}) collective-permute-start(bf16[80,2048]{1,0:T(8,128)(2,1)} %get-tuple-element.93), channel_id=1, source_target_pairs={{0,6},{1,7},{2,0},{3,1},{4,2},{5,3},{6,4},{7,5},{8,14},{9,15},{10,... | collective-permute-start | bytes 983048 | tf_op jit(solution)/shard_map/ppermute | solution.py:81
  149.6 2.7 %collective-permute-start.36 = (bf16[80,2048]{1,0:T(8,128)(2,1)}, bf16[80,2048]{1,0:T(8,128)(2,1)S(1)}, u32[]{:S(2)}, u32[]{:S(2)}) collective-permute-start(bf16[80,2048]{1,0:T(8,128)(2,1)} %get-tuple-element.91), channel_id=1, source_target_pairs={{0,6},{1,7},{2,0},{3,1},{4,2},{5,3},{6,4},{7,5},{8,14},{9,15},{10,... | collective-permute-start | bytes 983048 | tf_op jit(solution)/shard_map/ppermute | solution.py:81
  152.3 7.7 %weight_gradient.4 = (f32[80,2048]{1,0:T(8,128)}, f32[80,2048]{1,0:T(8,128)}, f32[80,2048]{1,0:T(8,128)}, f32[80,2048]{1,0:T(8,128)}) custom-call(s32[46]{0:T(128)} %dynamic-slice_bitcast_fusion.refs_0_, bf16[640,512]{1,0:T(8,128)(2,1)} %get-tuple-element.62.refs_1_, bf16[640,512]{1,0:T(8,128)(2,1)} %copy-done.3, bf16[160,512]{1,0:T(8,128)(2,1)} %copy-done.10, ...), custom_call_target="tpu_custom_call" | custom-call | flops 5000000000 | bytes 1048576 | tf_op jit(solution)/shard_map/weight_gradient/pallas_call | solution.py:353
  163.0 3.7 %collective-permute-done.35.refs_3_ = bf16[80,2048]{1,0:T(8,128)(2,1)S(1)} collective-permute-done((bf16[80,2048]{1,0:T(8,128)(2,1)}, bf16[80,2048]{1,0:T(8,128)(2,1)S(1)}, u32[]{:S(2)}, u32[]{:S(2)}) %collective-permute-start.35) | collective-permute-done | bytes 327712 | tf_op jit(solution)/shard_map/ppermute | solution.py:81
  166.7 3.8 %collective-permute-done.38.refs_5_ = bf16[80,2048]{1,0:T(8,128)(2,1)S(1)} collective-permute-done((bf16[80,2048]{1,0:T(8,128)(2,1)S(1)}, bf16[80,2048]{1,0:T(8,128)(2,1)S(1)}, u32[]{:S(2)}, u32[]{:S(2)}) %collective-permute-start.38) | collective-permute-done | bytes 327712 | tf_op jit(solution)/shard_map/ppermute | solution.py:81
  170.5 3.0 %collective-permute-done.34.refs_2_ = bf16[80,2048]{1,0:T(8,128)(2,1)S(1)} collective-permute-done((bf16[80,2048]{1,0:T(8,128)(2,1)S(1)}, bf16[80,2048]{1,0:T(8,128)(2,1)S(1)}, u32[]{:S(2)}, u32[]{:S(2)}) %collective-permute-start.34) | collective-permute-done | bytes 327712 | tf_op jit(solution)/shard_map/ppermute | solution.py:81
  174.2 5.6 %adam.1 = (f32[160,2048]{1,0:T(8,128)}, f32[160,2048]{1,0:T(8,128)}, f32[160,2048]{1,0:T(8,128)}) custom-call(f32[80,2048]{1,0:T(8,128)} %get-tuple-element.86.refs_0_, f32[80,2048]{1,0:T(8,128)} %get-tuple-element.87.refs_1_, bf16[80,2048]{1,0:T(8,128)(2,1)} %copy-done.26, bf16[80,2048]{1,0:T(8,128)(2,1)} %copy-done.22, bf16[80,2048]{1,0:T(8,128)(2,1)} %copy-done.24, ...), custom_call_target="tpu_custom_call" | custom-call | tf_op jit(solution)/shard_map/adam/pallas_call | solution.py:407
  (146 shorter events, 42.8 us)
Async XLA Ops:
  0.6 21.4 %collective-permute-start.1 = (bf16[160,2048]{1,0:T(8,128)(2,1)}, bf16[160,2048]{1,0:T(8,128)(2,1)S(1)}, u32[]{:S(2)}, u32[]{:S(2)}) collective-permute-start(bf16[160,2048]{1,0:T(8,128)(2,1)} %bitcast.24), channel_id=1, source_target_pairs={{0,16},{16,32},{32,48},{48,64},{64,80},{80,96},{96,112},{112,0},{1... | collective-permute-start | bytes 1966088 | tf_op jit(solution)/shard_map/ppermute | solution.py:442
  6.5 18.2 %collective-permute-start.7 = (bf16[160,2048]{1,0:T(8,128)(2,1)S(1)}, bf16[160,2048]{1,0:T(8,128)(2,1)S(1)}, u32[]{:S(2)}, u32[]{:S(2)}) collective-permute-start(bf16[160,2048]{1,0:T(8,128)(2,1)S(1)} %bitcast_convert_fusion.refs_6_), channel_id=1, source_target_pairs={{0,2},{1,3},{2,4},{3,5},{4,6},{5,7},{6,0},{7,1},{8,10},{9,11},{10,... | collective-permute-start | bytes 1966088 | tf_op jit(solution)/shard_map/ppermute | solution.py:81
  7.9 17.0 %collective-permute-start.6 = (bf16[160,2048]{1,0:T(8,128)(2,1)S(1)}, bf16[160,2048]{1,0:T(8,128)(2,1)}, u32[]{:S(2)}, u32[]{:S(2)}) collective-permute-start(bf16[160,2048]{1,0:T(8,128)(2,1)S(1)} %bitcast_convert_fusion.refs_6_), channel_id=1, source_target_pairs={{0,6},{1,7},{2,0},{3,1},{4,2},{5,3},{6,4},{7,5},{8,14},{9,15},{10,... | collective-permute-start | bytes 1966088 | tf_op jit(solution)/shard_map/ppermute | solution.py:81
  9.4 16.6 %collective-permute-start.10 = (bf16[160,2048]{1,0:T(8,128)(2,1)S(1)}, bf16[160,2048]{1,0:T(8,128)(2,1)S(1)}, u32[]{:S(2)}, u32[]{:S(2)}) collective-permute-start(bf16[160,2048]{1,0:T(8,128)(2,1)S(1)} %bitcast_convert_fusion.refs_6_), channel_id=1, source_target_pairs={{0,1},{1,0},{2,3},{3,2},{4,5},{5,4},{6,7},{7,6},{8,9},{9,8},{10,11... | collective-permute-start | bytes 1966088 | tf_op jit(solution)/shard_map/ppermute | solution.py:81
  10.8 74.9 %collective-permute-start = (bf16[512,2048]{1,0:T(8,128)(2,1)}, bf16[512,2048]{1,0:T(8,128)(2,1)S(1)}, u32[]{:S(2)}, u32[]{:S(2)}) collective-permute-start(bf16[512,2048]{1,0:T(8,128)(2,1)} %bitcast.11), channel_id=1, source_target_pairs={{0,8},{1,9},{2,10},{3,11},{4,12},{5,13},{6,14},{7,15},{8,0},{9,1},... | collective-permute-start | bytes 6291464 | tf_op jit(solution)/shard_map/ppermute | solution.py:81
  22.0 24.7 %collective-permute-start.4 = (bf16[160,2048]{1,0:T(8,128)(2,1)S(1)}, bf16[160,2048]{1,0:T(8,128)(2,1)S(1)}, u32[]{:S(2)}, u32[]{:S(2)}) collective-permute-start(bf16[160,2048]{1,0:T(8,128)(2,1)S(1)} %collective-permute-done.1.refs_6_.refs_16_), channel_id=1, source_target_pairs={{0,6},{1,7},{2,0},{3,1},{4,2},{5,3},{6,4},{7,5},{8,14},{9,15},{10,... | collective-permute-start | bytes 1966088 | tf_op jit(solution)/shard_map/ppermute | solution.py:81
  24.9 22.9 %collective-permute-start.2 = (bf16[160,2048]{1,0:T(8,128)(2,1)S(1)}, bf16[160,2048]{1,0:T(8,128)(2,1)S(1)}, u32[]{:S(2)}, u32[]{:S(2)}) collective-permute-start(bf16[160,2048]{1,0:T(8,128)(2,1)S(1)} %collective-permute-done.1.refs_6_.refs_16_), channel_id=1, source_target_pairs={{0,2},{1,3},{2,4},{3,5},{4,6},{5,7},{6,0},{7,1},{8,10},{9,11},{10,... | collective-permute-start | bytes 1966088 | tf_op jit(solution)/shard_map/ppermute | solution.py:81
  26.0 18.5 %collective-permute-start.9 = (bf16[80,2048]{1,0:T(8,128)(2,1)S(1)}, bf16[80,2048]{1,0:T(8,128)(2,1)}, u32[]{:S(2)}, u32[]{:S(2)}) collective-permute-start(bf16[80,2048]{1,0:T(8,128)(2,1)S(1)} %slice.19), channel_id=1, source_target_pairs={{0,6},{1,7},{2,0},{3,1},{4,2},{5,3},{6,4},{7,5},{8,14},{9,15},{10,... | collective-permute-start | bytes 983048 | tf_op jit(solution)/shard_map/ppermute | solution.py:81
  33.8 22.3 %collective-permute-start.11 = (bf16[160,2048]{1,0:T(8,128)(2,1)}, bf16[160,2048]{1,0:T(8,128)(2,1)}, u32[]{:S(2)}, u32[]{:S(2)}) collective-permute-start(bf16[160,2048]{1,0:T(8,128)(2,1)} %collective-permute-done.6.refs_7_), channel_id=1, source_target_pairs={{0,1},{1,0},{2,3},{3,2},{4,5},{5,4},{6,7},{7,6},{8,9},{9,8},{10,11... | collective-permute-start | bytes 1966088 | tf_op jit(solution)/shard_map/ppermute | solution.py:81
  54.7 16.9 %collective-permute-start.15 = (bf16[160,2048]{1,0:T(8,128)(2,1)S(1)}, bf16[160,2048]{1,0:T(8,128)(2,1)S(1)}, u32[]{:S(2)}, u32[]{:S(2)}) collective-permute-start(bf16[160,2048]{1,0:T(8,128)(2,1)S(1)} %copy-done.13), channel_id=1, source_target_pairs={{0,1},{1,0},{2,3},{3,2},{4,5},{5,4},{6,7},{7,6},{8,9},{9,8},{10,11... | collective-permute-start | bytes 1966088 | tf_op jit(solution)/shard_map/ppermute | solution.py:81
  54.8 14.8 %collective-permute-start.5 = (bf16[80,2048]{1,0:T(8,128)(2,1)}, bf16[80,2048]{1,0:T(8,128)(2,1)S(1)}, u32[]{:S(2)}, u32[]{:S(2)}) collective-permute-start(bf16[80,2048]{1,0:T(8,128)(2,1)} %slice.17), channel_id=1, source_target_pairs={{0,6},{1,7},{2,0},{3,1},{4,2},{5,3},{6,4},{7,5},{8,14},{9,15},{10,... | collective-permute-start | bytes 983048 | tf_op jit(solution)/shard_map/ppermute | solution.py:81
  56.2 13.5 %collective-permute-start.3 = (bf16[80,2048]{1,0:T(8,128)(2,1)}, bf16[80,2048]{1,0:T(8,128)(2,1)S(1)}, u32[]{:S(2)}, u32[]{:S(2)}) collective-permute-start(bf16[80,2048]{1,0:T(8,128)(2,1)} %slice.16), channel_id=1, source_target_pairs={{0,2},{1,3},{2,4},{3,5},{4,6},{5,7},{6,0},{7,1},{8,10},{9,11},{10,... | collective-permute-start | bytes 983048 | tf_op jit(solution)/shard_map/ppermute | solution.py:81
  58.6 15.8 %collective-permute-start.16 = (bf16[160,2048]{1,0:T(8,128)(2,1)S(1)}, bf16[160,2048]{1,0:T(8,128)(2,1)S(1)}, u32[]{:S(2)}, u32[]{:S(2)}) collective-permute-start(bf16[160,2048]{1,0:T(8,128)(2,1)S(1)} %copy-done.7), channel_id=1, source_target_pairs={{0,1},{1,0},{2,3},{3,2},{4,5},{5,4},{6,7},{7,6},{8,9},{9,8},{10,11... | collective-permute-start | bytes 1966088 | tf_op jit(solution)/shard_map/ppermute | solution.py:81
  73.5 53.5 %collective-permute-start.32 = (bf16[512,2048]{1,0:T(8,128)(2,1)S(1)}, bf16[512,2048]{1,0:T(8,128)(2,1)}, u32[]{:S(2)}, u32[]{:S(2)}) collective-permute-start(bf16[512,2048]{1,0:T(8,128)(2,1)S(1)} %bitcast.17), channel_id=1, source_target_pairs={{0,1},{1,0},{2,3},{3,2},{4,5},{5,4},{6,7},{7,6},{8,9},{9,8},{10,11... | collective-permute-start | bytes 6291464 | tf_op jit(solution)/shard_map/ppermute | solution.py:81
  85.8 15.4 %collective-permute-start.20 = (bf16[256,1024]{1,0:T(8,128)(2,1)}, bf16[256,1024]{1,0:T(8,128)(2,1)S(1)}, u32[]{:S(2)}, u32[]{:S(2)}) collective-permute-start(bf16[256,1024]{1,0:T(8,128)(2,1)} %get-tuple-element.58), channel_id=1, source_target_pairs={{0,8},{1,9},{2,10},{3,11},{4,12},{5,13},{6,14},{7,15},{8,0},{9,1},... | collective-permute-start | bytes 1572872 | tf_op jit(solution)/shard_map/ppermute | solution.py:81
  86.4 51.7 %collective-permute-start.28 = (bf16[512,2048]{1,0:T(8,128)(2,1)S(1)}, bf16[512,2048]{1,0:T(8,128)(2,1)S(1)}, u32[]{:S(2)}, u32[]{:S(2)}) collective-permute-start(bf16[512,2048]{1,0:T(8,128)(2,1)S(1)} %collective-permute-done.refs_4_.refs_5_), channel_id=1, source_target_pairs={{0,1},{1,0},{2,3},{3,2},{4,5},{5,4},{6,7},{7,6},{8,9},{9,8},{10,11... | collective-permute-start | bytes 6291464 | tf_op jit(solution)/shard_map/ppermute | solution.py:81
  99.6 11.1 %collective-permute-start.22 = (bf16[256,512]{1,0:T(8,128)(2,1)}, bf16[256,512]{1,0:T(8,128)(2,1)S(1)}, u32[]{:S(2)}, u32[]{:S(2)}) collective-permute-start(bf16[256,512]{1,0:T(8,128)(2,1)} %get-tuple-element.64), channel_id=1, source_target_pairs={{0,8},{1,9},{2,10},{3,11},{4,12},{5,13},{6,14},{7,15},{8,0},{9,1},... | collective-permute-start | bytes 786440 | tf_op jit(solution)/shard_map/ppermute | solution.py:81
  100.3 12.9 %collective-permute-start.23 = (bf16[256,512]{1,0:T(8,128)(2,1)}, bf16[256,512]{1,0:T(8,128)(2,1)S(1)}, u32[]{:S(2)}, u32[]{:S(2)}) collective-permute-start(bf16[256,512]{1,0:T(8,128)(2,1)} %get-tuple-element.65), channel_id=1, source_target_pairs={{0,8},{1,9},{2,10},{3,11},{4,12},{5,13},{6,14},{7,15},{8,0},{9,1},... | collective-permute-start | bytes 786440 | tf_op jit(solution)/shard_map/ppermute | solution.py:81
  110.1 10.8 %collective-permute-start.24 = (bf16[160,512]{1,0:T(8,128)(2,1)}, bf16[160,512]{1,0:T(8,128)(2,1)S(1)}, u32[]{:S(2)}, u32[]{:S(2)}) collective-permute-start(bf16[160,512]{1,0:T(8,128)(2,1)} %get-tuple-element.66), channel_id=1, source_target_pairs={{0,8},{1,9},{2,10},{3,11},{4,12},{5,13},{6,14},{7,15},{8,0},{9,1},... | collective-permute-start | bytes 491528 | tf_op jit(solution)/shard_map/ppermute | solution.py:81
  127.0 11.1 %collective-permute-start.21 = (bf16[640,512]{1,0:T(8,128)(2,1)S(1)}, bf16[640,512]{1,0:T(8,128)(2,1)S(1)}, u32[]{:S(2)}, u32[]{:S(2)}) collective-permute-start(bf16[640,512]{1,0:T(8,128)(2,1)S(1)} %copy-done.27), channel_id=1, source_target_pairs={{0,1},{1,0},{2,3},{3,2},{4,5},{5,4},{6,7},{7,6},{8,9},{9,8},{10,11... | collective-permute-start | bytes 1966088 | tf_op jit(solution)/shard_map/ppermute | solution.py:81
  147.4 12.7 %collective-permute-start.37 = (bf16[80,2048]{1,0:T(8,128)(2,1)}, bf16[80,2048]{1,0:T(8,128)(2,1)S(1)}, u32[]{:S(2)}, u32[]{:S(2)}) collective-permute-start(bf16[80,2048]{1,0:T(8,128)(2,1)} %get-tuple-element.93), channel_id=1, source_target_pairs={{0,6},{1,7},{2,0},{3,1},{4,2},{5,3},{6,4},{7,5},{8,14},{9,15},{10,... | collective-permute-start | bytes 983048 | tf_op jit(solution)/shard_map/ppermute | solution.py:81
  149.6 13.2 %collective-permute-start.33 = (bf16[80,2048]{1,0:T(8,128)(2,1)}, bf16[80,2048]{1,0:T(8,128)(2,1)S(1)}, u32[]{:S(2)}, u32[]{:S(2)}) collective-permute-start(bf16[80,2048]{1,0:T(8,128)(2,1)} %get-tuple-element.89), channel_id=1, source_target_pairs={{0,2},{1,3},{2,4},{3,5},{4,6},{5,7},{6,0},{7,1},{8,10},{9,11},{10,... | collective-permute-start | bytes 983048 | tf_op jit(solution)/shard_map/ppermute | solution.py:81
  149.6 17.1 %collective-permute-start.35 = (bf16[80,2048]{1,0:T(8,128)(2,1)}, bf16[80,2048]{1,0:T(8,128)(2,1)S(1)}, u32[]{:S(2)}, u32[]{:S(2)}) collective-permute-start(bf16[80,2048]{1,0:T(8,128)(2,1)} %get-tuple-element.90), channel_id=1, source_target_pairs={{0,2},{1,3},{2,4},{3,5},{4,6},{5,7},{6,0},{7,1},{8,10},{9,11},{10,... | collective-permute-start | bytes 983048 | tf_op jit(solution)/shard_map/ppermute | solution.py:81
  149.6 17.1 %collective-permute-start.36 = (bf16[80,2048]{1,0:T(8,128)(2,1)}, bf16[80,2048]{1,0:T(8,128)(2,1)S(1)}, u32[]{:S(2)}, u32[]{:S(2)}) collective-permute-start(bf16[80,2048]{1,0:T(8,128)(2,1)} %get-tuple-element.91), channel_id=1, source_target_pairs={{0,6},{1,7},{2,0},{3,1},{4,2},{5,3},{6,4},{7,5},{8,14},{9,15},{10,... | collective-permute-start | bytes 983048 | tf_op jit(solution)/shard_map/ppermute | solution.py:81
  (50 other events, 328.0 us)

commit v8 on v6

--- a/solution.py
+++ b/solution.py
@@ -27,6 +27,7 @@
 SHARD = 160
 ROWS = 8 * SHARD
 UNIT = 32
+PART = SHARD // 2
 HALF = HD // 2
 CORE = 4 * SHARD
 EXCHANGED = 2 * HD
@@ -96,6 +97,14 @@
     return jnp.concatenate([front * cosine - back * sine, back * cosine + front * sine], axis=0)
 
 
+def split(refs, counts):
+    out, refs = [], list(refs)
+    for count in counts:
+        out.append(refs[:count])
+        refs = refs[count:]
+    return out + [refs]
+
+
 ANY = pl.BlockSpec(memory_space=pl.ANY)
 
 
@@ -110,10 +119,10 @@
             num_scalar_prefetch=1,
             grid=(1,),
             in_specs=[spec for _, spec in operands[1:]],
-            out_specs=[block(shape) for shape, _ in outs],
+            out_specs=[spec[0] if spec else block(shape) for shape, _, *spec in outs],
             scratch_shapes=scratch,
         ),
-        out_shape=[jax.ShapeDtypeStruct(shape, dtype) for shape, dtype in outs],
+        out_shape=[jax.ShapeDtypeStruct(shape, dtype) for shape, dtype, *_ in outs],
         compiler_params=params(56),
         cost_estimate=cost(microseconds),
         name=name,
@@ -174,6 +183,7 @@
 
 
 SCALE = INV_ROOT * math.log2(math.e)
+SPAN = 2 * SEQ
 
 
 def softmax_parts(scores, diagonal):
@@ -269,8 +279,6 @@
 
 
 TILE = 512
-SPAN = 2 * SEQ
-PART = SHARD // 2
 
 
 def fill(table, held, grads, backs):
@@ -290,14 +298,6 @@
                 first = lanes.stop
 
 
-def split(refs, counts):
-    out, refs = [], list(refs)
-    for count in counts:
-        out.append(refs[:count])
-        refs = refs[count:]
-    return out + [refs]
-
-
 def first_kernel(counts, table, *refs):
     grads, backs, tokens, (out, held) = split(refs, counts)
 
@@ -308,20 +308,19 @@
     out[...] = dot(held[:, :SPAN], tokens[0][...]) + dot(held[:, SPAN:], tokens[1][...])
 
 
-def second_kernel(steps, counts, table, *refs):
-    grads, backs, tokens, (before, *outs, held) = split(refs, counts)
+def second_kernel(parts, counts, table, *refs):
+    grads, backs, tokens, befores, rest = split(refs, (*counts, len(parts)))
+    outs, held = rest[:-1], rest[-1]
 
     @pl.when(pl.program_id(0) == 0)
     def _():
         fill(table, held, grads, backs)
 
-    for at, step in enumerate(steps):
-        rows = pl.ds(pl.multiple_of(table[AT_STEP + step], SHARD), SHARD)
-        total = before[rows, :] + dot(held[rows, :SPAN], tokens[0][...])
+    for (step, first, _), before, out in zip(parts, befores, outs):
+        rows = pl.ds(pl.multiple_of(table[AT_STEP + step] + first, 16), PART)
+        total = before[...] + dot(held[rows, :SPAN], tokens[0][...])
         total += dot(held[rows, SPAN:], tokens[1][...])
-        total = total.astype(BF)
-        outs[2 * at][...] = total[:PART]
-        outs[2 * at + 1][...] = total[PART:]
+        out[...] = total.astype(out.dtype)
 
 
 def weight_call(kernel, table, grads, backs, tokens, more, outs, microseconds):
@@ -332,7 +331,8 @@
             num_scalar_prefetch=1,
             grid=(D // TILE,),
             in_specs=[block(value.shape) for value in grads + backs]
-            + [pl.BlockSpec((x.shape[0], TILE), tile) for x in tokens + more],
+            + [pl.BlockSpec((x.shape[0], TILE), tile) for x in tokens]
+            + [pl.BlockSpec((PART, TILE), index) for _, index in more],
             out_specs=[pl.BlockSpec((rows, TILE), tile) for rows, _ in outs],
             scratch_shapes=[pltpu.VMEM((CORE, 2 * SPAN), BF)],
         ),
@@ -340,7 +340,11 @@
         compiler_params=params(56),
         cost_estimate=cost(microseconds),
         name="weight_gradient",
-    )(table, *grads, *backs, *tokens, *more)
+    )(table, *grads, *backs, *tokens, *[value for value, _ in more])
+
+
+def part_index(step, first):
+    return lambda t, table: (table[AT_STEP + step] // PART + first // PART, t)
 
 
 def adam_kernel(a, b, c, weight, one, two, weight_out, one_out, two_out):
@@ -360,25 +364,24 @@
 
 def adam_body(*refs):
     pairs, rest = refs[:6], refs[6:]
-    half = pl.program_id(0) // (PART // ADAM_ROWS)
     for at in range(2):
 
-        @pl.when(half == at)
+        @pl.when(pl.program_id(0) == at)
         def _():
             adam_kernel(*pairs[at::2], *rest)
 
 
-ADAM_ROWS = 16
+ADAM_TILE = 1024
 
 
 def adam(pairs, weight, one, two):
-    steps = PART // ADAM_ROWS
-    straight = pl.BlockSpec((ADAM_ROWS, D), lambda k: (k, 0))
-    low = pl.BlockSpec((ADAM_ROWS, D), lambda k: (jnp.minimum(k, steps - 1), 0))
-    high = pl.BlockSpec((ADAM_ROWS, D), lambda k: (jnp.maximum(k - steps, 0), 0))
+    straight = pl.BlockSpec((PART, ADAM_TILE), lambda k, t: (k, t))
+    last = D // ADAM_TILE - 1
+    low = pl.BlockSpec((PART, ADAM_TILE), lambda k, t: (0, jnp.where(k == 0, t, last)))
+    high = pl.BlockSpec((PART, ADAM_TILE), lambda k, t: (0, jnp.where(k == 0, 0, t)))
     return pl.pallas_call(
         adam_body,
-        grid=(2 * steps,),
+        grid=(2, D // ADAM_TILE),
         in_specs=[low, high] * 3 + [straight] * 3,
         out_specs=[straight] * 3,
         out_shape=[jax.ShapeDtypeStruct((SHARD, D), F32)] * 3,
@@ -471,27 +474,30 @@
         6.0,
     )
 
-    def weight_blocks(steps):
+    def weight_blocks(parts):
         return weight_call(
-            lambda *refs: second_kernel(steps, *refs),
+            lambda *refs: second_kernel(parts, *refs),
             table,
             [second[0], send(second[1], TO_CORE)],
             back_second,
             [plane_after, send(plane_after, TO_CORE)],
-            [before],
-            [(PART, BF)] * (2 * len(steps)),
+            [(before, part_index(step, first)) for step, first, _ in parts],
+            [(PART, dtype) for _, _, dtype in parts],
             5.0,
         )
 
     up, down = ALONG_Y[1], ALONG_Y[3]
-    far_low, far_high = weight_blocks((2,))
+    far_low, far_high, next_high, last_low = weight_blocks(
+        ((2, 0, BF), (2, PART, BF), (1, PART, BF), (3, 0, BF))
+    )
     far_low, far_high = send(far_low, up), send(far_high, down)
-    next_low, next_high, last_low, last_high, own_low, own_high = weight_blocks((1, 3, 0))
-    from_below = [None, send(next_high, up)]
-    from_above = [send(last_low, down), None]
-    from_below[0] = send((next_low.astype(F32) + far_low.astype(F32)).astype(BF), up)
-    from_above[1] = send((last_high.astype(F32) + far_high.astype(F32)).astype(BF), down)
-    pairs = [(own_low, own_high), from_below, from_above]
+    from_below, from_above = [None, send(next_high, up)], [send(last_low, down), None]
+    next_low, last_high, *own_parts = weight_blocks(
+        ((1, 0, F32), (3, PART, F32), (0, 0, F32), (0, PART, F32))
+    )
+    from_below[0] = send((next_low + far_low.astype(F32)).astype(BF), up)
+    from_above[1] = send((last_high + far_high.astype(F32)).astype(BF), down)
+    pairs = [own_parts, from_below, from_above]
     updated = adam(pairs, master, moment_one[0], moment_two[0])
     return tuple(value[None] for value in updated)
 

time: 170 us -> 168 us (0.988)
  Pallas kernels: 79.8 us -> 77.6 us
    pallas_call x1, Pallas kernels: 8.38 us -> 5.62 us  [adam(): pl.pallas_call(adam_body, grid=(2, D // ADAM_TILE), in_specs=[low, high]...]
    unnamed x58 -> x56, local copies, waits for them, and re-layouts: 4.79 us -> 5.59 us
  transfers between devices with their start and end apart: 35 -> 35, of which waited for: 11 -> 11; matrix products, arithmetic and copies ran while one was open for 3% -> 2% of each run, Pallas kernels for 38% -> 39%
where the time goes in v8:
time: 168 us; the launch traced here: 167 us
  Pallas kernels  77.6 us (46%)
  starting transfers between devices  39.8 us (24%)
  waiting for transfers between devices  37.1 us (22%)
  local copies, waits for them, and re-layouts  7.39 us (4%)
  other arithmetic  3.71 us (2%)
    pallas_call x6, Pallas kernels, call(): pl.pallas_call(kernel, grid_spec=pltpu.PrefetchScalarGridSpec(num_scalar_...  48.6 us
    ppermute x34, starting transfers between devices, send(): return lax.ppermute(value, 'fsdp', pairs)  36.3 us
    ppermute x34, waiting for transfers between devices, send(): return lax.ppermute(value, 'fsdp', pairs)  33.1 us
    pallas_call x3, Pallas kernels, weight_call(): pl.pallas_call(lambda *refs: kernel((len(grads), len(backs), len(tokens))...  23.4 us
    pallas_call x1, Pallas kernels, adam(): pl.pallas_call(adam_body, grid=(2, D // ADAM_TILE), in_specs=[low, high]...  5.62 us
    unnamed x56, local copies, waits for them, and re-layouts  5.59 us
    ppermute x1, waiting for transfers between devices, per_device(): lax.ppermute(snapshot[0], 'blk', [(g, (g + 1) % 8) for g in range(8)])  4 us
    ppermute x1, starting transfers between devices, per_device(): lax.ppermute(snapshot[0], 'blk', [(g, (g + 1) % 8) for g in range(8)])  3.6 us
  transfers between devices with their start and end apart: 35, of which 11 were waited for; matrix products, arithmetic and copies ran while one was open for 2% of the time, Pallas kernels for 39%

profile of v8, /device:TPU:1, one launch (start us, length us, event | category | flops | bytes accessed | tf_op | source)
XLA Modules:
  0.0 166.6 jit_solution(8425418866333956764)
XLA Ops:
  5.8 3.6 %collective-permute-start.1 = (bf16[160,2048]{1,0:T(8,128)(2,1)S(1)}, bf16[160,2048]{1,0:T(8,128)(2,1)}, u32[]{:S(2)}, u32[]{:S(2)}) collective-permute-start(bf16[160,2048]{1,0:T(8,128)(2,1)S(1)} %bitcast.24), channel_id=1, source_target_pairs={{0,16},{16,32},{32,48},{48,64},{64,80},{80,96},{96,112},{112,0},{1... | collective-permute-start | bytes 1966088 | tf_op jit(solution)/shard_map/ppermute | solution.py:418
  11.8 8.3 %collective-permute-done.6.refs_9_ = bf16[160,2048]{1,0:T(8,128)(2,1)S(1)} collective-permute-done((bf16[160,2048]{1,0:T(8,128)(2,1)S(1)}, bf16[160,2048]{1,0:T(8,128)(2,1)S(1)}, u32[]{:S(2)}, u32[]{:S(2)}) %collective-permute-start.6) | collective-permute-done | bytes 655392 | tf_op jit(solution)/shard_map/ppermute | solution.py:80
  21.7 4.0 %collective-permute-done.1.refs_6_.refs_14_ = bf16[160,2048]{1,0:T(8,128)(2,1)} collective-permute-done((bf16[160,2048]{1,0:T(8,128)(2,1)S(1)}, bf16[160,2048]{1,0:T(8,128)(2,1)}, u32[]{:S(2)}, u32[]{:S(2)}) %collective-permute-start.1) | collective-permute-done | bytes 655392 | tf_op jit(solution)/shard_map/ppermute | solution.py:418
  27.0 2.2 %collective-permute-start.9 = (bf16[160,2048]{1,0:T(8,128)(2,1)}, bf16[160,2048]{1,0:T(8,128)(2,1)}, u32[]{:S(2)}, u32[]{:S(2)}) collective-permute-start(bf16[160,2048]{1,0:T(8,128)(2,1)} %collective-permute-done.5.refs_7_), channel_id=1, source_target_pairs={{0,1},{1,0},{2,3},{3,2},{4,5},{5,4},{6,7},{7,6},{8,9},{9,8},{10,11... | collective-permute-start | bytes 1966088 | tf_op jit(solution)/shard_map/ppermute | solution.py:80
  29.2 7.2 %collective-permute-done.7.refs_8_ = bf16[160,2048]{1,0:T(8,128)(2,1)} collective-permute-done((bf16[160,2048]{1,0:T(8,128)(2,1)S(1)}, bf16[160,2048]{1,0:T(8,128)(2,1)}, u32[]{:S(2)}, u32[]{:S(2)}) %collective-permute-start.7) | collective-permute-done | bytes 655392 | tf_op jit(solution)/shard_map/ppermute | solution.py:80
  36.4 2.2 %collective-permute-start.10 = (bf16[160,2048]{1,0:T(8,128)(2,1)}, bf16[160,2048]{1,0:T(8,128)(2,1)}, u32[]{:S(2)}, u32[]{:S(2)}) collective-permute-start(bf16[160,2048]{1,0:T(8,128)(2,1)} %collective-permute-done.7.refs_8_), channel_id=1, source_target_pairs={{0,1},{1,0},{2,3},{3,2},{4,5},{5,4},{6,7},{7,6},{8,9},{9,8},{10,11... | collective-permute-start | bytes 1966088 | tf_op jit(solution)/shard_map/ppermute | solution.py:80
  40.5 2.3 %collective-permute-start.3 = (bf16[160,2048]{1,0:T(8,128)(2,1)}, bf16[160,2048]{1,0:T(8,128)(2,1)}, u32[]{:S(2)}, u32[]{:S(2)}) collective-permute-start(bf16[160,2048]{1,0:T(8,128)(2,1)} %collective-permute-done.2.refs_7_.refs_15_), channel_id=1, source_target_pairs={{0,6},{1,7},{2,0},{3,1},{4,2},{5,3},{6,4},{7,5},{8,14},{9,15},{10,... | collective-permute-start | bytes 1966088 | tf_op jit(solution)/shard_map/ppermute | solution.py:80
  45.0 3.1 %collective-permute-start.12 = (bf16[160,2048]{1,0:T(8,128)(2,1)}, bf16[160,2048]{1,0:T(8,128)(2,1)S(1)}, u32[]{:S(2)}, u32[]{:S(2)}) collective-permute-start(bf16[160,2048]{1,0:T(8,128)(2,1)} %collective-permute-done.1.refs_6_.refs_14_), channel_id=1, source_target_pairs={{0,1},{1,0},{2,3},{3,2},{4,5},{5,4},{6,7},{7,6},{8,9},{9,8},{10,11... | collective-permute-start | bytes 1966088 | tf_op jit(solution)/shard_map/ppermute | solution.py:80
  48.8 8.8 %project.3 = (bf16[1280,256]{1,0:T(8,128)(2,1)}, bf16[1280,256]{1,0:T(8,128)(2,1)}, bf16[256,512]{1,0:T(8,128)(2,1)}) custom-call(s32[46]{0:T(128)} %dynamic-slice_bitcast_fusion.refs_0_, bf16[16,128]{1,0:T(8,128)(2,1)} %broadcast_1_refs_1_.2.refs_1_, bf16[512,2048]{1,0:T(8,128)(2,1)} %bitcast.12, bf16[512,2048]{1,0:T(8,128)(2,1)} %bitcast.13, ...), custom_call_target="tpu_custom_call" | custom-call | flops 500000000 | bytes 1048576 | tf_op jit(solution)/shard_map/project/pallas_call | solution.py:116
  62.9 8.9 %project.4 = (bf16[1280,256]{1,0:T(8,128)(2,1)}, bf16[1280,256]{1,0:T(8,128)(2,1)}, bf16[256,1024]{1,0:T(8,128)(2,1)}) custom-call(s32[46]{0:T(128)} %dynamic-slice_bitcast_fusion.refs_0_, bf16[256,512]{1,0:T(8,128)(2,1)} %get-tuple-element.50.refs_1_, bf16[512,2048]{1,0:T(8,128)(2,1)} %bitcast.14, bf16[512,2048]{1,0:T(8,128)(2,1)} %bitcast.15, ...), custom_call_target="tpu_custom_call" | custom-call | flops 500000000 | bytes 1048576 | tf_op jit(solution)/shard_map/project/pallas_call | solution.py:116
  73.3 11.9 %project.5 = (bf16[1280,256]{1,0:T(8,128)(2,1)}, bf16[1280,256]{1,0:T(8,128)(2,1)}, bf16[1280,256]{1,0:T(8,128)(2,1)}, bf16[1280,256]{1,0:T(8,128)(2,1)}, bf16[2...) custom-call(s32[46]{0:T(128)} %dynamic-slice_bitcast_fusion.refs_0_, bf16[16,128]{1,0:T(8,128)(2,1)} %broadcast_1_refs_1_.2.refs_1_, ...), custom_call_target="tpu_custom_call" | custom-call | flops 8000000000 | bytes 1048576 | tf_op jit(solution)/shard_map/project/pallas_call | solution.py:116
  87.5 8.1 %attend.3 = (bf16[640,512]{1,0:T(8,128)(2,1)}, bf16[640,512]{1,0:T(8,128)(2,1)}, bf16[160,512]{1,0:T(8,128)(2,1)}, bf16[160,512]{1,0:T(8,128)(2,1)}) custom-call(s32[46]{0:T(128)} %dynamic-slice_bitcast_fusion.refs_0_, bf16[1280,256]{1,0:T(8,128)(2,1)} %get-tuple-element.55.refs_1_, bf16[256,1024]{1,0:T(8,128)(2,1)} %copy-done.21, ...), custom_call_target="tpu_custom_call" | custom-call | flops 8000000000 | bytes 1048576 | tf_op jit(solution)/shard_map/attend/pallas_call | solution.py:116
  96.4 2.3 %collective-permute-done.19.refs_4_.refs_6_ = bf16[256,512]{1,0:T(8,128)(2,1)S(1)} collective-permute-done((bf16[256,512]{1,0:T(8,128)(2,1)}, bf16[256,512]{1,0:T(8,128)(2,1)S(1)}, u32[]{:S(2)}, u32[]{:S(2)}) %collective-permute-start.19) | collective-permute-done | bytes 262176 | tf_op jit(solution)/shard_map/ppermute | solution.py:80
  99.5 5.2 %attend.4 = (bf16[640,256]{1,0:T(8,128)(2,1)}, bf16[640,256]{1,0:T(8,128)(2,1)}, bf16[160,256]{1,0:T(8,128)(2,1)}, bf16[160,256]{1,0:T(8,128)(2,1)}) custom-call(s32[46]{0:T(128)} %dynamic-slice_bitcast_fusion.refs_0_, bf16[1280,256]{1,0:T(8,128)(2,1)} %get-tuple-element.68.refs_1_, bf16[256,512]{1,0:T(8,128)(2,1)} %copy-done.24, ...), custom_call_target="tpu_custom_call" | custom-call | flops 4499999744 | bytes 1048576 | tf_op jit(solution)/shard_map/attend/pallas_call | solution.py:116
  106.7 5.6 %attend.5 = (bf16[640,256]{1,0:T(8,128)(2,1)}, bf16[640,256]{1,0:T(8,128)(2,1)}, bf16[160,512]{1,0:T(8,128)(2,1)}, bf16[160,512]{1,0:T(8,128)(2,1)}) custom-call(s32[46]{0:T(128)} %dynamic-slice_bitcast_fusion.refs_0_, bf16[160,256]{1,0:T(8,128)(2,1)} %get-tuple-element.70.refs_1_, bf16[160,256]{1,0:T(8,128)(2,1)} %get-tuple-element.71.refs_2_, ...), custom_call_target="tpu_custom_call" | custom-call | flops 4499999744 | bytes 1048576 | tf_op jit(solution)/shard_map/attend/pallas_call | solution.py:116
  115.7 8.0 %weight_gradient.3.refs_7_.refs_8_.refs_9_.refs_10_ = f32[640,2048]{1,0:T(8,128)} custom-call(s32[46]{0:T(128)} %dynamic-slice_bitcast_fusion.refs_0_, bf16[640,256]{1,0:T(8,128)(2,1)} %get-tuple-element.78.refs_1_, bf16[640,256]{1,0:T(8,128)(2,1)} %get-tuple-element.79.refs_2_, bf16[640,256]{1,0:T(8,128)(2,1)} %copy-done.22, bf16[640,256]{1,0:T(8,128)(2,1)} %copy-done.23, ...), custom_call_target="tpu_custom_call" | custom-call | flops 6000000000 | bytes 1048576 | tf_op jit(solution)/shard_map/weight_gradient/pallas_call | solution.py:328
  125.4 7.6 %weight_gradient.5 = (bf16[80,2048]{1,0:T(8,128)(2,1)}, bf16[80,2048]{1,0:T(8,128)(2,1)}, bf16[80,2048]{1,0:T(8,128)(2,1)}, bf16[80,2048]{1,0:T(8,128)(2,1)}) custom-call(s32[46]{0:T(128)} %dynamic-slice_bitcast_fusion.refs_0_, bf16[640,512]{1,0:T(8,128)(2,1)} %get-tuple-element.60.refs_1_, bf16[640,512]{1,0:T(8,128)(2,1)} %copy-done.3, ...), custom_call_target="tpu_custom_call" | custom-call | flops 5000000000 | bytes 1048576 | tf_op jit(solution)/shard_map/weight_gradient/pallas_call | solution.py:328
  133.1 3.3 %collective-permute-start.33 = (bf16[80,2048]{1,0:T(8,128)(2,1)}, bf16[80,2048]{1,0:T(8,128)(2,1)S(1)}, u32[]{:S(2)}, u32[]{:S(2)}) collective-permute-start(bf16[80,2048]{1,0:T(8,128)(2,1)} %get-tuple-element.91), channel_id=1, source_target_pairs={{0,6},{1,7},{2,0},{3,1},{4,2},{5,3},{6,4},{7,5},{8,14},{9,15},{10,... | collective-permute-start | bytes 983048 | tf_op jit(solution)/shard_map/ppermute | solution.py:80
  136.3 2.7 %collective-permute-start.32 = (bf16[80,2048]{1,0:T(8,128)(2,1)}, bf16[80,2048]{1,0:T(8,128)(2,1)S(1)}, u32[]{:S(2)}, u32[]{:S(2)}) collective-permute-start(bf16[80,2048]{1,0:T(8,128)(2,1)} %get-tuple-element.89), channel_id=1, source_target_pairs={{0,6},{1,7},{2,0},{3,1},{4,2},{5,3},{6,4},{7,5},{8,14},{9,15},{10,... | collective-permute-start | bytes 983048 | tf_op jit(solution)/shard_map/ppermute | solution.py:80
  139.0 7.7 %weight_gradient.4 = (f32[80,2048]{1,0:T(8,128)}, f32[80,2048]{1,0:T(8,128)}, f32[80,2048]{1,0:T(8,128)}, f32[80,2048]{1,0:T(8,128)}) custom-call(s32[46]{0:T(128)} %dynamic-slice_bitcast_fusion.refs_0_, bf16[640,512]{1,0:T(8,128)(2,1)} %get-tuple-element.60.refs_1_, bf16[640,512]{1,0:T(8,128)(2,1)} %copy-done.3, bf16[160,512]{1,0:T(8,128)(2,1)} %copy-done.5, ...), custom_call_target="tpu_custom_call" | custom-call | flops 5000000000 | bytes 1048576 | tf_op jit(solution)/shard_map/weight_gradient/pallas_call | solution.py:328
  149.7 3.7 %collective-permute-done.31.refs_3_ = bf16[80,2048]{1,0:T(8,128)(2,1)S(1)} collective-permute-done((bf16[80,2048]{1,0:T(8,128)(2,1)}, bf16[80,2048]{1,0:T(8,128)(2,1)S(1)}, u32[]{:S(2)}, u32[]{:S(2)}) %collective-permute-start.31) | collective-permute-done | bytes 327712 | tf_op jit(solution)/shard_map/ppermute | solution.py:80
  153.4 3.8 %collective-permute-done.34.refs_5_ = bf16[80,2048]{1,0:T(8,128)(2,1)S(1)} collective-permute-done((bf16[80,2048]{1,0:T(8,128)(2,1)S(1)}, bf16[80,2048]{1,0:T(8,128)(2,1)S(1)}, u32[]{:S(2)}, u32[]{:S(2)}) %collective-permute-start.34) | collective-permute-done | bytes 327712 | tf_op jit(solution)/shard_map/ppermute | solution.py:80
  157.2 3.0 %collective-permute-done.30.refs_2_ = bf16[80,2048]{1,0:T(8,128)(2,1)S(1)} collective-permute-done((bf16[80,2048]{1,0:T(8,128)(2,1)S(1)}, bf16[80,2048]{1,0:T(8,128)(2,1)S(1)}, u32[]{:S(2)}, u32[]{:S(2)}) %collective-permute-start.30) | collective-permute-done | bytes 327712 | tf_op jit(solution)/shard_map/ppermute | solution.py:80
  160.9 5.6 %adam.1 = (f32[160,2048]{1,0:T(8,128)}, f32[160,2048]{1,0:T(8,128)}, f32[160,2048]{1,0:T(8,128)}) custom-call(f32[80,2048]{1,0:T(8,128)} %get-tuple-element.84.refs_0_, f32[80,2048]{1,0:T(8,128)} %get-tuple-element.85.refs_1_, bf16[80,2048]{1,0:T(8,128)(2,1)} %copy-done.18, bf16[80,2048]{1,0:T(8,128)(2,1)} %copy-done.15, bf16[80,2048]{1,0:T(8,128)(2,1)} %copy-done.16, ...), custom_call_target="tpu_custom_call" | custom-call | tf_op jit(solution)/shard_map/adam/pallas_call | solution.py:382
  (120 shorter events, 36.4 us)
Async XLA Ops:
  2.1 18.0 %collective-permute-start.6 = (bf16[160,2048]{1,0:T(8,128)(2,1)S(1)}, bf16[160,2048]{1,0:T(8,128)(2,1)S(1)}, u32[]{:S(2)}, u32[]{:S(2)}) collective-permute-start(bf16[160,2048]{1,0:T(8,128)(2,1)S(1)} %bitcast_convert_fusion.refs_6_), channel_id=1, source_target_pairs={{0,2},{1,3},{2,4},{3,5},{4,6},{5,7},{6,0},{7,1},{8,10},{9,11},{10,... | collective-permute-start | bytes 1966088 | tf_op jit(solution)/shard_map/ppermute | solution.py:80
  4.3 15.9 %collective-permute-start.5 = (bf16[160,2048]{1,0:T(8,128)(2,1)S(1)}, bf16[160,2048]{1,0:T(8,128)(2,1)}, u32[]{:S(2)}, u32[]{:S(2)}) collective-permute-start(bf16[160,2048]{1,0:T(8,128)(2,1)S(1)} %bitcast_convert_fusion.refs_6_), channel_id=1, source_target_pairs={{0,6},{1,7},{2,0},{3,1},{4,2},{5,3},{6,4},{7,5},{8,14},{9,15},{10,... | collective-permute-start | bytes 1966088 | tf_op jit(solution)/shard_map/ppermute | solution.py:80
  5.8 19.9 %collective-permute-start.1 = (bf16[160,2048]{1,0:T(8,128)(2,1)S(1)}, bf16[160,2048]{1,0:T(8,128)(2,1)}, u32[]{:S(2)}, u32[]{:S(2)}) collective-permute-start(bf16[160,2048]{1,0:T(8,128)(2,1)S(1)} %bitcast.24), channel_id=1, source_target_pairs={{0,16},{16,32},{32,48},{48,64},{64,80},{80,96},{96,112},{112,0},{1... | collective-permute-start | bytes 1966088 | tf_op jit(solution)/shard_map/ppermute | solution.py:418
  9.4 62.4 %collective-permute-start = (bf16[512,2048]{1,0:T(8,128)(2,1)}, bf16[512,2048]{1,0:T(8,128)(2,1)S(1)}, u32[]{:S(2)}, u32[]{:S(2)}) collective-permute-start(bf16[512,2048]{1,0:T(8,128)(2,1)} %bitcast.11), channel_id=1, source_target_pairs={{0,8},{1,9},{2,10},{3,11},{4,12},{5,13},{6,14},{7,15},{8,0},{9,1},... | collective-permute-start | bytes 6291464 | tf_op jit(solution)/shard_map/ppermute | solution.py:80
  10.2 16.8 %collective-permute-start.8 = (bf16[160,2048]{1,0:T(8,128)(2,1)S(1)}, bf16[160,2048]{1,0:T(8,128)(2,1)S(1)}, u32[]{:S(2)}, u32[]{:S(2)}) collective-permute-start(bf16[160,2048]{1,0:T(8,128)(2,1)S(1)} %bitcast_convert_fusion.refs_6_), channel_id=1, source_target_pairs={{0,1},{1,0},{2,3},{3,2},{4,5},{5,4},{6,7},{7,6},{8,9},{9,8},{10,11... | collective-permute-start | bytes 1966088 | tf_op jit(solution)/shard_map/ppermute | solution.py:80
  20.2 16.3 %collective-permute-start.7 = (bf16[160,2048]{1,0:T(8,128)(2,1)S(1)}, bf16[160,2048]{1,0:T(8,128)(2,1)}, u32[]{:S(2)}, u32[]{:S(2)}) collective-permute-start(bf16[160,2048]{1,0:T(8,128)(2,1)S(1)} %collective-permute-done.6.refs_9_), channel_id=1, source_target_pairs={{0,2},{1,3},{2,4},{3,5},{4,6},{5,7},{6,0},{7,1},{8,10},{9,11},{10,... | collective-permute-start | bytes 1966088 | tf_op jit(solution)/shard_map/ppermute | solution.py:80
  20.2 18.5 %collective-permute-start.11 = (bf16[160,2048]{1,0:T(8,128)(2,1)S(1)}, bf16[160,2048]{1,0:T(8,128)(2,1)S(1)}, u32[]{:S(2)}, u32[]{:S(2)}) collective-permute-start(bf16[160,2048]{1,0:T(8,128)(2,1)S(1)} %collective-permute-done.6.refs_9_), channel_id=1, source_target_pairs={{0,1},{1,0},{2,3},{3,2},{4,5},{5,4},{6,7},{7,6},{8,9},{9,8},{10,11... | collective-permute-start | bytes 1966088 | tf_op jit(solution)/shard_map/ppermute | solution.py:80
  25.7 14.8 %collective-permute-start.2 = (bf16[160,2048]{1,0:T(8,128)(2,1)}, bf16[160,2048]{1,0:T(8,128)(2,1)}, u32[]{:S(2)}, u32[]{:S(2)}) collective-permute-start(bf16[160,2048]{1,0:T(8,128)(2,1)} %collective-permute-done.1.refs_6_.refs_14_), channel_id=1, source_target_pairs={{0,6},{1,7},{2,0},{3,1},{4,2},{5,3},{6,4},{7,5},{8,14},{9,15},{10,... | collective-permute-start | bytes 1966088 | tf_op jit(solution)/shard_map/ppermute | solution.py:80
  27.0 18.0 %collective-permute-start.9 = (bf16[160,2048]{1,0:T(8,128)(2,1)}, bf16[160,2048]{1,0:T(8,128)(2,1)}, u32[]{:S(2)}, u32[]{:S(2)}) collective-permute-start(bf16[160,2048]{1,0:T(8,128)(2,1)} %collective-permute-done.5.refs_7_), channel_id=1, source_target_pairs={{0,1},{1,0},{2,3},{3,2},{4,5},{5,4},{6,7},{7,6},{8,9},{9,8},{10,11... | collective-permute-start | bytes 1966088 | tf_op jit(solution)/shard_map/ppermute | solution.py:80
  36.4 11.7 %collective-permute-start.10 = (bf16[160,2048]{1,0:T(8,128)(2,1)}, bf16[160,2048]{1,0:T(8,128)(2,1)}, u32[]{:S(2)}, u32[]{:S(2)}) collective-permute-start(bf16[160,2048]{1,0:T(8,128)(2,1)} %collective-permute-done.7.refs_8_), channel_id=1, source_target_pairs={{0,1},{1,0},{2,3},{3,2},{4,5},{5,4},{6,7},{7,6},{8,9},{9,8},{10,11... | collective-permute-start | bytes 1966088 | tf_op jit(solution)/shard_map/ppermute | solution.py:80
  38.6 19.0 %collective-permute-start.4 = (bf16[160,2048]{1,0:T(8,128)(2,1)}, bf16[160,2048]{1,0:T(8,128)(2,1)}, u32[]{:S(2)}, u32[]{:S(2)}) collective-permute-start(bf16[160,2048]{1,0:T(8,128)(2,1)} %collective-permute-done.1.refs_6_.refs_14_), channel_id=1, source_target_pairs={{0,2},{1,3},{2,4},{3,5},{4,6},{5,7},{6,0},{7,1},{8,10},{9,11},{10,... | collective-permute-start | bytes 1966088 | tf_op jit(solution)/shard_map/ppermute | solution.py:80
  40.5 17.2 %collective-permute-start.3 = (bf16[160,2048]{1,0:T(8,128)(2,1)}, bf16[160,2048]{1,0:T(8,128)(2,1)}, u32[]{:S(2)}, u32[]{:S(2)}) collective-permute-start(bf16[160,2048]{1,0:T(8,128)(2,1)} %collective-permute-done.2.refs_7_.refs_15_), channel_id=1, source_target_pairs={{0,6},{1,7},{2,0},{3,1},{4,2},{5,3},{6,4},{7,5},{8,14},{9,15},{10,... | collective-permute-start | bytes 1966088 | tf_op jit(solution)/shard_map/ppermute | solution.py:80
  45.0 13.3 %collective-permute-start.12 = (bf16[160,2048]{1,0:T(8,128)(2,1)}, bf16[160,2048]{1,0:T(8,128)(2,1)S(1)}, u32[]{:S(2)}, u32[]{:S(2)}) collective-permute-start(bf16[160,2048]{1,0:T(8,128)(2,1)} %collective-permute-done.1.refs_6_.refs_14_), channel_id=1, source_target_pairs={{0,1},{1,0},{2,3},{3,2},{4,5},{5,4},{6,7},{7,6},{8,9},{9,8},{10,11... | collective-permute-start | bytes 1966088 | tf_op jit(solution)/shard_map/ppermute | solution.py:80
  58.3 54.5 %collective-permute-start.28 = (bf16[512,2048]{1,0:T(8,128)(2,1)S(1)}, bf16[512,2048]{1,0:T(8,128)(2,1)}, u32[]{:S(2)}, u32[]{:S(2)}) collective-permute-start(bf16[512,2048]{1,0:T(8,128)(2,1)S(1)} %bitcast.17), channel_id=1, source_target_pairs={{0,1},{1,0},{2,3},{3,2},{4,5},{5,4},{6,7},{7,6},{8,9},{9,8},{10,11... | collective-permute-start | bytes 6291464 | tf_op jit(solution)/shard_map/ppermute | solution.py:80
  71.8 14.9 %collective-permute-start.16 = (bf16[256,1024]{1,0:T(8,128)(2,1)}, bf16[256,1024]{1,0:T(8,128)(2,1)S(1)}, u32[]{:S(2)}, u32[]{:S(2)}) collective-permute-start(bf16[256,1024]{1,0:T(8,128)(2,1)} %get-tuple-element.56), channel_id=1, source_target_pairs={{0,8},{1,9},{2,10},{3,11},{4,12},{5,13},{6,14},{7,15},{8,0},{9,1},... | collective-permute-start | bytes 1572872 | tf_op jit(solution)/shard_map/ppermute | solution.py:80
  72.7 51.1 %collective-permute-start.24 = (bf16[512,2048]{1,0:T(8,128)(2,1)S(1)}, bf16[512,2048]{1,0:T(8,128)(2,1)S(1)}, u32[]{:S(2)}, u32[]{:S(2)}) collective-permute-start(bf16[512,2048]{1,0:T(8,128)(2,1)S(1)} %collective-permute-done.refs_2_.refs_3_.refs_5_), channel_id=1, source_target_pairs={{0,1},{1,0},{2,3},{3,2},{4,5},{5,4},{6,7},{7,6},{8,9},{9,8},{10,11... | collective-permute-start | bytes 6291464 | tf_op jit(solution)/shard_map/ppermute | solution.py:80
  85.2 11.2 %collective-permute-start.18 = (bf16[256,512]{1,0:T(8,128)(2,1)}, bf16[256,512]{1,0:T(8,128)(2,1)S(1)}, u32[]{:S(2)}, u32[]{:S(2)}) collective-permute-start(bf16[256,512]{1,0:T(8,128)(2,1)} %get-tuple-element.62), channel_id=1, source_target_pairs={{0,8},{1,9},{2,10},{3,11},{4,12},{5,13},{6,14},{7,15},{8,0},{9,1},... | collective-permute-start | bytes 786440 | tf_op jit(solution)/shard_map/ppermute | solution.py:80
  86.0 12.7 %collective-permute-start.19 = (bf16[256,512]{1,0:T(8,128)(2,1)}, bf16[256,512]{1,0:T(8,128)(2,1)S(1)}, u32[]{:S(2)}, u32[]{:S(2)}) collective-permute-start(bf16[256,512]{1,0:T(8,128)(2,1)} %get-tuple-element.63), channel_id=1, source_target_pairs={{0,8},{1,9},{2,10},{3,11},{4,12},{5,13},{6,14},{7,15},{8,0},{9,1},... | collective-permute-start | bytes 786440 | tf_op jit(solution)/shard_map/ppermute | solution.py:80
  95.7 11.0 %collective-permute-start.20 = (bf16[160,512]{1,0:T(8,128)(2,1)}, bf16[160,512]{1,0:T(8,128)(2,1)S(1)}, u32[]{:S(2)}, u32[]{:S(2)}) collective-permute-start(bf16[160,512]{1,0:T(8,128)(2,1)} %get-tuple-element.64), channel_id=1, source_target_pairs={{0,8},{1,9},{2,10},{3,11},{4,12},{5,13},{6,14},{7,15},{8,0},{9,1},... | collective-permute-start | bytes 491528 | tf_op jit(solution)/shard_map/ppermute | solution.py:80
  112.8 10.9 %collective-permute-start.17 = (bf16[640,512]{1,0:T(8,128)(2,1)S(1)}, bf16[640,512]{1,0:T(8,128)(2,1)S(1)}, u32[]{:S(2)}, u32[]{:S(2)}) collective-permute-start(bf16[640,512]{1,0:T(8,128)(2,1)S(1)} %copy-done.20), channel_id=1, source_target_pairs={{0,1},{1,0},{2,3},{3,2},{4,5},{5,4},{6,7},{7,6},{8,9},{9,8},{10,11... | collective-permute-start | bytes 1966088 | tf_op jit(solution)/shard_map/ppermute | solution.py:80
  133.1 13.7 %collective-permute-start.33 = (bf16[80,2048]{1,0:T(8,128)(2,1)}, bf16[80,2048]{1,0:T(8,128)(2,1)S(1)}, u32[]{:S(2)}, u32[]{:S(2)}) collective-permute-start(bf16[80,2048]{1,0:T(8,128)(2,1)} %get-tuple-element.91), channel_id=1, source_target_pairs={{0,6},{1,7},{2,0},{3,1},{4,2},{5,3},{6,4},{7,5},{8,14},{9,15},{10,... | collective-permute-start | bytes 983048 | tf_op jit(solution)/shard_map/ppermute | solution.py:80
  136.3 13.2 %collective-permute-start.29 = (bf16[80,2048]{1,0:T(8,128)(2,1)}, bf16[80,2048]{1,0:T(8,128)(2,1)S(1)}, u32[]{:S(2)}, u32[]{:S(2)}) collective-permute-start(bf16[80,2048]{1,0:T(8,128)(2,1)} %get-tuple-element.87), channel_id=1, source_target_pairs={{0,2},{1,3},{2,4},{3,5},{4,6},{5,7},{6,0},{7,1},{8,10},{9,11},{10,... | collective-permute-start | bytes 983048 | tf_op jit(solution)/shard_map/ppermute | solution.py:80
  136.3 17.1 %collective-permute-start.31 = (bf16[80,2048]{1,0:T(8,128)(2,1)}, bf16[80,2048]{1,0:T(8,128)(2,1)S(1)}, u32[]{:S(2)}, u32[]{:S(2)}) collective-permute-start(bf16[80,2048]{1,0:T(8,128)(2,1)} %get-tuple-element.88), channel_id=1, source_target_pairs={{0,2},{1,3},{2,4},{3,5},{4,6},{5,7},{6,0},{7,1},{8,10},{9,11},{10,... | collective-permute-start | bytes 983048 | tf_op jit(solution)/shard_map/ppermute | solution.py:80
  136.3 17.1 %collective-permute-start.32 = (bf16[80,2048]{1,0:T(8,128)(2,1)}, bf16[80,2048]{1,0:T(8,128)(2,1)S(1)}, u32[]{:S(2)}, u32[]{:S(2)}) collective-permute-start(bf16[80,2048]{1,0:T(8,128)(2,1)} %get-tuple-element.89), channel_id=1, source_target_pairs={{0,6},{1,7},{2,0},{3,1},{4,2},{5,3},{6,4},{7,5},{8,14},{9,15},{10,... | collective-permute-start | bytes 983048 | tf_op jit(solution)/shard_map/ppermute | solution.py:80
  (39 other events, 235.2 us)

commit v9 on v8

--- a/solution.py
+++ b/solution.py
@@ -186,45 +186,23 @@
 SPAN = 2 * SEQ
 
 
-def softmax_parts(scores, diagonal):
-    scores = scores * SCALE
-    low = scores.shape[0] - HD
-    masked = jnp.where(diagonal, scores[low:], MASKED)
-    if low:
-        scores = jnp.concatenate([scores[:low], masked], axis=0)
-    else:
-        scores = masked
+def softmax_parts(scores, causal):
+    scores = jnp.where(causal, scores * SCALE, MASKED)
     power = jnp.exp2(scores - jnp.max(scores, axis=0, keepdims=True))
     return power, (1.0 / HEADS) / jnp.sum(power, axis=0, keepdims=True)
 
 
-def side_by_side(heads, half):
-    return jnp.concatenate([q[:, half * HD : (half + 1) * HD] for q in heads], axis=1)
-
-
 def attention_gradient(student, teacher, cosine, sine):
-    key_s = student[4]
-    rows_s, rows_t = key_s.T, teacher[4].T
-    lane = lax.broadcasted_iota(jnp.int32, (HD, 4 * HD), 1) % HD
-    diagonal = lax.broadcasted_iota(jnp.int32, (HD, 4 * HD), 0) <= lane
-    query_parts, key_grad = [], None
-    for half in range(2):
-        extent = (half + 1) * HD
-        q_s = side_by_side(student[:4], half)
-        q_t = side_by_side(teacher[:4], half)
-        power_s, inverse_s = softmax_parts(dot(rows_s[:extent], q_s), diagonal)
-        power_t, inverse_t = softmax_parts(dot(rows_t[:extent], q_t), diagonal)
-        spread = (power_s * inverse_s - power_t * inverse_t).astype(BF)
-        query_parts.append(dot(key_s[:, :extent], spread))
-        part = dot(q_s, spread, ((1,), (1,)))
-        if half == 0:
-            key_grad = part
-        else:
-            key_grad = jnp.concatenate([part[:, :HD] + key_grad, part[:, HD:]], axis=1)
-    grads = [
-        jnp.concatenate([p[:, h * HD : (h + 1) * HD] for p in query_parts], axis=1)
-        for h in range(4)
-    ] + [key_grad]
+    lane = lax.broadcasted_iota(jnp.int32, (SEQ, 4 * SEQ), 1) % SEQ
+    causal = lax.broadcasted_iota(jnp.int32, (SEQ, 4 * SEQ), 0) <= lane
+    queries = jnp.concatenate(student[:4], axis=1)
+    power_s, inverse_s = softmax_parts(dot(student[4].T, queries), causal)
+    others = jnp.concatenate(teacher[:4], axis=1)
+    power_t, inverse_t = softmax_parts(dot(teacher[4].T, others), causal)
+    spread = (power_s * inverse_s - power_t * inverse_t).astype(BF)
+    query_grads = dot(student[4], spread)
+    grads = [query_grads[:, h * SEQ : (h + 1) * SEQ] for h in range(4)]
+    grads.append(dot(queries, spread, ((1,), (1,))))
     return [rotated(g * INV_ROOT, cosine, -sine).astype(BF) for g in grads]
 
 
@@ -250,14 +228,17 @@
     for n in range(8):
         row = pl.multiple_of(table[AT_CORE + n], SHARD)
         target = out if n < 4 else other
-        target[n % 4 * SHARD : (n % 4 + 1) * SHARD, :] = grads[pl.ds(row, SHARD), :]
+        lanes = slice(target.shape[1] - count * SEQ, target.shape[1])
+        target[n % 4 * SHARD : (n % 4 + 1) * SHARD, lanes] = grads[pl.ds(row, SHARD), :]
     for n in range(10):
         row = pl.multiple_of(ROWS + table[AT_BACK + n] * UNIT, UNIT)
         target = back if n < 5 else back_other
         unit = slice(n % 5 * UNIT, (n % 5 + 1) * UNIT)
         target[unit, target.shape[1] - count * SEQ :] = grads[pl.ds(row, UNIT), :]
-    for value, target in zip(carried, (back, back_other)):
-        target[:, : value.shape[1]] = value[...]
+    for value, target in zip(carried, (back, back_other, other)):
+        target[: value.shape[0], : value.shape[1]] = value[...]
+    for value in carried[3:]:
+        other[CORE:, :] = value[...]
 
 
 def attend(table, angles, sequences, carried=()):
@@ -272,13 +253,14 @@
         lambda *refs: attend_kernel(count, len(carried), *refs),
         "attend",
         operands,
-        [((CORE, count * SEQ), BF)] * 2 + [((SHARD, wide), BF)] * 2,
+        [((CORE, count * SEQ), BF), ((CORE + (SHARD if carried else 0), wide), BF)]
+        + [((SHARD, wide), BF)] * 2,
         [pltpu.VMEM((ROWS + EXCHANGED, count * SEQ), BF)] * 3,
         1.0 + 3.5 * count,
     )
 
 
-TILE = 512
+TILE = 1024
 
 
 def fill(table, held, grads, backs):
@@ -298,53 +280,39 @@
                 first = lanes.stop
 
 
-def first_kernel(counts, table, *refs):
-    grads, backs, tokens, (out, held) = split(refs, counts)
+def weight_kernel(parts, counts, table, *refs):
+    grads, backs, tokens, rest = split(refs, counts)
+    outs, held = rest[:-1], rest[-1]
 
     @pl.when(pl.program_id(0) == 0)
     def _():
         fill(table, held, grads, backs)
 
-    out[...] = dot(held[:, :SPAN], tokens[0][...]) + dot(held[:, SPAN:], tokens[1][...])
-
-
-def second_kernel(parts, counts, table, *refs):
-    grads, backs, tokens, befores, rest = split(refs, (*counts, len(parts)))
-    outs, held = rest[:-1], rest[-1]
-
-    @pl.when(pl.program_id(0) == 0)
-    def _():
-        fill(table, held, grads, backs)
-
-    for (step, first, _), before, out in zip(parts, befores, outs):
+    for (step, first, _), out in zip(parts, outs):
         rows = pl.ds(pl.multiple_of(table[AT_STEP + step] + first, 16), PART)
-        total = before[...] + dot(held[rows, :SPAN], tokens[0][...])
-        total += dot(held[rows, SPAN:], tokens[1][...])
+        total = dot(held[rows, :SPAN], tokens[0][...])
+        for n in range(1, 4):
+            total += dot(held[rows, n * SPAN : (n + 1) * SPAN], tokens[n][...])
         out[...] = total.astype(out.dtype)
 
 
-def weight_call(kernel, table, grads, backs, tokens, more, outs, microseconds):
+def weight_gradient(parts, table, grads, backs, tokens):
     tile = lambda t, table: (0, t)
     return pl.pallas_call(
-        lambda *refs: kernel((len(grads), len(backs), len(tokens)), *refs),
+        lambda *refs: weight_kernel(parts, (len(grads), len(backs), len(tokens)), *refs),
         grid_spec=pltpu.PrefetchScalarGridSpec(
             num_scalar_prefetch=1,
             grid=(D // TILE,),
-            in_specs=[block(value.shape) for value in grads + backs]
-            + [pl.BlockSpec((x.shape[0], TILE), tile) for x in tokens]
-            + [pl.BlockSpec((PART, TILE), index) for _, index in more],
-            out_specs=[pl.BlockSpec((rows, TILE), tile) for rows, _ in outs],
-            scratch_shapes=[pltpu.VMEM((CORE, 2 * SPAN), BF)],
+            in_specs=[block((rows, x.shape[1]), at) for x, rows, at in grads + backs]
+            + [pl.BlockSpec((SPAN, TILE), tile)] * 4,
+            out_specs=[pl.BlockSpec((PART, TILE), tile)] * len(parts),
+            scratch_shapes=[pltpu.VMEM((CORE, 4 * SPAN), BF)],
         ),
-        out_shape=[jax.ShapeDtypeStruct((rows, D), dtype) for rows, dtype in outs],
+        out_shape=[jax.ShapeDtypeStruct((PART, D), dtype) for _, _, dtype in parts],
         compiler_params=params(56),
-        cost_estimate=cost(microseconds),
+        cost_estimate=cost(8.0),
         name="weight_gradient",
-    )(table, *grads, *backs, *tokens, *[value for value, _ in more])
-
-
-def part_index(step, first):
-    return lambda t, table: (table[AT_STEP + step] // PART + first // PART, t)
+    )(table, *[x for x, _, _ in grads + backs], *tokens)
 
 
 def adam_kernel(a, b, c, weight, one, two, weight_out, one_out, two_out):
@@ -371,18 +339,13 @@
             adam_kernel(*pairs[at::2], *rest)
 
 
-ADAM_TILE = 1024
-
-
 def adam(pairs, weight, one, two):
-    straight = pl.BlockSpec((PART, ADAM_TILE), lambda k, t: (k, t))
-    last = D // ADAM_TILE - 1
-    low = pl.BlockSpec((PART, ADAM_TILE), lambda k, t: (0, jnp.where(k == 0, t, last)))
-    high = pl.BlockSpec((PART, ADAM_TILE), lambda k, t: (0, jnp.where(k == 0, 0, t)))
+    straight = pl.BlockSpec((PART, D), lambda k: (k, 0))
+    whole = pl.BlockSpec((PART, D), lambda k: (0, 0))
     return pl.pallas_call(
         adam_body,
-        grid=(2, D // ADAM_TILE),
-        in_specs=[low, high] * 3 + [straight] * 3,
+        grid=(2,),
+        in_specs=[whole] * 6 + [straight] * 3,
         out_specs=[straight] * 3,
         out_shape=[jax.ShapeDtypeStruct((SHARD, D), F32)] * 3,
         compiler_params=params(56),
@@ -431,60 +394,47 @@
     got_own = send(given, TO_PLANE)
     plane_after, _ = lax.optimization_barrier((plane, own_t[0]))
     plane_two = [(plane_after, 0), (plane_after, 1)]
-    *made, given_s, given_t = project(
+    *made, given_0, given_1 = project(
         table,
         angles,
         plane_two,
         [student_rows, teacher_rows],
         two + [(0, 1), (1, 1)],
-        [[0, 1], [2, 3]],
+        [[0, 2], [1, 3]],
     )
     plane_s, plane_t = made[:2], made[2:]
-    got_s, got_t = send(given_s, TO_PLANE), send(given_t, TO_PLANE)
+    got_0, got_1 = send(given_0, TO_PLANE), send(given_1, TO_PLANE)
 
     second = attend(
         table,
         angles,
         [[(plane_s[n], (got_own, n)), (plane_t[n], (got_own, 2 + n))] for n in range(2)],
     )
-    got_s, got_t, _ = lax.optimization_barrier((got_s, got_t, second[2]))
-    first = [attend(table, angles, [[(own_s[0], (got_s, 0)), (own_t[0], (got_t, 0))]])]
+    got_0, _ = lax.optimization_barrier((got_0, second[2]))
+    first = [attend(table, angles, [[(own_s[0], (got_0, 0)), (own_t[0], (got_0, 1))]])]
     back_first = [send(second[2], TO_PLANE), send(second[3], TO_PLANE)]
-    got_s, got_t, *back_first, carried = lax.optimization_barrier(
-        (got_s, got_t, *back_first, first[0][2])
-    )
-    back_first[1] = send(back_first[1], TO_CORE)
+    core_second, core_own = send(second[1], TO_CORE), send(own, TO_CORE)
+    core_plane = send(plane_after, TO_CORE)
+    got_1, *back_first, core_second, core_own, core_plane, carried = lax.optimization_barrier(
+        (got_1, *back_first, core_second, core_own, core_plane, first[0][2])
+    )
     first.append(
         attend(
             table,
             angles,
-            [[(own_s[1], (got_s, 1)), (own_t[1], (got_t, 1))]],
-            (carried, first[0][3]),
+            [[(own_s[1], (got_1, 0)), (own_t[1], (got_1, 1))]],
+            (carried, first[0][3], first[0][1], back_first[1]),
         )
     )
     back_second = [send(first[1][2], TO_PLANE), send(first[1][3], TO_BOTH)]
-    (before,) = weight_call(
-        first_kernel,
-        table,
-        [part[0] for part in first] + [send(part[1], TO_CORE) for part in first],
-        back_first,
-        [own, send(own, TO_CORE)],
-        [],
-        [(CORE, F32)],
-        6.0,
-    )
+    core_first = send(first[1][1], TO_CORE)
+    grads = [(first[0][0], CORE, 0), (first[1][0], CORE, 0), (core_first, CORE, 0)]
+    grads += [(second[0], CORE, 0), (core_second, CORE, 0)]
+    backs = [(back_first[0], SHARD, 0), (core_first, SHARD, CORE // SHARD)]
+    backs += [(value, SHARD, 0) for value in back_second]
 
     def weight_blocks(parts):
-        return weight_call(
-            lambda *refs: second_kernel(parts, *refs),
-            table,
-            [second[0], send(second[1], TO_CORE)],
-            back_second,
-            [plane_after, send(plane_after, TO_CORE)],
-            [(before, part_index(step, first)) for step, first, _ in parts],
-            [(PART, dtype) for _, _, dtype in parts],
-            5.0,
-        )
+        return weight_gradient(parts, table, grads, backs, [own, core_own, plane_after, core_plane])
 
     up, down = ALONG_Y[1], ALONG_Y[3]
     far_low, far_high, next_high, last_low = weight_blocks(

time: 168 us -> 175 us (1.042)
  waiting for transfers between devices: 37.1 us -> 48.8 us
  Pallas kernels: 77.6 us -> 75.5 us
    ppermute x34 -> x32, waiting for transfers between devices: 33.1 us -> 44.9 us  [send(): return lax.ppermute(value, 'fsdp', pairs)]
    pallas_call x4 -> x3, Pallas kernels: 29 us -> 27.4 us  [the longest x2 22.4 us: weight_gradient(): pl.pallas_call(lambda *refs: weight_kernel(parts, (len(grads), len(backs)...]
    unnamed x56 -> x58, local copies, waits for them, and re-layouts: 5.59 us -> 4.01 us
    ppermute x34 -> x32, starting transfers between devices: 36.3 us -> 35 us  [send(): return lax.ppermute(value, 'fsdp', pairs)]
  transfers between devices with their start and end apart: 35 -> 33, of which waited for: 11 -> 14; matrix products, arithmetic and copies ran while one was open for 2% -> 2% of each run, Pallas kernels for 39% -> 31%
where the time goes in v9:
time: 175 us; the launch traced here: 173 us
  Pallas kernels  75.5 us (43%)
  waiting for transfers between devices  48.8 us (28%)
  starting transfers between devices  38.6 us (22%)
  local copies, waits for them, and re-layouts  5.8 us (3%)
  other arithmetic  3.7 us (2%)
    pallas_call x6, Pallas kernels, call(): pl.pallas_call(kernel, grid_spec=pltpu.PrefetchScalarGridSpec(num_scalar_...  48.1 us
    ppermute x32, waiting for transfers between devices, send(): return lax.ppermute(value, 'fsdp', pairs)  44.9 us
    ppermute x32, starting transfers between devices, send(): return lax.ppermute(value, 'fsdp', pairs)  35 us
    pallas_call x2, Pallas kernels, weight_gradient(): pl.pallas_call(lambda *refs: weight_kernel(parts, (len(grads), len(backs)...  22.4 us
    pallas_call x1, Pallas kernels, adam(): pl.pallas_call(adam_body, grid=(2,), in_specs=[whole] * 6 + [straight] *...  4.96 us
    unnamed x58, local copies, waits for them, and re-layouts  4.01 us
    ppermute x1, waiting for transfers between devices, per_device(): lax.ppermute(snapshot[0], 'blk', [(g, (g + 1) % 8) for g in range(8)])  3.89 us
    ppermute x1, starting transfers between devices, per_device(): lax.ppermute(snapshot[0], 'blk', [(g, (g + 1) % 8) for g in range(8)])  3.6 us
  transfers between devices with their start and end apart: 33, of which 14 were waited for; matrix products, arithmetic and copies ran while one was open for 2% of the time, Pallas kernels for 31%

profile of v9, /device:TPU:1, one launch (start us, length us, event | category | flops | bytes accessed | tf_op | source)
XLA Modules:
  0.0 173.3 jit_solution(4627371288554951729)
XLA Ops:
  5.8 3.6 %collective-permute-start.8 = (bf16[160,2048]{1,0:T(8,128)(2,1)S(1)}, bf16[160,2048]{1,0:T(8,128)(2,1)S(1)}, u32[]{:S(2)}, u32[]{:S(2)}) collective-permute-start(bf16[160,2048]{1,0:T(8,128)(2,1)S(1)} %bitcast.25), channel_id=1, source_target_pairs={{0,16},{16,32},{32,48},{48,64},{64,80},{80,96},{96,112},{112,0},{1... | collective-permute-start | bytes 1966088 | tf_op jit(solution)/shard_map/ppermute | solution.py:381
  11.5 8.5 %collective-permute-done.1.refs_9_ = bf16[160,2048]{1,0:T(8,128)(2,1)S(1)} collective-permute-done((bf16[160,2048]{1,0:T(8,128)(2,1)S(1)}, bf16[160,2048]{1,0:T(8,128)(2,1)S(1)}, u32[]{:S(2)}, u32[]{:S(2)}) %collective-permute-start.1) | collective-permute-done | bytes 655392 | tf_op jit(solution)/shard_map/ppermute | solution.py:80
  21.8 3.9 %collective-permute-done.8.refs_6_.refs_14_ = bf16[160,2048]{1,0:T(8,128)(2,1)S(1)} collective-permute-done((bf16[160,2048]{1,0:T(8,128)(2,1)S(1)}, bf16[160,2048]{1,0:T(8,128)(2,1)S(1)}, u32[]{:S(2)}, u32[]{:S(2)}) %collective-permute-start.8) | collective-permute-done | bytes 655392 | tf_op jit(solution)/shard_map/ppermute | solution.py:381
  29.1 7.1 %collective-permute-done.2.refs_8_ = bf16[160,2048]{1,0:T(8,128)(2,1)} collective-permute-done((bf16[160,2048]{1,0:T(8,128)(2,1)S(1)}, bf16[160,2048]{1,0:T(8,128)(2,1)}, u32[]{:S(2)}, u32[]{:S(2)}) %collective-permute-start.2) | collective-permute-done | bytes 655392 | tf_op jit(solution)/shard_map/ppermute | solution.py:80
  36.2 2.3 %collective-permute-start.5 = (bf16[160,2048]{1,0:T(8,128)(2,1)}, bf16[160,2048]{1,0:T(8,128)(2,1)}, u32[]{:S(2)}, u32[]{:S(2)}) collective-permute-start(bf16[160,2048]{1,0:T(8,128)(2,1)} %collective-permute-done.2.refs_8_), channel_id=1, source_target_pairs={{0,1},{1,0},{2,3},{3,2},{4,5},{5,4},{6,7},{7,6},{8,9},{9,8},{10,11... | collective-permute-start | bytes 1966088 | tf_op jit(solution)/shard_map/ppermute | solution.py:80
  40.2 2.3 %collective-permute-start.10 = (bf16[160,2048]{1,0:T(8,128)(2,1)}, bf16[160,2048]{1,0:T(8,128)(2,1)}, u32[]{:S(2)}, u32[]{:S(2)}) collective-permute-start(bf16[160,2048]{1,0:T(8,128)(2,1)} %collective-permute-done.9.refs_7_.refs_15_), channel_id=1, source_target_pairs={{0,6},{1,7},{2,0},{3,1},{4,2},{5,3},{6,4},{7,5},{8,14},{9,15},{10,... | collective-permute-start | bytes 1966088 | tf_op jit(solution)/shard_map/ppermute | solution.py:80
  42.5 3.2 %collective-permute-start.12 = (bf16[160,2048]{1,0:T(8,128)(2,1)S(1)}, bf16[160,2048]{1,0:T(8,128)(2,1)S(1)}, u32[]{:S(2)}, u32[]{:S(2)}) collective-permute-start(bf16[160,2048]{1,0:T(8,128)(2,1)S(1)} %collective-permute-done.8.refs_6_.refs_14_), channel_id=1, source_target_pairs={{0,1},{1,0},{2,3},{3,2},{4,5},{5,4},{6,7},{7,6},{8,9},{9,8},{10,11... | collective-permute-start | bytes 1966088 | tf_op jit(solution)/shard_map/ppermute | solution.py:80
  48.5 8.8 %project.3 = (bf16[1280,256]{1,0:T(8,128)(2,1)}, bf16[1280,256]{1,0:T(8,128)(2,1)}, bf16[256,512]{1,0:T(8,128)(2,1)}) custom-call(s32[46]{0:T(128)} %dynamic-slice_bitcast_fusion.refs_0_, bf16[16,128]{1,0:T(8,128)(2,1)} %broadcast_1_refs_1_.2.refs_1_, bf16[512,2048]{1,0:T(8,128)(2,1)} %bitcast.12, bf16[512,2048]{1,0:T(8,128)(2,1)} %bitcast.13, ...), custom_call_target="tpu_custom_call" | custom-call | flops 500000000 | bytes 1048576 | tf_op jit(solution)/shard_map/project/pallas_call | solution.py:116
  62.6 8.9 %project.4 = (bf16[1280,256]{1,0:T(8,128)(2,1)}, bf16[1280,256]{1,0:T(8,128)(2,1)}, bf16[256,1024]{1,0:T(8,128)(2,1)}) custom-call(s32[46]{0:T(128)} %dynamic-slice_bitcast_fusion.refs_0_, bf16[256,512]{1,0:T(8,128)(2,1)} %get-tuple-element.52.refs_1_, bf16[512,2048]{1,0:T(8,128)(2,1)} %bitcast.14, bf16[512,2048]{1,0:T(8,128)(2,1)} %bitcast.15, ...), custom_call_target="tpu_custom_call" | custom-call | flops 500000000 | bytes 1048576 | tf_op jit(solution)/shard_map/project/pallas_call | solution.py:116
  72.9 11.9 %project.5 = (bf16[1280,256]{1,0:T(8,128)(2,1)}, bf16[1280,256]{1,0:T(8,128)(2,1)}, bf16[1280,256]{1,0:T(8,128)(2,1)}, bf16[1280,256]{1,0:T(8,128)(2,1)}, bf16[2...) custom-call(s32[46]{0:T(128)} %dynamic-slice_bitcast_fusion.refs_0_, bf16[16,128]{1,0:T(8,128)(2,1)} %broadcast_1_refs_1_.2.refs_1_, ...), custom_call_target="tpu_custom_call" | custom-call | flops 8000000000 | bytes 1048576 | tf_op jit(solution)/shard_map/project/pallas_call | solution.py:116
  86.5 7.9 %attend.3 = (bf16[640,512]{1,0:T(8,128)(2,1)}, bf16[640,512]{1,0:T(8,128)(2,1)}, bf16[160,512]{1,0:T(8,128)(2,1)}, bf16[160,512]{1,0:T(8,128)(2,1)}) custom-call(s32[46]{0:T(128)} %dynamic-slice_bitcast_fusion.refs_0_, bf16[1280,256]{1,0:T(8,128)(2,1)} %get-tuple-element.58.refs_1_, bf16[256,1024]{1,0:T(8,128)(2,1)} %copy-done.21, ...), custom_call_target="tpu_custom_call" | custom-call | flops 8000000000 | bytes 1048576 | tf_op jit(solution)/shard_map/attend/pallas_call | solution.py:116
  96.9 5.2 %attend.4 = (bf16[640,256]{1,0:T(8,128)(2,1)}, bf16[640,256]{1,0:T(8,128)(2,1)}, bf16[160,256]{1,0:T(8,128)(2,1)}, bf16[160,256]{1,0:T(8,128)(2,1)}) custom-call(s32[46]{0:T(128)} %dynamic-slice_bitcast_fusion.refs_0_, bf16[1280,256]{1,0:T(8,128)(2,1)} %get-tuple-element.50.refs_1_, bf16[256,512]{1,0:T(8,128)(2,1)} %copy-done.24, ...), custom_call_target="tpu_custom_call" | custom-call | flops 4499999744 | bytes 1048576 | tf_op jit(solution)/shard_map/attend/pallas_call | solution.py:116
  102.7 3.5 %collective-permute-done.19.refs_6_ = bf16[160,512]{1,0:T(8,128)(2,1)S(1)} collective-permute-done((bf16[160,512]{1,0:T(8,128)(2,1)}, bf16[160,512]{1,0:T(8,128)(2,1)S(1)}, u32[]{:S(2)}, u32[]{:S(2)}) %collective-permute-start.19) | collective-permute-done | bytes 163872 | tf_op jit(solution)/shard_map/ppermute | solution.py:80
  106.2 3.5 %collective-permute-done.20.refs_4_ = bf16[160,512]{1,0:T(8,128)(2,1)S(1)} collective-permute-done((bf16[160,512]{1,0:T(8,128)(2,1)}, bf16[160,512]{1,0:T(8,128)(2,1)S(1)}, u32[]{:S(2)}, u32[]{:S(2)}) %collective-permute-start.20) | collective-permute-done | bytes 163872 | tf_op jit(solution)/shard_map/ppermute | solution.py:80
  110.4 5.5 %attend.5 = (bf16[640,256]{1,0:T(8,128)(2,1)}, bf16[800,512]{1,0:T(8,128)(2,1)}, bf16[160,512]{1,0:T(8,128)(2,1)}, bf16[160,512]{1,0:T(8,128)(2,1)}) custom-call(s32[46]{0:T(128)} %dynamic-slice_bitcast_fusion.refs_0_, bf16[160,256]{1,0:T(8,128)(2,1)} %get-tuple-element.70.refs_1_, bf16[160,256]{1,0:T(8,128)(2,1)} %get-tuple-element.71.refs_2_, ...), custom_call_target="tpu_custom_call" | custom-call | flops 4499999744 | bytes 1048576 | tf_op jit(solution)/shard_map/attend/pallas_call | solution.py:116
  118.6 4.2 %collective-permute-done.25.refs_8_ = bf16[160,512]{1,0:T(8,128)(2,1)S(1)} collective-permute-done((bf16[160,512]{1,0:T(8,128)(2,1)}, bf16[160,512]{1,0:T(8,128)(2,1)S(1)}, u32[]{:S(2)}, u32[]{:S(2)}) %collective-permute-start.25) | collective-permute-done | bytes 163872 | tf_op jit(solution)/shard_map/ppermute | solution.py:80
  122.8 3.7 %collective-permute-done.26.refs_9_ = bf16[160,512]{1,0:T(8,128)(2,1)S(1)} collective-permute-done((bf16[160,512]{1,0:T(8,128)(2,1)}, bf16[160,512]{1,0:T(8,128)(2,1)S(1)}, u32[]{:S(2)}, u32[]{:S(2)}) %collective-permute-start.26) | collective-permute-done | bytes 163872 | tf_op jit(solution)/shard_map/ppermute | solution.py:80
  127.4 11.2 %weight_gradient.3 = (bf16[80,2048]{1,0:T(8,128)(2,1)}, bf16[80,2048]{1,0:T(8,128)(2,1)}, bf16[80,2048]{1,0:T(8,128)(2,1)}, bf16[80,2048]{1,0:T(8,128)(2,1)}) custom-call(s32[46]{0:T(128)} %dynamic-slice_bitcast_fusion.refs_0_, bf16[640,256]{1,0:T(8,128)(2,1)} %get-tuple-element.65.refs_1_, bf16[640,256]{1,0:T(8,128)(2,1)} %get-tuple-element.77.refs_2_, ...), custom_call_target="tpu_custom_call" | custom-call | flops 8000000000 | bytes 1048576 | tf_op jit(solution)/shard_map/weight_gradient/pallas_call | solution.py:301
  138.6 3.3 %collective-permute-start.31 = (bf16[80,2048]{1,0:T(8,128)(2,1)}, bf16[80,2048]{1,0:T(8,128)(2,1)S(1)}, u32[]{:S(2)}, u32[]{:S(2)}) collective-permute-start(bf16[80,2048]{1,0:T(8,128)(2,1)} %get-tuple-element.93), channel_id=1, source_target_pairs={{0,6},{1,7},{2,0},{3,1},{4,2},{5,3},{6,4},{7,5},{8,14},{9,15},{10,... | collective-permute-start | bytes 983048 | tf_op jit(solution)/shard_map/ppermute | solution.py:80
  141.9 2.7 %collective-permute-start.30 = (bf16[80,2048]{1,0:T(8,128)(2,1)}, bf16[80,2048]{1,0:T(8,128)(2,1)S(1)}, u32[]{:S(2)}, u32[]{:S(2)}) collective-permute-start(bf16[80,2048]{1,0:T(8,128)(2,1)} %get-tuple-element.91), channel_id=1, source_target_pairs={{0,6},{1,7},{2,0},{3,1},{4,2},{5,3},{6,4},{7,5},{8,14},{9,15},{10,... | collective-permute-start | bytes 983048 | tf_op jit(solution)/shard_map/ppermute | solution.py:80
  144.6 11.3 %weight_gradient.2 = (f32[80,2048]{1,0:T(8,128)}, f32[80,2048]{1,0:T(8,128)}, f32[80,2048]{1,0:T(8,128)}, f32[80,2048]{1,0:T(8,128)}) custom-call(s32[46]{0:T(128)} %dynamic-slice_bitcast_fusion.refs_0_, bf16[640,256]{1,0:T(8,128)(2,1)} %get-tuple-element.65.refs_1_, bf16[640,256]{1,0:T(8,128)(2,1)} %get-tuple-element.77.refs_2_, ...), custom_call_target="tpu_custom_call" | custom-call | flops 8000000000 | bytes 1048576 | tf_op jit(solution)/shard_map/weight_gradient/pallas_call | solution.py:301
  159.2 6.2 %collective-permute-done.32.refs_5_ = bf16[80,2048]{1,0:T(8,128)(2,1)S(1)} collective-permute-done((bf16[80,2048]{1,0:T(8,128)(2,1)S(1)}, bf16[80,2048]{1,0:T(8,128)(2,1)S(1)}, u32[]{:S(2)}, u32[]{:S(2)}) %collective-permute-start.32) | collective-permute-done | bytes 327712 | tf_op jit(solution)/shard_map/ppermute | solution.py:80
  165.4 2.2 %collective-permute-done.28.refs_2_ = bf16[80,2048]{1,0:T(8,128)(2,1)S(1)} collective-permute-done((bf16[80,2048]{1,0:T(8,128)(2,1)S(1)}, bf16[80,2048]{1,0:T(8,128)(2,1)S(1)}, u32[]{:S(2)}, u32[]{:S(2)}) %collective-permute-start.28) | collective-permute-done | bytes 327712 | tf_op jit(solution)/shard_map/ppermute | solution.py:80
  168.3 5.0 %adam.1 = (f32[160,2048]{1,0:T(8,128)}, f32[160,2048]{1,0:T(8,128)}, f32[160,2048]{1,0:T(8,128)}) custom-call(f32[80,2048]{1,0:T(8,128)} %get-tuple-element.86.refs_0_, f32[80,2048]{1,0:T(8,128)} %get-tuple-element.87.refs_1_, bf16[80,2048]{1,0:T(8,128)(2,1)} %copy-done.15, bf16[80,2048]{1,0:T(8,128)(2,1)} %copy-done.12, bf16[80,2048]{1,0:T(8,128)(2,1)} %copy-done.13, ...), custom_call_target="tpu_custom_call" | custom-call | tf_op jit(solution)/shard_map/adam/pallas_call | solution.py:345
  (117 shorter events, 36.6 us)
Async XLA Ops:
  2.1 17.9 %collective-permute-start.1 = (bf16[160,2048]{1,0:T(8,128)(2,1)S(1)}, bf16[160,2048]{1,0:T(8,128)(2,1)S(1)}, u32[]{:S(2)}, u32[]{:S(2)}) collective-permute-start(bf16[160,2048]{1,0:T(8,128)(2,1)S(1)} %bitcast_convert_fusion.refs_6_), channel_id=1, source_target_pairs={{0,2},{1,3},{2,4},{3,5},{4,6},{5,7},{6,0},{7,1},{8,10},{9,11},{10,... | collective-permute-start | bytes 1966088 | tf_op jit(solution)/shard_map/ppermute | solution.py:80
  4.3 15.8 %collective-permute-start = (bf16[160,2048]{1,0:T(8,128)(2,1)S(1)}, bf16[160,2048]{1,0:T(8,128)(2,1)S(1)}, u32[]{:S(2)}, u32[]{:S(2)}) collective-permute-start(bf16[160,2048]{1,0:T(8,128)(2,1)S(1)} %bitcast_convert_fusion.refs_6_), channel_id=1, source_target_pairs={{0,6},{1,7},{2,0},{3,1},{4,2},{5,3},{6,4},{7,5},{8,14},{9,15},{10,... | collective-permute-start | bytes 1966088 | tf_op jit(solution)/shard_map/ppermute | solution.py:80
  5.8 19.8 %collective-permute-start.8 = (bf16[160,2048]{1,0:T(8,128)(2,1)S(1)}, bf16[160,2048]{1,0:T(8,128)(2,1)S(1)}, u32[]{:S(2)}, u32[]{:S(2)}) collective-permute-start(bf16[160,2048]{1,0:T(8,128)(2,1)S(1)} %bitcast.25), channel_id=1, source_target_pairs={{0,16},{16,32},{32,48},{48,64},{64,80},{80,96},{96,112},{112,0},{1... | collective-permute-start | bytes 1966088 | tf_op jit(solution)/shard_map/ppermute | solution.py:381
  9.4 17.4 %collective-permute-start.3 = (bf16[160,2048]{1,0:T(8,128)(2,1)S(1)}, bf16[160,2048]{1,0:T(8,128)(2,1)S(1)}, u32[]{:S(2)}, u32[]{:S(2)}) collective-permute-start(bf16[160,2048]{1,0:T(8,128)(2,1)S(1)} %bitcast_convert_fusion.refs_6_), channel_id=1, source_target_pairs={{0,1},{1,0},{2,3},{3,2},{4,5},{5,4},{6,7},{7,6},{8,9},{9,8},{10,11... | collective-permute-start | bytes 1966088 | tf_op jit(solution)/shard_map/ppermute | solution.py:80
  10.8 60.7 %collective-permute-start.7 = (bf16[512,2048]{1,0:T(8,128)(2,1)}, bf16[512,2048]{1,0:T(8,128)(2,1)}, u32[]{:S(2)}, u32[]{:S(2)}) collective-permute-start(bf16[512,2048]{1,0:T(8,128)(2,1)} %bitcast.11), channel_id=1, source_target_pairs={{0,8},{1,9},{2,10},{3,11},{4,12},{5,13},{6,14},{7,15},{8,0},{9,1},... | collective-permute-start | bytes 6291464 | tf_op jit(solution)/shard_map/ppermute | solution.py:80
  20.1 16.2 %collective-permute-start.2 = (bf16[160,2048]{1,0:T(8,128)(2,1)S(1)}, bf16[160,2048]{1,0:T(8,128)(2,1)}, u32[]{:S(2)}, u32[]{:S(2)}) collective-permute-start(bf16[160,2048]{1,0:T(8,128)(2,1)S(1)} %collective-permute-done.1.refs_9_), channel_id=1, source_target_pairs={{0,2},{1,3},{2,4},{3,5},{4,6},{5,7},{6,0},{7,1},{8,10},{9,11},{10,... | collective-permute-start | bytes 1966088 | tf_op jit(solution)/shard_map/ppermute | solution.py:80
  20.1 18.4 %collective-permute-start.6 = (bf16[160,2048]{1,0:T(8,128)(2,1)S(1)}, bf16[160,2048]{1,0:T(8,128)(2,1)S(1)}, u32[]{:S(2)}, u32[]{:S(2)}) collective-permute-start(bf16[160,2048]{1,0:T(8,128)(2,1)S(1)} %collective-permute-done.1.refs_9_), channel_id=1, source_target_pairs={{0,1},{1,0},{2,3},{3,2},{4,5},{5,4},{6,7},{7,6},{8,9},{9,8},{10,11... | collective-permute-start | bytes 1966088 | tf_op jit(solution)/shard_map/ppermute | solution.py:80
  25.6 14.6 %collective-permute-start.9 = (bf16[160,2048]{1,0:T(8,128)(2,1)S(1)}, bf16[160,2048]{1,0:T(8,128)(2,1)}, u32[]{:S(2)}, u32[]{:S(2)}) collective-permute-start(bf16[160,2048]{1,0:T(8,128)(2,1)S(1)} %collective-permute-done.8.refs_6_.refs_14_), channel_id=1, source_target_pairs={{0,6},{1,7},{2,0},{3,1},{4,2},{5,3},{6,4},{7,5},{8,14},{9,15},{10,... | collective-permute-start | bytes 1966088 | tf_op jit(solution)/shard_map/ppermute | solution.py:80
  26.9 15.6 %collective-permute-start.4 = (bf16[160,2048]{1,0:T(8,128)(2,1)S(1)}, bf16[160,2048]{1,0:T(8,128)(2,1)}, u32[]{:S(2)}, u32[]{:S(2)}) collective-permute-start(bf16[160,2048]{1,0:T(8,128)(2,1)S(1)} %collective-permute-done.refs_7_), channel_id=1, source_target_pairs={{0,1},{1,0},{2,3},{3,2},{4,5},{5,4},{6,7},{7,6},{8,9},{9,8},{10,11... | collective-permute-start | bytes 1966088 | tf_op jit(solution)/shard_map/ppermute | solution.py:80
  36.2 11.7 %collective-permute-start.5 = (bf16[160,2048]{1,0:T(8,128)(2,1)}, bf16[160,2048]{1,0:T(8,128)(2,1)}, u32[]{:S(2)}, u32[]{:S(2)}) collective-permute-start(bf16[160,2048]{1,0:T(8,128)(2,1)} %collective-permute-done.2.refs_8_), channel_id=1, source_target_pairs={{0,1},{1,0},{2,3},{3,2},{4,5},{5,4},{6,7},{7,6},{8,9},{9,8},{10,11... | collective-permute-start | bytes 1966088 | tf_op jit(solution)/shard_map/ppermute | solution.py:80
  38.5 18.9 %collective-permute-start.11 = (bf16[160,2048]{1,0:T(8,128)(2,1)S(1)}, bf16[160,2048]{1,0:T(8,128)(2,1)}, u32[]{:S(2)}, u32[]{:S(2)}) collective-permute-start(bf16[160,2048]{1,0:T(8,128)(2,1)S(1)} %collective-permute-done.8.refs_6_.refs_14_), channel_id=1, source_target_pairs={{0,2},{1,3},{2,4},{3,5},{4,6},{5,7},{6,0},{7,1},{8,10},{9,11},{10,... | collective-permute-start | bytes 1966088 | tf_op jit(solution)/shard_map/ppermute | solution.py:80
  40.2 17.2 %collective-permute-start.10 = (bf16[160,2048]{1,0:T(8,128)(2,1)}, bf16[160,2048]{1,0:T(8,128)(2,1)}, u32[]{:S(2)}, u32[]{:S(2)}) collective-permute-start(bf16[160,2048]{1,0:T(8,128)(2,1)} %collective-permute-done.9.refs_7_.refs_15_), channel_id=1, source_target_pairs={{0,6},{1,7},{2,0},{3,1},{4,2},{5,3},{6,4},{7,5},{8,14},{9,15},{10,... | collective-permute-start | bytes 1966088 | tf_op jit(solution)/shard_map/ppermute | solution.py:80
  42.5 15.6 %collective-permute-start.12 = (bf16[160,2048]{1,0:T(8,128)(2,1)S(1)}, bf16[160,2048]{1,0:T(8,128)(2,1)S(1)}, u32[]{:S(2)}, u32[]{:S(2)}) collective-permute-start(bf16[160,2048]{1,0:T(8,128)(2,1)S(1)} %collective-permute-done.8.refs_6_.refs_14_), channel_id=1, source_target_pairs={{0,1},{1,0},{2,3},{3,2},{4,5},{5,4},{6,7},{7,6},{8,9},{9,8},{10,11... | collective-permute-start | bytes 1966088 | tf_op jit(solution)/shard_map/ppermute | solution.py:80
  47.9 10.7 %collective-permute-start.13 = (bf16[160,2048]{1,0:T(8,128)(2,1)}, bf16[160,2048]{1,0:T(8,128)(2,1)S(1)}, u32[]{:S(2)}, u32[]{:S(2)}) collective-permute-start(bf16[160,2048]{1,0:T(8,128)(2,1)} %collective-permute-done.9.refs_7_.refs_15_), channel_id=1, source_target_pairs={{0,1},{1,0},{2,3},{3,2},{4,5},{5,4},{6,7},{7,6},{8,9},{9,8},{10,11... | collective-permute-start | bytes 1966088 | tf_op jit(solution)/shard_map/ppermute | solution.py:80
  58.1 38.2 %collective-permute-start.22 = (bf16[512,2048]{1,0:T(8,128)(2,1)S(1)}, bf16[512,2048]{1,0:T(8,128)(2,1)S(1)}, u32[]{:S(2)}, u32[]{:S(2)}) collective-permute-start(bf16[512,2048]{1,0:T(8,128)(2,1)S(1)} %bitcast.18), channel_id=1, source_target_pairs={{0,1},{1,0},{2,3},{3,2},{4,5},{5,4},{6,7},{7,6},{8,9},{9,8},{10,11... | collective-permute-start | bytes 6291464 | tf_op jit(solution)/shard_map/ppermute | solution.py:80
  71.5 14.2 %collective-permute-start.17 = (bf16[256,1024]{1,0:T(8,128)(2,1)}, bf16[256,1024]{1,0:T(8,128)(2,1)S(1)}, u32[]{:S(2)}, u32[]{:S(2)}) collective-permute-start(bf16[256,1024]{1,0:T(8,128)(2,1)} %get-tuple-element.59), channel_id=1, source_target_pairs={{0,8},{1,9},{2,10},{3,11},{4,12},{5,13},{6,14},{7,15},{8,0},{9,1},... | collective-permute-start | bytes 1572872 | tf_op jit(solution)/shard_map/ppermute | solution.py:80
  72.2 37.5 %collective-permute-start.23 = (bf16[512,2048]{1,0:T(8,128)(2,1)}, bf16[512,2048]{1,0:T(8,128)(2,1)S(1)}, u32[]{:S(2)}, u32[]{:S(2)}) collective-permute-start(bf16[512,2048]{1,0:T(8,128)(2,1)} %collective-permute-done.7.refs_2_.refs_3_.refs_12_), channel_id=1, source_target_pairs={{0,1},{1,0},{2,3},{3,2},{4,5},{5,4},{6,7},{7,6},{8,9},{9,8},{10,11... | collective-permute-start | bytes 6291464 | tf_op jit(solution)/shard_map/ppermute | solution.py:80
  94.4 15.4 %collective-permute-start.21 = (bf16[640,512]{1,0:T(8,128)(2,1)}, bf16[640,512]{1,0:T(8,128)(2,1)S(1)}, u32[]{:S(2)}, u32[]{:S(2)}) collective-permute-start(bf16[640,512]{1,0:T(8,128)(2,1)} %get-tuple-element.68), channel_id=1, source_target_pairs={{0,1},{1,0},{2,3},{3,2},{4,5},{5,4},{6,7},{7,6},{8,9},{9,8},{10,11... | collective-permute-start | bytes 1966088 | tf_op jit(solution)/shard_map/ppermute | solution.py:80
  95.5 10.7 %collective-permute-start.19 = (bf16[160,512]{1,0:T(8,128)(2,1)}, bf16[160,512]{1,0:T(8,128)(2,1)S(1)}, u32[]{:S(2)}, u32[]{:S(2)}) collective-permute-start(bf16[160,512]{1,0:T(8,128)(2,1)} %get-tuple-element.63), channel_id=1, source_target_pairs={{0,8},{1,9},{2,10},{3,11},{4,12},{5,13},{6,14},{7,15},{8,0},{9,1},... | collective-permute-start | bytes 491528 | tf_op jit(solution)/shard_map/ppermute | solution.py:80
  96.3 13.4 %collective-permute-start.20 = (bf16[160,512]{1,0:T(8,128)(2,1)}, bf16[160,512]{1,0:T(8,128)(2,1)S(1)}, u32[]{:S(2)}, u32[]{:S(2)}) collective-permute-start(bf16[160,512]{1,0:T(8,128)(2,1)} %get-tuple-element.67), channel_id=1, source_target_pairs={{0,8},{1,9},{2,10},{3,11},{4,12},{5,13},{6,14},{7,15},{8,0},{9,1},... | collective-permute-start | bytes 491528 | tf_op jit(solution)/shard_map/ppermute | solution.py:80
  138.6 17.3 %collective-permute-start.31 = (bf16[80,2048]{1,0:T(8,128)(2,1)}, bf16[80,2048]{1,0:T(8,128)(2,1)S(1)}, u32[]{:S(2)}, u32[]{:S(2)}) collective-permute-start(bf16[80,2048]{1,0:T(8,128)(2,1)} %get-tuple-element.93), channel_id=1, source_target_pairs={{0,6},{1,7},{2,0},{3,1},{4,2},{5,3},{6,4},{7,5},{8,14},{9,15},{10,... | collective-permute-start | bytes 983048 | tf_op jit(solution)/shard_map/ppermute | solution.py:80
  141.9 16.7 %collective-permute-start.27 = (bf16[80,2048]{1,0:T(8,128)(2,1)}, bf16[80,2048]{1,0:T(8,128)(2,1)S(1)}, u32[]{:S(2)}, u32[]{:S(2)}) collective-permute-start(bf16[80,2048]{1,0:T(8,128)(2,1)} %get-tuple-element.89), channel_id=1, source_target_pairs={{0,2},{1,3},{2,4},{3,5},{4,6},{5,7},{6,0},{7,1},{8,10},{9,11},{10,... | collective-permute-start | bytes 983048 | tf_op jit(solution)/shard_map/ppermute | solution.py:80
  141.9 17.2 %collective-permute-start.29 = (bf16[80,2048]{1,0:T(8,128)(2,1)}, bf16[80,2048]{1,0:T(8,128)(2,1)S(1)}, u32[]{:S(2)}, u32[]{:S(2)}) collective-permute-start(bf16[80,2048]{1,0:T(8,128)(2,1)} %get-tuple-element.90), channel_id=1, source_target_pairs={{0,2},{1,3},{2,4},{3,5},{4,6},{5,7},{6,0},{7,1},{8,10},{9,11},{10,... | collective-permute-start | bytes 983048 | tf_op jit(solution)/shard_map/ppermute | solution.py:80
  141.9 17.2 %collective-permute-start.30 = (bf16[80,2048]{1,0:T(8,128)(2,1)}, bf16[80,2048]{1,0:T(8,128)(2,1)S(1)}, u32[]{:S(2)}, u32[]{:S(2)}) collective-permute-start(bf16[80,2048]{1,0:T(8,128)(2,1)} %get-tuple-element.91), channel_id=1, source_target_pairs={{0,6},{1,7},{2,0},{3,1},{4,2},{5,3},{6,4},{7,5},{8,14},{9,15},{10,... | collective-permute-start | bytes 983048 | tf_op jit(solution)/shard_map/ppermute | solution.py:80
  (38 other events, 324.3 us)

commit v10 on v8

--- a/solution.py
+++ b/solution.py
@@ -166,8 +166,7 @@
 
 
 def project(table, angles, xs, sets, jobs, groups, carried=None):
-    if carried is None:
-        carried = jnp.zeros((16, 128), BF)
+    carried = angles[0] if carried is None else carried
     operands = [(table, None), (carried, block(carried.shape))]
     operands += [(x, block((SEQ, D), at)) for x, at in xs]
     operands += [(value, block((HALF, SEQ))) for value in angles]
@@ -186,45 +185,23 @@
 SPAN = 2 * SEQ
 
 
-def softmax_parts(scores, diagonal):
-    scores = scores * SCALE
-    low = scores.shape[0] - HD
-    masked = jnp.where(diagonal, scores[low:], MASKED)
-    if low:
-        scores = jnp.concatenate([scores[:low], masked], axis=0)
-    else:
-        scores = masked
+def softmax_parts(scores, causal):
+    scores = jnp.where(causal, scores * SCALE, MASKED)
     power = jnp.exp2(scores - jnp.max(scores, axis=0, keepdims=True))
     return power, (1.0 / HEADS) / jnp.sum(power, axis=0, keepdims=True)
 
 
-def side_by_side(heads, half):
-    return jnp.concatenate([q[:, half * HD : (half + 1) * HD] for q in heads], axis=1)
-
-
 def attention_gradient(student, teacher, cosine, sine):
-    key_s = student[4]
-    rows_s, rows_t = key_s.T, teacher[4].T
-    lane = lax.broadcasted_iota(jnp.int32, (HD, 4 * HD), 1) % HD
-    diagonal = lax.broadcasted_iota(jnp.int32, (HD, 4 * HD), 0) <= lane
-    query_parts, key_grad = [], None
-    for half in range(2):
-        extent = (half + 1) * HD
-        q_s = side_by_side(student[:4], half)
-        q_t = side_by_side(teacher[:4], half)
-        power_s, inverse_s = softmax_parts(dot(rows_s[:extent], q_s), diagonal)
-        power_t, inverse_t = softmax_parts(dot(rows_t[:extent], q_t), diagonal)
-        spread = (power_s * inverse_s - power_t * inverse_t).astype(BF)
-        query_parts.append(dot(key_s[:, :extent], spread))
-        part = dot(q_s, spread, ((1,), (1,)))
-        if half == 0:
-            key_grad = part
-        else:
-            key_grad = jnp.concatenate([part[:, :HD] + key_grad, part[:, HD:]], axis=1)
-    grads = [
-        jnp.concatenate([p[:, h * HD : (h + 1) * HD] for p in query_parts], axis=1)
-        for h in range(4)
-    ] + [key_grad]
+    lane = lax.broadcasted_iota(jnp.int32, (SEQ, 4 * SEQ), 1) % SEQ
+    causal = lax.broadcasted_iota(jnp.int32, (SEQ, 4 * SEQ), 0) <= lane
+    queries = jnp.concatenate(student[:4], axis=1)
+    power_s, inverse_s = softmax_parts(dot(student[4].T, queries), causal)
+    others = jnp.concatenate(teacher[:4], axis=1)
+    power_t, inverse_t = softmax_parts(dot(teacher[4].T, others), causal)
+    spread = (power_s * inverse_s - power_t * inverse_t).astype(BF)
+    query_grads = dot(student[4], spread)
+    grads = [query_grads[:, h * SEQ : (h + 1) * SEQ] for h in range(4)]
+    grads.append(dot(queries, spread, ((1,), (1,))))
     return [rotated(g * INV_ROOT, cosine, -sine).astype(BF) for g in grads]
 
 
@@ -278,7 +255,7 @@
     )
 
 
-TILE = 512
+TILE = 1024
 
 
 def fill(table, held, grads, backs):
@@ -371,18 +348,31 @@
             adam_kernel(*pairs[at::2], *rest)
 
 
-ADAM_TILE = 1024
+def add_kernel(a, b, c, d, low, high):
+    low[...] = (a[...] + b[...].astype(F32)).astype(BF)
+    high[...] = (c[...] + d[...].astype(F32)).astype(BF)
+
+
+def add(*values):
+    whole = pl.BlockSpec((PART, D), lambda: (0, 0))
+    return pl.pallas_call(
+        add_kernel,
+        in_specs=[whole] * 4,
+        out_specs=[whole] * 2,
+        out_shape=[jax.ShapeDtypeStruct((PART, D), BF)] * 2,
+        compiler_params=params(56),
+        cost_estimate=cost(0.5),
+        name="add",
+    )(*values)
 
 
 def adam(pairs, weight, one, two):
-    straight = pl.BlockSpec((PART, ADAM_TILE), lambda k, t: (k, t))
-    last = D // ADAM_TILE - 1
-    low = pl.BlockSpec((PART, ADAM_TILE), lambda k, t: (0, jnp.where(k == 0, t, last)))
-    high = pl.BlockSpec((PART, ADAM_TILE), lambda k, t: (0, jnp.where(k == 0, 0, t)))
+    straight = pl.BlockSpec((PART, D), lambda k: (k, 0))
+    whole = pl.BlockSpec((PART, D), lambda k: (0, 0))
     return pl.pallas_call(
         adam_body,
-        grid=(2, D // ADAM_TILE),
-        in_specs=[low, high] * 3 + [straight] * 3,
+        grid=(2,),
+        in_specs=[whole] * 6 + [straight] * 3,
         out_specs=[straight] * 3,
         out_shape=[jax.ShapeDtypeStruct((SHARD, D), F32)] * 3,
         compiler_params=params(56),
@@ -495,8 +485,8 @@
     next_low, last_high, *own_parts = weight_blocks(
         ((1, 0, F32), (3, PART, F32), (0, 0, F32), (0, PART, F32))
     )
-    from_below[0] = send((next_low + far_low.astype(F32)).astype(BF), up)
-    from_above[1] = send((last_high + far_high.astype(F32)).astype(BF), down)
+    next_low, last_high = add(next_low, far_low, last_high, far_high)
+    from_below[0], from_above[1] = send(next_low, up), send(last_high, down)
     pairs = [own_parts, from_below, from_above]
     updated = adam(pairs, master, moment_one[0], moment_two[0])
     return tuple(value[None] for value in updated)

time: 168 us -> 165 us (0.982)
  waiting for transfers between devices: 37.1 us -> 34.3 us
    ppermute x34, waiting for transfers between devices: 33.1 us -> 30.3 us  [send(): return lax.ppermute(value, 'fsdp', pairs)]
    pallas_call x1 -> x2, Pallas kernels: 5.62 us -> 7.34 us  [the longest x1 4.96 us: adam(): pl.pallas_call(adam_body, grid=(2,), in_specs=[whole] * 6 + [straight] *...]
    unnamed x56 -> x58, local copies, waits for them, and re-layouts: 5.59 us -> 6.95 us
  transfers between devices with their start and end apart: 35 -> 35, of which waited for: 11 -> 9; matrix products, arithmetic and copies ran while one was open for 2% -> 1% of each run, Pallas kernels for 39% -> 40%
where the time goes in v10:
time: 165 us; the launch traced here: 164 us
  Pallas kernels  77.4 us (47%)
  starting transfers between devices  41 us (25%)
  waiting for transfers between devices  34.3 us (21%)
  local copies, waits for them, and re-layouts  8.13 us (5%)
  other arithmetic  2.43 us (1%)
    pallas_call x6, Pallas kernels, call(): pl.pallas_call(kernel, grid_spec=pltpu.PrefetchScalarGridSpec(num_scalar_...  47.8 us
    ppermute x34, starting transfers between devices, send(): return lax.ppermute(value, 'fsdp', pairs)  37.4 us
    ppermute x34, waiting for transfers between devices, send(): return lax.ppermute(value, 'fsdp', pairs)  30.3 us
    pallas_call x3, Pallas kernels, weight_call(): pl.pallas_call(lambda *refs: kernel((len(grads), len(backs), len(tokens))...  22.3 us
    unnamed x58, local copies, waits for them, and re-layouts  6.95 us
    pallas_call x1, Pallas kernels, adam(): pl.pallas_call(adam_body, grid=(2,), in_specs=[whole] * 6 + [straight] *...  4.96 us
    ppermute x1, waiting for transfers between devices, per_device(): lax.ppermute(snapshot[0], 'blk', [(g, (g + 1) % 8) for g in range(8)])  4 us
    ppermute x1, starting transfers between devices, per_device(): lax.ppermute(snapshot[0], 'blk', [(g, (g + 1) % 8) for g in range(8)])  3.6 us
  transfers between devices with their start and end apart: 35, of which 9 were waited for; matrix products, arithmetic and copies ran while one was open for 1% of the time, Pallas kernels for 40%

profile of v10, /device:TPU:1, one launch (start us, length us, event | category | flops | bytes accessed | tf_op | source)
XLA Modules:
  0.0 164.1 jit_solution(5403042105631136458)
XLA Ops:
  5.8 3.6 %collective-permute-start.1 = (bf16[160,2048]{1,0:T(8,128)(2,1)S(1)}, bf16[160,2048]{1,0:T(8,128)(2,1)}, u32[]{:S(2)}, u32[]{:S(2)}) collective-permute-start(bf16[160,2048]{1,0:T(8,128)(2,1)S(1)} %bitcast.24), channel_id=1, source_target_pairs={{0,16},{16,32},{32,48},{48,64},{64,80},{80,96},{96,112},{112,0},{1... | collective-permute-start | bytes 1966088 | tf_op jit(solution)/shard_map/ppermute | solution.py:408
  11.8 8.3 %collective-permute-done.6.refs_9_ = bf16[160,2048]{1,0:T(8,128)(2,1)S(1)} collective-permute-done((bf16[160,2048]{1,0:T(8,128)(2,1)S(1)}, bf16[160,2048]{1,0:T(8,128)(2,1)S(1)}, u32[]{:S(2)}, u32[]{:S(2)}) %collective-permute-start.6) | collective-permute-done | bytes 655392 | tf_op jit(solution)/shard_map/ppermute | solution.py:80
  21.7 4.0 %collective-permute-done.1.refs_6_.refs_14_ = bf16[160,2048]{1,0:T(8,128)(2,1)} collective-permute-done((bf16[160,2048]{1,0:T(8,128)(2,1)S(1)}, bf16[160,2048]{1,0:T(8,128)(2,1)}, u32[]{:S(2)}, u32[]{:S(2)}) %collective-permute-start.1) | collective-permute-done | bytes 655392 | tf_op jit(solution)/shard_map/ppermute | solution.py:408
  27.0 2.2 %collective-permute-start.9 = (bf16[160,2048]{1,0:T(8,128)(2,1)}, bf16[160,2048]{1,0:T(8,128)(2,1)}, u32[]{:S(2)}, u32[]{:S(2)}) collective-permute-start(bf16[160,2048]{1,0:T(8,128)(2,1)} %collective-permute-done.5.refs_7_), channel_id=1, source_target_pairs={{0,1},{1,0},{2,3},{3,2},{4,5},{5,4},{6,7},{7,6},{8,9},{9,8},{10,11... | collective-permute-start | bytes 1966088 | tf_op jit(solution)/shard_map/ppermute | solution.py:80
  29.2 7.2 %collective-permute-done.7.refs_8_ = bf16[160,2048]{1,0:T(8,128)(2,1)} collective-permute-done((bf16[160,2048]{1,0:T(8,128)(2,1)S(1)}, bf16[160,2048]{1,0:T(8,128)(2,1)}, u32[]{:S(2)}, u32[]{:S(2)}) %collective-permute-start.7) | collective-permute-done | bytes 655392 | tf_op jit(solution)/shard_map/ppermute | solution.py:80
  36.4 2.2 %collective-permute-start.10 = (bf16[160,2048]{1,0:T(8,128)(2,1)}, bf16[160,2048]{1,0:T(8,128)(2,1)}, u32[]{:S(2)}, u32[]{:S(2)}) collective-permute-start(bf16[160,2048]{1,0:T(8,128)(2,1)} %collective-permute-done.7.refs_8_), channel_id=1, source_target_pairs={{0,1},{1,0},{2,3},{3,2},{4,5},{5,4},{6,7},{7,6},{8,9},{9,8},{10,11... | collective-permute-start | bytes 1966088 | tf_op jit(solution)/shard_map/ppermute | solution.py:80
  40.5 2.3 %collective-permute-start.3 = (bf16[160,2048]{1,0:T(8,128)(2,1)}, bf16[160,2048]{1,0:T(8,128)(2,1)}, u32[]{:S(2)}, u32[]{:S(2)}) collective-permute-start(bf16[160,2048]{1,0:T(8,128)(2,1)} %collective-permute-done.2.refs_7_.refs_15_), channel_id=1, source_target_pairs={{0,6},{1,7},{2,0},{3,1},{4,2},{5,3},{6,4},{7,5},{8,14},{9,15},{10,... | collective-permute-start | bytes 1966088 | tf_op jit(solution)/shard_map/ppermute | solution.py:80
  45.0 3.1 %collective-permute-start.12 = (bf16[160,2048]{1,0:T(8,128)(2,1)}, bf16[160,2048]{1,0:T(8,128)(2,1)S(1)}, u32[]{:S(2)}, u32[]{:S(2)}) collective-permute-start(bf16[160,2048]{1,0:T(8,128)(2,1)} %collective-permute-done.1.refs_6_.refs_14_), channel_id=1, source_target_pairs={{0,1},{1,0},{2,3},{3,2},{4,5},{5,4},{6,7},{7,6},{8,9},{9,8},{10,11... | collective-permute-start | bytes 1966088 | tf_op jit(solution)/shard_map/ppermute | solution.py:80
  48.2 8.9 %project.3 = (bf16[1280,256]{1,0:T(8,128)(2,1)}, bf16[1280,256]{1,0:T(8,128)(2,1)}, bf16[256,512]{1,0:T(8,128)(2,1)}) custom-call(s32[46]{0:T(128)} %dynamic-slice_bitcast_fusion.refs_0_, f32[64,256]{1,0:T(8,128)} %get-tuple-element.100.refs_1_.refs_4_.refs_9_.refs_5_.refs_7_, bf16[512,2048]{1,0:T(8,128)(2,1)} %bitcast.12, bf16[512,2048]{1,0:T(8,128)(2,1)} %bitcast.13, ...), custom_call_target="tpu_custom_call" | custom-call | flops 500000000 | bytes 1048576 | tf_op jit(solution)/shard_map/project/pallas_call | solution.py:116
  62.8 8.9 %project.4 = (bf16[1280,256]{1,0:T(8,128)(2,1)}, bf16[1280,256]{1,0:T(8,128)(2,1)}, bf16[256,1024]{1,0:T(8,128)(2,1)}) custom-call(s32[46]{0:T(128)} %dynamic-slice_bitcast_fusion.refs_0_, bf16[256,512]{1,0:T(8,128)(2,1)} %get-tuple-element.52.refs_1_, bf16[512,2048]{1,0:T(8,128)(2,1)} %bitcast.14, bf16[512,2048]{1,0:T(8,128)(2,1)} %bitcast.15, ...), custom_call_target="tpu_custom_call" | custom-call | flops 500000000 | bytes 1048576 | tf_op jit(solution)/shard_map/project/pallas_call | solution.py:116
  73.3 11.9 %project.5 = (bf16[1280,256]{1,0:T(8,128)(2,1)}, bf16[1280,256]{1,0:T(8,128)(2,1)}, bf16[1280,256]{1,0:T(8,128)(2,1)}, bf16[1280,256]{1,0:T(8,128)(2,1)}, bf16[2...) custom-call(s32[46]{0:T(128)} %dynamic-slice_bitcast_fusion.refs_0_, ...), custom_call_target="tpu_custom_call" | custom-call | flops 8000000000 | bytes 1048576 | tf_op jit(solution)/shard_map/project/pallas_call | solution.py:116
  87.6 7.7 %attend.3 = (bf16[640,512]{1,0:T(8,128)(2,1)}, bf16[640,512]{1,0:T(8,128)(2,1)}, bf16[160,512]{1,0:T(8,128)(2,1)}, bf16[160,512]{1,0:T(8,128)(2,1)}) custom-call(s32[46]{0:T(128)} %dynamic-slice_bitcast_fusion.refs_0_, bf16[1280,256]{1,0:T(8,128)(2,1)} %get-tuple-element.57.refs_1_, bf16[256,1024]{1,0:T(8,128)(2,1)} %copy-done.22, ...), custom_call_target="tpu_custom_call" | custom-call | flops 8000000000 | bytes 1048576 | tf_op jit(solution)/shard_map/attend/pallas_call | solution.py:116
  95.9 3.1 %collective-permute-done.19.refs_4_.refs_6_ = bf16[256,512]{1,0:T(8,128)(2,1)S(1)} collective-permute-done((bf16[256,512]{1,0:T(8,128)(2,1)}, bf16[256,512]{1,0:T(8,128)(2,1)S(1)}, u32[]{:S(2)}, u32[]{:S(2)}) %collective-permute-start.19) | collective-permute-done | bytes 262176 | tf_op jit(solution)/shard_map/ppermute | solution.py:80
  99.7 5.0 %attend.4 = (bf16[640,256]{1,0:T(8,128)(2,1)}, bf16[640,256]{1,0:T(8,128)(2,1)}, bf16[160,256]{1,0:T(8,128)(2,1)}, bf16[160,256]{1,0:T(8,128)(2,1)}) custom-call(s32[46]{0:T(128)} %dynamic-slice_bitcast_fusion.refs_0_, bf16[1280,256]{1,0:T(8,128)(2,1)} %get-tuple-element.70.refs_1_, bf16[256,512]{1,0:T(8,128)(2,1)} %copy-done.25, ...), custom_call_target="tpu_custom_call" | custom-call | flops 4499999744 | bytes 1048576 | tf_op jit(solution)/shard_map/attend/pallas_call | solution.py:116
  106.6 5.3 %attend.5 = (bf16[640,256]{1,0:T(8,128)(2,1)}, bf16[640,256]{1,0:T(8,128)(2,1)}, bf16[160,512]{1,0:T(8,128)(2,1)}, bf16[160,512]{1,0:T(8,128)(2,1)}) custom-call(s32[46]{0:T(128)} %dynamic-slice_bitcast_fusion.refs_0_, bf16[160,256]{1,0:T(8,128)(2,1)} %get-tuple-element.72.refs_1_, bf16[160,256]{1,0:T(8,128)(2,1)} %get-tuple-element.73.refs_2_, ...), custom_call_target="tpu_custom_call" | custom-call | flops 4499999744 | bytes 1048576 | tf_op jit(solution)/shard_map/attend/pallas_call | solution.py:116
  115.4 7.6 %weight_gradient.3.refs_7_.refs_8_.refs_9_.refs_10_ = f32[640,2048]{1,0:T(8,128)} custom-call(s32[46]{0:T(128)} %dynamic-slice_bitcast_fusion.refs_0_, bf16[640,256]{1,0:T(8,128)(2,1)} %get-tuple-element.80.refs_1_, bf16[640,256]{1,0:T(8,128)(2,1)} %get-tuple-element.81.refs_2_, bf16[640,256]{1,0:T(8,128)(2,1)} %copy-done.23, bf16[640,256]{1,0:T(8,128)(2,1)} %copy-done.24, ...), custom_call_target="tpu_custom_call" | custom-call | flops 6000000000 | bytes 1048576 | tf_op jit(solution)/shard_map/weight_gradient/pallas_call | solution.py:305
  124.6 7.2 %weight_gradient.5 = (bf16[80,2048]{1,0:T(8,128)(2,1)}, bf16[80,2048]{1,0:T(8,128)(2,1)}, bf16[80,2048]{1,0:T(8,128)(2,1)}, bf16[80,2048]{1,0:T(8,128)(2,1)}) custom-call(s32[46]{0:T(128)} %dynamic-slice_bitcast_fusion.refs_0_, bf16[640,512]{1,0:T(8,128)(2,1)} %get-tuple-element.62.refs_1_, bf16[640,512]{1,0:T(8,128)(2,1)} %copy-done.3, ...), custom_call_target="tpu_custom_call" | custom-call | flops 5000000000 | bytes 1048576 | tf_op jit(solution)/shard_map/weight_gradient/pallas_call | solution.py:305
  131.9 3.4 %collective-permute-start.30 = (bf16[80,2048]{1,0:T(8,128)(2,1)}, bf16[80,2048]{1,0:T(8,128)(2,1)S(1)}, u32[]{:S(2)}, u32[]{:S(2)}) collective-permute-start(bf16[80,2048]{1,0:T(8,128)(2,1)} %get-tuple-element.91), channel_id=1, source_target_pairs={{0,6},{1,7},{2,0},{3,1},{4,2},{5,3},{6,4},{7,5},{8,14},{9,15},{10,... | collective-permute-start | bytes 983048 | tf_op jit(solution)/shard_map/ppermute | solution.py:80
  135.4 2.7 %collective-permute-start.33 = (bf16[80,2048]{1,0:T(8,128)(2,1)}, bf16[80,2048]{1,0:T(8,128)(2,1)S(1)}, u32[]{:S(2)}, u32[]{:S(2)}) collective-permute-start(bf16[80,2048]{1,0:T(8,128)(2,1)} %get-tuple-element.94), channel_id=1, source_target_pairs={{0,6},{1,7},{2,0},{3,1},{4,2},{5,3},{6,4},{7,5},{8,14},{9,15},{10,... | collective-permute-start | bytes 983048 | tf_op jit(solution)/shard_map/ppermute | solution.py:80
  138.0 7.5 %weight_gradient.4 = (f32[80,2048]{1,0:T(8,128)}, f32[80,2048]{1,0:T(8,128)}, f32[80,2048]{1,0:T(8,128)}, f32[80,2048]{1,0:T(8,128)}) custom-call(s32[46]{0:T(128)} %dynamic-slice_bitcast_fusion.refs_0_, bf16[640,512]{1,0:T(8,128)(2,1)} %get-tuple-element.62.refs_1_, bf16[640,512]{1,0:T(8,128)(2,1)} %copy-done.3, bf16[160,512]{1,0:T(8,128)(2,1)} %copy-done.5, ...), custom_call_target="tpu_custom_call" | custom-call | flops 5000000000 | bytes 1048576 | tf_op jit(solution)/shard_map/weight_gradient/pallas_call | solution.py:305
  146.4 2.4 %add.5 = (bf16[80,2048]{1,0:T(8,128)(2,1)}, bf16[80,2048]{1,0:T(8,128)(2,1)}) custom-call(f32[80,2048]{1,0:T(8,128)} %get-tuple-element.88.a, bf16[80,2048]{1,0:T(8,128)(2,1)} %copy-done.18, f32[80,2048]{1,0:T(8,128)} %get-tuple-element.90.c, bf16[80,2048]{1,0:T(8,128)(2,1)} %copy-done.19), custom_call_target="tpu_custom_call" | custom-call | flops 500000000 | bytes 1048576 | tf_op jit(solution)/shard_map/add/pallas_call | solution.py:358
  148.7 2.7 %collective-permute-start.34 = (bf16[80,2048]{1,0:T(8,128)(2,1)}, bf16[80,2048]{1,0:T(8,128)(2,1)S(1)}, u32[]{:S(2)}, u32[]{:S(2)}) collective-permute-start(bf16[80,2048]{1,0:T(8,128)(2,1)} %get-tuple-element.95), channel_id=1, source_target_pairs={{0,6},{1,7},{2,0},{3,1},{4,2},{5,3},{6,4},{7,5},{8,14},{9,15},{10,... | collective-permute-start | bytes 983048 | tf_op jit(solution)/shard_map/ppermute | solution.py:80
  151.4 6.8 %collective-permute-done.31.refs_2_ = bf16[80,2048]{1,0:T(8,128)(2,1)S(1)} collective-permute-done((bf16[80,2048]{1,0:T(8,128)(2,1)}, bf16[80,2048]{1,0:T(8,128)(2,1)S(1)}, u32[]{:S(2)}, u32[]{:S(2)}) %collective-permute-start.31) | collective-permute-done | bytes 327712 | tf_op jit(solution)/shard_map/ppermute | solution.py:80
  159.1 5.0 %adam.1 = (f32[160,2048]{1,0:T(8,128)}, f32[160,2048]{1,0:T(8,128)}, f32[160,2048]{1,0:T(8,128)}) custom-call(f32[80,2048]{1,0:T(8,128)} %get-tuple-element.86.refs_0_, f32[80,2048]{1,0:T(8,128)} %get-tuple-element.87.refs_1_, bf16[80,2048]{1,0:T(8,128)(2,1)} %copy-done.16, bf16[80,2048]{1,0:T(8,128)(2,1)} %copy-done.14, bf16[80,2048]{1,0:T(8,128)(2,1)} %copy-done.15, ...), custom_call_target="tpu_custom_call" | custom-call | tf_op jit(solution)/shard_map/adam/pallas_call | solution.py:372
  (120 shorter events, 34.1 us)
Async XLA Ops:
  2.1 18.0 %collective-permute-start.6 = (bf16[160,2048]{1,0:T(8,128)(2,1)S(1)}, bf16[160,2048]{1,0:T(8,128)(2,1)S(1)}, u32[]{:S(2)}, u32[]{:S(2)}) collective-permute-start(bf16[160,2048]{1,0:T(8,128)(2,1)S(1)} %bitcast_convert_fusion.refs_6_), channel_id=1, source_target_pairs={{0,2},{1,3},{2,4},{3,5},{4,6},{5,7},{6,0},{7,1},{8,10},{9,11},{10,... | collective-permute-start | bytes 1966088 | tf_op jit(solution)/shard_map/ppermute | solution.py:80
  4.3 15.9 %collective-permute-start.5 = (bf16[160,2048]{1,0:T(8,128)(2,1)S(1)}, bf16[160,2048]{1,0:T(8,128)(2,1)}, u32[]{:S(2)}, u32[]{:S(2)}) collective-permute-start(bf16[160,2048]{1,0:T(8,128)(2,1)S(1)} %bitcast_convert_fusion.refs_6_), channel_id=1, source_target_pairs={{0,6},{1,7},{2,0},{3,1},{4,2},{5,3},{6,4},{7,5},{8,14},{9,15},{10,... | collective-permute-start | bytes 1966088 | tf_op jit(solution)/shard_map/ppermute | solution.py:80
  5.8 19.9 %collective-permute-start.1 = (bf16[160,2048]{1,0:T(8,128)(2,1)S(1)}, bf16[160,2048]{1,0:T(8,128)(2,1)}, u32[]{:S(2)}, u32[]{:S(2)}) collective-permute-start(bf16[160,2048]{1,0:T(8,128)(2,1)S(1)} %bitcast.24), channel_id=1, source_target_pairs={{0,16},{16,32},{32,48},{48,64},{64,80},{80,96},{96,112},{112,0},{1... | collective-permute-start | bytes 1966088 | tf_op jit(solution)/shard_map/ppermute | solution.py:408
  9.4 62.3 %collective-permute-start = (bf16[512,2048]{1,0:T(8,128)(2,1)}, bf16[512,2048]{1,0:T(8,128)(2,1)S(1)}, u32[]{:S(2)}, u32[]{:S(2)}) collective-permute-start(bf16[512,2048]{1,0:T(8,128)(2,1)} %bitcast.11), channel_id=1, source_target_pairs={{0,8},{1,9},{2,10},{3,11},{4,12},{5,13},{6,14},{7,15},{8,0},{9,1},... | collective-permute-start | bytes 6291464 | tf_op jit(solution)/shard_map/ppermute | solution.py:80
  10.2 16.8 %collective-permute-start.8 = (bf16[160,2048]{1,0:T(8,128)(2,1)S(1)}, bf16[160,2048]{1,0:T(8,128)(2,1)S(1)}, u32[]{:S(2)}, u32[]{:S(2)}) collective-permute-start(bf16[160,2048]{1,0:T(8,128)(2,1)S(1)} %bitcast_convert_fusion.refs_6_), channel_id=1, source_target_pairs={{0,1},{1,0},{2,3},{3,2},{4,5},{5,4},{6,7},{7,6},{8,9},{9,8},{10,11... | collective-permute-start | bytes 1966088 | tf_op jit(solution)/shard_map/ppermute | solution.py:80
  20.2 16.3 %collective-permute-start.7 = (bf16[160,2048]{1,0:T(8,128)(2,1)S(1)}, bf16[160,2048]{1,0:T(8,128)(2,1)}, u32[]{:S(2)}, u32[]{:S(2)}) collective-permute-start(bf16[160,2048]{1,0:T(8,128)(2,1)S(1)} %collective-permute-done.6.refs_9_), channel_id=1, source_target_pairs={{0,2},{1,3},{2,4},{3,5},{4,6},{5,7},{6,0},{7,1},{8,10},{9,11},{10,... | collective-permute-start | bytes 1966088 | tf_op jit(solution)/shard_map/ppermute | solution.py:80
  20.2 18.5 %collective-permute-start.11 = (bf16[160,2048]{1,0:T(8,128)(2,1)S(1)}, bf16[160,2048]{1,0:T(8,128)(2,1)S(1)}, u32[]{:S(2)}, u32[]{:S(2)}) collective-permute-start(bf16[160,2048]{1,0:T(8,128)(2,1)S(1)} %collective-permute-done.6.refs_9_), channel_id=1, source_target_pairs={{0,1},{1,0},{2,3},{3,2},{4,5},{5,4},{6,7},{7,6},{8,9},{9,8},{10,11... | collective-permute-start | bytes 1966088 | tf_op jit(solution)/shard_map/ppermute | solution.py:80
  25.7 14.8 %collective-permute-start.2 = (bf16[160,2048]{1,0:T(8,128)(2,1)}, bf16[160,2048]{1,0:T(8,128)(2,1)}, u32[]{:S(2)}, u32[]{:S(2)}) collective-permute-start(bf16[160,2048]{1,0:T(8,128)(2,1)} %collective-permute-done.1.refs_6_.refs_14_), channel_id=1, source_target_pairs={{0,6},{1,7},{2,0},{3,1},{4,2},{5,3},{6,4},{7,5},{8,14},{9,15},{10,... | collective-permute-start | bytes 1966088 | tf_op jit(solution)/shard_map/ppermute | solution.py:80
  27.0 18.0 %collective-permute-start.9 = (bf16[160,2048]{1,0:T(8,128)(2,1)}, bf16[160,2048]{1,0:T(8,128)(2,1)}, u32[]{:S(2)}, u32[]{:S(2)}) collective-permute-start(bf16[160,2048]{1,0:T(8,128)(2,1)} %collective-permute-done.5.refs_7_), channel_id=1, source_target_pairs={{0,1},{1,0},{2,3},{3,2},{4,5},{5,4},{6,7},{7,6},{8,9},{9,8},{10,11... | collective-permute-start | bytes 1966088 | tf_op jit(solution)/shard_map/ppermute | solution.py:80
  36.4 11.7 %collective-permute-start.10 = (bf16[160,2048]{1,0:T(8,128)(2,1)}, bf16[160,2048]{1,0:T(8,128)(2,1)}, u32[]{:S(2)}, u32[]{:S(2)}) collective-permute-start(bf16[160,2048]{1,0:T(8,128)(2,1)} %collective-permute-done.7.refs_8_), channel_id=1, source_target_pairs={{0,1},{1,0},{2,3},{3,2},{4,5},{5,4},{6,7},{7,6},{8,9},{9,8},{10,11... | collective-permute-start | bytes 1966088 | tf_op jit(solution)/shard_map/ppermute | solution.py:80
  38.6 18.4 %collective-permute-start.4 = (bf16[160,2048]{1,0:T(8,128)(2,1)}, bf16[160,2048]{1,0:T(8,128)(2,1)}, u32[]{:S(2)}, u32[]{:S(2)}) collective-permute-start(bf16[160,2048]{1,0:T(8,128)(2,1)} %collective-permute-done.1.refs_6_.refs_14_), channel_id=1, source_target_pairs={{0,2},{1,3},{2,4},{3,5},{4,6},{5,7},{6,0},{7,1},{8,10},{9,11},{10,... | collective-permute-start | bytes 1966088 | tf_op jit(solution)/shard_map/ppermute | solution.py:80
  40.5 16.5 %collective-permute-start.3 = (bf16[160,2048]{1,0:T(8,128)(2,1)}, bf16[160,2048]{1,0:T(8,128)(2,1)}, u32[]{:S(2)}, u32[]{:S(2)}) collective-permute-start(bf16[160,2048]{1,0:T(8,128)(2,1)} %collective-permute-done.2.refs_7_.refs_15_), channel_id=1, source_target_pairs={{0,6},{1,7},{2,0},{3,1},{4,2},{5,3},{6,4},{7,5},{8,14},{9,15},{10,... | collective-permute-start | bytes 1966088 | tf_op jit(solution)/shard_map/ppermute | solution.py:80
  45.0 13.1 %collective-permute-start.12 = (bf16[160,2048]{1,0:T(8,128)(2,1)}, bf16[160,2048]{1,0:T(8,128)(2,1)S(1)}, u32[]{:S(2)}, u32[]{:S(2)}) collective-permute-start(bf16[160,2048]{1,0:T(8,128)(2,1)} %collective-permute-done.1.refs_6_.refs_14_), channel_id=1, source_target_pairs={{0,1},{1,0},{2,3},{3,2},{4,5},{5,4},{6,7},{7,6},{8,9},{9,8},{10,11... | collective-permute-start | bytes 1966088 | tf_op jit(solution)/shard_map/ppermute | solution.py:80
  48.1 10.6 %collective-permute-start.13 = (bf16[160,2048]{1,0:T(8,128)(2,1)}, bf16[160,2048]{1,0:T(8,128)(2,1)S(1)}, u32[]{:S(2)}, u32[]{:S(2)}) collective-permute-start(bf16[160,2048]{1,0:T(8,128)(2,1)} %collective-permute-done.2.refs_7_.refs_15_), channel_id=1, source_target_pairs={{0,1},{1,0},{2,3},{3,2},{4,5},{5,4},{6,7},{7,6},{8,9},{9,8},{10,11... | collective-permute-start | bytes 1966088 | tf_op jit(solution)/shard_map/ppermute | solution.py:80
  58.1 54.4 %collective-permute-start.28 = (bf16[512,2048]{1,0:T(8,128)(2,1)S(1)}, bf16[512,2048]{1,0:T(8,128)(2,1)}, u32[]{:S(2)}, u32[]{:S(2)}) collective-permute-start(bf16[512,2048]{1,0:T(8,128)(2,1)S(1)} %bitcast.17), channel_id=1, source_target_pairs={{0,1},{1,0},{2,3},{3,2},{4,5},{5,4},{6,7},{7,6},{8,9},{9,8},{10,11... | collective-permute-start | bytes 6291464 | tf_op jit(solution)/shard_map/ppermute | solution.py:80
  71.7 15.1 %collective-permute-start.16 = (bf16[256,1024]{1,0:T(8,128)(2,1)}, bf16[256,1024]{1,0:T(8,128)(2,1)S(1)}, u32[]{:S(2)}, u32[]{:S(2)}) collective-permute-start(bf16[256,1024]{1,0:T(8,128)(2,1)} %get-tuple-element.58), channel_id=1, source_target_pairs={{0,8},{1,9},{2,10},{3,11},{4,12},{5,13},{6,14},{7,15},{8,0},{9,1},... | collective-permute-start | bytes 1572872 | tf_op jit(solution)/shard_map/ppermute | solution.py:80
  72.7 50.3 %collective-permute-start.24 = (bf16[512,2048]{1,0:T(8,128)(2,1)S(1)}, bf16[512,2048]{1,0:T(8,128)(2,1)S(1)}, u32[]{:S(2)}, u32[]{:S(2)}) collective-permute-start(bf16[512,2048]{1,0:T(8,128)(2,1)S(1)} %collective-permute-done.refs_2_.refs_3_.refs_5_), channel_id=1, source_target_pairs={{0,1},{1,0},{2,3},{3,2},{4,5},{5,4},{6,7},{7,6},{8,9},{9,8},{10,11... | collective-permute-start | bytes 6291464 | tf_op jit(solution)/shard_map/ppermute | solution.py:80
  85.2 10.7 %collective-permute-start.18 = (bf16[256,512]{1,0:T(8,128)(2,1)}, bf16[256,512]{1,0:T(8,128)(2,1)S(1)}, u32[]{:S(2)}, u32[]{:S(2)}) collective-permute-start(bf16[256,512]{1,0:T(8,128)(2,1)} %get-tuple-element.64), channel_id=1, source_target_pairs={{0,8},{1,9},{2,10},{3,11},{4,12},{5,13},{6,14},{7,15},{8,0},{9,1},... | collective-permute-start | bytes 786440 | tf_op jit(solution)/shard_map/ppermute | solution.py:80
  85.9 13.1 %collective-permute-start.19 = (bf16[256,512]{1,0:T(8,128)(2,1)}, bf16[256,512]{1,0:T(8,128)(2,1)S(1)}, u32[]{:S(2)}, u32[]{:S(2)}) collective-permute-start(bf16[256,512]{1,0:T(8,128)(2,1)} %get-tuple-element.65), channel_id=1, source_target_pairs={{0,8},{1,9},{2,10},{3,11},{4,12},{5,13},{6,14},{7,15},{8,0},{9,1},... | collective-permute-start | bytes 786440 | tf_op jit(solution)/shard_map/ppermute | solution.py:80
  95.3 11.3 %collective-permute-start.20 = (bf16[160,512]{1,0:T(8,128)(2,1)}, bf16[160,512]{1,0:T(8,128)(2,1)S(1)}, u32[]{:S(2)}, u32[]{:S(2)}) collective-permute-start(bf16[160,512]{1,0:T(8,128)(2,1)} %get-tuple-element.66), channel_id=1, source_target_pairs={{0,8},{1,9},{2,10},{3,11},{4,12},{5,13},{6,14},{7,15},{8,0},{9,1},... | collective-permute-start | bytes 491528 | tf_op jit(solution)/shard_map/ppermute | solution.py:80
  131.9 13.7 %collective-permute-start.29 = (bf16[80,2048]{1,0:T(8,128)(2,1)}, bf16[80,2048]{1,0:T(8,128)(2,1)S(1)}, u32[]{:S(2)}, u32[]{:S(2)}) collective-permute-start(bf16[80,2048]{1,0:T(8,128)(2,1)} %get-tuple-element.89), channel_id=1, source_target_pairs={{0,2},{1,3},{2,4},{3,5},{4,6},{5,7},{6,0},{7,1},{8,10},{9,11},{10,... | collective-permute-start | bytes 983048 | tf_op jit(solution)/shard_map/ppermute | solution.py:80
  131.9 13.6 %collective-permute-start.30 = (bf16[80,2048]{1,0:T(8,128)(2,1)}, bf16[80,2048]{1,0:T(8,128)(2,1)S(1)}, u32[]{:S(2)}, u32[]{:S(2)}) collective-permute-start(bf16[80,2048]{1,0:T(8,128)(2,1)} %get-tuple-element.91), channel_id=1, source_target_pairs={{0,6},{1,7},{2,0},{3,1},{4,2},{5,3},{6,4},{7,5},{8,14},{9,15},{10,... | collective-permute-start | bytes 983048 | tf_op jit(solution)/shard_map/ppermute | solution.py:80
  135.4 16.1 %collective-permute-start.32 = (bf16[80,2048]{1,0:T(8,128)(2,1)}, bf16[80,2048]{1,0:T(8,128)(2,1)S(1)}, u32[]{:S(2)}, u32[]{:S(2)}) collective-permute-start(bf16[80,2048]{1,0:T(8,128)(2,1)} %get-tuple-element.93), channel_id=1, source_target_pairs={{0,2},{1,3},{2,4},{3,5},{4,6},{5,7},{6,0},{7,1},{8,10},{9,11},{10,... | collective-permute-start | bytes 983048 | tf_op jit(solution)/shard_map/ppermute | solution.py:80
  135.4 16.1 %collective-permute-start.33 = (bf16[80,2048]{1,0:T(8,128)(2,1)}, bf16[80,2048]{1,0:T(8,128)(2,1)S(1)}, u32[]{:S(2)}, u32[]{:S(2)}) collective-permute-start(bf16[80,2048]{1,0:T(8,128)(2,1)} %get-tuple-element.94), channel_id=1, source_target_pairs={{0,6},{1,7},{2,0},{3,1},{4,2},{5,3},{6,4},{7,5},{8,14},{9,15},{10,... | collective-permute-start | bytes 983048 | tf_op jit(solution)/shard_map/ppermute | solution.py:80
  (40 other events, 228.9 us)

commit v11 on v10

--- a/solution.py
+++ b/solution.py
@@ -112,7 +112,7 @@
     return pl.BlockSpec(shape, lambda s, table: (row, column))
 
 
-def call(kernel, name, operands, outs, scratch, microseconds):
+def call(kernel, name, operands, outs, scratch, microseconds, mib=32):
     return pl.pallas_call(
         kernel,
         grid_spec=pltpu.PrefetchScalarGridSpec(
@@ -123,7 +123,7 @@
             scratch_shapes=scratch,
         ),
         out_shape=[jax.ShapeDtypeStruct(shape, dtype) for shape, dtype, *_ in outs],
-        compiler_params=params(56),
+        compiler_params=params(mib),
         cost_estimate=cost(microseconds),
         name=name,
     )(*[value for value, _ in operands])
@@ -252,6 +252,7 @@
         [((CORE, count * SEQ), BF)] * 2 + [((SHARD, wide), BF)] * 2,
         [pltpu.VMEM((ROWS + EXCHANGED, count * SEQ), BF)] * 3,
         1.0 + 3.5 * count,
+        32,
     )
 
 
@@ -314,7 +315,7 @@
             scratch_shapes=[pltpu.VMEM((CORE, 2 * SPAN), BF)],
         ),
         out_shape=[jax.ShapeDtypeStruct((rows, D), dtype) for rows, dtype in outs],
-        compiler_params=params(56),
+        compiler_params=params(32),
         cost_estimate=cost(microseconds),
         name="weight_gradient",
     )(table, *grads, *backs, *tokens, *[value for value, _ in more])
@@ -360,7 +361,7 @@
         in_specs=[whole] * 4,
         out_specs=[whole] * 2,
         out_shape=[jax.ShapeDtypeStruct((PART, D), BF)] * 2,
-        compiler_params=params(56),
+        compiler_params=params(32),
         cost_estimate=cost(0.5),
         name="add",
     )(*values)
@@ -375,7 +376,7 @@
         in_specs=[whole] * 6 + [straight] * 3,
         out_specs=[straight] * 3,
         out_shape=[jax.ShapeDtypeStruct((SHARD, D), F32)] * 3,
-        compiler_params=params(56),
+        compiler_params=params(32),
         name="adam",
     )(*[value for pair in pairs for value in pair], weight, one, two)
 

time: 165 us -> 149 us (0.903)
  Pallas kernels: 77.4 us -> 49.3 us
  waiting for transfers between devices: 34.3 us -> 49.2 us
  local copies, waits for them, and re-layouts: 8.13 us -> 4.57 us
  starting transfers between devices: 41 us -> 43.2 us
    pallas_call x6, Pallas kernels: 47.8 us -> 31.3 us  [call(): pl.pallas_call(kernel, grid_spec=pltpu.PrefetchScalarGridSpec(num_scalar_...]
    ppermute x34, waiting for transfers between devices: 30.3 us -> 45 us  [send(): return lax.ppermute(value, 'fsdp', pairs)]
    pallas_call x3, Pallas kernels: 22.3 us -> 15.4 us  [weight_call(): pl.pallas_call(lambda *refs: kernel((len(grads), len(backs), len(tokens))...]
    unnamed x58 -> x20, local copies, waits for them, and re-layouts: 6.95 us -> 3.87 us
    pallas_call x1, Pallas kernels: 4.96 us -> 2.55 us  [adam(): pl.pallas_call(adam_body, grid=(2,), in_specs=[whole] * 6 + [straight] *...]
    ppermute x34, starting transfers between devices: 37.4 us -> 39.7 us  [send(): return lax.ppermute(value, 'fsdp', pairs)]
    pallas_call x1, Pallas kernels: 2.38 us -> 0.14 us  [add(): pl.pallas_call(add_kernel, in_specs=[whole] * 4, out_specs=[whole] * 2, o...]
  transfers between devices with their start and end apart: 35 -> 35, of which waited for: 9 -> 15; matrix products, arithmetic and copies ran while one was open for 1% -> 1% of each run, Pallas kernels for 40% -> 28%
where the time goes in v11:
time: 149 us
  Pallas kernels  49.3 us (33%)
  waiting for transfers between devices  49.2 us (33%)
  starting transfers between devices  43.2 us (29%)
  local copies, waits for them, and re-layouts  4.57 us (3%)
  other arithmetic  1.86 us (1%)
    ppermute x34, waiting for transfers between devices, send(): return lax.ppermute(value, 'fsdp', pairs)  45 us
    ppermute x34, starting transfers between devices, send(): return lax.ppermute(value, 'fsdp', pairs)  39.7 us
    pallas_call x6, Pallas kernels, call(): pl.pallas_call(kernel, grid_spec=pltpu.PrefetchScalarGridSpec(num_scalar_...  31.3 us
    pallas_call x3, Pallas kernels, weight_call(): pl.pallas_call(lambda *refs: kernel((len(grads), len(backs), len(tokens))...  15.4 us
    ppermute x1, waiting for transfers between devices, per_device(): lax.ppermute(snapshot[0], 'blk', [(g, (g + 1) % 8) for g in range(8)])  4.21 us
    unnamed x20, local copies, waits for them, and re-layouts  3.87 us
    ppermute x1, starting transfers between devices, per_device(): lax.ppermute(snapshot[0], 'blk', [(g, (g + 1) % 8) for g in range(8)])  3.6 us
  transfers between devices with their start and end apart: 35, of which 15 were waited for; matrix products, arithmetic and copies ran while one was open for 1% of the time, Pallas kernels for 28%

profile of v11, /device:TPU:1, one launch (start us, length us, event | category | flops | bytes accessed | tf_op | source)
XLA Modules:
  0.0 149.1 jit_solution(11231411308769513108)
XLA Ops:
  5.9 3.6 %collective-permute-start.1 = (bf16[160,2048]{1,0:T(8,128)(2,1)}, bf16[160,2048]{1,0:T(8,128)(2,1)}, u32[]{:S(2)}, u32[]{:S(2)}) collective-permute-start(bf16[160,2048]{1,0:T(8,128)(2,1)} %bitcast.24), channel_id=1, source_target_pairs={{0,16},{16,32},{32,48},{48,64},{64,80},{80,96},{96,112},{112,0},{1... | collective-permute-start | bytes 1966088 | tf_op jit(solution)/shard_map/ppermute | solution.py:409
  11.9 8.3 %collective-permute-done.6.refs_9_ = bf16[160,2048]{1,0:T(8,128)(2,1)S(1)} collective-permute-done((bf16[160,2048]{1,0:T(8,128)(2,1)S(1)}, bf16[160,2048]{1,0:T(8,128)(2,1)S(1)}, u32[]{:S(2)}, u32[]{:S(2)}) %collective-permute-start.6) | collective-permute-done | bytes 655392 | tf_op jit(solution)/shard_map/ppermute | solution.py:80
  21.8 4.2 %collective-permute-done.1.refs_6_.refs_14_ = bf16[160,2048]{1,0:T(8,128)(2,1)} collective-permute-done((bf16[160,2048]{1,0:T(8,128)(2,1)}, bf16[160,2048]{1,0:T(8,128)(2,1)}, u32[]{:S(2)}, u32[]{:S(2)}) %collective-permute-start.1) | collective-permute-done | bytes 655392 | tf_op jit(solution)/shard_map/ppermute | solution.py:409
  30.3 6.2 %collective-permute-done.7.refs_8_ = bf16[160,2048]{1,0:T(8,128)(2,1)} collective-permute-done((bf16[160,2048]{1,0:T(8,128)(2,1)S(1)}, bf16[160,2048]{1,0:T(8,128)(2,1)}, u32[]{:S(2)}, u32[]{:S(2)}) %collective-permute-start.7) | collective-permute-done | bytes 655392 | tf_op jit(solution)/shard_map/ppermute | solution.py:80
  40.8 2.3 %collective-permute-start.3 = (bf16[160,2048]{1,0:T(8,128)(2,1)}, bf16[160,2048]{1,0:T(8,128)(2,1)}, u32[]{:S(2)}, u32[]{:S(2)}) collective-permute-start(bf16[160,2048]{1,0:T(8,128)(2,1)} %collective-permute-done.2.refs_7_.refs_15_), channel_id=1, source_target_pairs={{0,6},{1,7},{2,0},{3,1},{4,2},{5,3},{6,4},{7,5},{8,14},{9,15},{10,... | collective-permute-start | bytes 1966088 | tf_op jit(solution)/shard_map/ppermute | solution.py:80
  44.1 3.2 %collective-permute-start.12 = (bf16[160,2048]{1,0:T(8,128)(2,1)}, bf16[160,2048]{1,0:T(8,128)(2,1)S(1)}, u32[]{:S(2)}, u32[]{:S(2)}) collective-permute-start(bf16[160,2048]{1,0:T(8,128)(2,1)} %collective-permute-done.1.refs_6_.refs_14_), channel_id=1, source_target_pairs={{0,1},{1,0},{2,3},{3,2},{4,5},{5,4},{6,7},{7,6},{8,9},{9,8},{10,11... | collective-permute-start | bytes 1966088 | tf_op jit(solution)/shard_map/ppermute | solution.py:80
  49.6 5.7 %project.3 = (bf16[1280,256]{1,0:T(8,128)(2,1)S(1)}, bf16[1280,256]{1,0:T(8,128)(2,1)S(1)}, bf16[256,512]{1,0:T(8,128)(2,1)S(1)}) custom-call(s32[46]{0:T(128)S(1)} %dynamic-slice_bitcast_fusion.refs_0_, f32[64,256]{1,0:T(8,128)S(1)} %get-tuple-element.100.refs_1_.refs_4_.refs_9_.refs_5_.refs_7_, bf16[512,2048]{1,0:T(8,128)(2,1)S(1)} %bitcast.12, ...), custom_call_target="tpu_custom_call" | custom-call | flops 500000000 | bytes 1048576 | tf_op jit(solution)/shard_map/project/pallas_call | solution.py:116
  62.2 5.4 %project.4 = (bf16[1280,256]{1,0:T(8,128)(2,1)S(1)}, bf16[1280,256]{1,0:T(8,128)(2,1)S(1)}, bf16[256,1024]{1,0:T(8,128)(2,1)S(1)}) custom-call(s32[46]{0:T(128)S(1)} %dynamic-slice_bitcast_fusion.refs_0_, bf16[256,512]{1,0:T(8,128)(2,1)S(1)} %get-tuple-element.52.refs_1_, bf16[512,2048]{1,0:T(8,128)(2,1)S(1)} %bitcast.15, bf16[512,2048]{1,0:T(8,128)(2,1)S(1)} %bitcast.16, ...), custom_call_target="tpu_custom_call" | custom-call | flops 500000000 | bytes 1048576 | tf_op jit(solution)/shard_map/project/pallas_call | solution.py:116
  69.9 2.3 %collective-permute-start.24 = (bf16[512,2048]{1,0:T(8,128)(2,1)}, bf16[512,2048]{1,0:T(8,128)(2,1)S(1)}, u32[]{:S(2)}, u32[]{:S(2)}) collective-permute-start(bf16[512,2048]{1,0:T(8,128)(2,1)} %collective-permute-done.refs_2_.refs_3_.refs_5_), channel_id=1, source_target_pairs={{0,1},{1,0},{2,3},{3,2},{4,5},{5,4},{6,7},{7,6},{8,9},{9,8},{10,11... | collective-permute-start | bytes 6291464 | tf_op jit(solution)/shard_map/ppermute | solution.py:80
  72.2 10.4 %project.5 = (bf16[1280,256]{1,0:T(8,128)(2,1)S(1)}, bf16[1280,256]{1,0:T(8,128)(2,1)S(1)}, bf16[1280,256]{1,0:T(8,128)(2,1)S(1)}, bf16[1280,256]{1,0:T(8,128)(2...) custom-call(s32[46]{0:T(128)S(1)} %dynamic-slice_bitcast_fusion.refs_0_, ...), custom_call_target="tpu_custom_call" | custom-call | flops 8000000000 | bytes 1048576 | tf_op jit(solution)/shard_map/project/pallas_call | solution.py:116
  84.1 4.5 %attend.3 = (bf16[640,512]{1,0:T(8,128)(2,1)S(1)}, bf16[640,512]{1,0:T(8,128)(2,1)S(1)}, bf16[160,512]{1,0:T(8,128)(2,1)S(1)}, bf16[160,512]{1,0:T(8,128)(2,1)S(1)}) custom-call(s32[46]{0:T(128)S(1)} %dynamic-slice_bitcast_fusion.refs_0_, bf16[1280,256]{1,0:T(8,128)(2,1)S(1)} %get-tuple-element.57.refs_1_, ...), custom_call_target="tpu_custom_call" | custom-call | flops 8000000000 | bytes 1048576 | tf_op jit(solution)/shard_map/attend/pallas_call | solution.py:116
  90.6 5.6 %collective-permute-done.19.refs_4_.refs_6_ = bf16[256,512]{1,0:T(8,128)(2,1)S(1)} collective-permute-done((bf16[256,512]{1,0:T(8,128)(2,1)S(1)}, bf16[256,512]{1,0:T(8,128)(2,1)S(1)}, u32[]{:S(2)}, u32[]{:S(2)}) %collective-permute-start.19) | collective-permute-done | bytes 262176 | tf_op jit(solution)/shard_map/ppermute | solution.py:80
  96.9 2.7 %attend.4 = (bf16[640,256]{1,0:T(8,128)(2,1)S(1)}, bf16[640,256]{1,0:T(8,128)(2,1)S(1)}, bf16[160,256]{1,0:T(8,128)(2,1)S(1)}, bf16[160,256]{1,0:T(8,128)(2,1)S(1)}) custom-call(s32[46]{0:T(128)S(1)} %dynamic-slice_bitcast_fusion.refs_0_, bf16[1280,256]{1,0:T(8,128)(2,1)S(1)} %get-tuple-element.70.refs_1_, ...), custom_call_target="tpu_custom_call" | custom-call | flops 4499999744 | bytes 1048576 | tf_op jit(solution)/shard_map/attend/pallas_call | solution.py:116
  103.1 2.7 %attend.5 = (bf16[640,256]{1,0:T(8,128)(2,1)S(1)}, bf16[640,256]{1,0:T(8,128)(2,1)S(1)}, bf16[160,512]{1,0:T(8,128)(2,1)S(1)}, bf16[160,512]{1,0:T(8,128)(2,1)S(1)}) custom-call(s32[46]{0:T(128)S(1)} %dynamic-slice_bitcast_fusion.refs_0_, bf16[160,256]{1,0:T(8,128)(2,1)S(1)} %get-tuple-element.72.refs_1_, bf16[160,256]{1,0:T(8,128)(2,1)S(1)} %get-tuple-element.73.refs_2_, ...), custom_call_target="tpu_custom_call" | custom-call | flops 4499999744 | bytes 1048576 | tf_op jit(solution)/shard_map/attend/pallas_call | solution.py:116
  109.3 4.5 %weight_gradient.3.refs_7_.refs_8_.refs_9_.refs_10_ = f32[640,2048]{1,0:T(8,128)S(1)} custom-call(s32[46]{0:T(128)S(1)} %dynamic-slice_bitcast_fusion.refs_0_, bf16[640,256]{1,0:T(8,128)(2,1)S(1)} %get-tuple-element.80.refs_1_, bf16[640,256]{1,0:T(8,128)(2,1)S(1)} %get-tuple-element.81.refs_2_, bf16[640,256]{1,0:T(8,128)(2,1)S(1)} %collective-permute-done.25.refs_3_, ...), custom_call_target="tpu_custom_call" | custom-call | flops 6000000000 | bytes 1048576 | tf_op jit(solution)/shard_map/weight_gradient/pallas_call | solution.py:306
  113.7 3.0 %collective-permute-done.23.refs_4_ = bf16[160,512]{1,0:T(8,128)(2,1)S(1)} collective-permute-done((bf16[160,512]{1,0:T(8,128)(2,1)S(1)}, bf16[160,512]{1,0:T(8,128)(2,1)S(1)}, u32[]{:S(2)}, u32[]{:S(2)}) %collective-permute-start.23) | collective-permute-done | bytes 163872 | tf_op jit(solution)/shard_map/ppermute | solution.py:80
  116.7 5.3 %weight_gradient.5 = (bf16[80,2048]{1,0:T(8,128)(2,1)S(1)}, bf16[80,2048]{1,0:T(8,128)(2,1)S(1)}, bf16[80,2048]{1,0:T(8,128)(2,1)S(1)}, bf16[80,2048]{1,0:T(8,128)(2,1)S(1)}) custom-call(s32[46]{0:T(128)S(1)} %dynamic-slice_bitcast_fusion.refs_0_, bf16[640,512]{1,0:T(8,128)(2,1)S(1)} %get-tuple-element.62.refs_1_, ...), custom_call_target="tpu_custom_call" | custom-call | flops 5000000000 | bytes 1048576 | tf_op jit(solution)/shard_map/weight_gradient/pallas_call | solution.py:306
  122.1 2.7 %collective-permute-start.30 = (bf16[80,2048]{1,0:T(8,128)(2,1)S(1)}, bf16[80,2048]{1,0:T(8,128)(2,1)S(1)}, u32[]{:S(2)}, u32[]{:S(2)}) collective-permute-start(bf16[80,2048]{1,0:T(8,128)(2,1)S(1)} %get-tuple-element.91), channel_id=1, source_target_pairs={{0,6},{1,7},{2,0},{3,1},{4,2},{5,3},{6,4},{7,5},{8,14},{9,15},{10,... | collective-permute-start | bytes 983048 | tf_op jit(solution)/shard_map/ppermute | solution.py:80
  124.8 2.7 %collective-permute-start.33 = (bf16[80,2048]{1,0:T(8,128)(2,1)S(1)}, bf16[80,2048]{1,0:T(8,128)(2,1)S(1)}, u32[]{:S(2)}, u32[]{:S(2)}) collective-permute-start(bf16[80,2048]{1,0:T(8,128)(2,1)S(1)} %get-tuple-element.94), channel_id=1, source_target_pairs={{0,6},{1,7},{2,0},{3,1},{4,2},{5,3},{6,4},{7,5},{8,14},{9,15},{10,... | collective-permute-start | bytes 983048 | tf_op jit(solution)/shard_map/ppermute | solution.py:80
  127.5 5.6 %weight_gradient.4 = (f32[80,2048]{1,0:T(8,128)S(1)}, f32[80,2048]{1,0:T(8,128)S(1)}, f32[80,2048]{1,0:T(8,128)S(1)}, f32[80,2048]{1,0:T(8,128)S(1)}) custom-call(s32[46]{0:T(128)S(1)} %dynamic-slice_bitcast_fusion.refs_0_, bf16[640,512]{1,0:T(8,128)(2,1)S(1)} %get-tuple-element.62.refs_1_, bf16[640,512]{1,0:T(8,128)(2,1)S(1)} %collective-permute-done.17.refs_2_, ...), custom_call_target="tpu_custom_call" | custom-call | flops 5000000000 | bytes 1048576 | tf_op jit(solution)/shard_map/weight_gradient/pallas_call | solution.py:306
  133.4 2.7 %collective-permute-start.34 = (bf16[80,2048]{1,0:T(8,128)(2,1)S(1)}, bf16[80,2048]{1,0:T(8,128)(2,1)S(1)}, u32[]{:S(2)}, u32[]{:S(2)}) collective-permute-start(bf16[80,2048]{1,0:T(8,128)(2,1)S(1)} %get-tuple-element.95), channel_id=1, source_target_pairs={{0,6},{1,7},{2,0},{3,1},{4,2},{5,3},{6,4},{7,5},{8,14},{9,15},{10,... | collective-permute-start | bytes 983048 | tf_op jit(solution)/shard_map/ppermute | solution.py:80
  136.0 3.5 %collective-permute-done.32.refs_3_ = bf16[80,2048]{1,0:T(8,128)(2,1)S(1)} collective-permute-done((bf16[80,2048]{1,0:T(8,128)(2,1)S(1)}, bf16[80,2048]{1,0:T(8,128)(2,1)S(1)}, u32[]{:S(2)}, u32[]{:S(2)}) %collective-permute-start.32) | collective-permute-done | bytes 327712 | tf_op jit(solution)/shard_map/ppermute | solution.py:80
  139.5 7.0 %collective-permute-done.31.refs_2_ = bf16[80,2048]{1,0:T(8,128)(2,1)S(1)} collective-permute-done((bf16[80,2048]{1,0:T(8,128)(2,1)S(1)}, bf16[80,2048]{1,0:T(8,128)(2,1)S(1)}, u32[]{:S(2)}, u32[]{:S(2)}) %collective-permute-start.31) | collective-permute-done | bytes 327712 | tf_op jit(solution)/shard_map/ppermute | solution.py:80
  146.5 2.6 %adam.1 = (f32[160,2048]{1,0:T(8,128)}, f32[160,2048]{1,0:T(8,128)}, f32[160,2048]{1,0:T(8,128)}) custom-call(f32[80,2048]{1,0:T(8,128)S(1)} %get-tuple-element.86.refs_0_, f32[80,2048]{1,0:T(8,128)S(1)} %get-tuple-element.87.refs_1_, bf16[80,2048]{1,0:T(8,128)(2,1)S(1)} %collective-permute-done.31.refs_2_, ...), custom_call_target="tpu_custom_call" | custom-call | tf_op jit(solution)/shard_map/adam/pallas_call | solution.py:373
  (82 shorter events, 41.8 us)
Async XLA Ops:
  2.2 18.0 %collective-permute-start.6 = (bf16[160,2048]{1,0:T(8,128)(2,1)S(1)}, bf16[160,2048]{1,0:T(8,128)(2,1)S(1)}, u32[]{:S(2)}, u32[]{:S(2)}) collective-permute-start(bf16[160,2048]{1,0:T(8,128)(2,1)S(1)} %bitcast_convert_fusion.refs_6_), channel_id=1, source_target_pairs={{0,2},{1,3},{2,4},{3,5},{4,6},{5,7},{6,0},{7,1},{8,10},{9,11},{10,... | collective-permute-start | bytes 1966088 | tf_op jit(solution)/shard_map/ppermute | solution.py:80
  4.4 15.9 %collective-permute-start.5 = (bf16[160,2048]{1,0:T(8,128)(2,1)S(1)}, bf16[160,2048]{1,0:T(8,128)(2,1)}, u32[]{:S(2)}, u32[]{:S(2)}) collective-permute-start(bf16[160,2048]{1,0:T(8,128)(2,1)S(1)} %bitcast_convert_fusion.refs_6_), channel_id=1, source_target_pairs={{0,6},{1,7},{2,0},{3,1},{4,2},{5,3},{6,4},{7,5},{8,14},{9,15},{10,... | collective-permute-start | bytes 1966088 | tf_op jit(solution)/shard_map/ppermute | solution.py:80
  5.9 20.1 %collective-permute-start.1 = (bf16[160,2048]{1,0:T(8,128)(2,1)}, bf16[160,2048]{1,0:T(8,128)(2,1)}, u32[]{:S(2)}, u32[]{:S(2)}) collective-permute-start(bf16[160,2048]{1,0:T(8,128)(2,1)} %bitcast.24), channel_id=1, source_target_pairs={{0,16},{16,32},{32,48},{48,64},{64,80},{80,96},{96,112},{112,0},{1... | collective-permute-start | bytes 1966088 | tf_op jit(solution)/shard_map/ppermute | solution.py:409
  9.5 59.7 %collective-permute-start = (bf16[512,2048]{1,0:T(8,128)(2,1)}, bf16[512,2048]{1,0:T(8,128)(2,1)}, u32[]{:S(2)}, u32[]{:S(2)}) collective-permute-start(bf16[512,2048]{1,0:T(8,128)(2,1)} %bitcast.11), channel_id=1, source_target_pairs={{0,8},{1,9},{2,10},{3,11},{4,12},{5,13},{6,14},{7,15},{8,0},{9,1},... | collective-permute-start | bytes 6291464 | tf_op jit(solution)/shard_map/ppermute | solution.py:80
  10.2 17.0 %collective-permute-start.8 = (bf16[160,2048]{1,0:T(8,128)(2,1)S(1)}, bf16[160,2048]{1,0:T(8,128)(2,1)S(1)}, u32[]{:S(2)}, u32[]{:S(2)}) collective-permute-start(bf16[160,2048]{1,0:T(8,128)(2,1)S(1)} %bitcast_convert_fusion.refs_6_), channel_id=1, source_target_pairs={{0,1},{1,0},{2,3},{3,2},{4,5},{5,4},{6,7},{7,6},{8,9},{9,8},{10,11... | collective-permute-start | bytes 1966088 | tf_op jit(solution)/shard_map/ppermute | solution.py:80
  20.2 16.3 %collective-permute-start.7 = (bf16[160,2048]{1,0:T(8,128)(2,1)S(1)}, bf16[160,2048]{1,0:T(8,128)(2,1)}, u32[]{:S(2)}, u32[]{:S(2)}) collective-permute-start(bf16[160,2048]{1,0:T(8,128)(2,1)S(1)} %collective-permute-done.6.refs_9_), channel_id=1, source_target_pairs={{0,2},{1,3},{2,4},{3,5},{4,6},{5,7},{6,0},{7,1},{8,10},{9,11},{10,... | collective-permute-start | bytes 1966088 | tf_op jit(solution)/shard_map/ppermute | solution.py:80
  20.2 18.5 %collective-permute-start.11 = (bf16[160,2048]{1,0:T(8,128)(2,1)S(1)}, bf16[160,2048]{1,0:T(8,128)(2,1)S(1)}, u32[]{:S(2)}, u32[]{:S(2)}) collective-permute-start(bf16[160,2048]{1,0:T(8,128)(2,1)S(1)} %collective-permute-done.6.refs_9_), channel_id=1, source_target_pairs={{0,1},{1,0},{2,3},{3,2},{4,5},{5,4},{6,7},{7,6},{8,9},{9,8},{10,11... | collective-permute-start | bytes 1966088 | tf_op jit(solution)/shard_map/ppermute | solution.py:80
  26.0 14.8 %collective-permute-start.2 = (bf16[160,2048]{1,0:T(8,128)(2,1)}, bf16[160,2048]{1,0:T(8,128)(2,1)}, u32[]{:S(2)}, u32[]{:S(2)}) collective-permute-start(bf16[160,2048]{1,0:T(8,128)(2,1)} %collective-permute-done.1.refs_6_.refs_14_), channel_id=1, source_target_pairs={{0,6},{1,7},{2,0},{3,1},{4,2},{5,3},{6,4},{7,5},{8,14},{9,15},{10,... | collective-permute-start | bytes 1966088 | tf_op jit(solution)/shard_map/ppermute | solution.py:80
  28.1 16.0 %collective-permute-start.9 = (bf16[160,2048]{1,0:T(8,128)(2,1)}, bf16[160,2048]{1,0:T(8,128)(2,1)}, u32[]{:S(2)}, u32[]{:S(2)}) collective-permute-start(bf16[160,2048]{1,0:T(8,128)(2,1)} %collective-permute-done.5.refs_7_), channel_id=1, source_target_pairs={{0,1},{1,0},{2,3},{3,2},{4,5},{5,4},{6,7},{7,6},{8,9},{9,8},{10,11... | collective-permute-start | bytes 1966088 | tf_op jit(solution)/shard_map/ppermute | solution.py:80
  39.5 17.9 %collective-permute-start.4 = (bf16[160,2048]{1,0:T(8,128)(2,1)}, bf16[160,2048]{1,0:T(8,128)(2,1)}, u32[]{:S(2)}, u32[]{:S(2)}) collective-permute-start(bf16[160,2048]{1,0:T(8,128)(2,1)} %collective-permute-done.1.refs_6_.refs_14_), channel_id=1, source_target_pairs={{0,2},{1,3},{2,4},{3,5},{4,6},{5,7},{6,0},{7,1},{8,10},{9,11},{10,... | collective-permute-start | bytes 1966088 | tf_op jit(solution)/shard_map/ppermute | solution.py:80
  40.8 16.6 %collective-permute-start.3 = (bf16[160,2048]{1,0:T(8,128)(2,1)}, bf16[160,2048]{1,0:T(8,128)(2,1)}, u32[]{:S(2)}, u32[]{:S(2)}) collective-permute-start(bf16[160,2048]{1,0:T(8,128)(2,1)} %collective-permute-done.2.refs_7_.refs_15_), channel_id=1, source_target_pairs={{0,6},{1,7},{2,0},{3,1},{4,2},{5,3},{6,4},{7,5},{8,14},{9,15},{10,... | collective-permute-start | bytes 1966088 | tf_op jit(solution)/shard_map/ppermute | solution.py:80
  44.1 14.3 %collective-permute-start.12 = (bf16[160,2048]{1,0:T(8,128)(2,1)}, bf16[160,2048]{1,0:T(8,128)(2,1)S(1)}, u32[]{:S(2)}, u32[]{:S(2)}) collective-permute-start(bf16[160,2048]{1,0:T(8,128)(2,1)} %collective-permute-done.1.refs_6_.refs_14_), channel_id=1, source_target_pairs={{0,1},{1,0},{2,3},{3,2},{4,5},{5,4},{6,7},{7,6},{8,9},{9,8},{10,11... | collective-permute-start | bytes 1966088 | tf_op jit(solution)/shard_map/ppermute | solution.py:80
  47.3 11.5 %collective-permute-start.13 = (bf16[160,2048]{1,0:T(8,128)(2,1)}, bf16[160,2048]{1,0:T(8,128)(2,1)S(1)}, u32[]{:S(2)}, u32[]{:S(2)}) collective-permute-start(bf16[160,2048]{1,0:T(8,128)(2,1)} %collective-permute-done.2.refs_7_.refs_15_), channel_id=1, source_target_pairs={{0,1},{1,0},{2,3},{3,2},{4,5},{5,4},{6,7},{7,6},{8,9},{9,8},{10,11... | collective-permute-start | bytes 1966088 | tf_op jit(solution)/shard_map/ppermute | solution.py:80
  58.4 48.5 %collective-permute-start.28 = (bf16[512,2048]{1,0:T(8,128)(2,1)S(1)}, bf16[512,2048]{1,0:T(8,128)(2,1)S(1)}, u32[]{:S(2)}, u32[]{:S(2)}) collective-permute-start(bf16[512,2048]{1,0:T(8,128)(2,1)S(1)} %bitcast.14), channel_id=1, source_target_pairs={{0,1},{1,0},{2,3},{3,2},{4,5},{5,4},{6,7},{7,6},{8,9},{9,8},{10,11... | collective-permute-start | bytes 6291464 | tf_op jit(solution)/shard_map/ppermute | solution.py:80
  69.2 15.0 %collective-permute-start.16 = (bf16[256,1024]{1,0:T(8,128)(2,1)S(1)}, bf16[256,1024]{1,0:T(8,128)(2,1)S(1)}, u32[]{:S(2)}, u32[]{:S(2)}) collective-permute-start(bf16[256,1024]{1,0:T(8,128)(2,1)S(1)} %get-tuple-element.58), channel_id=1, source_target_pairs={{0,8},{1,9},{2,10},{3,11},{4,12},{5,13},{6,14},{7,15},{8,0},{9,1},... | collective-permute-start | bytes 1572872 | tf_op jit(solution)/shard_map/ppermute | solution.py:80
  69.9 46.9 %collective-permute-start.24 = (bf16[512,2048]{1,0:T(8,128)(2,1)}, bf16[512,2048]{1,0:T(8,128)(2,1)S(1)}, u32[]{:S(2)}, u32[]{:S(2)}) collective-permute-start(bf16[512,2048]{1,0:T(8,128)(2,1)} %collective-permute-done.refs_2_.refs_3_.refs_5_), channel_id=1, source_target_pairs={{0,1},{1,0},{2,3},{3,2},{4,5},{5,4},{6,7},{7,6},{8,9},{9,8},{10,11... | collective-permute-start | bytes 6291464 | tf_op jit(solution)/shard_map/ppermute | solution.py:80
  83.4 12.8 %collective-permute-start.19 = (bf16[256,512]{1,0:T(8,128)(2,1)S(1)}, bf16[256,512]{1,0:T(8,128)(2,1)S(1)}, u32[]{:S(2)}, u32[]{:S(2)}) collective-permute-start(bf16[256,512]{1,0:T(8,128)(2,1)S(1)} %get-tuple-element.65), channel_id=1, source_target_pairs={{0,8},{1,9},{2,10},{3,11},{4,12},{5,13},{6,14},{7,15},{8,0},{9,1},... | collective-permute-start | bytes 786440 | tf_op jit(solution)/shard_map/ppermute | solution.py:80
  88.7 12.7 %collective-permute-start.20 = (bf16[160,512]{1,0:T(8,128)(2,1)S(1)}, bf16[160,512]{1,0:T(8,128)(2,1)S(1)}, u32[]{:S(2)}, u32[]{:S(2)}) collective-permute-start(bf16[160,512]{1,0:T(8,128)(2,1)S(1)} %get-tuple-element.66), channel_id=1, source_target_pairs={{0,8},{1,9},{2,10},{3,11},{4,12},{5,13},{6,14},{7,15},{8,0},{9,1},... | collective-permute-start | bytes 491528 | tf_op jit(solution)/shard_map/ppermute | solution.py:80
  122.1 11.1 %collective-permute-start.29 = (bf16[80,2048]{1,0:T(8,128)(2,1)S(1)}, bf16[80,2048]{1,0:T(8,128)(2,1)S(1)}, u32[]{:S(2)}, u32[]{:S(2)}) collective-permute-start(bf16[80,2048]{1,0:T(8,128)(2,1)S(1)} %get-tuple-element.89), channel_id=1, source_target_pairs={{0,2},{1,3},{2,4},{3,5},{4,6},{5,7},{6,0},{7,1},{8,10},{9,11},{10,... | collective-permute-start | bytes 983048 | tf_op jit(solution)/shard_map/ppermute | solution.py:80
  122.1 11.0 %collective-permute-start.30 = (bf16[80,2048]{1,0:T(8,128)(2,1)S(1)}, bf16[80,2048]{1,0:T(8,128)(2,1)S(1)}, u32[]{:S(2)}, u32[]{:S(2)}) collective-permute-start(bf16[80,2048]{1,0:T(8,128)(2,1)S(1)} %get-tuple-element.91), channel_id=1, source_target_pairs={{0,6},{1,7},{2,0},{3,1},{4,2},{5,3},{6,4},{7,5},{8,14},{9,15},{10,... | collective-permute-start | bytes 983048 | tf_op jit(solution)/shard_map/ppermute | solution.py:80
  124.8 14.7 %collective-permute-start.32 = (bf16[80,2048]{1,0:T(8,128)(2,1)S(1)}, bf16[80,2048]{1,0:T(8,128)(2,1)S(1)}, u32[]{:S(2)}, u32[]{:S(2)}) collective-permute-start(bf16[80,2048]{1,0:T(8,128)(2,1)S(1)} %get-tuple-element.93), channel_id=1, source_target_pairs={{0,2},{1,3},{2,4},{3,5},{4,6},{5,7},{6,0},{7,1},{8,10},{9,11},{10,... | collective-permute-start | bytes 983048 | tf_op jit(solution)/shard_map/ppermute | solution.py:80
  124.8 14.7 %collective-permute-start.33 = (bf16[80,2048]{1,0:T(8,128)(2,1)S(1)}, bf16[80,2048]{1,0:T(8,128)(2,1)S(1)}, u32[]{:S(2)}, u32[]{:S(2)}) collective-permute-start(bf16[80,2048]{1,0:T(8,128)(2,1)S(1)} %get-tuple-element.94), channel_id=1, source_target_pairs={{0,6},{1,7},{2,0},{3,1},{4,2},{5,3},{6,4},{7,5},{8,14},{9,15},{10,... | collective-permute-start | bytes 983048 | tf_op jit(solution)/shard_map/ppermute | solution.py:80
  133.3 13.2 %collective-permute-start.31 = (bf16[80,2048]{1,0:T(8,128)(2,1)S(1)}, bf16[80,2048]{1,0:T(8,128)(2,1)S(1)}, u32[]{:S(2)}, u32[]{:S(2)}) collective-permute-start(bf16[80,2048]{1,0:T(8,128)(2,1)S(1)} %get-tuple-element.92), channel_id=1, source_target_pairs={{0,2},{1,3},{2,4},{3,5},{4,6},{5,7},{6,0},{7,1},{8,10},{9,11},{10,... | collective-permute-start | bytes 983048 | tf_op jit(solution)/shard_map/ppermute | solution.py:80
  133.4 13.1 %collective-permute-start.34 = (bf16[80,2048]{1,0:T(8,128)(2,1)S(1)}, bf16[80,2048]{1,0:T(8,128)(2,1)S(1)}, u32[]{:S(2)}, u32[]{:S(2)}) collective-permute-start(bf16[80,2048]{1,0:T(8,128)(2,1)S(1)} %get-tuple-element.95), channel_id=1, source_target_pairs={{0,6},{1,7},{2,0},{3,1},{4,2},{5,3},{6,4},{7,5},{8,14},{9,15},{10,... | collective-permute-start | bytes 983048 | tf_op jit(solution)/shard_map/ppermute | solution.py:80
  (21 other events, 201.5 us)

commit v12 on v11

--- a/solution.py
+++ b/solution.py
@@ -422,34 +422,26 @@
     got_own = send(given, TO_PLANE)
     plane_after, _ = lax.optimization_barrier((plane, own_t[0]))
     plane_two = [(plane_after, 0), (plane_after, 1)]
-    *made, given_s, given_t = project(
-        table,
-        angles,
-        plane_two,
-        [student_rows, teacher_rows],
-        two + [(0, 1), (1, 1)],
-        [[0, 1], [2, 3]],
-    )
-    plane_s, plane_t = made[:2], made[2:]
-    got_s, got_t = send(given_s, TO_PLANE), send(given_t, TO_PLANE)
+    *plane_s, given = project(table, angles, plane_two, [student_rows], two, [[0, 1]])
+    got_s = send(given, TO_PLANE)
+    *plane_t, given_0, given_1 = project(table, angles, plane_two, [teacher_rows], two, [[0], [1]])
+    got_t = [send(given_0, TO_PLANE), send(given_1, TO_PLANE)]
 
     second = attend(
         table,
         angles,
         [[(plane_s[n], (got_own, n)), (plane_t[n], (got_own, 2 + n))] for n in range(2)],
     )
-    got_s, got_t, _ = lax.optimization_barrier((got_s, got_t, second[2]))
-    first = [attend(table, angles, [[(own_s[0], (got_s, 0)), (own_t[0], (got_t, 0))]])]
+    got_s, got_t[0], _ = lax.optimization_barrier((got_s, got_t[0], second[2]))
+    first = [attend(table, angles, [[(own_s[0], (got_s, 0)), (own_t[0], (got_t[0], 0))]])]
     back_first = [send(second[2], TO_PLANE), send(second[3], TO_PLANE)]
-    got_s, got_t, *back_first, carried = lax.optimization_barrier(
-        (got_s, got_t, *back_first, first[0][2])
-    )
+    got_t[1], *back_first, carried = lax.optimization_barrier((got_t[1], *back_first, first[0][2]))
     back_first[1] = send(back_first[1], TO_CORE)
     first.append(
         attend(
             table,
             angles,
-            [[(own_s[1], (got_s, 1)), (own_t[1], (got_t, 1))]],
+            [[(own_s[1], (got_s, 1)), (own_t[1], (got_t[1], 0))]],
             (carried, first[0][3]),
         )
     )

time: 149 us -> 152 us (1.020)
  starting transfers between devices: 43.2 us -> 47.8 us
  waiting for transfers between devices: 49.2 us -> 46.4 us
  local copies, waits for them, and re-layouts: 4.57 us -> 6.16 us
    ppermute x34 -> x35, starting transfers between devices: 39.7 us -> 44.3 us  [send(): return lax.ppermute(value, 'fsdp', pairs)]
    ppermute x1, waiting for transfers between devices: 4.21 us -> 2.61 us  [per_device(): lax.ppermute(snapshot[0], 'blk', [(g, (g + 1) % 8) for g in range(8)])]
    unnamed x20 -> x22, local copies, waits for them, and re-layouts: 3.87 us -> 5.46 us
    ppermute x34 -> x35, waiting for transfers between devices: 45 us -> 43.8 us  [send(): return lax.ppermute(value, 'fsdp', pairs)]
    pallas_call x6 -> x7, Pallas kernels: 31.3 us -> 31.9 us  [call(): pl.pallas_call(kernel, grid_spec=pltpu.PrefetchScalarGridSpec(num_scalar_...]
  transfers between devices with their start and end apart: 35 -> 36, of which waited for: 15 -> 15; matrix products, arithmetic and copies ran while one was open for 1% -> 1% of each run, Pallas kernels for 28% -> 27%
where the time goes in v12:
time: 152 us
  Pallas kernels  48.5 us (32%)
  starting transfers between devices  47.8 us (31%)
  waiting for transfers between devices  46.4 us (31%)
  local copies, waits for them, and re-layouts  6.16 us (4%)
  other arithmetic  1.78 us (1%)
    ppermute x35, starting transfers between devices, send(): return lax.ppermute(value, 'fsdp', pairs)  44.3 us
    ppermute x35, waiting for transfers between devices, send(): return lax.ppermute(value, 'fsdp', pairs)  43.8 us
    pallas_call x7, Pallas kernels, call(): pl.pallas_call(kernel, grid_spec=pltpu.PrefetchScalarGridSpec(num_scalar_...  31.9 us
    pallas_call x3, Pallas kernels, weight_call(): pl.pallas_call(lambda *refs: kernel((len(grads), len(backs), len(tokens))...  14 us
    unnamed x22, local copies, waits for them, and re-layouts  5.46 us
    ppermute x1, starting transfers between devices, per_device(): lax.ppermute(snapshot[0], 'blk', [(g, (g + 1) % 8) for g in range(8)])  3.6 us
  transfers between devices with their start and end apart: 36, of which 15 were waited for; matrix products, arithmetic and copies ran while one was open for 1% of the time, Pallas kernels for 27%

profile of v12, /device:TPU:1, one launch (start us, length us, event | category | flops | bytes accessed | tf_op | source)
XLA Modules:
  0.0 151.6 jit_solution(11550429688963655034)
XLA Ops:
  4.3 3.6 %collective-permute-start.1 = (bf16[160,2048]{1,0:T(8,128)(2,1)S(1)}, bf16[160,2048]{1,0:T(8,128)(2,1)}, u32[]{:S(2)}, u32[]{:S(2)}) collective-permute-start(bf16[160,2048]{1,0:T(8,128)(2,1)S(1)} %bitcast.24), channel_id=1, source_target_pairs={{0,16},{16,32},{32,48},{48,64},{64,80},{80,96},{96,112},{112,0},{1... | collective-permute-start | bytes 1966088 | tf_op jit(solution)/shard_map/ppermute | solution.py:409
  10.8 9.4 %collective-permute-done.6.refs_9_ = bf16[160,2048]{1,0:T(8,128)(2,1)S(1)} collective-permute-done((bf16[160,2048]{1,0:T(8,128)(2,1)S(1)}, bf16[160,2048]{1,0:T(8,128)(2,1)S(1)}, u32[]{:S(2)}, u32[]{:S(2)}) %collective-permute-start.6) | collective-permute-done | bytes 655392 | tf_op jit(solution)/shard_map/ppermute | solution.py:80
  29.7 6.7 %collective-permute-done.7.refs_8_ = bf16[160,2048]{1,0:T(8,128)(2,1)} collective-permute-done((bf16[160,2048]{1,0:T(8,128)(2,1)S(1)}, bf16[160,2048]{1,0:T(8,128)(2,1)}, u32[]{:S(2)}, u32[]{:S(2)}) %collective-permute-start.7) | collective-permute-done | bytes 655392 | tf_op jit(solution)/shard_map/ppermute | solution.py:80
  39.5 3.0 %collective-permute-start.3 = (bf16[160,2048]{1,0:T(8,128)(2,1)}, bf16[160,2048]{1,0:T(8,128)(2,1)}, u32[]{:S(2)}, u32[]{:S(2)}) collective-permute-start(bf16[160,2048]{1,0:T(8,128)(2,1)} %collective-permute-done.2.refs_7_), channel_id=1, source_target_pairs={{0,6},{1,7},{2,0},{3,1},{4,2},{5,3},{6,4},{7,5},{8,14},{9,15},{10,... | collective-permute-start | bytes 1966088 | tf_op jit(solution)/shard_map/ppermute | solution.py:80
  43.4 2.7 %collective-permute-start.12 = (bf16[160,2048]{1,0:T(8,128)(2,1)}, bf16[160,2048]{1,0:T(8,128)(2,1)S(1)}, u32[]{:S(2)}, u32[]{:S(2)}) collective-permute-start(bf16[160,2048]{1,0:T(8,128)(2,1)} %collective-permute-done.1.refs_6_), channel_id=1, source_target_pairs={{0,1},{1,0},{2,3},{3,2},{4,5},{5,4},{6,7},{7,6},{8,9},{9,8},{10,11... | collective-permute-start | bytes 1966088 | tf_op jit(solution)/shard_map/ppermute | solution.py:80
  50.0 5.7 %project.4 = (bf16[1280,256]{1,0:T(8,128)(2,1)S(1)}, bf16[1280,256]{1,0:T(8,128)(2,1)S(1)}, bf16[256,512]{1,0:T(8,128)(2,1)S(1)}) custom-call(s32[46]{0:T(128)S(1)} %dynamic-slice_bitcast_fusion.refs_0_, f32[64,256]{1,0:T(8,128)S(1)} %get-tuple-element.100.refs_1_.refs_4_.refs_9_.refs_5_.refs_7_, bf16[512,2048]{1,0:T(8,128)(2,1)S(1)} %bitcast.12, ...), custom_call_target="tpu_custom_call" | custom-call | flops 500000000 | bytes 1048576 | tf_op jit(solution)/shard_map/project/pallas_call | solution.py:116
  61.0 5.4 %project.5 = (bf16[1280,256]{1,0:T(8,128)(2,1)S(1)}, bf16[1280,256]{1,0:T(8,128)(2,1)S(1)}, bf16[256,1024]{1,0:T(8,128)(2,1)S(1)}) custom-call(s32[46]{0:T(128)S(1)} %dynamic-slice_bitcast_fusion.refs_0_, bf16[256,512]{1,0:T(8,128)(2,1)S(1)} %get-tuple-element.52.refs_1_, bf16[512,2048]{1,0:T(8,128)(2,1)S(1)} %bitcast.14, bf16[512,2048]{1,0:T(8,128)(2,1)S(1)} %bitcast.15, ...), custom_call_target="tpu_custom_call" | custom-call | flops 500000000 | bytes 1048576 | tf_op jit(solution)/shard_map/project/pallas_call | solution.py:116
  68.7 3.1 %collective-permute-done.refs_2_.refs_3_.refs_5_ = bf16[512,2048]{1,0:T(8,128)(2,1)S(1)} collective-permute-done((bf16[512,2048]{1,0:T(8,128)(2,1)}, bf16[512,2048]{1,0:T(8,128)(2,1)S(1)}, u32[]{:S(2)}, u32[]{:S(2)}) %collective-permute-start) | collective-permute-done | bytes 2097184 | tf_op jit(solution)/shard_map/ppermute | solution.py:80
  71.7 4.8 %collective-permute-start.25 = (bf16[512,2048]{1,0:T(8,128)(2,1)S(1)}, bf16[512,2048]{1,0:T(8,128)(2,1)S(1)}, u32[]{:S(2)}, u32[]{:S(2)}) collective-permute-start(bf16[512,2048]{1,0:T(8,128)(2,1)S(1)} %collective-permute-done.refs_2_.refs_3_.refs_5_), channel_id=1, source_target_pairs={{0,1},{1,0},{2,3},{3,2},{4,5},{5,4},{6,7},{7,6},{8,9},{9,8},{10,11... | collective-permute-start | bytes 6291464 | tf_op jit(solution)/shard_map/ppermute | solution.py:80
  76.5 5.3 %project.7 = (bf16[1280,256]{1,0:T(8,128)(2,1)S(1)}, bf16[1280,256]{1,0:T(8,128)(2,1)S(1)}, bf16[256,256]{1,0:T(8,128)(2,1)S(1)}, bf16[256,256]{1,0:T(8,128)(2,1)S(1)}) custom-call(s32[46]{0:T(128)S(1)} %dynamic-slice_bitcast_fusion.refs_0_, f32[64,256]{1,0:T(8,128)S(1)} %get-tuple-element.100.refs_1_.refs_4_.refs_9_.refs_5_.refs_7_, ...), custom_call_target="tpu_custom_call" | custom-call | flops 500000000 | bytes 1048576 | tf_op jit(solution)/shard_map/project/pallas_call | solution.py:116
  82.8 5.7 %project.6 = (bf16[1280,256]{1,0:T(8,128)(2,1)S(1)}, bf16[1280,256]{1,0:T(8,128)(2,1)S(1)}, bf16[256,512]{1,0:T(8,128)(2,1)S(1)}) custom-call(s32[46]{0:T(128)S(1)} %dynamic-slice_bitcast_fusion.refs_0_, f32[64,256]{1,0:T(8,128)S(1)} %get-tuple-element.100.refs_1_.refs_4_.refs_9_.refs_5_.refs_7_, ...), custom_call_target="tpu_custom_call" | custom-call | flops 500000000 | bytes 1048576 | tf_op jit(solution)/shard_map/project/pallas_call | solution.py:116
  90.0 4.5 %attend.3 = (bf16[640,512]{1,0:T(8,128)(2,1)S(1)}, bf16[640,512]{1,0:T(8,128)(2,1)S(1)}, bf16[160,512]{1,0:T(8,128)(2,1)S(1)}, bf16[160,512]{1,0:T(8,128)(2,1)S(1)}) custom-call(s32[46]{0:T(128)S(1)} %dynamic-slice_bitcast_fusion.refs_0_, bf16[1280,256]{1,0:T(8,128)(2,1)S(1)} %get-tuple-element.57.refs_1_, ...), custom_call_target="tpu_custom_call" | custom-call | flops 8000000000 | bytes 1048576 | tf_op jit(solution)/shard_map/attend/pallas_call | solution.py:116
  96.7 2.7 %attend.4 = (bf16[640,256]{1,0:T(8,128)(2,1)S(1)}, bf16[640,256]{1,0:T(8,128)(2,1)S(1)}, bf16[160,256]{1,0:T(8,128)(2,1)S(1)}, bf16[160,256]{1,0:T(8,128)(2,1)S(1)}) custom-call(s32[46]{0:T(128)S(1)} %dynamic-slice_bitcast_fusion.refs_0_, bf16[1280,256]{1,0:T(8,128)(2,1)S(1)} %get-tuple-element.67.refs_1_, ...), custom_call_target="tpu_custom_call" | custom-call | flops 4499999744 | bytes 1048576 | tf_op jit(solution)/shard_map/attend/pallas_call | solution.py:116
  102.5 3.5 %collective-permute-done.20 = bf16[160,512]{1,0:T(8,128)(2,1)S(1)} collective-permute-done((bf16[160,512]{1,0:T(8,128)(2,1)S(1)}, bf16[160,512]{1,0:T(8,128)(2,1)S(1)}, u32[]{:S(2)}, u32[]{:S(2)}) %collective-permute-start.20) | collective-permute-done | bytes 163872 | tf_op jit(solution)/shard_map/ppermute | solution.py:80
  106.0 2.7 %attend.5 = (bf16[640,256]{1,0:T(8,128)(2,1)S(1)}, bf16[640,256]{1,0:T(8,128)(2,1)S(1)}, bf16[160,512]{1,0:T(8,128)(2,1)S(1)}, bf16[160,512]{1,0:T(8,128)(2,1)S(1)}) custom-call(s32[46]{0:T(128)S(1)} %dynamic-slice_bitcast_fusion.refs_0_, bf16[160,256]{1,0:T(8,128)(2,1)S(1)} %get-tuple-element.73.refs_1_, bf16[160,256]{1,0:T(8,128)(2,1)S(1)} %get-tuple-element.74.refs_2_, ...), custom_call_target="tpu_custom_call" | custom-call | flops 4499999744 | bytes 1048576 | tf_op jit(solution)/shard_map/attend/pallas_call | solution.py:116
  112.2 4.5 %weight_gradient.3.refs_7_.refs_8_.refs_9_.refs_10_ = f32[640,2048]{1,0:T(8,128)S(1)} custom-call(s32[46]{0:T(128)S(1)} %dynamic-slice_bitcast_fusion.refs_0_, bf16[640,256]{1,0:T(8,128)(2,1)S(1)} %get-tuple-element.80.refs_1_, bf16[640,256]{1,0:T(8,128)(2,1)S(1)} %get-tuple-element.81.refs_2_, bf16[640,256]{1,0:T(8,128)(2,1)S(1)} %collective-permute-done.26.refs_3_, ...), custom_call_target="tpu_custom_call" | custom-call | flops 6000000000 | bytes 1048576 | tf_op jit(solution)/shard_map/weight_gradient/pallas_call | solution.py:306
  116.6 3.2 %collective-permute-done.24.refs_4_ = bf16[160,512]{1,0:T(8,128)(2,1)S(1)} collective-permute-done((bf16[160,512]{1,0:T(8,128)(2,1)S(1)}, bf16[160,512]{1,0:T(8,128)(2,1)S(1)}, u32[]{:S(2)}, u32[]{:S(2)}) %collective-permute-start.24) | collective-permute-done | bytes 163872 | tf_op jit(solution)/shard_map/ppermute | solution.py:80
  119.8 4.7 %weight_gradient.5 = (bf16[80,2048]{1,0:T(8,128)(2,1)S(1)}, bf16[80,2048]{1,0:T(8,128)(2,1)S(1)}, bf16[80,2048]{1,0:T(8,128)(2,1)S(1)}, bf16[80,2048]{1,0:T(8,128)(2,1)S(1)}) custom-call(s32[46]{0:T(128)S(1)} %dynamic-slice_bitcast_fusion.refs_0_, bf16[640,512]{1,0:T(8,128)(2,1)S(1)} %get-tuple-element.62.refs_1_, ...), custom_call_target="tpu_custom_call" | custom-call | flops 5000000000 | bytes 1048576 | tf_op jit(solution)/shard_map/weight_gradient/pallas_call | solution.py:306
  124.6 2.7 %collective-permute-start.31 = (bf16[80,2048]{1,0:T(8,128)(2,1)S(1)}, bf16[80,2048]{1,0:T(8,128)(2,1)S(1)}, u32[]{:S(2)}, u32[]{:S(2)}) collective-permute-start(bf16[80,2048]{1,0:T(8,128)(2,1)S(1)} %get-tuple-element.91), channel_id=1, source_target_pairs={{0,6},{1,7},{2,0},{3,1},{4,2},{5,3},{6,4},{7,5},{8,14},{9,15},{10,... | collective-permute-start | bytes 983048 | tf_op jit(solution)/shard_map/ppermute | solution.py:80
  127.3 2.7 %collective-permute-start.34 = (bf16[80,2048]{1,0:T(8,128)(2,1)S(1)}, bf16[80,2048]{1,0:T(8,128)(2,1)S(1)}, u32[]{:S(2)}, u32[]{:S(2)}) collective-permute-start(bf16[80,2048]{1,0:T(8,128)(2,1)S(1)} %get-tuple-element.94), channel_id=1, source_target_pairs={{0,6},{1,7},{2,0},{3,1},{4,2},{5,3},{6,4},{7,5},{8,14},{9,15},{10,... | collective-permute-start | bytes 983048 | tf_op jit(solution)/shard_map/ppermute | solution.py:80
  130.0 4.8 %weight_gradient.4 = (f32[80,2048]{1,0:T(8,128)S(1)}, f32[80,2048]{1,0:T(8,128)S(1)}, f32[80,2048]{1,0:T(8,128)S(1)}, f32[80,2048]{1,0:T(8,128)S(1)}) custom-call(s32[46]{0:T(128)S(1)} %dynamic-slice_bitcast_fusion.refs_0_, bf16[640,512]{1,0:T(8,128)(2,1)S(1)} %get-tuple-element.62.refs_1_, bf16[640,512]{1,0:T(8,128)(2,1)S(1)} %collective-permute-done.17.refs_2_, ...), custom_call_target="tpu_custom_call" | custom-call | flops 5000000000 | bytes 1048576 | tf_op jit(solution)/shard_map/weight_gradient/pallas_call | solution.py:306
  135.1 2.7 %collective-permute-start.35 = (bf16[80,2048]{1,0:T(8,128)(2,1)S(1)}, bf16[80,2048]{1,0:T(8,128)(2,1)S(1)}, u32[]{:S(2)}, u32[]{:S(2)}) collective-permute-start(bf16[80,2048]{1,0:T(8,128)(2,1)S(1)} %get-tuple-element.95), channel_id=1, source_target_pairs={{0,6},{1,7},{2,0},{3,1},{4,2},{5,3},{6,4},{7,5},{8,14},{9,15},{10,... | collective-permute-start | bytes 983048 | tf_op jit(solution)/shard_map/ppermute | solution.py:80
  137.8 4.2 %collective-permute-done.33.refs_3_ = bf16[80,2048]{1,0:T(8,128)(2,1)S(1)} collective-permute-done((bf16[80,2048]{1,0:T(8,128)(2,1)S(1)}, bf16[80,2048]{1,0:T(8,128)(2,1)S(1)}, u32[]{:S(2)}, u32[]{:S(2)}) %collective-permute-start.33) | collective-permute-done | bytes 327712 | tf_op jit(solution)/shard_map/ppermute | solution.py:80
  141.9 7.0 %collective-permute-done.32.refs_2_ = bf16[80,2048]{1,0:T(8,128)(2,1)S(1)} collective-permute-done((bf16[80,2048]{1,0:T(8,128)(2,1)S(1)}, bf16[80,2048]{1,0:T(8,128)(2,1)S(1)}, u32[]{:S(2)}, u32[]{:S(2)}) %collective-permute-start.32) | collective-permute-done | bytes 327712 | tf_op jit(solution)/shard_map/ppermute | solution.py:80
  (87 shorter events, 46.0 us)
Async XLA Ops:
  2.1 18.0 %collective-permute-start.6 = (bf16[160,2048]{1,0:T(8,128)(2,1)S(1)}, bf16[160,2048]{1,0:T(8,128)(2,1)S(1)}, u32[]{:S(2)}, u32[]{:S(2)}) collective-permute-start(bf16[160,2048]{1,0:T(8,128)(2,1)S(1)} %bitcast_convert_fusion.refs_6_), channel_id=1, source_target_pairs={{0,2},{1,3},{2,4},{3,5},{4,6},{5,7},{6,0},{7,1},{8,10},{9,11},{10,... | collective-permute-start | bytes 1966088 | tf_op jit(solution)/shard_map/ppermute | solution.py:80
  4.3 20.0 %collective-permute-start.1 = (bf16[160,2048]{1,0:T(8,128)(2,1)S(1)}, bf16[160,2048]{1,0:T(8,128)(2,1)}, u32[]{:S(2)}, u32[]{:S(2)}) collective-permute-start(bf16[160,2048]{1,0:T(8,128)(2,1)S(1)} %bitcast.24), channel_id=1, source_target_pairs={{0,16},{16,32},{32,48},{48,64},{64,80},{80,96},{96,112},{112,0},{1... | collective-permute-start | bytes 1966088 | tf_op jit(solution)/shard_map/ppermute | solution.py:409
  7.9 18.1 %collective-permute-start.5 = (bf16[160,2048]{1,0:T(8,128)(2,1)S(1)}, bf16[160,2048]{1,0:T(8,128)(2,1)}, u32[]{:S(2)}, u32[]{:S(2)}) collective-permute-start(bf16[160,2048]{1,0:T(8,128)(2,1)S(1)} %bitcast_convert_fusion.refs_6_), channel_id=1, source_target_pairs={{0,6},{1,7},{2,0},{3,1},{4,2},{5,3},{6,4},{7,5},{8,14},{9,15},{10,... | collective-permute-start | bytes 1966088 | tf_op jit(solution)/shard_map/ppermute | solution.py:80
  9.4 17.2 %collective-permute-start.8 = (bf16[160,2048]{1,0:T(8,128)(2,1)S(1)}, bf16[160,2048]{1,0:T(8,128)(2,1)S(1)}, u32[]{:S(2)}, u32[]{:S(2)}) collective-permute-start(bf16[160,2048]{1,0:T(8,128)(2,1)S(1)} %bitcast_convert_fusion.refs_6_), channel_id=1, source_target_pairs={{0,1},{1,0},{2,3},{3,2},{4,5},{5,4},{6,7},{7,6},{8,9},{9,8},{10,11... | collective-permute-start | bytes 1966088 | tf_op jit(solution)/shard_map/ppermute | solution.py:80
  20.2 16.3 %collective-permute-start.7 = (bf16[160,2048]{1,0:T(8,128)(2,1)S(1)}, bf16[160,2048]{1,0:T(8,128)(2,1)}, u32[]{:S(2)}, u32[]{:S(2)}) collective-permute-start(bf16[160,2048]{1,0:T(8,128)(2,1)S(1)} %collective-permute-done.6.refs_9_), channel_id=1, source_target_pairs={{0,2},{1,3},{2,4},{3,5},{4,6},{5,7},{6,0},{7,1},{8,10},{9,11},{10,... | collective-permute-start | bytes 1966088 | tf_op jit(solution)/shard_map/ppermute | solution.py:80
  20.2 18.5 %collective-permute-start.11 = (bf16[160,2048]{1,0:T(8,128)(2,1)S(1)}, bf16[160,2048]{1,0:T(8,128)(2,1)S(1)}, u32[]{:S(2)}, u32[]{:S(2)}) collective-permute-start(bf16[160,2048]{1,0:T(8,128)(2,1)S(1)} %collective-permute-done.6.refs_9_), channel_id=1, source_target_pairs={{0,1},{1,0},{2,3},{3,2},{4,5},{5,4},{6,7},{7,6},{8,9},{9,8},{10,11... | collective-permute-start | bytes 1966088 | tf_op jit(solution)/shard_map/ppermute | solution.py:80
  24.3 15.1 %collective-permute-start.2 = (bf16[160,2048]{1,0:T(8,128)(2,1)}, bf16[160,2048]{1,0:T(8,128)(2,1)}, u32[]{:S(2)}, u32[]{:S(2)}) collective-permute-start(bf16[160,2048]{1,0:T(8,128)(2,1)} %collective-permute-done.1.refs_6_), channel_id=1, source_target_pairs={{0,6},{1,7},{2,0},{3,1},{4,2},{5,3},{6,4},{7,5},{8,14},{9,15},{10,... | collective-permute-start | bytes 1966088 | tf_op jit(solution)/shard_map/ppermute | solution.py:80
  26.0 45.7 %collective-permute-start = (bf16[512,2048]{1,0:T(8,128)(2,1)}, bf16[512,2048]{1,0:T(8,128)(2,1)S(1)}, u32[]{:S(2)}, u32[]{:S(2)}) collective-permute-start(bf16[512,2048]{1,0:T(8,128)(2,1)} %bitcast.11), channel_id=1, source_target_pairs={{0,8},{1,9},{2,10},{3,11},{4,12},{5,13},{6,14},{7,15},{8,0},{9,1},... | collective-permute-start | bytes 6291464 | tf_op jit(solution)/shard_map/ppermute | solution.py:80
  27.5 16.0 %collective-permute-start.9 = (bf16[160,2048]{1,0:T(8,128)(2,1)}, bf16[160,2048]{1,0:T(8,128)(2,1)}, u32[]{:S(2)}, u32[]{:S(2)}) collective-permute-start(bf16[160,2048]{1,0:T(8,128)(2,1)} %collective-permute-done.5.refs_7_), channel_id=1, source_target_pairs={{0,1},{1,0},{2,3},{3,2},{4,5},{5,4},{6,7},{7,6},{8,9},{9,8},{10,11... | collective-permute-start | bytes 1966088 | tf_op jit(solution)/shard_map/ppermute | solution.py:80
  39.5 17.9 %collective-permute-start.4 = (bf16[160,2048]{1,0:T(8,128)(2,1)}, bf16[160,2048]{1,0:T(8,128)(2,1)}, u32[]{:S(2)}, u32[]{:S(2)}) collective-permute-start(bf16[160,2048]{1,0:T(8,128)(2,1)} %collective-permute-done.1.refs_6_), channel_id=1, source_target_pairs={{0,2},{1,3},{2,4},{3,5},{4,6},{5,7},{6,0},{7,1},{8,10},{9,11},{10,... | collective-permute-start | bytes 1966088 | tf_op jit(solution)/shard_map/ppermute | solution.py:80
  39.5 17.9 %collective-permute-start.3 = (bf16[160,2048]{1,0:T(8,128)(2,1)}, bf16[160,2048]{1,0:T(8,128)(2,1)}, u32[]{:S(2)}, u32[]{:S(2)}) collective-permute-start(bf16[160,2048]{1,0:T(8,128)(2,1)} %collective-permute-done.2.refs_7_), channel_id=1, source_target_pairs={{0,6},{1,7},{2,0},{3,1},{4,2},{5,3},{6,4},{7,5},{8,14},{9,15},{10,... | collective-permute-start | bytes 1966088 | tf_op jit(solution)/shard_map/ppermute | solution.py:80
  43.4 14.7 %collective-permute-start.12 = (bf16[160,2048]{1,0:T(8,128)(2,1)}, bf16[160,2048]{1,0:T(8,128)(2,1)S(1)}, u32[]{:S(2)}, u32[]{:S(2)}) collective-permute-start(bf16[160,2048]{1,0:T(8,128)(2,1)} %collective-permute-done.1.refs_6_), channel_id=1, source_target_pairs={{0,1},{1,0},{2,3},{3,2},{4,5},{5,4},{6,7},{7,6},{8,9},{9,8},{10,11... | collective-permute-start | bytes 1966088 | tf_op jit(solution)/shard_map/ppermute | solution.py:80
  46.1 12.0 %collective-permute-start.13 = (bf16[160,2048]{1,0:T(8,128)(2,1)}, bf16[160,2048]{1,0:T(8,128)(2,1)S(1)}, u32[]{:S(2)}, u32[]{:S(2)}) collective-permute-start(bf16[160,2048]{1,0:T(8,128)(2,1)} %collective-permute-done.2.refs_7_), channel_id=1, source_target_pairs={{0,1},{1,0},{2,3},{3,2},{4,5},{5,4},{6,7},{7,6},{8,9},{9,8},{10,11... | collective-permute-start | bytes 1966088 | tf_op jit(solution)/shard_map/ppermute | solution.py:80
  66.4 22.7 %collective-permute-start.16 = (bf16[256,1024]{1,0:T(8,128)(2,1)S(1)}, bf16[256,1024]{1,0:T(8,128)(2,1)S(1)}, u32[]{:S(2)}, u32[]{:S(2)}) collective-permute-start(bf16[256,1024]{1,0:T(8,128)(2,1)S(1)} %get-tuple-element.58), channel_id=1, source_target_pairs={{0,8},{1,9},{2,10},{3,11},{4,12},{5,13},{6,14},{7,15},{8,0},{9,1},... | collective-permute-start | bytes 1572872 | tf_op jit(solution)/shard_map/ppermute | solution.py:80
  68.0 41.9 %collective-permute-start.29 = (bf16[512,2048]{1,0:T(8,128)(2,1)S(1)}, bf16[512,2048]{1,0:T(8,128)(2,1)S(1)}, u32[]{:S(2)}, u32[]{:S(2)}) collective-permute-start(bf16[512,2048]{1,0:T(8,128)(2,1)S(1)} %bitcast.16), channel_id=1, source_target_pairs={{0,1},{1,0},{2,3},{3,2},{4,5},{5,4},{6,7},{7,6},{8,9},{9,8},{10,11... | collective-permute-start | bytes 6291464 | tf_op jit(solution)/shard_map/ppermute | solution.py:80
  71.7 48.1 %collective-permute-start.25 = (bf16[512,2048]{1,0:T(8,128)(2,1)S(1)}, bf16[512,2048]{1,0:T(8,128)(2,1)S(1)}, u32[]{:S(2)}, u32[]{:S(2)}) collective-permute-start(bf16[512,2048]{1,0:T(8,128)(2,1)S(1)} %collective-permute-done.refs_2_.refs_3_.refs_5_), channel_id=1, source_target_pairs={{0,1},{1,0},{2,3},{3,2},{4,5},{5,4},{6,7},{7,6},{8,9},{9,8},{10,11... | collective-permute-start | bytes 6291464 | tf_op jit(solution)/shard_map/ppermute | solution.py:80
  81.8 12.8 %collective-permute-start.22 = (bf16[256,256]{1,0:T(8,128)(2,1)S(1)}, bf16[256,256]{1,0:T(8,128)(2,1)S(1)}, u32[]{:S(2)}, u32[]{:S(2)}) collective-permute-start(bf16[256,256]{1,0:T(8,128)(2,1)S(1)} %get-tuple-element.69), channel_id=1, source_target_pairs={{0,8},{1,9},{2,10},{3,11},{4,12},{5,13},{6,14},{7,15},{8,0},{9,1},... | collective-permute-start | bytes 393224 | tf_op jit(solution)/shard_map/ppermute | solution.py:80
  99.4 11.0 %collective-permute-start.26 = (bf16[640,256]{1,0:T(8,128)(2,1)S(1)}, bf16[640,256]{1,0:T(8,128)(2,1)S(1)}, u32[]{:S(2)}, u32[]{:S(2)}) collective-permute-start(bf16[640,256]{1,0:T(8,128)(2,1)S(1)} %get-tuple-element.82), channel_id=1, source_target_pairs={{0,1},{1,0},{2,3},{3,2},{4,5},{5,4},{6,7},{7,6},{8,9},{9,8},{10,11... | collective-permute-start | bytes 983048 | tf_op jit(solution)/shard_map/ppermute | solution.py:80
  124.5 10.4 %collective-permute-start.30 = (bf16[80,2048]{1,0:T(8,128)(2,1)S(1)}, bf16[80,2048]{1,0:T(8,128)(2,1)S(1)}, u32[]{:S(2)}, u32[]{:S(2)}) collective-permute-start(bf16[80,2048]{1,0:T(8,128)(2,1)S(1)} %get-tuple-element.89), channel_id=1, source_target_pairs={{0,2},{1,3},{2,4},{3,5},{4,6},{5,7},{6,0},{7,1},{8,10},{9,11},{10,... | collective-permute-start | bytes 983048 | tf_op jit(solution)/shard_map/ppermute | solution.py:80
  124.6 10.3 %collective-permute-start.31 = (bf16[80,2048]{1,0:T(8,128)(2,1)S(1)}, bf16[80,2048]{1,0:T(8,128)(2,1)S(1)}, u32[]{:S(2)}, u32[]{:S(2)}) collective-permute-start(bf16[80,2048]{1,0:T(8,128)(2,1)S(1)} %get-tuple-element.91), channel_id=1, source_target_pairs={{0,6},{1,7},{2,0},{3,1},{4,2},{5,3},{6,4},{7,5},{8,14},{9,15},{10,... | collective-permute-start | bytes 983048 | tf_op jit(solution)/shard_map/ppermute | solution.py:80
  127.3 14.7 %collective-permute-start.33 = (bf16[80,2048]{1,0:T(8,128)(2,1)S(1)}, bf16[80,2048]{1,0:T(8,128)(2,1)S(1)}, u32[]{:S(2)}, u32[]{:S(2)}) collective-permute-start(bf16[80,2048]{1,0:T(8,128)(2,1)S(1)} %get-tuple-element.93), channel_id=1, source_target_pairs={{0,2},{1,3},{2,4},{3,5},{4,6},{5,7},{6,0},{7,1},{8,10},{9,11},{10,... | collective-permute-start | bytes 983048 | tf_op jit(solution)/shard_map/ppermute | solution.py:80
  127.3 14.7 %collective-permute-start.34 = (bf16[80,2048]{1,0:T(8,128)(2,1)S(1)}, bf16[80,2048]{1,0:T(8,128)(2,1)S(1)}, u32[]{:S(2)}, u32[]{:S(2)}) collective-permute-start(bf16[80,2048]{1,0:T(8,128)(2,1)S(1)} %get-tuple-element.94), channel_id=1, source_target_pairs={{0,6},{1,7},{2,0},{3,1},{4,2},{5,3},{6,4},{7,5},{8,14},{9,15},{10,... | collective-permute-start | bytes 983048 | tf_op jit(solution)/shard_map/ppermute | solution.py:80
  135.0 13.9 %collective-permute-start.32 = (bf16[80,2048]{1,0:T(8,128)(2,1)S(1)}, bf16[80,2048]{1,0:T(8,128)(2,1)S(1)}, u32[]{:S(2)}, u32[]{:S(2)}) collective-permute-start(bf16[80,2048]{1,0:T(8,128)(2,1)S(1)} %get-tuple-element.92), channel_id=1, source_target_pairs={{0,2},{1,3},{2,4},{3,5},{4,6},{5,7},{6,0},{7,1},{8,10},{9,11},{10,... | collective-permute-start | bytes 983048 | tf_op jit(solution)/shard_map/ppermute | solution.py:80
  135.1 13.8 %collective-permute-start.35 = (bf16[80,2048]{1,0:T(8,128)(2,1)S(1)}, bf16[80,2048]{1,0:T(8,128)(2,1)S(1)}, u32[]{:S(2)}, u32[]{:S(2)}) collective-permute-start(bf16[80,2048]{1,0:T(8,128)(2,1)S(1)} %get-tuple-element.95), channel_id=1, source_target_pairs={{0,6},{1,7},{2,0},{3,1},{4,2},{5,3},{6,4},{7,5},{8,14},{9,15},{10,... | collective-permute-start | bytes 983048 | tf_op jit(solution)/shard_map/ppermute | solution.py:80
  (23 other events, 164.1 us)
